TPU v7x, 32 devices: a whole 2x2x4 slice. The times are simulated.
32 devices in a mesh: rep: 8 (over y, x, core), exp: 4 (over z).
Axes of the slice: x: 2, y: 2, z: 4, core: 2. Of those that a mesh axis runs over, the one named last changes fastest.
Arguments:
- inputs: bfloat16 [18912, 768], P(('rep', 'exp')), may hold values from -6 to 6
- routes: int32 [18912, 2], P(('rep', 'exp')), may hold values from 0 to 3, all different within a row; in each aligned block of 591 rows (0 to 590, 591 to 1181, ...) at most 591 rows name the same one
- ln1_gain: float32 [768], replicated, may hold values from 0.5 to 1.5
- ln1_bias: float32 [768], replicated, may hold values from -1.5 to 1.5
- w_qkv: bfloat16 [768, 2304], replicated, may hold values from -0.21875 to 0.21875
- query_bias: float32 [768], replicated, may hold values from -2.5 to 2.5
- value_bias: float32 [768], replicated, may hold values from -2.5 to 2.5
- w_out: bfloat16 [768, 768], replicated, may hold values from -1.75 to 1.75
- out_bias: float32 [768], replicated, may hold values from -2.5 to 2.5
- ln2_gain: float32 [768], replicated, may hold values from 0.5 to 1.5
- ln2_bias: float32 [768], replicated, may hold values from -1.5 to 1.5
- router: bfloat16 [768, 4], replicated, may hold values from -0.15625 to 0.15625
- experts_in: bfloat16 [4, 768, 3072], P('exp'), may hold values from -0.21875 to 0.21875
- experts_in_bias: float32 [4, 3072], P('exp'), may hold values from -2.5 to 2.5
- experts_out: bfloat16 [4, 3072, 768], P('exp'), may hold values from -0.875 to 0.875
- experts_out_bias: float32 [4, 768], P('exp'), may hold values from -4 to 4
- cotangent: bfloat16 [18912, 768], P(('rep', 'exp')), may hold values from -6 to 6
Outputs:
- out: bfloat16 [18912, 768], P(('rep', 'exp'))
- grad_inputs: bfloat16 [18912, 768], P(('rep', 'exp'))
- grad_ln1_gain: float32 [768], replicated
- grad_ln1_bias: float32 [768], replicated
- grad_w_qkv: float32 [768, 2304], replicated
- grad_query_bias: float32 [768], replicated
- grad_value_bias: float32 [768], replicated
- grad_w_out: float32 [768, 768], replicated
- grad_out_bias: float32 [768], replicated
- grad_ln2_gain: float32 [768], replicated
- grad_ln2_bias: float32 [768], replicated
- grad_router: float32 [768, 4], replicated
- grad_experts_in: float32 [4, 768, 3072], P('exp')
- grad_experts_in_bias: float32 [4, 3072], P('exp')
- grad_experts_out: float32 [4, 3072, 768], P('exp')
- grad_experts_out_bias: float32 [4, 768], P('exp')
Inputs may be any that keep to these rules, and one draw needn't show every extreme that they name: `routes`: each row names 2 different experts. Within the 591 rows of one device, no expert is named more than 591 times, a bound that some block reaches.
All inputs are finite; a program needn't handle non-finite values.
Results may differ from a plain program's by a relative error of at most 0.015.
Values may be sent and summed in bfloat16 or wider, within the bound.
No kernel may reach another device: no remote copies, remote signals or barrier semaphores. Data moves between devices by JAX's collectives and lax.ppermute only.
A program may use at most 256 MiB of HBM per device.

v0:
```python
import jax
import jax.numpy as jnp
from jax import lax
from jax.sharding import PartitionSpec as P

HEADS = 12
HEAD_DIM = 64
SEQ = 197


NORM_EPS = 1e-06


def layer_norm(values, gain_vec, offset):
    average = jnp.mean(values, axis=-1, keepdims=True)
    centred = values - average
    spread = jnp.mean(centred * centred, axis=-1, keepdims=True)
    return centred * lax.rsqrt(spread + NORM_EPS) * gain_vec + offset


def gelu_exact(values):
    return jax.nn.gelu(values, approximate=False)


def slot_table(route_ids, expert_count, capacity):
    flat_ids = route_ids.reshape(-1)
    one_hot = (flat_ids[:, None] == jnp.arange(expert_count, dtype=jnp.int32)[None, :]).astype(
        jnp.int32
    )
    earlier = jnp.cumsum(one_hot, axis=0) - one_hot
    position = jnp.sum(earlier * one_hot, axis=1)
    return flat_ids * capacity + position


def expert_front(rows, experts_in, experts_in_bias):
    pre_act = jnp.einsum("sjcd,jdf->sjcf", rows, experts_in, preferred_element_type=jnp.float32)
    pre_act = pre_act + experts_in_bias[None, :, None, :]
    activ_f, gelu_pull = jax.vjp(gelu_exact, pre_act)
    return (activ_f.astype(jnp.bfloat16), gelu_pull)


def on_device(
    inputs,
    routes,
    ln1_gain,
    ln1_bias,
    w_qkv,
    query_bias,
    value_bias,
    w_out,
    out_bias,
    ln2_gain,
    ln2_bias,
    router,
    experts_in,
    experts_in_bias,
    experts_out,
    experts_out_bias,
    cotangent,
):
    tok_count, model_width = inputs.shape
    top_count = routes.shape[1]
    groups = lax.axis_size("exp")
    local_experts = experts_in.shape[0]
    expert_count = local_experts * groups
    capacity = 4 * tok_count // expert_count
    slot_count = expert_count * capacity
    heads_shape = (tok_count // SEQ, SEQ, HEADS, HEAD_DIM)
    score_scale = HEAD_DIM ** (-0.5)
    inputs_f = inputs.astype(jnp.float32)
    normed_f, ln1_pull = jax.vjp(layer_norm, inputs_f, ln1_gain, ln1_bias)
    normed_b = normed_f.astype(jnp.bfloat16)
    joined = jnp.dot(normed_b, w_qkv, preferred_element_type=jnp.float32)
    query_b = (joined[:, :model_width] + query_bias).astype(jnp.bfloat16).reshape(heads_shape)
    key_b = joined[:, model_width : 2 * model_width].astype(jnp.bfloat16).reshape(heads_shape)
    value_b = (joined[:, 2 * model_width :] + value_bias).astype(jnp.bfloat16).reshape(heads_shape)
    scores = (
        jnp.einsum("bqhd,bkhd->bhqk", query_b, key_b, preferred_element_type=jnp.float32)
        * score_scale
    )
    top_score = jnp.max(scores, axis=-1, keepdims=True)
    log_total = top_score + jnp.log(jnp.sum(jnp.exp(scores - top_score), axis=-1, keepdims=True))
    probs_b = jnp.exp(scores - log_total).astype(jnp.bfloat16)
    context = jnp.einsum("bhqk,bkhd->bqhd", probs_b, value_b, preferred_element_type=jnp.float32)
    context_b = context.reshape(tok_count, model_width).astype(jnp.bfloat16)
    hidden = inputs_f + jnp.dot(context_b, w_out, preferred_element_type=jnp.float32) + out_bias
    mixed_f, ln2_pull = jax.vjp(layer_norm, hidden, ln2_gain, ln2_bias)
    mixed_b = mixed_f.astype(jnp.bfloat16)
    logits = jnp.dot(mixed_b, router, preferred_element_type=jnp.float32)
    gate_probs = jax.nn.softmax(logits, axis=-1)
    route_hot = (
        routes[:, :, None] == jnp.arange(expert_count, dtype=jnp.int32)[None, None, :]
    ).astype(jnp.float32)
    gate_vals = jnp.sum(gate_probs[:, None, :] * route_hot, axis=-1)
    slot_ids = slot_table(routes, expert_count, capacity)
    send_rows = (
        jnp.zeros((slot_count, model_width), jnp.bfloat16)
        .at[slot_ids]
        .set(jnp.repeat(mixed_b, top_count, axis=0))
        .reshape(groups, local_experts, capacity, model_width)
    )
    received = lax.all_to_all(send_rows, "exp", split_axis=0, concat_axis=0, tiled=True)
    activ_b, gelu_pull = expert_front(received, experts_in, experts_in_bias)
    expert_out = jnp.einsum(
        "sjcf,jfd->sjcd", activ_b, experts_out, preferred_element_type=jnp.float32
    )
    expert_out = (expert_out + experts_out_bias[None, :, None, :]).astype(jnp.bfloat16)
    returned = lax.all_to_all(expert_out, "exp", split_axis=0, concat_axis=0, tiled=True)
    returned_rows = returned.reshape(slot_count, model_width)[slot_ids].reshape(
        tok_count, top_count, model_width
    )
    returned_f = returned_rows.astype(jnp.float32)
    result = hidden + jnp.sum(gate_vals[:, :, None] * returned_f, axis=1)
    upstream = cotangent.astype(jnp.float32)
    route_grad = jnp.sum(upstream[:, None, :] * returned_f, axis=-1)
    sent_grad = (
        (gate_vals[:, :, None] * upstream[:, None, :])
        .astype(jnp.bfloat16)
        .reshape(tok_count * top_count, model_width)
    )
    grad_buffer = jnp.zeros((slot_count, model_width), jnp.bfloat16).at[slot_ids].set(sent_grad)
    grad_buffer = grad_buffer.reshape(groups, local_experts, capacity, model_width)
    grad_rows = lax.all_to_all(grad_buffer, "exp", split_axis=0, concat_axis=0, tiled=True)
    activ_back, pull_back = (activ_b, gelu_pull)
    grad_eout_w = jnp.einsum(
        "sjcf,sjcd->jfd", activ_back, grad_rows, preferred_element_type=jnp.float32
    )
    grad_eout_b = jnp.sum(grad_rows.astype(jnp.float32), axis=(0, 2))
    grad_activ = jnp.einsum(
        "sjcd,jfd->sjcf", grad_rows, experts_out, preferred_element_type=jnp.float32
    )
    grad_pre = pull_back(grad_activ)[0].astype(jnp.bfloat16)
    grad_ein_w = jnp.einsum(
        "sjcd,sjcf->jdf", received, grad_pre, preferred_element_type=jnp.float32
    )
    grad_ein_b = jnp.sum(grad_pre.astype(jnp.float32), axis=(0, 2))
    grad_rows_in = jnp.einsum(
        "sjcf,jdf->sjcd", grad_pre, experts_in, preferred_element_type=jnp.float32
    ).astype(jnp.bfloat16)
    grad_back = lax.all_to_all(grad_rows_in, "exp", split_axis=0, concat_axis=0, tiled=True)
    grad_routed = grad_back.reshape(slot_count, model_width)[slot_ids].reshape(
        tok_count, top_count, model_width
    )
    grad_probs = jnp.sum(route_grad[:, :, None] * route_hot, axis=1)
    grad_logits = (
        gate_probs * (grad_probs - jnp.sum(grad_probs * gate_probs, axis=-1, keepdims=True))
    ).astype(jnp.bfloat16)
    grad_router = jnp.einsum("td,te->de", mixed_b, grad_logits, preferred_element_type=jnp.float32)
    grad_mixed = jnp.einsum("te,de->td", grad_logits, router, preferred_element_type=jnp.float32)
    grad_mixed = grad_mixed + jnp.sum(grad_routed.astype(jnp.float32), axis=1)
    grad_hidden_ln, grad_ln2_g, grad_ln2_b = ln2_pull(grad_mixed)
    grad_hidden = upstream + grad_hidden_ln
    grad_att = grad_hidden.astype(jnp.bfloat16)
    grad_wout = jnp.einsum("td,te->de", context_b, grad_att, preferred_element_type=jnp.float32)
    grad_obias = jnp.sum(grad_att.astype(jnp.float32), axis=0)
    grad_context = jnp.einsum("te,de->td", grad_att, w_out, preferred_element_type=jnp.float32)
    grad_context = grad_context.astype(jnp.bfloat16).reshape(heads_shape)
    scores_again = (
        jnp.einsum("bqhd,bkhd->bhqk", query_b, key_b, preferred_element_type=jnp.float32)
        * score_scale
    )
    probs_again = jnp.exp(scores_again - log_total)
    probs_again_b = probs_again.astype(jnp.bfloat16)
    grad_value = jnp.einsum(
        "bhqk,bqhd->bkhd", probs_again_b, grad_context, preferred_element_type=jnp.float32
    ).astype(jnp.bfloat16)
    grad_weights = jnp.einsum(
        "bqhd,bkhd->bhqk", grad_context, value_b, preferred_element_type=jnp.float32
    )
    row_inner = jnp.sum(grad_weights * probs_again, axis=-1, keepdims=True)
    grad_scores = (probs_again * (grad_weights - row_inner)).astype(jnp.bfloat16)
    grad_query = (
        jnp.einsum("bhqk,bkhd->bqhd", grad_scores, key_b, preferred_element_type=jnp.float32)
        * score_scale
    ).astype(jnp.bfloat16)
    grad_key = (
        jnp.einsum("bhqk,bqhd->bkhd", grad_scores, query_b, preferred_element_type=jnp.float32)
        * score_scale
    ).astype(jnp.bfloat16)
    grad_joined = jnp.concatenate(
        [
            grad_query.reshape(tok_count, model_width),
            grad_key.reshape(tok_count, model_width),
            grad_value.reshape(tok_count, model_width),
        ],
        axis=1,
    )
    grad_wqkv = jnp.einsum("td,te->de", normed_b, grad_joined, preferred_element_type=jnp.float32)
    grad_qbias = jnp.sum(grad_joined[:, :model_width].astype(jnp.float32), axis=0)
    grad_vbias = jnp.sum(grad_joined[:, 2 * model_width :].astype(jnp.float32), axis=0)
    grad_normed = jnp.einsum("te,de->td", grad_joined, w_qkv, preferred_element_type=jnp.float32)
    grad_in_ln, grad_ln1_g, grad_ln1_b = ln1_pull(grad_normed)
    grad_inputs = (grad_hidden + grad_in_ln).astype(jnp.bfloat16)
    expert_sums = (
        lax.psum(grad_ein_w.astype(jnp.bfloat16), "rep").astype(jnp.float32),
        lax.psum(grad_ein_b.astype(jnp.bfloat16), "rep").astype(jnp.float32),
        lax.psum(grad_eout_w.astype(jnp.bfloat16), "rep").astype(jnp.float32),
        lax.psum(grad_eout_b.astype(jnp.bfloat16), "rep").astype(jnp.float32),
    )
    dense_sums = lax.psum(
        (
            grad_ln1_g,
            grad_ln1_b,
            grad_wqkv,
            grad_qbias,
            grad_vbias,
            grad_wout,
            grad_obias,
            grad_ln2_g,
            grad_ln2_b,
            grad_router,
        ),
        ("rep", "exp"),
    )
    return (
        result.astype(jnp.bfloat16),
        grad_inputs,
        dense_sums[0],
        dense_sums[1],
        dense_sums[2],
        dense_sums[3],
        dense_sums[4],
        dense_sums[5],
        dense_sums[6],
        dense_sums[7],
        dense_sums[8],
        dense_sums[9],
        expert_sums[0],
        expert_sums[1],
        expert_sums[2],
        expert_sums[3],
    )


def solution(mesh):
    placed = (
        P(("rep", "exp"), None),
        P(("rep", "exp"), None),
        P(),
        P(),
        P(),
        P(),
        P(),
        P(),
        P(),
        P(),
        P(),
        P(),
        P("exp", None, None),
        P("exp", None),
        P("exp", None, None),
        P("exp", None),
        P(("rep", "exp"), None),
    )
    return jax.shard_map(
        on_device,
        mesh=mesh,
        in_specs=placed,
        out_specs=(
            P(("rep", "exp"), None),
            P(("rep", "exp"), None),
            P(),
            P(),
            P(),
            P(),
            P(),
            P(),
            P(),
            P(),
            P(),
            P(),
            P("exp", None, None),
            P("exp", None),
            P("exp", None, None),
            P("exp", None),
        ),
        check_vma=False,
    )
```

profile of v0, /device:TPU:0, one launch (start us, length us, event | category | flops | bytes accessed | tf_op | source)
XLA Modules:
  0.0 855.6 jit_solution(5647185600215041906)
XLA Ops:
  19.2 3.1 reduce-window.6
  26.8 3.7 fusion.93
  33.1 4.0 reshape.319
  37.1 4.2 copy.130
  41.3 4.0 reshape.320
  45.3 4.2 copy.131
  49.5 4.0 reshape.318
  53.5 4.2 copy.132
  57.7 2.9 multiply_reduce_fusion.1
  63.7 2.2 copy.134
  65.9 4.3 convert_element_type.163
  70.2 2.9 fusion.101
  78.4 4.9 reshape.302
  84.0 11.1 %scatter_custom_fusion = bf16[2364,768]{1,0:T(8,128)(2,1)} fusion(s32[1182]{0:T(1024)S(1)} %fusion.86, bf16[1182,768]{1,0:T(8,128)(2,1)} %reshape.302, bf16[]{:T(256)} %constant.17.clone.1), kind=kCustom, calls=%fused_computation.105 | custom fusion | bytes 3631616 | tf_op jit(solution)/shard_map/scatter | solution.py:99
  95.1 4.7 reshape.265
  99.9 16.2 %all-to-all-start = ((bf16[4,1,591,768]{3,2,1,0:T(8,128)(2,1)}), bf16[4,1,591,768]{3,2,1,0:T(8,128)(2,1)}, u32[]{:S(2)}, u32[]{:S(2)}) async-start(bf16[4,1,591,768]{3,2,1,0:T(8,128)(2,1)} %bitcast.274), calls=%async_computation | async-start | bytes 7274496 | tf_op jit(solution)/shard_map/all_to_all | solution.py:102
  116.1 2.6 convert_element_type.172
  118.7 3.9 mul.261
  122.6 5.4 mul.269
  134.1 15.9 %scatter_custom_fusion.1 = bf16[2364,768]{1,0:T(8,128)(2,1)} fusion(s32[1182]{0:T(1024)S(1)} %fusion.86, f32[1182,768]{1,0:T(8,128)} %mul.269, f32[1182]{0:T(1024)S(1)} %mul.267, bf16[]{:T(256)} %constant.17.clone.1), kind=kCustom, calls=%fused_computation.91 | custom fusion | flops 1815552 | bytes 7270402 | tf_op jit(solution)/shard_map/scatter | solution.py:121
  150.0 4.8 reshape.271
  156.1 41.6 %all-to-all-done = bf16[4,1,591,768]{3,2,1,0:T(8,128)(2,1)} async-done(((bf16[4,1,591,768]{3,2,1,0:T(8,128)(2,1)}), bf16[4,1,591,768]{3,2,1,0:T(8,128)(2,1)}, u32[]{:S(2)}, u32[]{:S(2)}) %all-to-all-start) | async-done | bytes 3631136 | tf_op jit(solution)/shard_map/all_to_all | solution.py:102
  197.7 4.8 all-to-all-start.2
  202.5 19.6 %fusion.39 = f32[4,591,3072]{2,1,0:T(8,128)} fusion(bf16[1,768,3072]{2,1,0:T(8,128)(2,1)} %param.29, bf16[4,1,591,768]{3,2,1,0:T(8,128)(2,1)} %all-to-all-done), kind=kOutput, calls=%fused_computation.57 | convolution fusion | flops 11154751488 | bytes 37398528 | tf_op jit(solution)/shard_map/sjcd,jdf->sjcf/dot_general | solution.py:36
  222.1 78.8 %fusion.45 = bf16[4,1,591,768]{3,2,1,0:T(8,128)(2,1)} fusion(f32[768]{0:T(1024)S(1)} %reduce.12, bf16[1,3072,768]{2,1,0:T(8,128)(2,1)} %param.31, f32[4,591,3072]{2,1,0:T(8,128)} %fusion.39, f32[3072]{0:T(1024)S(1)} %bitcast.280), kind=kOutput, calls=%fused_computation.61 | convolution fusion | flops 11637688320 | bytes 37413888 | tf_op jit(solution)/shard_map/sjcf,jfd->sjcd/dot_general | solution.py:104
  301.0 5.0 all-to-all-start.1
  306.0 83.1 %fusion.103 = (bf16[3072]{0:T(1024)(128)(2,1)}, bf16[4,1,591,3072]{3,2,0,1:T(8,128)(2,1)}) fusion(bf16[1,3072,768]{2,1,0:T(8,128)(2,1)} %param.31, bf16[4,1,591,768]{3,2,1,0:T(8,128)(2,1)} %all-to-all-done.2, f32[3072]{0:T(1024)S(1)} %bitcast.281, f32[4,591,3072]{2,1,0:T(8,128)} %fusion.39), kind=kOutput, calls=%fused_computation.162 | convolution fusion | flops 11692151808 | bytes 51941376 | tf_op jit(solution)/shard_map/sjcd,jfd->sjcf/dot_general | solution.py:129
  389.1 16.1 %convert_bitcast_fusion = bf16[4,1,591,768]{3,2,1,0:T(8,128)(2,1)} fusion(bf16[1,768,3072]{2,1,0:T(8,128)(2,1)S(1)} %copy-done.49, bf16[4,1,591,3072]{3,2,0,1:T(8,128)(2,1)} %get-tuple-element.61), kind=kOutput, calls=%fused_computation.66 | convolution fusion | flops 11156567040 | bytes 22874112 | tf_op jit(solution)/shard_map/sjcf,jdf->sjcd/dot_general | solution.py:137
  405.2 5.1 all-to-all-start.3
  410.3 75.4 %fusion.41 = bf16[1,3072,768]{2,1,0:T(8,128)(2,1)} fusion(bf16[4,1,591,768]{3,2,1,0:T(8,128)(2,1)} %all-to-all-done.2, f32[4,591,3072]{2,1,0:T(8,128)} %fusion.39, f32[3072]{0:T(1024)S(1)} %bitcast.282), kind=kOutput, calls=%fused_computation.59 | convolution fusion | flops 11636416512 | bytes 37410816 | tf_op jit(solution)/shard_map/sjcf,sjcd->jfd/dot_general | solution.py:125
  485.7 15.6 %fusion.42 = bf16[1,768,3072]{2,1,0:T(8,128)(2,1)} fusion(bf16[4,1,591,3072]{3,2,0,1:T(8,128)(2,1)S(1)} %copy-done.54, bf16[4,1,591,768]{3,2,1,0:T(8,128)(2,1)} %all-to-all-done), kind=kOutput, calls=%fused_computation.60 | convolution fusion | flops 11157110784 | bytes 22874112 | tf_op jit(solution)/shard_map/sjcd,sjcf->jdf/dot_general | solution.py:133
  501.3 4.8 reshape.270
  506.1 8.2 gather_fusion
  514.4 5.1 reshape.280
  519.5 11.1 %multiply_reduce_fusion.2 = (f32[591,2]{1,0:T(8,128)}, f32[591,768]{1,0:T(8,128)}) fusion(f32[591,2,768]{2,1,0:T(2,128)} %reshape.280, f32[591,768]{1,0:T(8,128)} %convert_element_type.172, f32[591,2]{1,0:T(8,128)} %copy.135), kind=kLoop, calls=%fused_computation.68 | loop fusion | flops 3176034 | bytes 7271664 | tf_op jit(solution)/shard_map/reduce_sum | solution.py:115
  535.1 4.9 reshape.274
  540.0 8.5 gather_fusion.1
  548.5 5.5 reshape.281
  554.0 8.4 reduce_sum.304
  562.4 3.8 multiply_reduce_fusion.4
  566.9 3.8 fusion.100
  575.7 4.0 reshape.321
  579.8 4.3 copy.145
  584.0 5.6 convert_reduce_fusion.1
  589.7 2.2 copy.155
  591.8 4.2 reshape.278
  596.0 6.2 multiply_reduce_fusion
  602.2 4.5 multiply_convert_fusion
  609.8 2.2 copy.152
  612.0 4.0 reshape.277
  616.0 4.0 convert_reduce_fusion.2
  620.0 2.2 copy.149
  622.1 4.1 reshape.276
  630.4 5.0 fusion.104
  635.5 5.6 fusion.91
  641.1 2.6 reduce_sum.321
  645.0 24.5 %all-reduce.3 = (bf16[1,3072]{1,0:T(2,128)(2,1)}, bf16[1,768]{1,0:T(2,128)(2,1)}) all-reduce(bf16[1,3072]{1,0:T(2,128)(2,1)S(1)} %reduce_sum.320, bf16[1,768]{1,0:T(2,128)(2,1)} %reduce_sum.322), channel_id=1, replica_groups=mesh['rep'=8,'exp'=4] {'rep'}, use_global_device_ids=true, to_apply=%region_43.44 | all-reduce | flops 3840 | bytes 15360 | tf_op jit(solution)/shard_map/psum | solution.py:196
  672.1 7.7 convert_element_type.197
  679.8 4.5 convert_element_type.201
  686.3 5.5 fusion.98
  693.6 42.8 %all-reduce.1 = (f32[768]{0:T(1024)}, f32[768]{0:T(1024)}, f32[768]{0:T(1024)}, f32[768]{0:T(1024)}, f32[768]{0:T(1024)}, /*index=5*/f32[768]{0:T(1024)}, f32[768]{0:T(1024)}, f32[768,4]{0,1:T(4,128)}) all-reduce(f32[768]{0:T(1024)} %get-tuple-element.20, ...), channel_id=1, replica_groups=mesh['rep'=8,'exp'=4] {'rep','exp'}, use_global_device_ids=true, to_apply=%region_25.26 | all-reduce | flops 8448 | bytes 67584 | tf_op jit(solution)/shard_map/psum | solution.py:200
  737.1 3.9 add_convert_fusion
  741.0 99.5 %all-reduce.8.cloned.1.call-done = (f32[768,2304]{1,0:T(8,128)}, f32[768,768]{1,0:T(8,128)}) async-done(((f32[768,2304]{1,0:T(8,128)}, f32[768,768]{1,0:T(8,128)}), (f32[768,2304]{1,0:T(8,128)}, f32[768,768]{1,0:T(8,128)})) %all-reduce.8.cloned.1.call-update) | async-done | bytes 9437200 | tf_op jit(solution)/shard_map/psum | solution.py:200
  840.5 6.6 copy.177
  (182 shorter events, 62.8 us)
Async XLA Ops:
  7.2 19.6 %copy-start = (bf16[768,2304]{1,0:T(8,128)(2,1)S(1)}, bf16[768,2304]{1,0:T(8,128)(2,1)}, u32[]{:S(2)}) copy-start(bf16[768,2304]{1,0:T(8,128)(2,1)} %param.21) | copy-start | bytes 10616836
  11.2 19.3 %copy-start.26 = (f32[591]{0:T(1024)}, f32[591]{0:T(1024)S(1)}, u32[]{:S(2)}) copy-start(f32[591]{0:T(1024)S(1)} %broadcast_multiply_fusion.2) | copy-start | bytes 7096
  12.8 0.6 copy-start.38
  13.4 17.1 %copy-start.34 = (f32[591]{0:T(1024)}, f32[591]{0:T(1024)S(1)}, u32[]{:S(2)}) copy-start(f32[591]{0:T(1024)S(1)} %fusion.87) | copy-start | bytes 7096
  26.8 4.7 copy-start.47
  26.8 4.7 copy-start.48
  57.7 4.5 copy-start.10
  60.6 3.1 copy-start.1
  62.2 1.6 copy-start.14
  62.2 8.0 copy-start.52
  65.9 9.0 %copy-start.41 = (f32[768]{0:T(1024)S(1)}, f32[768]{0:T(1024)}, u32[]{:S(2)}) copy-start(f32[768]{0:T(1024)} %param.26) | copy-start | bytes 9220
  65.9 9.0 %copy-start.46 = (f32[768]{0:T(1024)S(1)}, f32[768]{0:T(1024)}, u32[]{:S(2)}) copy-start(f32[768]{0:T(1024)} %param.27) | copy-start | bytes 9220
  73.1 1.2 copy-start.3
  73.1 1.2 copy-start.22
  73.5 0.8 copy-start.40
  74.3 0.6 copy-start.29
  75.3 0.9 copy-start.8
  99.9 97.8 %all-to-all-start = ((bf16[4,1,591,768]{3,2,1,0:T(8,128)(2,1)}), bf16[4,1,591,768]{3,2,1,0:T(8,128)(2,1)}, u32[]{:S(2)}, u32[]{:S(2)}) async-start(bf16[4,1,591,768]{3,2,1,0:T(8,128)(2,1)} %bitcast.274), calls=%async_computation | async-start | bytes 7274496 | tf_op jit(solution)/shard_map/all_to_all | solution.py:102
  116.1 14.7 %copy-start.24 = (s32[591,2]{0,1:T(2,128)S(1)}, s32[591,2]{0,1:T(2,128)}, u32[]{:S(2)}) copy-start(s32[591,2]{0,1:T(2,128)} %param.18) | copy-start | bytes 14188
  129.6 0.6 copy-start.18
  129.6 0.6 copy-start.20
  130.2 0.6 copy-start.28
  197.7 103.3 %all-to-all-start.2 = ((bf16[4,1,591,768]{3,2,1,0:T(8,128)(2,1)}), bf16[4,1,591,768]{3,2,1,0:T(8,128)(2,1)}, u32[]{:S(2)}, u32[]{:S(2)}) async-start(bf16[4,1,591,768]{3,2,1,0:T(8,128)(2,1)} %bitcast.275), calls=%async_computation.2 | async-start | bytes 7274496 | tf_op jit(solution)/shard_map/all_to_all | solution.py:123
  202.5 19.6 %copy-start.51 = (f32[1,3072]{1,0:T(1,128)S(1)}, f32[1,3072]{1,0:T(1,128)}, u32[]{:S(2)}) copy-start(f32[1,3072]{1,0:T(1,128)} %param.30) | copy-start | bytes 36868
  301.0 104.2 %all-to-all-start.1 = ((bf16[4,1,591,768]{3,2,1,0:T(8,128)(2,1)}), bf16[4,1,591,768]{3,2,1,0:T(8,128)(2,1)}, u32[]{:S(2)}, u32[]{:S(2)}) async-start(bf16[4,1,591,768]{3,2,1,0:T(8,128)(2,1)} %fusion.45), calls=%async_computation.1 | async-start | bytes 7274496 | tf_op jit(solution)/shard_map/all_to_all | solution.py:108
  306.0 83.1 %copy-start.49 = (bf16[1,768,3072]{2,1,0:T(8,128)(2,1)S(1)}, bf16[1,768,3072]{2,1,0:T(8,128)(2,1)}, u32[]{:S(2)}) copy-start(bf16[1,768,3072]{2,1,0:T(8,128)(2,1)} %param.29) | copy-start | bytes 14155780
  405.2 129.9 %all-to-all-start.3 = ((bf16[4,1,591,768]{3,2,1,0:T(8,128)(2,1)}), bf16[4,1,591,768]{3,2,1,0:T(8,128)(2,1)}, u32[]{:S(2)}, u32[]{:S(2)}) async-start(bf16[4,1,591,768]{3,2,1,0:T(8,128)(2,1)} %convert_bitcast_fusion), calls=%async_computation.3 | async-start | bytes 7274496 | tf_op jit(solution)/shard_map/all_to_all | solution.py:140
  410.3 261.8 %all-reduce.10.cloned.1.call-start = ((), (), s32[]{:S(2)}) async-start(), calls=%async_computation.5 | async-start | bytes 18874368 | tf_op jit(solution)/shard_map/psum | solution.py:195
  410.3 75.4 %copy-start.54 = (bf16[4,1,591,3072]{3,2,0,1:T(8,128)(2,1)S(1)}, bf16[4,1,591,3072]{3,2,0,1:T(8,128)(2,1)}, u32[]{:S(2)}) copy-start(bf16[4,1,591,3072]{3,2,0,1:T(8,128)(2,1)} %get-tuple-element.61) | copy-start | bytes 43573252
  501.3 4.9 copy-start.25
  501.3 339.2 %all-reduce.8.cloned.1.call-start = ((), (), s32[]{:S(2)}) async-start(), calls=%async_computation.4 | async-start | bytes 18874368 | tf_op jit(solution)/shard_map/psum | solution.py:200
  514.4 18.7 %copy-start.19 = (f32[591,4]{0,1:T(4,128)S(1)}, f32[591,4]{0,1:T(4,128)}, u32[]{:S(2)}) copy-start(f32[591,4]{0,1:T(4,128)} %copy-done.18) | copy-start | bytes 28372
  514.4 18.7 %copy-start.21 = (f32[591]{0:T(1024)S(1)}, f32[591]{0:T(1024)}, u32[]{:S(2)}) copy-start(f32[591]{0:T(1024)} %copy-done.20) | copy-start | bytes 7096
  548.5 13.8 %copy-start.23 = (f32[591]{0:T(1024)S(1)}, f32[591]{0:T(1024)}, u32[]{:S(2)}) copy-start(f32[591]{0:T(1024)} %copy-done.22) | copy-start | bytes 7096
  548.5 13.8 %copy-start.30 = (f32[591]{0:T(1024)S(1)}, f32[591]{0:T(1024)}, u32[]{:S(2)}) copy-start(f32[591]{0:T(1024)} %copy-done.29) | copy-start | bytes 7096
  548.5 13.8 %copy-start.31 = (bf16[591,4]{0,1:T(4,128)(2,1)S(1)}, bf16[591,4]{0,1:T(4,128)(2,1)}, u32[]{:S(2)}) copy-start(bf16[591,4]{0,1:T(4,128)(2,1)} %multiply_convert_fusion.5) | copy-start | bytes 14188
  562.3 9.6 %copy-start.7 = (bf16[591,768]{1,0:T(8,128)(2,1)S(1)}, bf16[591,768]{1,0:T(8,128)(2,1)}, u32[]{:S(2)}) copy-start(bf16[591,768]{1,0:T(8,128)(2,1)} %param.33) | copy-start | bytes 2723332
  562.4 11.5 %copy-start.50 = (bf16[768,768]{1,0:T(8,128)(2,1)S(1)}, bf16[768,768]{1,0:T(8,128)(2,1)}, u32[]{:S(2)}) copy-start(bf16[768,768]{1,0:T(8,128)(2,1)} %param.24) | copy-start | bytes 3538948
  570.7 1.3 copy-start.4
  570.7 2.2 copy-start.37
  572.9 1.0 copy-start.16
  596.0 6.2 copy-start.15
  602.2 6.3 copy-start.11
  606.7 1.8 copy-start.2
  622.1 13.3 %copy-start.27 = (f32[591]{0:T(1024)S(1)}, f32[591]{0:T(1024)}, u32[]{:S(2)}) copy-start(f32[591]{0:T(1024)} %copy-done.26) | copy-start | bytes 7096
  622.1 13.3 %copy-start.35 = (f32[591]{0:T(1024)S(1)}, f32[591]{0:T(1024)}, u32[]{:S(2)}) copy-start(f32[591]{0:T(1024)} %copy-done.34) | copy-start | bytes 7096
  622.1 13.3 %copy-start.43 = (f32[768]{0:T(1024)S(1)}, f32[768]{0:T(1024)}, u32[]{:S(2)}) copy-start(f32[768]{0:T(1024)} %param.19) | copy-start | bytes 9220
  622.1 13.4 %copy-start.53 = (f32[768]{0:T(1024)S(1)}, f32[768]{0:T(1024)}, u32[]{:S(2)}) copy-start(f32[768]{0:T(1024)} %param.20) | copy-start | bytes 9220
  626.2 9.3 %copy-start.5 = (bf16[591,768]{1,0:T(8,128)(2,1)S(1)}, bf16[591,768]{1,0:T(8,128)(2,1)}, u32[]{:S(2)}) copy-start(bf16[591,768]{1,0:T(8,128)(2,1)} %param.17) | copy-start | bytes 2723332
  630.4 5.1 copy-start.17
  672.1 7.7 slice-start
  672.1 7.7 slice-start.1
  679.8 5.9 copy-start.42
  679.8 6.5 copy-start.44
  686.3 5.5 copy-start.39
  686.3 5.6 copy-start.9
  686.3 5.6 copy-start.32
  686.3 5.8 copy-start.6
  686.3 5.8 copy-start.36
  686.3 5.8 copy-start.45
  691.8 1.8 copy-start.12
  691.9 1.7 copy-start.33
  840.5 6.6 copy-start.13
Sparse Core Ops, SparseCore 0:
  501.4 139.7 all-reduce.9
  648.7 191.7 all-reduce.7
where the time goes:
time: 863 us; the launch traced here: 856 us
  matrix products  340 us (39%)
  local copies, waits for them, and re-layouts  170 us (20%)
  waiting for transfers between devices  141 us (16%)
  other arithmetic  90.9 us (11%)
  blocking collectives  67.4 us (8%)
  starting transfers between devices  31.2 us (4%)
  between operations  14.9 us (2%)
    psum x1, waiting for transfers between devices, on_device(): lax.psum((grad_ln1_g, grad_ln1_b, grad_wqkv, grad_qbias, grad_vbias, grad...  99.5 us
    dot_general x1, matrix products, on_device(): jnp.einsum('sjcd,jfd->sjcf', grad_rows, experts_out, preferred_element_ty...  83.1 us
    dot_general x1, matrix products, on_device(): jnp.einsum('sjcf,jfd->sjcd', activ_b, experts_out, preferred_element_type...  78.8 us
    dot_general x1, matrix products, on_device(): jnp.einsum('sjcf,sjcd->jfd', activ_back, grad_rows, preferred_element_typ...  75.4 us
    psum x1, blocking collectives, on_device(): lax.psum((grad_ln1_g, grad_ln1_b, grad_wqkv, grad_qbias, grad_vbias, grad...  42.8 us
    all_to_all x1, waiting for transfers between devices, on_device(): lax.all_to_all(send_rows, 'exp', split_axis=0, concat_axis=0, tiled=True)  41.6 us
    psum x1, blocking collectives, on_device(): lax.psum(grad_ein_b.astype(jnp.bfloat16), 'rep').astype(jnp.float32)  24.5 us
    unnamed x120, local copies, waits for them, and re-layouts  20.9 us
  transfers between devices with their start and end apart: 6, of which 2 were waited for; matrix products, arithmetic and copies ran while one was open for 58% of the time, Pallas kernels for 0%

commit v1 on v0

v1 whole, which is shorter than its diff:
```python
import functools

import jax
import jax.numpy as jnp
from jax import lax
from jax.experimental import pallas as pl
from jax.experimental.pallas import tpu as pltpu
from jax.sharding import PartitionSpec as P

HEADS = 12
HEAD_DIM = 64
SEQ = 197
NORM_EPS = 1e-06
F32 = jnp.float32
BF16 = jnp.bfloat16
LANES = 128
PAIR = LANES // HEAD_DIM
SEQ_PAD = 208
FF_TILE = 512
VMEM_BYTES = 58 * 2**20
TAIL_SCALE = 0.305
TAIL_COEFS = (
    0.1216396663821839,
    0.12246803351870969,
    0.10341227166034979,
    0.12105264456174025,
    -0.03803921974174099,
    0.18578799927872533,
    -0.1530311110530253,
    0.03670976324394601,
)
INV_SQRT_2PI = 0.3989422804014327


def dot(lhs, rhs):
    return lax.dot_general(lhs, rhs, (((1,), (0,)), ((), ())), preferred_element_type=F32)


def dot_rt(lhs, rhs):
    return lax.dot_general(lhs, rhs, (((1,), (1,)), ((), ())), preferred_element_type=F32)


def dot_lt(lhs, rhs):
    return lax.dot_general(lhs, rhs, (((0,), (0,)), ((), ())), preferred_element_type=F32)


def row_mean(values):
    return jnp.mean(values, axis=-1, keepdims=True)


def unit_norm(values):
    centred = values - row_mean(values)
    scale = lax.rsqrt(row_mean(centred * centred) + NORM_EPS)
    return centred * scale, scale


def column_sum(values):
    return jnp.sum(values, axis=0, keepdims=True)


def gelu_parts(pre):
    size = jnp.abs(pre)
    bell = jnp.exp(pre * pre * -0.5)
    frac = 1.0 / (1.0 + TAIL_SCALE * size)
    poly = jnp.full_like(pre, TAIL_COEFS[-1])
    for coef in TAIL_COEFS[-2::-1]:
        poly = poly * frac + coef
    tail = bell * (poly * frac)
    return jnp.where(pre >= 0, 1.0 - tail, tail), bell * INV_SQRT_2PI


def pair_masks(rows):
    lane = lax.broadcasted_iota(jnp.int32, (rows, LANES), 1)
    return [(lane >= h * HEAD_DIM) & (lane < (h + 1) * HEAD_DIM) for h in range(PAIR)]


def stack_heads(values, masks):
    return jnp.concatenate([jnp.where(m, values, 0.0) for m in masks], axis=0).astype(BF16)


def unstack_heads(values, masks):
    rows = values.shape[0] // PAIR
    picked = values[:rows]
    for h in range(1, PAIR):
        picked = jnp.where(masks[h], values[h * rows : (h + 1) * rows], picked)
    return picked


def probabilities(scores):
    key_id = lax.broadcasted_iota(jnp.int32, scores.shape, 1)
    scores = jnp.where(key_id < SEQ, scores, -1e30)
    weights = jnp.exp(scores - jnp.max(scores, axis=-1, keepdims=True))
    return weights * (1.0 / jnp.sum(weights, axis=-1, keepdims=True))


def attend_kernel(
    x_ref, g1_ref, b1_ref, wqkv_ref, qb_ref, vb_ref, wout_ref, ob_ref, g2_ref, b2_ref,
    qkv_ref, ctx_ref, hidden_ref, mixed_ref,
    qkv_s, ctx_s,
):
    toks, width = x_ref.shape
    spare = qkv_s.shape[0] - toks
    x = x_ref[...].astype(F32)
    unit, _ = unit_norm(x)
    normed = (unit * g1_ref[...] + b1_ref[...]).astype(BF16)
    for part, bias in ((0, qb_ref), (1, None), (2, vb_ref)):
        cols = pl.ds(part * width, width)
        joined = dot(normed, wqkv_ref[:, cols])
        if bias is not None:
            joined = joined + bias[...]
        joined = joined.astype(BF16)
        qkv_ref[:, cols] = joined
        qkv_s[0:toks, cols] = joined.astype(F32)
    qkv_s[toks:, :] = jnp.zeros((spare, 3 * width), F32)
    masks = pair_masks(SEQ_PAD)
    for img in range(toks // SEQ):
        rows = pl.ds(img * SEQ, SEQ_PAD)
        for at in range(0, width, LANES):
            query = stack_heads(qkv_s[rows, at : at + LANES], masks)
            key = qkv_s[rows, width + at : width + at + LANES].astype(BF16)
            value = qkv_s[rows, 2 * width + at : 2 * width + at + LANES].astype(BF16)
            probs = probabilities(dot_rt(query, key) * HEAD_DIM**-0.5).astype(BF16)
            ctx_s[rows, at : at + LANES] = unstack_heads(dot(probs, value), masks)
    ctx = ctx_s[0:toks, :].astype(BF16)
    ctx_ref[...] = ctx
    hidden = x + dot(ctx, wout_ref[...]) + ob_ref[...]
    hidden_ref[...] = hidden
    unit2, _ = unit_norm(hidden)
    mixed_ref[...] = (unit2 * g2_ref[...] + b2_ref[...]).astype(BF16)


def expert_kernel(
    me_ref,
    x_ref, up_ref, routes_ref, router_ref, router_t_ref, win_ref, bin_ref, wout_ref, bout_ref,
    part_ref, back_ref, activ_ref, gpre_ref, geout_ref, grouter_ref,
    out_s, back_s, probs_s, gate_s,
):
    step = pl.program_id(0)
    me = me_ref[0]

    @pl.when(step == 0)
    def _():
        logits = dot(x_ref[...], router_ref[...])
        weights = jnp.exp(logits - jnp.max(logits, axis=-1, keepdims=True))
        probs = weights / jnp.sum(weights, axis=-1, keepdims=True)
        probs_s[...] = probs
        mine = lax.broadcasted_iota(jnp.int32, probs.shape, 1) == me
        named = jnp.max((routes_ref[...] == me).astype(F32), axis=-1, keepdims=True)
        gate = jnp.sum(jnp.where(mine, probs, 0.0), axis=-1, keepdims=True) * named
        gate_s[...] = gate
        geout_ref[...] = (gate * up_ref[...].astype(F32)).astype(BF16)
        out_s[...] = jnp.zeros_like(out_s)
        back_s[...] = jnp.zeros_like(back_s)

    pre = dot(x_ref[...], win_ref[...]) + bin_ref[...]
    phi, bell = gelu_parts(pre)
    activ = (pre * phi).astype(BF16)
    activ_ref[...] = activ
    gpre = (dot_rt(geout_ref[...], wout_ref[...]) * (phi + pre * bell)).astype(BF16)
    gpre_ref[...] = gpre
    out_s[...] += dot(activ, wout_ref[...])
    back_s[...] += dot_rt(gpre, win_ref[...])

    @pl.when(step == pl.num_programs(0) - 1)
    def _():
        expert_out = (out_s[...] + bout_ref[...]).astype(BF16).astype(F32)
        gate = gate_s[...]
        probs = probs_s[...]
        part_ref[...] = (gate * expert_out).astype(BF16)
        route_grad = jnp.sum(up_ref[...].astype(F32) * expert_out, axis=-1, keepdims=True)
        mine = (lax.broadcasted_iota(jnp.int32, probs.shape, 1) == me).astype(F32)
        glogits = gate * route_grad * (mine - probs)
        back = back_s[...].astype(BF16).astype(F32)
        for other in range(probs.shape[1]):
            back = back + glogits[:, other : other + 1] * router_t_ref[other : other + 1, :]
        back_ref[...] = back.astype(BF16)
        coarse = glogits.astype(BF16)
        fine = (glogits - coarse.astype(F32)).astype(BF16)
        grouter_ref[...] = dot_lt(coarse, x_ref[...]) + dot_lt(fine, x_ref[...])


def expert_weights_kernel(count, *refs):
    tall, wide = refs[:count], refs[count : 2 * count]
    grad_ref = refs[2 * count]
    total = dot_lt(tall[0][...], wide[0][...])
    for lhs, rhs in zip(tall[1:], wide[1:]):
        total = total + dot_lt(lhs[...], rhs[...])
    grad_ref[0 : total.shape[0], :] = total.astype(BF16)


def expert_in_grads_kernel(count, *refs):
    expert_weights_kernel(count, *refs[: 2 * count], refs[3 * count])
    grad_ref = refs[3 * count]
    rows, tile = refs[0].shape[1], grad_ref.shape[1]
    sums = column_sum(refs[count][...].astype(F32))
    for ref in refs[count + 1 : 2 * count]:
        sums = sums + column_sum(ref[...].astype(F32))
    outs = column_sum(refs[2 * count][...].astype(F32))
    for ref in refs[2 * count + 1 : 3 * count]:
        outs = outs + column_sum(ref[...].astype(F32))
    spare = grad_ref.shape[0] - rows
    row_id = lax.broadcasted_iota(jnp.int32, (spare, tile), 0)
    small = jnp.where(row_id == 0, sums, jnp.where(row_id == 1, outs, 0.0))
    grad_ref[rows:, :] = small.astype(BF16)


def attend_back_kernel(
    gmix_ref, up_ref, x_ref, hidden_ref, qkv_ref, ctx_ref, g1_ref, b1_ref, wqkv_ref, wout_ref, g2_ref,
    ginput_ref, grads_ref, small_ref,
    qkv_s, gctx_s, gjoin_s,
):
    toks, width = x_ref.shape
    spare = qkv_s.shape[0] - toks
    gmix = gmix_ref[...].astype(F32)
    unit2, scale2 = unit_norm(hidden_ref[...])
    grad_g2 = column_sum(gmix * unit2)
    grad_b2 = column_sum(gmix)
    m2 = gmix * g2_ref[...]
    ghidden = up_ref[...].astype(F32) + scale2 * (m2 - row_mean(m2) - unit2 * row_mean(m2 * unit2))
    gatt = ghidden.astype(BF16)
    grad_ob = column_sum(gatt.astype(F32))
    grads_ref[0:width, 3 * width :] = dot_lt(ctx_ref[...], gatt).astype(BF16)
    gctx_s[0:toks, :] = dot_rt(gatt, wout_ref[...]).astype(BF16).astype(F32)
    gctx_s[toks:, :] = jnp.zeros((spare, width), F32)
    qkv_s[0:toks, :] = qkv_ref[...].astype(F32)
    qkv_s[toks:, :] = jnp.zeros((spare, 3 * width), F32)
    masks = pair_masks(SEQ_PAD)
    row_ok = lax.broadcasted_iota(jnp.int32, (SEQ_PAD, 1), 0) < SEQ
    for img in range(toks // SEQ):
        rows = pl.ds(img * SEQ, SEQ_PAD)
        for at in range(0, width, LANES):
            query = stack_heads(jnp.where(row_ok, qkv_s[rows, at : at + LANES], 0.0), masks)
            key = qkv_s[rows, width + at : width + at + LANES].astype(BF16)
            value = qkv_s[rows, 2 * width + at : 2 * width + at + LANES].astype(BF16)
            gctx = stack_heads(jnp.where(row_ok, gctx_s[rows, at : at + LANES], 0.0), masks)
            probs = probabilities(dot_rt(query, key) * HEAD_DIM**-0.5)
            gvalue = dot_lt(probs.astype(BF16), gctx)
            gweights = dot_rt(gctx, value)
            inner = jnp.sum(gweights * probs, axis=-1, keepdims=True)
            gscores = (probs * (gweights - inner)).astype(BF16)
            gquery = unstack_heads(dot(gscores, key), masks) * HEAD_DIM**-0.5
            gkey = dot_lt(gscores, query) * HEAD_DIM**-0.5
            gjoin_s[rows, at : at + LANES] = gquery
            gjoin_s[rows, width + at : width + at + LANES] = gkey
            gjoin_s[rows, 2 * width + at : 2 * width + at + LANES] = gvalue
    gjoin = gjoin_s[0:toks, :].astype(BF16)
    grad_qb = column_sum(gjoin[:, :width].astype(F32))
    grad_vb = column_sum(gjoin[:, 2 * width :].astype(F32))
    x = x_ref[...].astype(F32)
    unit1, scale1 = unit_norm(x)
    normed = (unit1 * g1_ref[...] + b1_ref[...]).astype(BF16)
    grads_ref[0:width, 0 : 3 * width] = dot_lt(normed, gjoin).astype(BF16)
    gnormed = dot_rt(gjoin, wqkv_ref[...])
    grad_g1 = column_sum(gnormed * unit1)
    grad_b1 = column_sum(gnormed)
    m1 = gnormed * g1_ref[...]
    ginput = ghidden + scale1 * (m1 - row_mean(m1) - unit1 * row_mean(m1 * unit1))
    ginput_ref[...] = ginput.astype(BF16)
    for at, small in enumerate((grad_g1, grad_b1, grad_qb, grad_vb, grad_ob, grad_g2, grad_b2)):
        small_ref[at : at + 1, :] = small
    small_ref[7:, :] = jnp.zeros((1, width), F32)


def params(**more):
    return pltpu.CompilerParams(vmem_limit_bytes=VMEM_BYTES, **more)


def cost(flops, moved):
    return pl.CostEstimate(flops=flops, bytes_accessed=moved, transcendentals=0)


def whole():
    return pl.BlockSpec(memory_space=pltpu.VMEM)


def attend(inputs, g1, b1, w_qkv, qb, vb, w_out, ob, g2, b2):
    toks, width = inputs.shape
    padded = -(-(toks - SEQ + SEQ_PAD) // 16) * 16
    return pl.pallas_call(
        attend_kernel,
        out_shape=(
            jax.ShapeDtypeStruct((toks, 3 * width), BF16),
            jax.ShapeDtypeStruct((toks, width), BF16),
            jax.ShapeDtypeStruct((toks, width), F32),
            jax.ShapeDtypeStruct((toks, width), BF16),
        ),
        in_specs=[whole()] * 10,
        out_specs=(whole(),) * 4,
        scratch_shapes=[pltpu.VMEM((padded, 3 * width), F32), pltpu.VMEM((padded, width), F32)],
        compiler_params=params(),
        cost_estimate=cost(16 * toks * width * width, 16 * 2**20),
        name="attend",
    )(inputs, g1, b1, w_qkv, qb, vb, w_out, ob, g2, b2)


def attend_back(gmix, up, inputs, hidden, qkv, ctx, g1, b1, w_qkv, w_out, g2):
    toks, width = inputs.shape
    padded = -(-(toks - SEQ + SEQ_PAD) // 16) * 16
    return pl.pallas_call(
        attend_back_kernel,
        out_shape=(
            jax.ShapeDtypeStruct((toks, width), BF16),
            jax.ShapeDtypeStruct((width, 4 * width), BF16),
            jax.ShapeDtypeStruct((8, width), F32),
        ),
        in_specs=[whole()] * 11,
        out_specs=(whole(),) * 3,
        scratch_shapes=[
            pltpu.VMEM((padded, 3 * width), F32),
            pltpu.VMEM((padded, width), F32),
            pltpu.VMEM((padded, 3 * width), F32),
        ],
        compiler_params=params(),
        cost_estimate=cost(32 * toks * width * width, 20 * 2**20),
        name="attend_back",
    )(gmix, up, inputs, hidden, qkv, ctx, g1, b1, w_qkv, w_out, g2)


def expert_block(me, rows, up, routes, router, router_t, w_in, b_in, w_out, b_out):
    toks, width = rows.shape
    experts = router.shape[1]
    hidden = w_in.shape[1]
    fixed = lambda shape: pl.BlockSpec(shape, lambda f, m: (0, 0))
    return pl.pallas_call(
        expert_kernel,
        out_shape=(
            jax.ShapeDtypeStruct((toks, width), BF16),
            jax.ShapeDtypeStruct((toks, width), BF16),
            jax.ShapeDtypeStruct((toks, hidden), BF16),
            jax.ShapeDtypeStruct((toks, hidden), BF16),
            jax.ShapeDtypeStruct((toks, width), BF16),
            jax.ShapeDtypeStruct((experts, width), F32),
        ),
        grid_spec=pltpu.PrefetchScalarGridSpec(
            num_scalar_prefetch=1,
            grid=(hidden // FF_TILE,),
            in_specs=[
                fixed((toks, width)),
                fixed((toks, width)),
                fixed(routes.shape),
                fixed(router.shape),
                fixed(router_t.shape),
                pl.BlockSpec((width, FF_TILE), lambda f, m: (0, f)),
                pl.BlockSpec((1, FF_TILE), lambda f, m: (0, f)),
                pl.BlockSpec((FF_TILE, width), lambda f, m: (f, 0)),
                fixed((1, width)),
            ],
            out_specs=(
                fixed((toks, width)),
                fixed((toks, width)),
                pl.BlockSpec((toks, FF_TILE), lambda f, m: (0, f)),
                pl.BlockSpec((toks, FF_TILE), lambda f, m: (0, f)),
                fixed((toks, width)),
                fixed((experts, width)),
            ),
            scratch_shapes=[
                pltpu.VMEM((toks, width), F32),
                pltpu.VMEM((toks, width), F32),
                pltpu.VMEM((toks, experts), F32),
                pltpu.VMEM((toks, 1), F32),
            ],
        ),
        compiler_params=params(),
        cost_estimate=cost(8 * toks * width * hidden, 20 * 2**20),
        name="expert_block",
    )(me, rows, up, routes, router, router_t, w_in, b_in, w_out, b_out)


def expert_out_grads(activs, geouts):
    count = len(activs)
    toks, hidden = activs[0].shape
    width = geouts[0].shape[1]
    return pl.pallas_call(
        functools.partial(expert_weights_kernel, count),
        out_shape=jax.ShapeDtypeStruct((width, hidden), BF16),
        grid=(hidden // width,),
        in_specs=[pl.BlockSpec((toks, width), lambda f: (0, f))] * count
        + [pl.BlockSpec((toks, width), lambda f: (0, 0))] * count,
        out_specs=pl.BlockSpec((width, width), lambda f: (0, f)),
        compiler_params=params(),
        cost_estimate=cost(2 * count * toks * width * hidden, 20 * 2**20),
        name="expert_out_grads",
    )(*activs, *geouts)


def expert_in_grads(rows, gpres, geouts, grad_rows):
    count = len(rows)
    toks, hidden = gpres[0].shape
    width = rows[0].shape[1]
    return pl.pallas_call(
        functools.partial(expert_in_grads_kernel, count),
        out_shape=jax.ShapeDtypeStruct((grad_rows, hidden), BF16),
        grid=(hidden // width,),
        in_specs=[pl.BlockSpec((toks, width), lambda f: (0, 0))] * count
        + [pl.BlockSpec((toks, width), lambda f: (0, f))] * count
        + [pl.BlockSpec((toks, width), lambda f: (0, 0))] * count,
        out_specs=pl.BlockSpec((grad_rows, width), lambda f: (0, f)),
        compiler_params=params(),
        cost_estimate=cost(2 * count * toks * width * hidden, 20 * 2**20),
        name="expert_in_grads",
    )(*rows, *gpres, *geouts)


def shift(values, axis, by):
    size = lax.axis_size(axis)
    return lax.ppermute(values, axis, [(i, (i + by) % size) for i in range(size)])


def ring_gather(values, axis):
    size = lax.axis_size(axis)
    found = {0: values}
    ahead = behind = values
    for k in range(1, (size + 1) // 2):
        ahead, behind = shift(ahead, axis, 1), shift(behind, axis, -1)
        found[k], found[size - k] = ahead, behind
    if size % 2 == 0:
        cut = middle_cut(values.shape[0])
        found[size // 2] = jnp.concatenate(
            [shift(ahead[:cut], axis, 1), shift(behind[cut:], axis, -1)], axis=0
        )
    return [found[k] for k in range(size)]


def middle_cut(rows):
    return rows // 16 * 8


def ring_return(values, axis):
    size = lax.axis_size(axis)
    back = [values[0]]
    for k in range(1, size):
        if 2 * k != size:
            back.append(shift(values[k], axis, -k))
            continue
        cut = middle_cut(values[k].shape[0])
        low, high = values[k][:cut], values[k][cut:]
        for _ in range(k):
            low, high = shift(low, axis, -1), shift(high, axis, 1)
        back.append(jnp.concatenate([low, high], axis=0))
    return back


def swap(values, axis, bit):
    return lax.ppermute(values, axis, [(i, i ^ bit) for i in range(lax.axis_size(axis))])


def half_of(values, dim, which):
    size = values.shape[dim] // 2
    return lax.dynamic_slice_in_dim(values, which * size, size, dim)


def halve(values, axis, bit, dim):
    mine = (lax.axis_index(axis) // bit) % 2
    got = swap(half_of(values, dim, 1 - mine), axis, bit)
    return (half_of(values, dim, mine).astype(F32) + got.astype(F32)).astype(values.dtype)


def unhalve(values, axis, bit, dim):
    mine = (lax.axis_index(axis) // bit) % 2
    got = swap(values, axis, bit)
    return jnp.where(
        mine == 0,
        jnp.concatenate([values, got], axis=dim),
        jnp.concatenate([got, values], axis=dim),
    )


def sum_over(values, axis, inner=None):
    size = lax.axis_size(axis)
    bits = [1 << b for b in range(size.bit_length() - 1)]
    first, rest = bits[:1], bits[1:]
    for bit in first:
        values = halve(values, axis, bit, 0)
    cut = values.shape[1] // 2
    parts = []
    for piece, order in ((values[:, :cut], rest), (values[:, cut:], rest[::-1])):
        for bit in order:
            piece = halve(piece, axis, bit, 1)
        parts.append(piece)
    if inner is not None:
        joined = inner(jnp.concatenate(parts, axis=1))
        width = parts[0].shape[1]
        parts = [joined[:, :width], joined[:, width:]]
    done = []
    for piece, order in zip(parts, (rest, rest[::-1])):
        for bit in order[::-1]:
            piece = unhalve(piece, axis, bit, 1)
        done.append(piece)
    values = jnp.concatenate(done, axis=1)
    for bit in first:
        values = unhalve(values, axis, bit, 0)
    return values


def sum_direct(values, axis):
    size = lax.axis_size(axis)
    me = lax.axis_index(axis)
    share = values.shape[0] // size
    take = lambda owner: lax.dynamic_slice_in_dim(values, (owner % size) * share, share, 0)
    total = take(me).astype(F32)
    for k in range(1, size):
        total = total + shift(take(me + k), axis, k).astype(F32)
    total = total.astype(values.dtype)
    result = jnp.zeros_like(values)
    result = lax.dynamic_update_slice_in_dim(result, total, me * share, 0)
    for k in range(1, size):
        result = lax.dynamic_update_slice_in_dim(
            result, shift(total, axis, k), ((me - k) % size) * share, 0
        )
    return result


def sum_small(values):
    for bit in [1 << b for b in range(lax.axis_size("rep").bit_length() - 1)]:
        values = values + swap(values, "rep", bit)
    return sum([shift(values, "exp", k) for k in range(1, lax.axis_size("exp"))], values)


def on_device(
    inputs,
    routes,
    ln1_gain,
    ln1_bias,
    w_qkv,
    query_bias,
    value_bias,
    w_out,
    out_bias,
    ln2_gain,
    ln2_bias,
    router,
    experts_in,
    experts_in_bias,
    experts_out,
    experts_out_bias,
    cotangent,
):
    width = inputs.shape[1]
    hidden_units = experts_in.shape[2]
    me = lax.axis_index("exp").astype(jnp.int32).reshape(1)
    row = lambda vec: vec.reshape(1, -1)
    g1, b1, g2, b2 = row(ln1_gain), row(ln1_bias), row(ln2_gain), row(ln2_bias)

    ups = ring_gather(cotangent, "exp")
    routes_all = ring_gather_small(routes, "exp")
    qkv, ctx, hidden, mixed = attend(
        inputs, g1, b1, w_qkv, row(query_bias), row(value_bias), w_out, row(out_bias), g2, b2
    )
    mixes = ring_gather(mixed, "exp")

    router_t = router.T.astype(F32)
    w_in, w_mid = experts_in[0], experts_out[0]
    blocks = [
        expert_block(
            me, mixes[k], ups[k], routes_all[k], router, router_t, w_in, experts_in_bias, w_mid, experts_out_bias
        )
        for k in range(len(mixes))
    ]
    parts, backs, activs, gpres, geouts, grouters = zip(*blocks)
    backs = ring_return(backs, "exp")
    parts = ring_return(parts, "exp")
    gmix = sum(b.astype(F32) for b in backs)
    result = (hidden + sum(p.astype(F32) for p in parts)).astype(BF16)
    grouter = sum_small(sum(grouters))

    out_grads = expert_out_grads(activs, geouts)
    in_grads = expert_in_grads(mixes, gpres, geouts, width + 16)
    out_sum = sum_over(out_grads, "rep").astype(F32)
    in_sum = sum_over(in_grads, "rep").astype(F32)
    blocks_down = hidden_units // width
    grad_experts_out = jnp.concatenate(
        [out_sum[:, j * width : (j + 1) * width] for j in range(blocks_down)], axis=0
    )[None]

    grad_inputs, dense, small = attend_back(
        gmix, cotangent, inputs, hidden, qkv, ctx, g1, b1, w_qkv, w_out, g2
    )
    dense = sum_over(dense, "rep", functools.partial(sum_direct, axis="exp")).astype(F32)
    small = sum_small(small)
    return (
        result,
        grad_inputs,
        small[0],
        small[1],
        dense[:, : 3 * width],
        small[2],
        small[3],
        dense[:, 3 * width :],
        small[4],
        small[5],
        small[6],
        grouter.T,
        in_sum[None, :width],
        in_sum[width : width + 1],
        grad_experts_out,
        in_sum[width + 1 : width + 2, :width],
    )


def ring_gather_small(values, axis):
    return [values] + [shift(values, axis, k) for k in range(1, lax.axis_size(axis))]


def solution(mesh):
    tokens = P(("rep", "exp"), None)
    expert3, expert2 = P("exp", None, None), P("exp", None)
    return jax.shard_map(
        on_device,
        mesh=mesh,
        in_specs=(tokens, tokens) + (P(),) * 10 + (expert3, expert2) * 2 + (tokens,),
        out_specs=(tokens, tokens) + (P(),) * 10 + (expert3, expert2) * 2,
        check_vma=False,
    )
```

time: 863 us -> 637 us (0.74)
  matrix products: 340 us -> 0 us
  Pallas kernels: 0 us -> 180 us
  local copies, waits for them, and re-layouts: 170 us -> 38.5 us
  starting transfers between devices: 31.2 us -> 134 us
  blocking collectives: 67.4 us -> 0 us
  waiting for transfers between devices: 141 us -> 195 us
  between operations: 14.9 us -> 1.94 us
  other arithmetic: 90.9 us -> 79.1 us
    dot_general x21 -> x0, matrix products: 340 us -> none  [the longest x1 83.1 us: on_device(): jnp.einsum('sjcd,jfd->sjcf', grad_rows, experts_out, preferred_element_ty...]
    ppermute x0 -> x71, waiting for transfers between devices: none -> 195 us  [the longest x35 105 us: shift(): lax.ppermute(values, axis, [(i, (i + by) % size) for i in range(size)])]
    pallas_call x0 -> x8, Pallas kernels: none -> 180 us  [the longest x4 95.3 us: expert_block(): pl.pallas_call(expert_kernel, out_shape=(jax.ShapeDtypeStruct((toks, widt...]
    ppermute x0 -> x71, starting transfers between devices: none -> 134 us  [the longest x35 102 us: shift(): lax.ppermute(values, axis, [(i, (i + by) % size) for i in range(size)])]
    psum x2 -> x0, waiting for transfers between devices: 99.5 us -> none  [the longest x1 99.5 us: on_device(): lax.psum((grad_ln1_g, grad_ln1_b, grad_wqkv, grad_qbias, grad_vbias, grad...]
    psum x2 -> x0, blocking collectives: 67.4 us -> none  [the longest x1 42.8 us: on_device(): lax.psum((grad_ln1_g, grad_ln1_b, grad_wqkv, grad_qbias, grad_vbias, grad...]
    reshape x16 -> x7, local copies, waits for them, and re-layouts: 69.4 us -> 8.87 us  [on_device(): row = lambda vec: vec.reshape(1, -1)]
    all_to_all x4 -> x0, waiting for transfers between devices: 41.6 us -> none  [the longest x1 41.6 us: on_device(): lax.all_to_all(send_rows, 'exp', split_axis=0, concat_axis=0, tiled=True)]
  transfers between devices with their start and end apart: 6 -> 71, of which waited for: 2 -> 28; matrix products, arithmetic and copies ran while one was open for 58% -> 13% of each run, Pallas kernels for 0% -> 27%
where the time goes in v1:
time: 637 us; the launch traced here: 629 us
  waiting for transfers between devices  195 us (31%)
  Pallas kernels  180 us (28%)
  starting transfers between devices  134 us (21%)
  other arithmetic  79.1 us (12%)
  local copies, waits for them, and re-layouts  38.5 us (6%)
    ppermute x35, waiting for transfers between devices, shift(): lax.ppermute(values, axis, [(i, (i + by) % size) for i in range(size)])  105 us
    ppermute x35, starting transfers between devices, shift(): lax.ppermute(values, axis, [(i, (i + by) % size) for i in range(size)])  102 us
    pallas_call x4, Pallas kernels, expert_block(): pl.pallas_call(expert_kernel, out_shape=(jax.ShapeDtypeStruct((toks, widt...  95.3 us
    ppermute x36, waiting for transfers between devices, swap(): lax.ppermute(values, axis, [(i, i ^ bit) for i in range(lax.axis_size(axi...  90.2 us
    ppermute x36, starting transfers between devices, swap(): lax.ppermute(values, axis, [(i, i ^ bit) for i in range(lax.axis_size(axi...  31.7 us
    pallas_call x1, Pallas kernels, attend_back(): pl.pallas_call(attend_back_kernel, out_shape=(jax.ShapeDtypeStruct((toks,...  28 us
    pallas_call x1, Pallas kernels, expert_in_grads(): pl.pallas_call(functools.partial(expert_in_grads_kernel, count), out_shap...  25.5 us
    pallas_call x1, Pallas kernels, expert_out_grads(): pl.pallas_call(functools.partial(expert_weights_kernel, count), out_shape...  20 us
  transfers between devices with their start and end apart: 71, of which 28 were waited for; matrix products, arithmetic and copies ran while one was open for 13% of the time, Pallas kernels for 27%

profile of v1, /device:TPU:0, one launch (start us, length us, event | category | flops | bytes accessed | tf_op | source)
XLA Modules:
  0.0 629.3 jit_solution(5675652549988946584)
XLA Ops:
  9.5 11.7 %attend.1 = (bf16[591,2304]{1,0:T(8,128)(2,1)}, bf16[591,768]{1,0:T(8,128)(2,1)}, f32[591,768]{1,0:T(8,128)}, bf16[591,768]{1,0:T(8,128)(2,1)}) custom-call(bf16[591,768]{1,0:T(8,128)(2,1)} %x_ref.3, f32[1,768]{1,0:T(1,128)} %reshape.56.g1_ref, f32[1,768]{1,0:T(1,128)} %reshape.57.b1_ref, bf16[768,2304]{1,0:T(8,128)(2,1)} %wqkv_ref.3, ...), custom_call_target="tpu_custom_call" | custom-call | flops 5577375744 | bytes 16777216 | tf_op jit(solution)/shard_map/attend/pallas_call | solution.py:279
  21.2 3.0 collective-permute-start
  24.2 2.0 collective-permute-start.5
  26.2 2.0 collective-permute-start.8
  30.8 23.8 %expert_block.4 = (bf16[591,768]{1,0:T(8,128)(2,1)}, bf16[591,768]{1,0:T(8,128)(2,1)}, bf16[591,3072]{1,0:T(8,128)(2,1)}, bf16[591,3072]{1,0:T(8,128)(2,1)}, bf16[591,768]{1,0:T(8,128)(2,1)}, /*index=5*/f32[4,768]{1,0:T(4,128)}) custom-call(s32[1]{0:T(128)} %bitcast.me_ref, bf16[591,768]{1,0:T(8,128)(2,1)} %get-tuple-element.48.x_ref.refs_0_, ...), custom_call_target="tpu_custom_call" | custom-call | flops 11154751488 | bytes 20971520 | tf_op jit(solution)/shard_map/expert_block/pallas_call | solution.py:324
  55.6 32.9 %collective-permute-start.10 = (s32[591,2]{1,0:T(8,128)}, s32[591,2]{1,0:T(8,128)S(1)}, u32[]{:S(2)}, u32[]{:S(2)}) collective-permute-start(s32[591,2]{1,0:T(8,128)} %copy.33.routes_ref), channel_id=1, source_target_pairs={{0,2},{1,3},{2,0},{3,1},{4,6},{5,7},{6,4},{7,5},{8,10},{9,11},{10,... | collective-permute-start | bytes 14192 | tf_op jit(solution)/shard_map/ppermute | solution.py:406
  89.5 1.6 collective-permute-start.4
  91.2 2.3 collective-permute-start.6
  93.5 12.7 %collective-permute-done.1.up_ref = bf16[591,768]{1,0:T(8,128)(2,1)} collective-permute-done((bf16[591,768]{1,0:T(8,128)(2,1)}, bf16[591,768]{1,0:T(8,128)(2,1)}, u32[]{:S(2)}, u32[]{:S(2)}) %collective-permute-start.1) | collective-permute-done | bytes 907808 | tf_op jit(solution)/shard_map/ppermute | solution.py:406
  106.3 1.8 collective-permute-start.9
  109.1 3.5 collective-permute-done.2.routes_ref
  112.6 5.1 collective-permute-start.7
  117.7 23.9 %expert_block.5 = (bf16[591,768]{1,0:T(8,128)(2,1)}, bf16[591,768]{1,0:T(8,128)(2,1)}, bf16[591,3072]{1,0:T(8,128)(2,1)}, bf16[591,3072]{1,0:T(8,128)(2,1)}, bf16[591,768]{1,0:T(8,128)(2,1)}, /*index=5*/f32[4,768]{1,0:T(4,128)}) custom-call(s32[1]{0:T(128)} %bitcast.me_ref, bf16[591,768]{1,0:T(8,128)(2,1)} %copy-done.7, ...), custom_call_target="tpu_custom_call" | custom-call | flops 11154751488 | bytes 20971520 | tf_op jit(solution)/shard_map/expert_block/pallas_call | solution.py:324
  141.6 9.3 %collective-permute-start.15 = (s32[591,2]{1,0:T(8,128)}, s32[591,2]{1,0:T(8,128)S(1)}, u32[]{:S(2)}, u32[]{:S(2)}) collective-permute-start(s32[591,2]{1,0:T(8,128)} %copy.33.routes_ref), channel_id=1, source_target_pairs={{0,3},{1,0},{2,1},{3,2},{4,7},{5,4},{6,5},{7,6},{8,11},{9,8},{10,9... | collective-permute-start | bytes 14192 | tf_op jit(solution)/shard_map/ppermute | solution.py:406
  150.9 7.1 %collective-permute-done.7 = bf16[288,768]{1,0:T(8,128)(2,1)S(1)} collective-permute-done((bf16[288,768]{1,0:T(8,128)(2,1)S(1)}, bf16[288,768]{1,0:T(8,128)(2,1)S(1)}, u32[]{:S(2)}, u32[]{:S(2)}) %collective-permute-start.7) | collective-permute-done | bytes 442400 | tf_op jit(solution)/shard_map/ppermute | solution.py:406
  160.8 23.8 %expert_block.6 = (bf16[591,768]{1,0:T(8,128)(2,1)}, bf16[591,768]{1,0:T(8,128)(2,1)}, bf16[591,3072]{1,0:T(8,128)(2,1)}, bf16[591,3072]{1,0:T(8,128)(2,1)}, bf16[591,768]{1,0:T(8,128)(2,1)}, /*index=5*/f32[4,768]{1,0:T(4,128)}) custom-call(s32[1]{0:T(128)} %bitcast.me_ref, bf16[591,768]{1,0:T(8,128)(2,1)} %copy-done.8, ...), custom_call_target="tpu_custom_call" | custom-call | flops 11154751488 | bytes 20971520 | tf_op jit(solution)/shard_map/expert_block/pallas_call | solution.py:324
  186.7 10.9 %collective-permute-start.20 = (bf16[303,768]{1,0:T(8,128)(2,1)S(1)}, bf16[303,768]{1,0:T(8,128)(2,1)S(1)}, u32[]{:S(2)}, u32[]{:S(2)}) collective-permute-start(bf16[303,768]{1,0:T(8,128)(2,1)S(1)} %slice.103), channel_id=1, source_target_pairs={{0,1},{1,2},{2,3},{3,0},{4,5},{5,6},{6,7},{7,4},{8,9},{9,10},{10,1... | collective-permute-start | bytes 1396232 | tf_op jit(solution)/shard_map/ppermute | solution.py:406
  198.3 23.9 %expert_block.7 = (bf16[591,768]{1,0:T(8,128)(2,1)}, bf16[591,768]{1,0:T(8,128)(2,1)}, bf16[591,3072]{1,0:T(8,128)(2,1)}, bf16[591,3072]{1,0:T(8,128)(2,1)}, bf16[591,768]{1,0:T(8,128)(2,1)}, /*index=5*/f32[4,768]{1,0:T(4,128)}) custom-call(s32[1]{0:T(128)} %bitcast.me_ref, bf16[591,768]{1,0:T(8,128)(2,1)} %copy-done.5, bf16[591,768]{1,0:T(8,128)(2,1)} %copy-done.6, ...), custom_call_target="tpu_custom_call" | custom-call | flops 11154751488 | bytes 20971520 | tf_op jit(solution)/shard_map/expert_block/pallas_call | solution.py:324
  225.6 3.4 collective-permute-start.17
  230.6 3.8 collective-permute-start.19
  234.5 20.0 %expert_out_grads.1 = bf16[768,3072]{1,0:T(8,128)(2,1)} custom-call(bf16[591,3072]{1,0:T(8,128)(2,1)} %get-tuple-element.74.refs_0_, bf16[591,3072]{1,0:T(8,128)(2,1)} %get-tuple-element.75.refs_1_, bf16[591,3072]{1,0:T(8,128)(2,1)} %get-tuple-element.76.refs_2_, bf16[591,3072]{1,0:T(8,128)(2,1)} %get-tuple-element.77.refs_3_, ...), custom_call_target="tpu_custom_call" | custom-call | flops 11154751488 | bytes 20971520 | tf_op jit(solution)/shard_map/expert_out_grads/pallas_call | solution.py:373
  255.9 15.8 %collective-permute-done.22 = bf16[591,768]{1,0:T(8,128)(2,1)S(1)} collective-permute-done((bf16[591,768]{1,0:T(8,128)(2,1)}, bf16[591,768]{1,0:T(8,128)(2,1)S(1)}, u32[]{:S(2)}, u32[]{:S(2)}) %collective-permute-start.22) | collective-permute-done | bytes 907808 | tf_op jit(solution)/shard_map/ppermute | solution.py:406
  272.8 6.2 collective-permute-done.19
  278.9 4.3 collective-permute-start.50
  283.3 8.1 %collective-permute-done.21 = bf16[303,768]{1,0:T(8,128)(2,1)S(1)} collective-permute-done((bf16[303,768]{1,0:T(8,128)(2,1)S(1)}, bf16[303,768]{1,0:T(8,128)(2,1)S(1)}, u32[]{:S(2)}, u32[]{:S(2)}) %collective-permute-start.21) | collective-permute-done | bytes 465440 | tf_op jit(solution)/shard_map/ppermute | solution.py:406
  291.4 3.5 convert_add_fusion.gmix_ref
  295.0 28.0 %attend_back.1 = (bf16[591,768]{1,0:T(8,128)(2,1)}, bf16[768,3072]{1,0:T(8,128)(2,1)}, f32[8,768]{1,0:T(8,128)}) custom-call(f32[591,768]{1,0:T(8,128)} %convert_add_fusion.gmix_ref, bf16[591,768]{1,0:T(8,128)(2,1)} %up_ref.3, bf16[591,768]{1,0:T(8,128)(2,1)} %x_ref.3, f32[591,768]{1,0:T(8,128)} %get-tuple-element.47.hidden_ref, ...), custom_call_target="tpu_custom_call" | custom-call | flops 11154751488 | bytes 20971520 | tf_op jit(solution)/shard_map/attend_back/pallas_call | solution.py:299
  326.0 3.8 collective-permute-start.11
  330.4 25.5 %expert_in_grads.1 = bf16[784,3072]{1,0:T(8,128)(2,1)} custom-call(bf16[591,768]{1,0:T(8,128)(2,1)} %get-tuple-element.48.x_ref.refs_0_, bf16[591,768]{1,0:T(8,128)(2,1)} %copy-done.7, bf16[591,768]{1,0:T(8,128)(2,1)} %copy-done.8, bf16[591,768]{1,0:T(8,128)(2,1)} %copy-done.5, bf16[591,3072]{1,0:T(8,128)(2,1)} %get-tuple-element.66.refs_4_, ...), custom_call_target="tpu_custom_call" | custom-call | flops 11154751488 | bytes 20971520 | tf_op jit(solution)/shard_map/expert_in_grads/pallas_call | solution.py:390
  356.1 2.0 constant_dynamic-slice_fusion.9
  358.2 2.0 collective-permute-start.14
  362.4 1.7 collective-permute-done.25
  364.3 15.1 %collective-permute-done.3 = bf16[591,768]{1,0:T(8,128)(2,1)S(1)} collective-permute-done((bf16[591,768]{1,0:T(8,128)(2,1)}, bf16[591,768]{1,0:T(8,128)(2,1)S(1)}, u32[]{:S(2)}, u32[]{:S(2)}) %collective-permute-start.3) | collective-permute-done | bytes 907808 | tf_op jit(solution)/shard_map/ppermute | solution.py:406
  379.4 18.7 %collective-permute-done.12 = bf16[288,768]{1,0:T(8,128)(2,1)S(1)} collective-permute-done((bf16[288,768]{1,0:T(8,128)(2,1)}, bf16[288,768]{1,0:T(8,128)(2,1)S(1)}, u32[]{:S(2)}, u32[]{:S(2)}) %collective-permute-start.12) | collective-permute-done | bytes 442400 | tf_op jit(solution)/shard_map/ppermute | solution.py:406
  398.1 2.0 collective-permute-start.28
  402.9 2.7 add_convert_fusion.1
  411.4 10.8 %collective-permute-done.62 = bf16[384,768]{1,0:T(8,128)(2,1)S(1)} collective-permute-done((bf16[384,768]{1,0:T(8,128)(2,1)S(1)}, bf16[384,768]{1,0:T(8,128)(2,1)S(1)}, u32[]{:S(2)}, u32[]{:S(2)}) %collective-permute-start.62) | collective-permute-done | bytes 589856 | tf_op jit(solution)/shard_map/ppermute | solution.py:444
  425.7 9.3 %collective-permute-done.52 = bf16[392,768]{1,0:T(8,128)(2,1)S(1)} collective-permute-done((bf16[392,768]{1,0:T(8,128)(2,1)S(1)}, bf16[392,768]{1,0:T(8,128)(2,1)S(1)}, u32[]{:S(2)}, u32[]{:S(2)}) %collective-permute-start.52) | collective-permute-done | bytes 602144 | tf_op jit(solution)/shard_map/ppermute | solution.py:444
  438.6 4.4 collective-permute-done.63
  447.1 2.3 collective-permute-done.53
  451.7 4.0 collective-permute-done.64
  458.2 14.7 %collective-permute-done.54 = bf16[392,384]{1,0:T(8,128)(2,1)S(1)} collective-permute-done((bf16[392,384]{1,0:T(8,128)(2,1)S(1)}, bf16[392,384]{1,0:T(8,128)(2,1)S(1)}, u32[]{:S(2)}, u32[]{:S(2)}) %collective-permute-start.54) | collective-permute-done | bytes 301088 | tf_op jit(solution)/shard_map/ppermute | solution.py:444
  477.9 8.6 %collective-permute-done.65 = bf16[384,768]{1,0:T(8,128)(2,1)S(1)} collective-permute-done((bf16[384,768]{1,0:T(8,128)(2,1)S(1)}, bf16[384,768]{1,0:T(8,128)(2,1)S(1)}, u32[]{:S(2)}, u32[]{:S(2)}) %collective-permute-start.65) | collective-permute-done | bytes 589856 | tf_op jit(solution)/shard_map/ppermute | solution.py:444
  487.7 15.8 %collective-permute-done.33 = bf16[384,384]{1,0:T(8,128)(2,1)S(1)} collective-permute-done((bf16[384,384]{1,0:T(8,128)(2,1)S(1)}, bf16[384,384]{1,0:T(8,128)(2,1)S(1)}, u32[]{:S(2)}, u32[]{:S(2)}) %collective-permute-start.33) | collective-permute-done | bytes 294944 | tf_op jit(solution)/shard_map/ppermute | solution.py:444
  503.5 2.0 collective-permute-done.31
  505.7 2.4 collective-permute-start.35
  509.8 4.0 collective-permute-done.34
  513.9 3.1 collective-permute-done.35
  517.1 2.8 collective-permute-start.37
  521.4 4.0 collective-permute-done.37
  526.4 3.7 collective-permute-done.38
  530.1 2.0 collective-permute-done.39
  535.5 3.6 collective-permute-done.40
  540.3 3.9 collective-permute-done.42
  544.4 1.8 pad_maximum_fusion
  546.2 7.9 %collective-permute-done.41 = bf16[384,768]{1,0:T(8,128)(2,1)S(1)} collective-permute-done((bf16[384,768]{1,0:T(8,128)(2,1)S(1)}, bf16[384,768]{1,0:T(8,128)(2,1)S(1)}, u32[]{:S(2)}, u32[]{:S(2)}) %collective-permute-start.41) | collective-permute-done | bytes 589856 | tf_op jit(solution)/shard_map/ppermute | solution.py:444
  554.8 1.7 pad_maximum_fusion.1
  556.5 16.5 %fusion.2 = f32[768,3072]{1,0:T(8,128)S(1)} fusion(bf16[384,3072]{1,0:T(8,128)(2,1)S(1)} %collective-permute-done.70, bf16[384,1536]{1,0:T(8,128)(2,1)S(1)} %maximum_select_fusion.8, bf16[384,1536]{1,0:T(8,128)(2,1)S(1)} %maximum_select_fusion.7, pred[]{:T(512)S(6)} %eq.59), kind=kLoop, calls=%fused_computation.8 | loop fusion | flops 33030144 | bytes 14155777 | tf_op jit(solution)/shard_map/convert_element_type | solution.py:568
  573.1 3.1 fusion.7
  576.2 6.1 maximum_bitcast_fusion
  582.3 18.0 %fusion = f32[784,3072]{1,0:T(8,128)S(1)} fusion(bf16[392,3072]{1,0:T(8,128)(2,1)} %collective-permute-done.60, bf16[392,1536]{1,0:T(8,128)(2,1)S(1)} %maximum_select_fusion.4, bf16[392,1536]{1,0:T(8,128)(2,1)S(1)} %maximum_select_fusion.3, pred[]{:T(512)S(6)} %eq.59), kind=kLoop, calls=%fused_computation.3 | loop fusion | flops 33718272 | bytes 14450689 | tf_op jit(solution)/shard_map/convert_element_type | solution.py:569
  601.5 4.4 slice_bitcast_fusion
  605.8 17.9 %fusion.1 = f32[768,3072]{1,0:T(8,128)S(1)} fusion(bf16[384,3072]{1,0:T(8,128)(2,1)} %collective-permute-done.44, bf16[384,1536]{1,0:T(8,128)(2,1)S(1)} %maximum_select_fusion.6, bf16[384,1536]{1,0:T(8,128)(2,1)S(1)} %maximum_select_fusion.5, pred[]{:T(512)S(6)} %eq.59), kind=kLoop, calls=%fused_computation.6 | loop fusion | flops 33030144 | bytes 14155777 | tf_op jit(solution)/shard_map/convert_element_type | solution.py:578
  623.7 3.5 slice.138
  (240 shorter events, 77.2 us)
Async XLA Ops:
  21.2 33.4 %collective-permute-start = (bf16[591,768]{1,0:T(8,128)(2,1)}, bf16[591,768]{1,0:T(8,128)(2,1)S(1)}, u32[]{:S(2)}, u32[]{:S(2)}) collective-permute-start(bf16[591,768]{1,0:T(8,128)(2,1)} %get-tuple-element.48.x_ref.refs_0_), channel_id=1, source_target_pairs={{0,1},{1,2},{2,3},{3,0},{4,5},{5,6},{6,7},{7,4},{8,9},{9,10},{10,1... | collective-permute-start | bytes 2723336 | tf_op jit(solution)/shard_map/ppermute | solution.py:406
  24.2 65.3 %collective-permute-start.5 = (bf16[591,768]{1,0:T(8,128)(2,1)}, bf16[591,768]{1,0:T(8,128)(2,1)S(1)}, u32[]{:S(2)}, u32[]{:S(2)}) collective-permute-start(bf16[591,768]{1,0:T(8,128)(2,1)} %get-tuple-element.48.x_ref.refs_0_), channel_id=1, source_target_pairs={{0,3},{1,0},{2,1},{3,2},{4,7},{5,4},{6,5},{7,6},{8,11},{9,8},{10,9... | collective-permute-start | bytes 2723336 | tf_op jit(solution)/shard_map/ppermute | solution.py:406
  26.2 64.9 %collective-permute-start.8 = (bf16[591,768]{1,0:T(8,128)(2,1)}, bf16[591,768]{1,0:T(8,128)(2,1)S(1)}, u32[]{:S(2)}, u32[]{:S(2)}) collective-permute-start(bf16[591,768]{1,0:T(8,128)(2,1)} %up_ref.3), channel_id=1, source_target_pairs={{0,3},{1,0},{2,1},{3,2},{4,7},{5,4},{6,5},{7,6},{8,11},{9,8},{10,9... | collective-permute-start | bytes 2723336 | tf_op jit(solution)/shard_map/ppermute | solution.py:406
  28.3 78.0 %collective-permute-start.1 = (bf16[591,768]{1,0:T(8,128)(2,1)}, bf16[591,768]{1,0:T(8,128)(2,1)}, u32[]{:S(2)}, u32[]{:S(2)}) collective-permute-start(bf16[591,768]{1,0:T(8,128)(2,1)} %up_ref.3), channel_id=1, source_target_pairs={{0,1},{1,2},{2,3},{3,0},{4,5},{5,6},{6,7},{7,4},{8,9},{9,10},{10,1... | collective-permute-start | bytes 2723336 | tf_op jit(solution)/shard_map/ppermute | solution.py:406
  29.2 83.4 %collective-permute-start.2 = (s32[591,2]{1,0:T(8,128)}, s32[591,2]{1,0:T(8,128)S(1)}, u32[]{:S(2)}, u32[]{:S(2)}) collective-permute-start(s32[591,2]{1,0:T(8,128)} %copy.33.routes_ref), channel_id=1, source_target_pairs={{0,1},{1,2},{2,3},{3,0},{4,5},{5,6},{6,7},{7,4},{8,9},{9,10},{10,1... | collective-permute-start | bytes 14192 | tf_op jit(solution)/shard_map/ppermute | solution.py:406
  55.6 103.5 %collective-permute-start.10 = (s32[591,2]{1,0:T(8,128)}, s32[591,2]{1,0:T(8,128)S(1)}, u32[]{:S(2)}, u32[]{:S(2)}) collective-permute-start(s32[591,2]{1,0:T(8,128)} %copy.33.routes_ref), channel_id=1, source_target_pairs={{0,2},{1,3},{2,0},{3,1},{4,6},{5,7},{6,4},{7,5},{8,10},{9,11},{10,... | collective-permute-start | bytes 14192 | tf_op jit(solution)/shard_map/ppermute | solution.py:406
  89.5 52.0 %collective-permute-start.4 = (bf16[288,768]{1,0:T(8,128)(2,1)S(1)}, bf16[288,768]{1,0:T(8,128)(2,1)S(1)}, u32[]{:S(2)}, u32[]{:S(2)}) collective-permute-start(bf16[288,768]{1,0:T(8,128)(2,1)S(1)} %slice.128), channel_id=1, source_target_pairs={{0,1},{1,2},{2,3},{3,0},{4,5},{5,6},{6,7},{7,4},{8,9},{9,10},{10,1... | collective-permute-start | bytes 1327112 | tf_op jit(solution)/shard_map/ppermute | solution.py:406
  91.2 67.8 %collective-permute-start.6 = (bf16[303,768]{1,0:T(8,128)(2,1)S(1)}, bf16[303,768]{1,0:T(8,128)(2,1)S(1)}, u32[]{:S(2)}, u32[]{:S(2)}) collective-permute-start(bf16[303,768]{1,0:T(8,128)(2,1)S(1)} %slice.129), channel_id=1, source_target_pairs={{0,3},{1,0},{2,1},{3,2},{4,7},{5,4},{6,5},{7,6},{8,11},{9,8},{10,9... | collective-permute-start | bytes 1396232 | tf_op jit(solution)/shard_map/ppermute | solution.py:406
  106.3 51.8 %collective-permute-start.9 = (bf16[303,768]{1,0:T(8,128)(2,1)S(1)}, bf16[303,768]{1,0:T(8,128)(2,1)S(1)}, u32[]{:S(2)}, u32[]{:S(2)}) collective-permute-start(bf16[303,768]{1,0:T(8,128)(2,1)S(1)} %slice.131), channel_id=1, source_target_pairs={{0,3},{1,0},{2,1},{3,2},{4,7},{5,4},{6,5},{7,6},{8,11},{9,8},{10,9... | collective-permute-start | bytes 1396232 | tf_op jit(solution)/shard_map/ppermute | solution.py:406
  112.6 45.5 %collective-permute-start.7 = (bf16[288,768]{1,0:T(8,128)(2,1)S(1)}, bf16[288,768]{1,0:T(8,128)(2,1)S(1)}, u32[]{:S(2)}, u32[]{:S(2)}) collective-permute-start(bf16[288,768]{1,0:T(8,128)(2,1)S(1)} %slice.130), channel_id=1, source_target_pairs={{0,1},{1,2},{2,3},{3,0},{4,5},{5,6},{6,7},{7,4},{8,9},{9,10},{10,1... | collective-permute-start | bytes 1327112 | tf_op jit(solution)/shard_map/ppermute | solution.py:406
  141.6 56.0 %collective-permute-start.15 = (s32[591,2]{1,0:T(8,128)}, s32[591,2]{1,0:T(8,128)S(1)}, u32[]{:S(2)}, u32[]{:S(2)}) collective-permute-start(s32[591,2]{1,0:T(8,128)} %copy.33.routes_ref), channel_id=1, source_target_pairs={{0,3},{1,0},{2,1},{3,2},{4,7},{5,4},{6,5},{7,6},{8,11},{9,8},{10,9... | collective-permute-start | bytes 14192 | tf_op jit(solution)/shard_map/ppermute | solution.py:406
  186.7 47.8 %collective-permute-start.20 = (bf16[303,768]{1,0:T(8,128)(2,1)S(1)}, bf16[303,768]{1,0:T(8,128)(2,1)S(1)}, u32[]{:S(2)}, u32[]{:S(2)}) collective-permute-start(bf16[303,768]{1,0:T(8,128)(2,1)S(1)} %slice.103), channel_id=1, source_target_pairs={{0,1},{1,2},{2,3},{3,0},{4,5},{5,6},{6,7},{7,4},{8,9},{9,10},{10,1... | collective-permute-start | bytes 1396232 | tf_op jit(solution)/shard_map/ppermute | solution.py:406
  197.6 33.1 %collective-permute-start.18 = (bf16[288,768]{1,0:T(8,128)(2,1)S(1)}, bf16[288,768]{1,0:T(8,128)(2,1)}, u32[]{:S(2)}, u32[]{:S(2)}) collective-permute-start(bf16[288,768]{1,0:T(8,128)(2,1)S(1)} %slice.102), channel_id=1, source_target_pairs={{0,3},{1,0},{2,1},{3,2},{4,7},{5,4},{6,5},{7,6},{8,11},{9,8},{10,9... | collective-permute-start | bytes 1327112 | tf_op jit(solution)/shard_map/ppermute | solution.py:406
  225.6 28.9 %collective-permute-start.17 = (bf16[591,768]{1,0:T(8,128)(2,1)}, bf16[591,768]{1,0:T(8,128)(2,1)S(1)}, u32[]{:S(2)}, u32[]{:S(2)}) collective-permute-start(bf16[591,768]{1,0:T(8,128)(2,1)} %get-tuple-element.54), channel_id=1, source_target_pairs={{0,3},{1,0},{2,1},{3,2},{4,7},{5,4},{6,5},{7,6},{8,11},{9,8},{10,9... | collective-permute-start | bytes 2723336 | tf_op jit(solution)/shard_map/ppermute | solution.py:406
  229.0 42.7 %collective-permute-start.22 = (bf16[591,768]{1,0:T(8,128)(2,1)}, bf16[591,768]{1,0:T(8,128)(2,1)S(1)}, u32[]{:S(2)}, u32[]{:S(2)}) collective-permute-start(bf16[591,768]{1,0:T(8,128)(2,1)} %get-tuple-element.56), channel_id=1, source_target_pairs={{0,1},{1,2},{2,3},{3,0},{4,5},{5,6},{6,7},{7,4},{8,9},{9,10},{10,1... | collective-permute-start | bytes 2723336 | tf_op jit(solution)/shard_map/ppermute | solution.py:406
  229.1 25.4 %collective-permute-start.47 = (f32[4,768]{1,0:T(4,128)S(1)}, f32[4,768]{1,0:T(4,128)S(1)}, u32[]{:S(2)}, u32[]{:S(2)}) collective-permute-start(f32[4,768]{1,0:T(4,128)S(1)} %add.327), channel_id=1, source_target_pairs={{0,16},{4,20},{8,24},{12,28},{16,0},{20,4},{24,8},{28,12},{1,17},{... | collective-permute-start | bytes 36872 | tf_op jit(solution)/shard_map/ppermute | solution.py:444
  230.6 48.3 %collective-permute-start.19 = (bf16[288,768]{1,0:T(8,128)(2,1)}, bf16[288,768]{1,0:T(8,128)(2,1)S(1)}, u32[]{:S(2)}, u32[]{:S(2)}) collective-permute-start(bf16[288,768]{1,0:T(8,128)(2,1)} %collective-permute-done.18), channel_id=1, source_target_pairs={{0,3},{1,0},{2,1},{3,2},{4,7},{5,4},{6,5},{7,6},{8,11},{9,8},{10,9... | collective-permute-start | bytes 1327112 | tf_op jit(solution)/shard_map/ppermute | solution.py:406
  234.5 56.9 %collective-permute-start.21 = (bf16[303,768]{1,0:T(8,128)(2,1)S(1)}, bf16[303,768]{1,0:T(8,128)(2,1)S(1)}, u32[]{:S(2)}, u32[]{:S(2)}) collective-permute-start(bf16[303,768]{1,0:T(8,128)(2,1)S(1)} %collective-permute-done.20), channel_id=1, source_target_pairs={{0,1},{1,2},{2,3},{3,0},{4,5},{5,6},{6,7},{7,4},{8,9},{9,10},{10,1... | collective-permute-start | bytes 1396232 | tf_op jit(solution)/shard_map/ppermute | solution.py:406
  254.4 105.8 %collective-permute-start.16 = (bf16[591,768]{1,0:T(8,128)(2,1)}, bf16[591,768]{1,0:T(8,128)(2,1)S(1)}, u32[]{:S(2)}, u32[]{:S(2)}) collective-permute-start(bf16[591,768]{1,0:T(8,128)(2,1)} %get-tuple-element.52), channel_id=1, source_target_pairs={{0,1},{1,2},{2,3},{3,0},{4,5},{5,6},{6,7},{7,4},{8,9},{9,10},{10,1... | collective-permute-start | bytes 2723336 | tf_op jit(solution)/shard_map/ppermute | solution.py:406
  254.5 71.4 %collective-permute-start.48 = (f32[4,768]{1,0:T(4,128)S(1)}, f32[4,768]{1,0:T(4,128)S(1)}, u32[]{:S(2)}, u32[]{:S(2)}) collective-permute-start(f32[4,768]{1,0:T(4,128)S(1)} %add.328), channel_id=1, source_target_pairs={{0,1},{1,2},{2,3},{3,0},{4,5},{5,6},{6,7},{7,4},{8,9},{9,10},{10,1... | collective-permute-start | bytes 36872 | tf_op jit(solution)/shard_map/ppermute | solution.py:406
  271.8 54.3 %collective-permute-start.49 = (f32[4,768]{1,0:T(4,128)S(1)}, f32[4,768]{1,0:T(4,128)S(1)}, u32[]{:S(2)}, u32[]{:S(2)}) collective-permute-start(f32[4,768]{1,0:T(4,128)S(1)} %add.328), channel_id=1, source_target_pairs={{0,2},{1,3},{2,0},{3,1},{4,6},{5,7},{6,4},{7,5},{8,10},{9,11},{10,... | collective-permute-start | bytes 36872 | tf_op jit(solution)/shard_map/ppermute | solution.py:406
  278.9 50.9 %collective-permute-start.50 = (f32[4,768]{1,0:T(4,128)S(1)}, f32[4,768]{1,0:T(4,128)S(1)}, u32[]{:S(2)}, u32[]{:S(2)}) collective-permute-start(f32[4,768]{1,0:T(4,128)S(1)} %add.328), channel_id=1, source_target_pairs={{0,3},{1,0},{2,1},{3,2},{4,7},{5,4},{6,5},{7,6},{8,11},{9,8},{10,9... | collective-permute-start | bytes 36872 | tf_op jit(solution)/shard_map/ppermute | solution.py:406
  325.5 77.4 %collective-permute-start.61 = (bf16[384,3072]{1,0:T(8,128)(2,1)}, bf16[384,3072]{1,0:T(8,128)(2,1)}, u32[]{:S(2)}, u32[]{:S(2)}) collective-permute-start(bf16[384,3072]{1,0:T(8,128)(2,1)} %constant_dynamic-slice_fusion.4), channel_id=1, source_target_pairs={{0,4},{4,0},{8,12},{12,8},{16,20},{20,16},{24,28},{28,24},{1,5},{5... | collective-permute-start | bytes 7077896 | tf_op jit(solution)/shard_map/ppermute | solution.py:444
  326.0 32.3 %collective-permute-start.13 = (bf16[303,768]{1,0:T(8,128)(2,1)S(1)}, bf16[303,768]{1,0:T(8,128)(2,1)}, u32[]{:S(2)}, u32[]{:S(2)}) collective-permute-start(bf16[303,768]{1,0:T(8,128)(2,1)S(1)} %slice.101), channel_id=1, source_target_pairs={{0,1},{1,2},{2,3},{3,0},{4,5},{5,6},{6,7},{7,4},{8,9},{9,10},{10,1... | collective-permute-start | bytes 1396232 | tf_op jit(solution)/shard_map/ppermute | solution.py:406
  326.0 32.1 %collective-permute-start.11 = (bf16[288,768]{1,0:T(8,128)(2,1)}, bf16[288,768]{1,0:T(8,128)(2,1)}, u32[]{:S(2)}, u32[]{:S(2)}) collective-permute-start(bf16[288,768]{1,0:T(8,128)(2,1)} %slice.100), channel_id=1, source_target_pairs={{0,3},{1,0},{2,1},{3,2},{4,7},{5,4},{6,5},{7,6},{8,11},{9,8},{10,9... | collective-permute-start | bytes 1327112 | tf_op jit(solution)/shard_map/ppermute | solution.py:406
  329.8 26.0 %collective-permute-start.24 = (f32[8,768]{1,0:T(8,128)S(1)}, f32[8,768]{1,0:T(8,128)S(1)}, u32[]{:S(2)}, u32[]{:S(2)}) collective-permute-start(f32[8,768]{1,0:T(8,128)S(1)} %add.278), channel_id=1, source_target_pairs={{0,8},{4,12},{8,0},{12,4},{16,24},{20,28},{24,16},{28,20},{1,9},{5... | collective-permute-start | bytes 73736 | tf_op jit(solution)/shard_map/ppermute | solution.py:444
  355.8 23.5 %collective-permute-start.3 = (bf16[591,768]{1,0:T(8,128)(2,1)}, bf16[591,768]{1,0:T(8,128)(2,1)S(1)}, u32[]{:S(2)}, u32[]{:S(2)}) collective-permute-start(bf16[591,768]{1,0:T(8,128)(2,1)} %get-tuple-element.50), channel_id=1, source_target_pairs={{0,3},{1,0},{2,1},{3,2},{4,7},{5,4},{6,5},{7,6},{8,11},{9,8},{10,9... | collective-permute-start | bytes 2723336 | tf_op jit(solution)/shard_map/ppermute | solution.py:406
  358.2 40.0 %collective-permute-start.12 = (bf16[288,768]{1,0:T(8,128)(2,1)}, bf16[288,768]{1,0:T(8,128)(2,1)S(1)}, u32[]{:S(2)}, u32[]{:S(2)}) collective-permute-start(bf16[288,768]{1,0:T(8,128)(2,1)} %collective-permute-done.11), channel_id=1, source_target_pairs={{0,3},{1,0},{2,1},{3,2},{4,7},{5,4},{6,5},{7,6},{8,11},{9,8},{10,9... | collective-permute-start | bytes 1327112 | tf_op jit(solution)/shard_map/ppermute | solution.py:406
  358.2 39.9 %collective-permute-start.14 = (bf16[303,768]{1,0:T(8,128)(2,1)}, bf16[303,768]{1,0:T(8,128)(2,1)S(1)}, u32[]{:S(2)}, u32[]{:S(2)}) collective-permute-start(bf16[303,768]{1,0:T(8,128)(2,1)} %collective-permute-done.13), channel_id=1, source_target_pairs={{0,1},{1,2},{2,3},{3,0},{4,5},{5,6},{6,7},{7,4},{8,9},{9,10},{10,1... | collective-permute-start | bytes 1396232 | tf_op jit(solution)/shard_map/ppermute | solution.py:406
  364.1 44.9 %collective-permute-start.51 = (bf16[392,3072]{1,0:T(8,128)(2,1)S(1)}, bf16[392,3072]{1,0:T(8,128)(2,1)S(1)}, u32[]{:S(2)}, u32[]{:S(2)}) collective-permute-start(bf16[392,3072]{1,0:T(8,128)(2,1)S(1)} %constant_dynamic-slice_fusion.9), channel_id=1, source_target_pairs={{0,4},{4,0},{8,12},{12,8},{16,20},{20,16},{24,28},{28,24},{1,5},{5... | collective-permute-start | bytes 7225352 | tf_op jit(solution)/shard_map/ppermute | solution.py:444
  379.4 22.3 %collective-permute-start.26 = (f32[8,768]{1,0:T(8,128)S(1)}, f32[8,768]{1,0:T(8,128)S(1)}, u32[]{:S(2)}, u32[]{:S(2)}) collective-permute-start(f32[8,768]{1,0:T(8,128)S(1)} %add.280), channel_id=1, source_target_pairs={{0,1},{1,2},{2,3},{3,0},{4,5},{5,6},{6,7},{7,4},{8,9},{9,10},{10,1... | collective-permute-start | bytes 73736 | tf_op jit(solution)/shard_map/ppermute | solution.py:406
  401.7 43.7 %collective-permute-start.29 = (bf16[384,3072]{1,0:T(8,128)(2,1)S(1)}, bf16[384,3072]{1,0:T(8,128)(2,1)S(1)}, u32[]{:S(2)}, u32[]{:S(2)}) collective-permute-start(bf16[384,3072]{1,0:T(8,128)(2,1)S(1)} %constant_dynamic-slice_fusion.14), channel_id=1, source_target_pairs={{0,4},{4,0},{8,12},{12,8},{16,20},{20,16},{24,28},{28,24},{1,5},{5... | collective-permute-start | bytes 7077896 | tf_op jit(solution)/shard_map/ppermute | solution.py:444
  405.8 16.3 %collective-permute-start.62 = (bf16[384,768]{1,0:T(8,128)(2,1)S(1)}, bf16[384,768]{1,0:T(8,128)(2,1)S(1)}, u32[]{:S(2)}, u32[]{:S(2)}) collective-permute-start(bf16[384,768]{1,0:T(8,128)(2,1)S(1)} %constant_dynamic-slice_fusion.3), channel_id=1, source_target_pairs={{0,8},{4,12},{8,0},{12,4},{16,24},{20,28},{24,16},{28,20},{1,9},{5... | collective-permute-start | bytes 1769480 | tf_op jit(solution)/shard_map/ppermute | solution.py:444
  407.4 16.5 %collective-permute-start.66 = (bf16[384,768]{1,0:T(8,128)(2,1)S(1)}, bf16[384,768]{1,0:T(8,128)(2,1)S(1)}, u32[]{:S(2)}, u32[]{:S(2)}) collective-permute-start(bf16[384,768]{1,0:T(8,128)(2,1)S(1)} %constant_dynamic-slice_fusion.1), channel_id=1, source_target_pairs={{0,16},{4,20},{8,24},{12,28},{16,0},{20,4},{24,8},{28,12},{1,17},{... | collective-permute-start | bytes 1769480 | tf_op jit(solution)/shard_map/ppermute | solution.py:444
  410.2 24.9 %collective-permute-start.52 = (bf16[392,768]{1,0:T(8,128)(2,1)S(1)}, bf16[392,768]{1,0:T(8,128)(2,1)S(1)}, u32[]{:S(2)}, u32[]{:S(2)}) collective-permute-start(bf16[392,768]{1,0:T(8,128)(2,1)S(1)} %constant_dynamic-slice_fusion.8), channel_id=1, source_target_pairs={{0,8},{4,12},{8,0},{12,4},{16,24},{20,28},{24,16},{28,20},{1,9},{5... | collective-permute-start | bytes 1806344 | tf_op jit(solution)/shard_map/ppermute | solution.py:444
  410.8 26.0 %collective-permute-start.56 = (bf16[392,768]{1,0:T(8,128)(2,1)S(1)}, bf16[392,768]{1,0:T(8,128)(2,1)S(1)}, u32[]{:S(2)}, u32[]{:S(2)}) collective-permute-start(bf16[392,768]{1,0:T(8,128)(2,1)S(1)} %constant_dynamic-slice_fusion.6), channel_id=1, source_target_pairs={{0,16},{4,20},{8,24},{12,28},{16,0},{20,4},{24,8},{28,12},{1,17},{... | collective-permute-start | bytes 1806344 | tf_op jit(solution)/shard_map/ppermute | solution.py:444
  422.4 20.6 %collective-permute-start.63 = (bf16[384,384]{1,0:T(8,128)(2,1)S(1)}, bf16[384,384]{1,0:T(8,128)(2,1)S(1)}, u32[]{:S(2)}, u32[]{:S(2)}) collective-permute-start(bf16[384,384]{1,0:T(8,128)(2,1)S(1)} %constant_dynamic-slice_fusion.2), channel_id=1, source_target_pairs={{0,16},{4,20},{8,24},{12,28},{16,0},{20,4},{24,8},{28,12},{1,17},{... | collective-permute-start | bytes 884744 | tf_op jit(solution)/shard_map/ppermute | solution.py:444
  424.2 20.5 %collective-permute-start.67 = (bf16[384,384]{1,0:T(8,128)(2,1)S(1)}, bf16[384,384]{1,0:T(8,128)(2,1)S(1)}, u32[]{:S(2)}, u32[]{:S(2)}) collective-permute-start(bf16[384,384]{1,0:T(8,128)(2,1)S(1)} %constant_dynamic-slice_fusion), channel_id=1, source_target_pairs={{0,8},{4,12},{8,0},{12,4},{16,24},{20,28},{24,16},{28,20},{1,9},{5... | collective-permute-start | bytes 884744 | tf_op jit(solution)/shard_map/ppermute | solution.py:444
  435.3 14.2 %collective-permute-start.53 = (bf16[392,384]{1,0:T(8,128)(2,1)S(1)}, bf16[392,384]{1,0:T(8,128)(2,1)S(1)}, u32[]{:S(2)}, u32[]{:S(2)}) collective-permute-start(bf16[392,384]{1,0:T(8,128)(2,1)S(1)} %constant_dynamic-slice_fusion.7), channel_id=1, source_target_pairs={{0,16},{4,20},{8,24},{12,28},{16,0},{20,4},{24,8},{28,12},{1,17},{... | collective-permute-start | bytes 903176 | tf_op jit(solution)/shard_map/ppermute | solution.py:444
  437.1 13.0 %collective-permute-start.57 = (bf16[392,384]{1,0:T(8,128)(2,1)S(1)}, bf16[392,384]{1,0:T(8,128)(2,1)S(1)}, u32[]{:S(2)}, u32[]{:S(2)}) collective-permute-start(bf16[392,384]{1,0:T(8,128)(2,1)S(1)} %constant_dynamic-slice_fusion.5), channel_id=1, source_target_pairs={{0,8},{4,12},{8,0},{12,4},{16,24},{20,28},{24,16},{28,20},{1,9},{5... | collective-permute-start | bytes 903176 | tf_op jit(solution)/shard_map/ppermute | solution.py:444
  443.1 12.7 %collective-permute-start.64 = (bf16[384,384]{1,0:T(8,128)(2,1)S(1)}, bf16[384,384]{1,0:T(8,128)(2,1)S(1)}, u32[]{:S(2)}, u32[]{:S(2)}) collective-permute-start(bf16[384,384]{1,0:T(8,128)(2,1)S(1)} %add_convert_fusion.13), channel_id=1, source_target_pairs={{0,16},{4,20},{8,24},{12,28},{16,0},{20,4},{24,8},{28,12},{1,17},{... | collective-permute-start | bytes 884744 | tf_op jit(solution)/shard_map/ppermute | solution.py:444
  444.8 11.7 %collective-permute-start.68 = (bf16[384,384]{1,0:T(8,128)(2,1)S(1)}, bf16[384,384]{1,0:T(8,128)(2,1)S(1)}, u32[]{:S(2)}, u32[]{:S(2)}) collective-permute-start(bf16[384,384]{1,0:T(8,128)(2,1)S(1)} %add_convert_fusion.12), channel_id=1, source_target_pairs={{0,8},{4,12},{8,0},{12,4},{16,24},{20,28},{24,16},{28,20},{1,9},{5... | collective-permute-start | bytes 884744 | tf_op jit(solution)/shard_map/ppermute | solution.py:444
  446.5 28.8 %collective-permute-start.32 = (bf16[384,768]{1,0:T(8,128)(2,1)S(1)}, bf16[384,768]{1,0:T(8,128)(2,1)S(1)}, u32[]{:S(2)}, u32[]{:S(2)}) collective-permute-start(bf16[384,768]{1,0:T(8,128)(2,1)S(1)} %constant_dynamic-slice_fusion.11), channel_id=1, source_target_pairs={{0,16},{4,20},{8,24},{12,28},{16,0},{20,4},{24,8},{28,12},{1,17},{... | collective-permute-start | bytes 1769480 | tf_op jit(solution)/shard_map/ppermute | solution.py:444
  449.4 27.3 %collective-permute-start.30 = (bf16[384,768]{1,0:T(8,128)(2,1)S(1)}, bf16[384,768]{1,0:T(8,128)(2,1)S(1)}, u32[]{:S(2)}, u32[]{:S(2)}) collective-permute-start(bf16[384,768]{1,0:T(8,128)(2,1)S(1)} %constant_dynamic-slice_fusion.13), channel_id=1, source_target_pairs={{0,8},{4,12},{8,0},{12,4},{16,24},{20,28},{24,16},{28,20},{1,9},{5... | collective-permute-start | bytes 1769480 | tf_op jit(solution)/shard_map/ppermute | solution.py:444
  450.1 22.8 %collective-permute-start.54 = (bf16[392,384]{1,0:T(8,128)(2,1)S(1)}, bf16[392,384]{1,0:T(8,128)(2,1)S(1)}, u32[]{:S(2)}, u32[]{:S(2)}) collective-permute-start(bf16[392,384]{1,0:T(8,128)(2,1)S(1)} %add_convert_fusion.11), channel_id=1, source_target_pairs={{0,16},{4,20},{8,24},{12,28},{16,0},{20,4},{24,8},{28,12},{1,17},{... | collective-permute-start | bytes 903176 | tf_op jit(solution)/shard_map/ppermute | solution.py:444
  455.8 18.8 %collective-permute-start.58 = (bf16[392,384]{1,0:T(8,128)(2,1)S(1)}, bf16[392,384]{1,0:T(8,128)(2,1)S(1)}, u32[]{:S(2)}, u32[]{:S(2)}) collective-permute-start(bf16[392,384]{1,0:T(8,128)(2,1)S(1)} %add_convert_fusion.10), channel_id=1, source_target_pairs={{0,8},{4,12},{8,0},{12,4},{16,24},{20,28},{24,16},{28,20},{1,9},{5... | collective-permute-start | bytes 903176 | tf_op jit(solution)/shard_map/ppermute | solution.py:444
  456.5 30.0 %collective-permute-start.65 = (bf16[384,768]{1,0:T(8,128)(2,1)S(1)}, bf16[384,768]{1,0:T(8,128)(2,1)S(1)}, u32[]{:S(2)}, u32[]{:S(2)}) collective-permute-start(bf16[384,768]{1,0:T(8,128)(2,1)S(1)} %maximum_select_fusion.13), channel_id=1, source_target_pairs={{0,8},{4,12},{8,0},{12,4},{16,24},{20,28},{24,16},{28,20},{1,9},{5... | collective-permute-start | bytes 1769480 | tf_op jit(solution)/shard_map/ppermute | solution.py:444
  472.9 35.2 %collective-permute-start.69 = (bf16[384,768]{1,0:T(8,128)(2,1)S(1)}, bf16[384,768]{1,0:T(8,128)(2,1)S(1)}, u32[]{:S(2)}, u32[]{:S(2)}) collective-permute-start(bf16[384,768]{1,0:T(8,128)(2,1)S(1)} %maximum_select_fusion.14), channel_id=1, source_target_pairs={{0,16},{4,20},{8,24},{12,28},{16,0},{20,4},{24,8},{28,12},{1,17},{... | collective-permute-start | bytes 1769480 | tf_op jit(solution)/shard_map/ppermute | solution.py:444
  474.6 59.8 %collective-permute-start.55 = (bf16[392,768]{1,0:T(8,128)(2,1)S(1)}, bf16[392,768]{1,0:T(8,128)(2,1)S(1)}, u32[]{:S(2)}, u32[]{:S(2)}) collective-permute-start(bf16[392,768]{1,0:T(8,128)(2,1)S(1)} %maximum_select_fusion.9), channel_id=1, source_target_pairs={{0,8},{4,12},{8,0},{12,4},{16,24},{20,28},{24,16},{28,20},{1,9},{5... | collective-permute-start | bytes 1806344 | tf_op jit(solution)/shard_map/ppermute | solution.py:444
  475.3 64.7 %collective-permute-start.59 = (bf16[392,768]{1,0:T(8,128)(2,1)S(1)}, bf16[392,768]{1,0:T(8,128)(2,1)S(1)}, u32[]{:S(2)}, u32[]{:S(2)}) collective-permute-start(bf16[392,768]{1,0:T(8,128)(2,1)S(1)} %maximum_select_fusion.10), channel_id=1, source_target_pairs={{0,16},{4,20},{8,24},{12,28},{16,0},{20,4},{24,8},{28,12},{1,17},{... | collective-permute-start | bytes 1806344 | tf_op jit(solution)/shard_map/ppermute | solution.py:444
  476.7 26.7 %collective-permute-start.33 = (bf16[384,384]{1,0:T(8,128)(2,1)S(1)}, bf16[384,384]{1,0:T(8,128)(2,1)S(1)}, u32[]{:S(2)}, u32[]{:S(2)}) collective-permute-start(bf16[384,384]{1,0:T(8,128)(2,1)S(1)} %constant_dynamic-slice_fusion.10), channel_id=1, source_target_pairs={{0,8},{4,12},{8,0},{12,4},{16,24},{20,28},{24,16},{28,20},{1,9},{5... | collective-permute-start | bytes 884744 | tf_op jit(solution)/shard_map/ppermute | solution.py:444
  486.5 19.0 %collective-permute-start.31 = (bf16[384,384]{1,0:T(8,128)(2,1)S(1)}, bf16[384,384]{1,0:T(8,128)(2,1)S(1)}, u32[]{:S(2)}, u32[]{:S(2)}) collective-permute-start(bf16[384,384]{1,0:T(8,128)(2,1)S(1)} %constant_dynamic-slice_fusion.12), channel_id=1, source_target_pairs={{0,16},{4,20},{8,24},{12,28},{16,0},{20,4},{24,8},{28,12},{1,17},{... | collective-permute-start | bytes 884744 | tf_op jit(solution)/shard_map/ppermute | solution.py:444
  505.7 8.2 %collective-permute-start.34 = (bf16[96,768]{1,0:T(8,128)(2,1)S(1)}, bf16[96,768]{1,0:T(8,128)(2,1)S(1)}, u32[]{:S(2)}, u32[]{:S(2)}) collective-permute-start(bf16[96,768]{1,0:T(8,128)(2,1)S(1)} %get-tuple-element.99), channel_id=1, source_target_pairs={{0,1},{1,2},{2,3},{3,0},{4,5},{5,6},{6,7},{7,4},{8,9},{9,10},{10,1... | collective-permute-start | bytes 442376 | tf_op jit(solution)/shard_map/ppermute | solution.py:406
  505.7 11.3 %collective-permute-start.35 = (bf16[96,768]{1,0:T(8,128)(2,1)S(1)}, bf16[96,768]{1,0:T(8,128)(2,1)S(1)}, u32[]{:S(2)}, u32[]{:S(2)}) collective-permute-start(bf16[96,768]{1,0:T(8,128)(2,1)S(1)} %get-tuple-element.100), channel_id=1, source_target_pairs={{0,2},{1,3},{2,0},{3,1},{4,6},{5,7},{6,4},{7,5},{8,10},{9,11},{10,... | collective-permute-start | bytes 442376 | tf_op jit(solution)/shard_map/ppermute | solution.py:406
  508.1 8.9 %collective-permute-start.36 = (bf16[96,768]{1,0:T(8,128)(2,1)S(1)}, bf16[96,768]{1,0:T(8,128)(2,1)S(1)}, u32[]{:S(2)}, u32[]{:S(2)}) collective-permute-start(bf16[96,768]{1,0:T(8,128)(2,1)S(1)} %get-tuple-element.101), channel_id=1, source_target_pairs={{0,3},{1,0},{2,1},{3,2},{4,7},{5,4},{6,5},{7,6},{8,11},{9,8},{10,9... | collective-permute-start | bytes 442376 | tf_op jit(solution)/shard_map/ppermute | solution.py:406
  517.1 8.3 %collective-permute-start.37 = (bf16[96,768]{1,0:T(8,128)(2,1)S(1)}, bf16[96,768]{1,0:T(8,128)(2,1)S(1)}, u32[]{:S(2)}, u32[]{:S(2)}) collective-permute-start(bf16[96,768]{1,0:T(8,128)(2,1)S(1)} %get-tuple-element.86), channel_id=1, source_target_pairs={{0,1},{1,2},{2,3},{3,0},{4,5},{5,6},{6,7},{7,4},{8,9},{9,10},{10,1... | collective-permute-start | bytes 442376 | tf_op jit(solution)/shard_map/ppermute | solution.py:406
  519.9 10.1 %collective-permute-start.38 = (bf16[96,768]{1,0:T(8,128)(2,1)S(1)}, bf16[96,768]{1,0:T(8,128)(2,1)S(1)}, u32[]{:S(2)}, u32[]{:S(2)}) collective-permute-start(bf16[96,768]{1,0:T(8,128)(2,1)S(1)} %get-tuple-element.86), channel_id=1, source_target_pairs={{0,2},{1,3},{2,0},{3,1},{4,6},{5,7},{6,4},{7,5},{8,10},{9,11},{10,... | collective-permute-start | bytes 442376 | tf_op jit(solution)/shard_map/ppermute | solution.py:406
  521.3 35.2 %collective-permute-start.70 = (bf16[384,3072]{1,0:T(8,128)(2,1)S(1)}, bf16[384,3072]{1,0:T(8,128)(2,1)S(1)}, u32[]{:S(2)}, u32[]{:S(2)}) collective-permute-start(bf16[384,3072]{1,0:T(8,128)(2,1)S(1)} %pad_maximum_fusion.2), channel_id=1, source_target_pairs={{0,4},{4,0},{8,12},{12,8},{16,20},{20,16},{24,28},{28,24},{1,5},{5... | collective-permute-start | bytes 7077896 | tf_op jit(solution)/shard_map/ppermute | solution.py:444
  532.2 6.9 %collective-permute-start.40 = (bf16[384,384]{1,0:T(8,128)(2,1)S(1)}, bf16[384,384]{1,0:T(8,128)(2,1)S(1)}, u32[]{:S(2)}, u32[]{:S(2)}) collective-permute-start(bf16[384,384]{1,0:T(8,128)(2,1)S(1)} %get-tuple-element.97), channel_id=1, source_target_pairs={{0,16},{4,20},{8,24},{12,28},{16,0},{20,4},{24,8},{28,12},{1,17},{... | collective-permute-start | bytes 884744 | tf_op jit(solution)/shard_map/ppermute | solution.py:444
  534.7 9.5 %collective-permute-start.42 = (bf16[384,384]{1,0:T(8,128)(2,1)S(1)}, bf16[384,384]{1,0:T(8,128)(2,1)S(1)}, u32[]{:S(2)}, u32[]{:S(2)}) collective-permute-start(bf16[384,384]{1,0:T(8,128)(2,1)S(1)} %get-tuple-element.98), channel_id=1, source_target_pairs={{0,8},{4,12},{8,0},{12,4},{16,24},{20,28},{24,16},{28,20},{1,9},{5... | collective-permute-start | bytes 884744 | tf_op jit(solution)/shard_map/ppermute | solution.py:444
  539.2 14.9 %collective-permute-start.41 = (bf16[384,768]{1,0:T(8,128)(2,1)S(1)}, bf16[384,768]{1,0:T(8,128)(2,1)S(1)}, u32[]{:S(2)}, u32[]{:S(2)}) collective-permute-start(bf16[384,768]{1,0:T(8,128)(2,1)S(1)} %maximum_select_fusion.11), channel_id=1, source_target_pairs={{0,8},{4,12},{8,0},{12,4},{16,24},{20,28},{24,16},{28,20},{1,9},{5... | collective-permute-start | bytes 1769480 | tf_op jit(solution)/shard_map/ppermute | solution.py:444
  544.3 10.1 %collective-permute-start.43 = (bf16[384,768]{1,0:T(8,128)(2,1)S(1)}, bf16[384,768]{1,0:T(8,128)(2,1)S(1)}, u32[]{:S(2)}, u32[]{:S(2)}) collective-permute-start(bf16[384,768]{1,0:T(8,128)(2,1)S(1)} %maximum_select_fusion.12), channel_id=1, source_target_pairs={{0,16},{4,20},{8,24},{12,28},{16,0},{20,4},{24,8},{28,12},{1,17},{... | collective-permute-start | bytes 1769480 | tf_op jit(solution)/shard_map/ppermute | solution.py:444
  546.2 36.1 %collective-permute-start.60 = (bf16[392,3072]{1,0:T(8,128)(2,1)}, bf16[392,3072]{1,0:T(8,128)(2,1)}, u32[]{:S(2)}, u32[]{:S(2)}) collective-permute-start(bf16[392,3072]{1,0:T(8,128)(2,1)} %pad_maximum_fusion), channel_id=1, source_target_pairs={{0,4},{4,0},{8,12},{12,8},{16,20},{20,16},{24,28},{28,24},{1,5},{5... | collective-permute-start | bytes 7225352 | tf_op jit(solution)/shard_map/ppermute | solution.py:444
  556.5 49.3 %collective-permute-start.44 = (bf16[384,3072]{1,0:T(8,128)(2,1)}, bf16[384,3072]{1,0:T(8,128)(2,1)}, u32[]{:S(2)}, u32[]{:S(2)}) collective-permute-start(bf16[384,3072]{1,0:T(8,128)(2,1)} %pad_maximum_fusion.1), channel_id=1, source_target_pairs={{0,4},{4,0},{8,12},{12,8},{16,20},{20,16},{24,28},{28,24},{1,5},{5... | collective-permute-start | bytes 7077896 | tf_op jit(solution)/shard_map/ppermute | solution.py:444
  (33 other events, 648.6 us)

commit v2 on v1

v2 whole, which is shorter than its diff:
```python
import functools

import jax
import jax.numpy as jnp
from jax import lax
from jax.experimental import pallas as pl
from jax.experimental.pallas import tpu as pltpu
from jax.sharding import PartitionSpec as P

HEADS = 12
HEAD_DIM = 64
SEQ = 197
NORM_EPS = 1e-06
F32 = jnp.float32
BF16 = jnp.bfloat16
LANES = 128
PAIR = LANES // HEAD_DIM
SEQ_PAD = 208
FF_TILE = 512
ROUTE_ROWS = 16
VMEM_BYTES = 58 * 2**20
COST_FLOPS = 4e8
FINAL_COST = 4
BACK_COST = 28
TAIL_SCALE = 0.305
TAIL_COEFS = (
    0.1216396663821839,
    0.12246803351870969,
    0.10341227166034979,
    0.12105264456174025,
    -0.03803921974174099,
    0.18578799927872533,
    -0.1530311110530253,
    0.03670976324394601,
)
INV_SQRT_2PI = 0.3989422804014327
VECS = ("g1", "b1", "qb", "vb", "ob", "g2", "b2", "none")


def dot(lhs, rhs):
    return lax.dot_general(lhs, rhs, (((1,), (0,)), ((), ())), preferred_element_type=F32)


def dot_rt(lhs, rhs):
    return lax.dot_general(lhs, rhs, (((1,), (1,)), ((), ())), preferred_element_type=F32)


def dot_lt(lhs, rhs):
    return lax.dot_general(lhs, rhs, (((0,), (0,)), ((), ())), preferred_element_type=F32)


def row_mean(values):
    return jnp.mean(values, axis=-1, keepdims=True)


def unit_norm(values):
    centred = values - row_mean(values)
    scale = lax.rsqrt(row_mean(centred * centred) + NORM_EPS)
    return centred * scale, scale


def column_sum(values):
    return jnp.sum(values, axis=0, keepdims=True)


def gelu_parts(pre):
    size = jnp.abs(pre)
    bell = jnp.exp(pre * pre * -0.5)
    frac = 1.0 / (1.0 + TAIL_SCALE * size)
    poly = jnp.full_like(pre, TAIL_COEFS[-1])
    for coef in TAIL_COEFS[-2::-1]:
        poly = poly * frac + coef
    tail = bell * (poly * frac)
    return jnp.where(pre >= 0, 1.0 - tail, tail), bell * INV_SQRT_2PI


def pair_masks(rows):
    lane = lax.broadcasted_iota(jnp.int32, (rows, LANES), 1)
    return [(lane >= h * HEAD_DIM) & (lane < (h + 1) * HEAD_DIM) for h in range(PAIR)]


def stack_heads(values, masks):
    return jnp.concatenate([jnp.where(m, values, 0.0) for m in masks], axis=0).astype(BF16)


def unstack_heads(values, masks):
    rows = values.shape[0] // PAIR
    picked = values[:rows]
    for h in range(1, PAIR):
        picked = jnp.where(masks[h], values[h * rows : (h + 1) * rows], picked)
    return picked


def probabilities(scores):
    key_id = lax.broadcasted_iota(jnp.int32, scores.shape, 1)
    scores = jnp.where(key_id < SEQ, scores, -1e30)
    weights = jnp.exp(scores - jnp.max(scores, axis=-1, keepdims=True))
    return weights * (1.0 / jnp.sum(weights, axis=-1, keepdims=True))


def attend_kernel(
    x_ref, vecs_ref, wqkv_ref, wout_ref,
    qkv_ref, ctx_ref, hidden_ref, mixed_ref,
    qkv_s, ctx_s,
):
    toks, width = x_ref.shape
    spare = qkv_s.shape[0] - toks
    x = x_ref[...].astype(F32)
    vec = lambda name: vecs_ref[VECS.index(name) : VECS.index(name) + 1, :]
    unit, _ = unit_norm(x)
    normed = (unit * vec("g1") + vec("b1")).astype(BF16)
    for part, bias in ((0, "qb"), (1, None), (2, "vb")):
        cols = pl.ds(part * width, width)
        joined = dot(normed, wqkv_ref[:, cols])
        if bias is not None:
            joined = joined + vec(bias)
        joined = joined.astype(BF16)
        qkv_ref[:, cols] = joined
        qkv_s[0:toks, cols] = joined.astype(F32)
    qkv_s[toks:, :] = jnp.zeros((spare, 3 * width), F32)
    masks = pair_masks(SEQ_PAD)
    for img in range(toks // SEQ):
        rows = pl.ds(img * SEQ, SEQ_PAD)
        for at in range(0, width, LANES):
            query = stack_heads(qkv_s[rows, at : at + LANES], masks)
            key = qkv_s[rows, width + at : width + at + LANES].astype(BF16)
            value = qkv_s[rows, 2 * width + at : 2 * width + at + LANES].astype(BF16)
            probs = probabilities(dot_rt(query, key) * HEAD_DIM**-0.5).astype(BF16)
            ctx_s[rows, at : at + LANES] = unstack_heads(dot(probs, value), masks)
    ctx = ctx_s[0:toks, :].astype(BF16)
    ctx_ref[...] = ctx
    hidden = x + dot(ctx, wout_ref[...]) + vec("ob")
    hidden_ref[...] = hidden
    unit2, _ = unit_norm(hidden)
    mixed_ref[...] = (unit2 * vec("g2") + vec("b2")).astype(BF16)


def expert_kernel(
    waits, me_ref, *refs,
):
    expert_body(me_ref, *refs[:8], *refs[8 + waits :])


def expert_body(
    me_ref,
    x_ref, up_ref, router_ref, router_t_ref, win_ref, bin_ref, wout_ref, bout_ref,
    part_ref, back_ref, activ_ref, gpre_ref, geout_ref, grouter_ref, gin_bias_ref, gout_bias_ref,
    out_s, back_s, probs_s, gate_s,
):
    step = pl.program_id(0)
    me = me_ref[0]
    toks = x_ref.shape[0]
    tail = up_ref.shape[0] - ROUTE_ROWS

    @pl.when(step == 0)
    def _():
        named = column_sum((up_ref[tail:, :].astype(F32) == me.astype(F32)).astype(F32))
        named = jnp.transpose(jnp.broadcast_to(named, (8, named.shape[1])))[:toks, 0:1]
        logits = dot(x_ref[...], router_ref[...])
        weights = jnp.exp(logits - jnp.max(logits, axis=-1, keepdims=True))
        probs = weights / jnp.sum(weights, axis=-1, keepdims=True)
        probs_s[...] = probs
        mine = lax.broadcasted_iota(jnp.int32, probs.shape, 1) == me
        gate = jnp.sum(jnp.where(mine, probs, 0.0), axis=-1, keepdims=True) * named
        gate_s[...] = gate
        geout = (gate * up_ref[0:toks, :].astype(F32)).astype(BF16)
        geout_ref[...] = geout
        gout_bias_ref[...] = column_sum(geout.astype(F32))
        out_s[...] = jnp.zeros_like(out_s)
        back_s[...] = jnp.zeros_like(back_s)

    pre = dot(x_ref[...], win_ref[...]) + bin_ref[...]
    phi, bell = gelu_parts(pre)
    activ = (pre * phi).astype(BF16)
    activ_ref[...] = activ
    gpre = (dot_rt(geout_ref[...], wout_ref[...]) * (phi + pre * bell)).astype(BF16)
    gpre_ref[...] = gpre
    gin_bias_ref[...] = column_sum(gpre.astype(F32))
    out_s[...] += dot(activ, wout_ref[...])
    back_s[...] += dot_rt(gpre, win_ref[...])

    @pl.when(step == pl.num_programs(0) - 1)
    def _():
        expert_out = (out_s[...] + bout_ref[...]).astype(BF16).astype(F32)
        gate = gate_s[...]
        probs = probs_s[...]
        part_ref[...] = (gate * expert_out).astype(BF16)
        route_grad = jnp.sum(up_ref[0:toks, :].astype(F32) * expert_out, axis=-1, keepdims=True)
        mine = (lax.broadcasted_iota(jnp.int32, probs.shape, 1) == me).astype(F32)
        glogits = gate * route_grad * (mine - probs)
        back = back_s[...].astype(BF16).astype(F32)
        for other in range(probs.shape[1]):
            back = back + glogits[:, other : other + 1] * router_t_ref[other : other + 1, :]
        back_ref[...] = back.astype(BF16)
        coarse = glogits.astype(BF16)
        fine = (glogits - coarse.astype(F32)).astype(BF16)
        grouter_ref[...] = dot_lt(coarse, x_ref[...]) + dot_lt(fine, x_ref[...])


def partial_grads_kernel(count, *refs):
    totals = [None, None]
    for k in range(count):
        rows, gpre, activ, geout = (refs[which * count + k][...] for which in range(4))
        for at, term in enumerate((dot_lt(rows, gpre), dot_lt(activ, geout))):
            totals[at] = term if totals[at] is None else totals[at] + term
    refs = refs[4 * count :]
    for at in range(2):
        refs[at][...] = totals[at]


def final_grads_kernel(count, half_ref, *refs):
    grad_ref = refs[-1]
    pieces, _, share, _ = grad_ref.shape
    grad_in, grad_out = refs[4 * count][...], refs[4 * count + 1][...]
    for k in range(count):
        rows, gpre, activ, geout = (refs[which * count + k][...] for which in range(4))
        grad_in = grad_in + dot_lt(rows, gpre)
        grad_out = grad_out + dot_lt(activ, geout)
    for piece in range(pieces):
        grad_ref[piece, 0] = grad_in[piece * share : (piece + 1) * share].astype(BF16)
        grad_ref[piece, 1] = grad_out[piece * share : (piece + 1) * share].astype(BF16)


def assemble_kernel(write, count, ids_ref, *refs):
    outs = refs[len(refs) - count :]
    at = pl.program_id(0)
    chosen = ((at // 2) ^ ids_ref[0]) * 2 + at % 2
    for which in range(4):

        @pl.when(chosen == which)
        def _(which=which):
            for piece in range(refs[which].shape[0]):
                write(refs[which][piece ^ ids_ref[1 + which % 2]].astype(F32), piece, *outs)


def write_dense(values, piece, qkv_ref, out_ref):
    share, cut = values.shape[0], qkv_ref.shape[1]
    rows = slice(piece * share, (piece + 1) * share)
    qkv_ref[rows, :] = values[:, :cut]
    out_ref[rows, :] = values[:, cut:]


def write_expert(values, piece, in_ref, out_ref):
    share, width = values.shape[1], out_ref.shape[2]
    rows = slice(piece * share, (piece + 1) * share)
    in_ref[rows, :] = values[0]
    for tile in range(out_ref.shape[0]):
        out_ref[tile, rows, :] = values[1, :, tile * width : (tile + 1) * width]


def attend_back_kernel(
    count, sums, core_ref, up_ref, x_ref, hidden_ref, qkv_ref, ctx_ref, vecs_ref, wqkv_ref, wout_ref, *refs,
):
    *refs, ginput_ref, keep_ref, send_ref, small_ref, qkv_s, gctx_s, gjoin_s = refs
    gmix_refs, refs = refs[:sums], refs[sums:]
    toks, width = x_ref.shape
    spare = qkv_s.shape[0] - toks
    vec = lambda name: vecs_ref[VECS.index(name) : VECS.index(name) + 1, :]

    def put(values, start):
        cols = slice(start, start + values.shape[1])
        pieces, share = keep_ref.shape[:2]
        for first, halves in ((0, (keep_ref, send_ref)), (1, (send_ref, keep_ref))):

            @pl.when(core_ref[0] == first)
            def _(halves=halves):
                for piece in range(2 * pieces):
                    rows = slice(piece * share, (piece + 1) * share)
                    halves[piece // pieces][piece % pieces, :, cols] = values[rows].astype(BF16)

    gmix = gmix_refs[0][...].astype(F32)
    for ref in gmix_refs[1:]:
        gmix = gmix + ref[...].astype(F32)
    unit2, scale2 = unit_norm(hidden_ref[...])
    grad_g2 = column_sum(gmix * unit2)
    grad_b2 = column_sum(gmix)
    m2 = gmix * vec("g2")
    ghidden = up_ref[...].astype(F32) + scale2 * (m2 - row_mean(m2) - unit2 * row_mean(m2 * unit2))
    gatt = ghidden.astype(BF16)
    grad_ob = column_sum(gatt.astype(F32))
    put(dot_lt(ctx_ref[...], gatt), 3 * width)
    gctx_s[0:toks, :] = dot_rt(gatt, wout_ref[...]).astype(BF16).astype(F32)
    gctx_s[toks:, :] = jnp.zeros((spare, width), F32)
    qkv_s[0:toks, :] = qkv_ref[...].astype(F32)
    qkv_s[toks:, :] = jnp.zeros((spare, 3 * width), F32)
    masks = pair_masks(SEQ_PAD)
    row_ok = lax.broadcasted_iota(jnp.int32, (SEQ_PAD, 1), 0) < SEQ
    for img in range(toks // SEQ):
        rows = pl.ds(img * SEQ, SEQ_PAD)
        for at in range(0, width, LANES):
            query = stack_heads(jnp.where(row_ok, qkv_s[rows, at : at + LANES], 0.0), masks)
            key = qkv_s[rows, width + at : width + at + LANES].astype(BF16)
            value = qkv_s[rows, 2 * width + at : 2 * width + at + LANES].astype(BF16)
            gctx = stack_heads(jnp.where(row_ok, gctx_s[rows, at : at + LANES], 0.0), masks)
            probs = probabilities(dot_rt(query, key) * HEAD_DIM**-0.5)
            gvalue = dot_lt(probs.astype(BF16), gctx)
            gweights = dot_rt(gctx, value)
            inner = jnp.sum(gweights * probs, axis=-1, keepdims=True)
            gscores = (probs * (gweights - inner)).astype(BF16)
            gquery = unstack_heads(dot(gscores, key), masks) * HEAD_DIM**-0.5
            gkey = dot_lt(gscores, query) * HEAD_DIM**-0.5
            gjoin_s[rows, at : at + LANES] = gquery
            gjoin_s[rows, width + at : width + at + LANES] = gkey
            gjoin_s[rows, 2 * width + at : 2 * width + at + LANES] = gvalue
    gjoin = gjoin_s[0:toks, :].astype(BF16)
    grad_qb = column_sum(gjoin[:, :width].astype(F32))
    grad_vb = column_sum(gjoin[:, 2 * width :].astype(F32))
    x = x_ref[...].astype(F32)
    unit1, scale1 = unit_norm(x)
    normed = (unit1 * vec("g1") + vec("b1")).astype(BF16)
    put(dot_lt(normed, gjoin), 0)
    gnormed = dot_rt(gjoin, wqkv_ref[...])
    grad_g1 = column_sum(gnormed * unit1)
    grad_b1 = column_sum(gnormed)
    m1 = gnormed * vec("g1")
    ginput = ghidden + scale1 * (m1 - row_mean(m1) - unit1 * row_mean(m1 * unit1))
    ginput_ref[...] = ginput.astype(BF16)
    for at, small in enumerate((grad_g1, grad_b1, grad_qb, grad_vb, grad_ob, grad_g2, grad_b2)):
        small_ref[at : at + 1, :] = small
    small_ref[7:, :] = jnp.zeros((small_ref.shape[0] - 7, width), F32)
    total = lambda which: sum((ref[...] for ref in refs[which:count:3][1:]), refs[which][...])
    router_sum, in_sum, out_sum = (total(which) for which in range(3))
    small_ref[8 : 8 + router_sum.shape[0], :] = router_sum
    at = 8 + -(-router_sum.shape[0] // 8) * 8
    for tile in range(in_sum.shape[1] // width):
        small_ref[at + tile : at + tile + 1, :] = in_sum[:, tile * width : (tile + 1) * width]
    at += in_sum.shape[1] // width
    small_ref[at : at + 1, :] = out_sum


def params(**more):
    return pltpu.CompilerParams(vmem_limit_bytes=VMEM_BYTES, **more)


def cost(micros):
    return pl.CostEstimate(flops=int(micros * COST_FLOPS), bytes_accessed=1024, transcendentals=0)


def whole():
    return pl.BlockSpec(memory_space=pltpu.VMEM)


def scalars():
    return pl.BlockSpec(memory_space=pltpu.SMEM)


def attend(inputs, vecs, w_qkv, w_out):
    toks, width = inputs.shape
    padded = -(-(toks - SEQ + SEQ_PAD) // 16) * 16
    return pl.pallas_call(
        attend_kernel,
        out_shape=(
            jax.ShapeDtypeStruct((toks, 3 * width), BF16),
            jax.ShapeDtypeStruct((toks, width), BF16),
            jax.ShapeDtypeStruct((toks, width), F32),
            jax.ShapeDtypeStruct((toks, width), BF16),
        ),
        in_specs=[whole()] * 4,
        out_specs=(whole(),) * 4,
        scratch_shapes=[pltpu.VMEM((padded, 3 * width), F32), pltpu.VMEM((padded, width), F32)],
        compiler_params=params(),
        cost_estimate=cost(12),
        name="attend",
    )(inputs, vecs, w_qkv, w_out)


def attend_back(core, gmixes, up, inputs, hidden, qkv, ctx, vecs, w_qkv, w_out, smalls, small_rows, pieces, after):
    toks, width = inputs.shape
    padded = -(-(toks - SEQ + SEQ_PAD) // 16) * 16
    half = jax.ShapeDtypeStruct((pieces, width // (2 * pieces), 4 * width), BF16)
    return pl.pallas_call(
        functools.partial(attend_back_kernel, len(smalls), len(gmixes)),
        out_shape=(
            jax.ShapeDtypeStruct((toks, width), BF16),
            half,
            half,
            jax.ShapeDtypeStruct((small_rows, width), F32),
        ),
        in_specs=[scalars()] + [whole()] * (8 + len(gmixes) + len(smalls)) + [pl.BlockSpec(memory_space=pl.ANY)] * len(after),
        out_specs=(whole(),) * 4,
        scratch_shapes=[
            pltpu.VMEM((padded, 3 * width), F32),
            pltpu.VMEM((padded, width), F32),
            pltpu.VMEM((padded, 3 * width), F32),
        ],
        compiler_params=params(),
        cost_estimate=cost(BACK_COST),
        name="attend_back",
    )(core, up, inputs, hidden, qkv, ctx, vecs, w_qkv, w_out, *gmixes, *smalls, *after)


def expert_block(me, rows, up, router, router_t, w_in, b_in, w_out, b_out, after=()):
    toks, width = rows.shape
    experts = router.shape[1]
    hidden = w_in.shape[1]
    fixed = lambda shape: pl.BlockSpec(shape, lambda f, m: (0, 0))
    return pl.pallas_call(
        functools.partial(expert_kernel, len(after)),
        out_shape=(
            jax.ShapeDtypeStruct((toks, width), BF16),
            jax.ShapeDtypeStruct((toks, width), BF16),
            jax.ShapeDtypeStruct((toks, hidden), BF16),
            jax.ShapeDtypeStruct((toks, hidden), BF16),
            jax.ShapeDtypeStruct((toks, width), BF16),
            jax.ShapeDtypeStruct((experts, width), F32),
            jax.ShapeDtypeStruct((1, hidden), F32),
            jax.ShapeDtypeStruct((1, width), F32),
        ),
        grid_spec=pltpu.PrefetchScalarGridSpec(
            num_scalar_prefetch=1,
            grid=(hidden // FF_TILE,),
            in_specs=[
                fixed((toks, width)),
                fixed(up.shape),
                fixed(router.shape),
                fixed(router_t.shape),
                pl.BlockSpec((width, FF_TILE), lambda f, m: (0, f)),
                pl.BlockSpec((1, FF_TILE), lambda f, m: (0, f)),
                pl.BlockSpec((FF_TILE, width), lambda f, m: (f, 0)),
                fixed((1, width)),
            ]
            + [pl.BlockSpec(memory_space=pl.ANY)] * len(after),
            out_specs=(
                fixed((toks, width)),
                fixed((toks, width)),
                pl.BlockSpec((toks, FF_TILE), lambda f, m: (0, f)),
                pl.BlockSpec((toks, FF_TILE), lambda f, m: (0, f)),
                fixed((toks, width)),
                fixed((experts, width)),
                pl.BlockSpec((1, FF_TILE), lambda f, m: (0, f)),
                fixed((1, width)),
            ),
            scratch_shapes=[
                pltpu.VMEM((toks, width), F32),
                pltpu.VMEM((toks, width), F32),
                pltpu.VMEM((toks, experts), F32),
                pltpu.VMEM((toks, 1), F32),
            ],
        ),
        compiler_params=params(),
        cost_estimate=cost(24),
        name="expert_block",
    )(me, rows, up, router, router_t, w_in, b_in, w_out, b_out, *after)


def partial_grads(rows, gpres, activs, geouts):
    count = len(rows)
    toks, width = rows[0].shape
    hidden = gpres[0].shape[1]
    fixed = pl.BlockSpec((toks, width), lambda f: (0, 0))
    tile = pl.BlockSpec((toks, width), lambda f: (0, f))
    total = pl.BlockSpec((width, width), lambda f: (0, f))
    return pl.pallas_call(
        functools.partial(partial_grads_kernel, count),
        out_shape=(jax.ShapeDtypeStruct((width, hidden), F32),) * 2,
        grid=(hidden // width,),
        in_specs=[fixed] * count + [tile] * (2 * count) + [fixed] * count,
        out_specs=(total,) * 2,
        compiler_params=params(),
        cost_estimate=cost(12 * count),
        name="partial_grads",
    )(*rows, *gpres, *activs, *geouts)


def final_grads(half, rows, gpres, activs, geouts, started, pieces, after=()):
    count = len(rows)
    toks, width = rows[0].shape
    hidden = gpres[0].shape[1]
    share = width // (2 * pieces)
    total = pl.BlockSpec((width // 2, width), lambda f, h: (h[0], f))
    return pl.pallas_call(
        functools.partial(final_grads_kernel, count),
        out_shape=jax.ShapeDtypeStruct((pieces, 2, share, hidden), BF16),
        grid_spec=pltpu.PrefetchScalarGridSpec(
            num_scalar_prefetch=1,
            grid=(hidden // width,),
            in_specs=[pl.BlockSpec((toks, width // 2), lambda f, h: (0, h[0]))] * count
            + [pl.BlockSpec((toks, width), lambda f, h: (0, f))] * count
            + [pl.BlockSpec((toks, width // 2), lambda f, h: (0, 2 * f + h[0]))] * count
            + [pl.BlockSpec((toks, width), lambda f, h: (0, 0))] * count
            + [total] * 2
            + [pl.BlockSpec(memory_space=pl.ANY)] * len(after),
            out_specs=pl.BlockSpec((pieces, 2, share, width), lambda f, h: (0, 0, 0, f)),
        ),
        compiler_params=params(),
        cost_estimate=cost(FINAL_COST),
        name="final_grads",
    )(half, *rows, *gpres, *activs, *geouts, *started, *after)


def assemble(ids, groups, write, outs, after):
    blocks = []
    for shape, dim in outs:
        block = tuple(n // 4 if d == dim else n for d, n in enumerate(shape))
        place = lambda at, ids, dim=dim, rank=len(shape): tuple(at if d == dim else 0 for d in range(rank))
        blocks.append(pl.BlockSpec(block, place))
    rank = groups[0].ndim
    return pl.pallas_call(
        functools.partial(assemble_kernel, write, len(outs)),
        out_shape=tuple(jax.ShapeDtypeStruct(shape, F32) for shape, _ in outs),
        grid_spec=pltpu.PrefetchScalarGridSpec(
            num_scalar_prefetch=1,
            grid=(4,),
            in_specs=[pl.BlockSpec(groups[0].shape, lambda at, ids: (0,) * rank)] * 4
            + [pl.BlockSpec(memory_space=pl.ANY)] * len(after),
            out_specs=tuple(blocks),
        ),
        compiler_params=params(),
        cost_estimate=cost(5),
        name="assemble",
    )(ids, *groups, *after)


def shift(values, axis, by):
    size = lax.axis_size(axis)
    return lax.ppermute(values, axis, [(i, (i + by) % size) for i in range(size)])


INNER_SWAP = [(1, 2), (2, 1)]
OUTWARD = [(1, 0), (2, 3)]


def at_end(axis):
    place = lax.axis_index(axis)
    return (place == 0) | (place == lax.axis_size(axis) - 1)


def gather_blocks(values, axis, hold=None):
    if lax.axis_size(axis) != 4:
        return ring_gather(values, axis), ()
    near = swap(values, axis, 1)
    inner = lax.ppermute(values, axis, INNER_SWAP)
    if hold is not None:
        near, inner = hold(near, inner)
    far = lax.ppermute(near, axis, INNER_SWAP)
    end = at_end(axis)
    second = jnp.where(end, lax.ppermute(inner, axis, OUTWARD), far)
    third = jnp.where(end, lax.ppermute(far, axis, OUTWARD), inner)
    return [values, near, second, third], (near, inner)


INWARD = [(0, 1), (3, 2)]


class Returns:
    def __init__(self, own, axis):
        self.axis, self.line = axis, lax.axis_size(axis) == 4
        self.sums, self.sent = [own], []

    def add(self, k, values, *hold):
        if not self.line:
            self.sums.append(shift(values, self.axis, -k))
        elif k == 1:
            self.near = values
            self.sent = [lax.ppermute(values, self.axis, INWARD)]
            self.sums += self.sent
        elif k == 2:
            if hold:
                values, *_ = lax.optimization_barrier((values, *hold))
            self.through = lax.ppermute(values, self.axis, INWARD)
            inner = lax.ppermute(values, self.axis, INNER_SWAP)
            self.sent = [self.through, inner]
            self.outward = add_rounded(self.near, inner)
        else:
            self.sums.append(swap(add_rounded(values, self.through), self.axis, 3))

    def send_outward(self, *before):
        if self.line:
            outward, *_ = lax.optimization_barrier((self.outward, *before))
            self.sums.append(lax.ppermute(outward, self.axis, OUTWARD))
            self.sent.append(self.sums[-1])


def ring_gather(values, axis):
    size = lax.axis_size(axis)
    found = {0: values}
    ahead = behind = values
    for k in range(1, (size + 1) // 2):
        ahead, behind = shift(ahead, axis, 1), shift(behind, axis, -1)
        found[k], found[size - k] = ahead, behind
    if size % 2 == 0:
        cut = middle_cut(values.shape[0])
        found[size // 2] = jnp.concatenate(
            [shift(ahead[:cut], axis, 1), shift(behind[cut:], axis, -1)], axis=0
        )
    return [found[k] for k in range(size)]


def middle_cut(rows):
    return rows // 16 * 8


def swap(values, axis, bit):
    return lax.ppermute(values, axis, [(i, i ^ bit) for i in range(lax.axis_size(axis))])


def axis_bit(axis, bit):
    return ((lax.axis_index(axis) // bit) % 2).astype(jnp.int32)


def halve(values, axis, bit):
    mine = axis_bit(axis, bit)
    size = values.shape[0] // 2
    part = lambda which: lax.dynamic_slice_in_dim(values, which * size, size, 0)
    got = swap(part(1 - mine), axis, bit)
    return add_rounded(part(mine), got)


def add_rounded(one, other):
    return (one.astype(F32) + other.astype(F32)).astype(one.dtype)


def sum_over(keep, send, axis, write, outs, inner=None, after=(), before_end=()):
    core = 1
    values = add_rounded(keep, swap(send, axis, core))
    if after:
        values, *_ = lax.optimization_barrier((values, *after))
    return values, lambda: sum_rest(values, axis, write, outs, inner, before_end)


def sum_rest(values, axis, write, outs, inner, before_end):
    size = lax.axis_size(axis)
    core, *rest = [1 << b for b in range(size.bit_length() - 1)]
    pieces = 1 << len(rest)
    orders = (rest, rest[::-1])
    parts = []
    for part, order in zip((values[:pieces], values[pieces:]), orders):
        for bit in order:
            part = halve(part, axis, bit)
        parts.append(part)
    if inner is not None:
        joined = jnp.concatenate(parts, axis=0)
        joined = inner(joined.reshape(-1, joined.shape[-1])).reshape(joined.shape)
        parts = [joined[:1], joined[1:]]
    ids = [axis_bit(axis, core)]
    done = []
    for part, order in zip(parts, orders):
        for bit in order[::-1]:
            part = jnp.concatenate([part, swap(part, axis, bit)], axis=0)
        done.append(part)
        ids.append(sum(axis_bit(axis, bit) * (pieces >> at + 1) for at, bit in enumerate(order)))
    got = [swap(part, axis, core) for part in done]
    return assemble(jnp.stack(ids), done + got, write, outs, before_end)


def sum_direct(values, axis):
    size = lax.axis_size(axis)
    me = lax.axis_index(axis)
    share = values.shape[0] // size
    take = lambda owner: lax.dynamic_slice_in_dim(values, (owner % size) * share, share, 0)
    total = take(me).astype(F32)
    for k in range(1, size):
        total = total + shift(take(me + k), axis, k).astype(F32)
    total = total.astype(values.dtype)
    result = jnp.zeros_like(values)
    result = lax.dynamic_update_slice_in_dim(result, total, me * share, 0)
    for k in range(1, size):
        result = lax.dynamic_update_slice_in_dim(
            result, shift(total, axis, k), ((me - k) % size) * share, 0
        )
    return result


def sum_small(values, local_rows):
    for bit in [1 << b for b in range(lax.axis_size("rep").bit_length() - 1)]:
        values = values + swap(values, "rep", bit)
    shared = values[: values.shape[0] - local_rows]
    shared = sum([shift(shared, "exp", k) for k in range(1, lax.axis_size("exp"))], shared)
    return shared, values[values.shape[0] - local_rows :]


def on_device(
    inputs,
    routes,
    ln1_gain,
    ln1_bias,
    w_qkv,
    query_bias,
    value_bias,
    w_out,
    out_bias,
    ln2_gain,
    ln2_bias,
    router,
    experts_in,
    experts_in_bias,
    experts_out,
    experts_out_bias,
    cotangent,
):
    toks, width = inputs.shape
    experts = router.shape[1]
    hidden_units = experts_in.shape[2]
    me = lax.axis_index("exp").astype(jnp.int32).reshape(1)
    core = axis_bit("rep", 1).reshape(1)
    vecs = jnp.stack(
        [ln1_gain, ln1_bias, query_bias, value_bias, out_bias, ln2_gain, ln2_bias, jnp.zeros_like(ln1_gain)]
    )
    tail = -(-toks // 16) * 16
    named = jnp.full((tail - toks + ROUTE_ROWS, width), -1.0, BF16)
    named = named.at[tail - toks : tail - toks + routes.shape[1], :toks].set(routes.T.astype(BF16))

    pieces = lax.axis_size("rep")
    ups, first_ups = gather_blocks(jnp.concatenate([cotangent, named], axis=0), "exp")
    qkv, ctx, hidden, mixed = attend(inputs, vecs, w_qkv, w_out)
    router_t = router.T.astype(F32)
    w_in, w_mid = experts_in[0], experts_out[0]
    run_block = lambda rows, up, after: expert_block(
        me, rows, up, router, router_t, w_in, experts_in_bias, w_mid, experts_out_bias, after
    )
    blocks, sums = [run_block(mixed, ups[0], first_ups)], None
    mixes, _ = gather_blocks(mixed, "exp", lambda *got: lax.optimization_barrier((*got, blocks[0][0]))[:2])
    last = len(mixes) - 1
    backs, parts = Returns(blocks[0][1], "exp"), Returns(blocks[0][0], "exp")
    sums, early = None, ()
    for k in range(1, last + 1):
        blocks.append(run_block(mixes[k], ups[k], early))
        hold = (mixes[last], ups[last]) if k == last - 1 else ()
        backs.add(k, blocks[k][1], *hold)
        if k < last:
            parts.add(k, blocks[k][0], *hold)
        if k == last - 2:
            listed = lambda which: [mixes[j] if which is None else blocks[j][which] for j in range(k + 1)]
            sums = partial_grads(listed(None), listed(3), listed(2), listed(4))
            early = (sums[0], *backs.sent, *parts.sent)
        elif k == last - 1:
            backs.send_outward(mixes[last], ups[last])
            early, middle_sent = (), tuple(backs.sent + parts.sent)
    _, _, activs, gpres, geouts, grouters, gin_bias, gout_bias = zip(*blocks)
    final = lambda half, after: final_grads(
        half, mixes[-2:], gpres[-2:], activs[-2:], geouts[-2:], sums, pieces, after
    )
    send = final(1 - core, middle_sent)
    keep = final(core, (send,))
    parts.add(last, lax.optimization_barrier((blocks[last][0], keep))[0])
    parts.send_outward(keep)
    result = sum((values.astype(F32) for values in parts.sums), hidden).astype(BF16)
    core_sum, expert_rest = sum_over(
        keep,
        send,
        "rep",
        write_expert,
        (((width, hidden_units), 0), ((hidden_units // width, width, width), 1)),
    )

    smalls = [part for trio in zip(grouters, gin_bias, gout_bias) for part in trio]
    shared_rows = 8 + -(-experts // 8) * 8
    small_rows = shared_rows + -(-(hidden_units // width + 1) // 8) * 8
    grad_inputs, dense_keep, dense_send, small = attend_back(
        core, backs.sums, cotangent, inputs, hidden, qkv, ctx, vecs, w_qkv, w_out,
        smalls, small_rows, pieces, (core_sum,),
    )
    grad_experts_in, grad_experts_out = expert_rest()
    _, dense_rest = sum_over(
        dense_keep,
        dense_send,
        "rep",
        write_dense,
        (((width, 3 * width), 0), ((width, width), 0)),
        functools.partial(sum_direct, axis="exp"),
        tuple(parts.sums[1:]),
        [grad_experts_out],
    )
    grad_qkv, grad_out = dense_rest()
    small, own = sum_small(small, small_rows - shared_rows)
    return (
        result,
        grad_inputs,
        small[0],
        small[1],
        grad_qkv,
        small[2],
        small[3],
        grad_out,
        small[4],
        small[5],
        small[6],
        small[8 : 8 + experts].T,
        grad_experts_in[None],
        own[: hidden_units // width].reshape(1, hidden_units),
        grad_experts_out.reshape(1, hidden_units, width),
        own[hidden_units // width : hidden_units // width + 1],
    )


def solution(mesh):
    tokens = P(("rep", "exp"), None)
    expert3, expert2 = P("exp", None, None), P("exp", None)
    return jax.shard_map(
        on_device,
        mesh=mesh,
        in_specs=(tokens, tokens) + (P(),) * 10 + (expert3, expert2) * 2 + (tokens,),
        out_specs=(tokens, tokens) + (P(),) * 10 + (expert3, expert2) * 2,
        check_vma=False,
    )
```

time: 637 us -> 488 us (0.77)
  waiting for transfers between devices: 195 us -> 119 us
  other arithmetic: 79.1 us -> 37.3 us
  starting transfers between devices: 134 us -> 103 us
  Pallas kernels: 180 us -> 209 us
  local copies, waits for them, and re-layouts: 38.5 us -> 10.9 us
    ppermute x35 -> x9, waiting for transfers between devices: 105 us -> 20.6 us  [shift(): lax.ppermute(values, axis, [(i, (i + by) % size) for i in range(size)])]
    ppermute x35 -> x9, starting transfers between devices: 102 us -> 39.5 us  [shift(): lax.ppermute(values, axis, [(i, (i + by) % size) for i in range(size)])]
    convert_element_type x19 -> x16, other arithmetic: 59.9 us -> 21.1 us  [the longest x14 17.2 us: add_rounded(): return (one.astype(F32) + other.astype(F32)).astype(one.dtype)]
    ppermute x0 -> x16, starting transfers between devices: none -> 28.9 us  [the longest x2 7.74 us: add(): self.sent = [lax.ppermute(values, self.axis, INWARD)]]
    pallas_call x7 -> x10, Pallas kernels: 169 us -> 197 us  [the longest x4 99.5 us: expert_block(): pl.pallas_call(functools.partial(expert_kernel, len(after)), out_shape=(j...]
    ppermute x0 -> x16, waiting for transfers between devices: none -> 16.5 us  [the longest x2 7.03 us: add(): self.sent = [lax.ppermute(values, self.axis, INWARD)]]
    slice x17 -> x5, local copies, waits for them, and re-layouts: 15.1 us -> 1.11 us  [the longest x1 0.58 us: on_device(): own[hidden_units // width:hidden_units // width + 1]]
    reshape x7 -> x0, local copies, waits for them, and re-layouts: 8.87 us -> none  [on_device(): row = lambda vec: vec.reshape(1, -1)]
  transfers between devices with their start and end apart: 71 -> 54, of which waited for: 28 -> 22; matrix products, arithmetic and copies ran while one was open for 13% -> 8% of each run, Pallas kernels for 27% -> 39%
where the time goes in v2:
time: 488 us; the launch traced here: 481 us
  Pallas kernels  209 us (43%)
  waiting for transfers between devices  119 us (24%)
  starting transfers between devices  103 us (21%)
  other arithmetic  37.3 us (8%)
  local copies, waits for them, and re-layouts  10.9 us (2%)
    pallas_call x4, Pallas kernels, expert_block(): pl.pallas_call(functools.partial(expert_kernel, len(after)), out_shape=(j...  99.5 us
    ppermute x29, waiting for transfers between devices, swap(): lax.ppermute(values, axis, [(i, i ^ bit) for i in range(lax.axis_size(axi...  81.7 us
    ppermute x9, starting transfers between devices, shift(): lax.ppermute(values, axis, [(i, (i + by) % size) for i in range(size)])  39.5 us
    ppermute x29, starting transfers between devices, swap(): lax.ppermute(values, axis, [(i, i ^ bit) for i in range(lax.axis_size(axi...  35 us
    pallas_call x1, Pallas kernels, attend_back(): pl.pallas_call(functools.partial(attend_back_kernel, len(smalls), len(gmi...  31 us
    pallas_call x2, Pallas kernels, final_grads(): pl.pallas_call(functools.partial(final_grads_kernel, count), out_shape=ja...  28.1 us
    ppermute x9, waiting for transfers between devices, shift(): lax.ppermute(values, axis, [(i, (i + by) % size) for i in range(size)])  20.6 us
    pallas_call x1, Pallas kernels, partial_grads(): pl.pallas_call(functools.partial(partial_grads_kernel, count), out_shape=...  20.5 us
  transfers between devices with their start and end apart: 54, of which 22 were waited for; matrix products, arithmetic and copies ran while one was open for 8% of the time, Pallas kernels for 39%

profile of v2, /device:TPU:0, one launch (start us, length us, event | category | flops | bytes accessed | tf_op | source)
XLA Modules:
  0.0 481.3 jit_solution(15380633891068108324)
XLA Ops:
  3.4 5.9 %collective-permute-start = (bf16[608,768]{1,0:T(8,128)(2,1)S(1)}, bf16[608,768]{1,0:T(8,128)(2,1)}, u32[]{:S(2)}, u32[]{:S(2)}) collective-permute-start(bf16[608,768]{1,0:T(8,128)(2,1)S(1)} %fusion.1.refs_1_), channel_id=1, source_target_pairs={{0,1},{1,0},{2,3},{3,2},{4,5},{5,4},{6,7},{7,6},{8,9},{9,8},{10,11... | collective-permute-start | bytes 2801672 | tf_op jit(solution)/shard_map/ppermute | solution.py:594
  10.1 11.6 %attend.1 = (bf16[591,2304]{1,0:T(8,128)(2,1)}, bf16[591,768]{1,0:T(8,128)(2,1)}, f32[591,768]{1,0:T(8,128)}, bf16[591,768]{1,0:T(8,128)(2,1)}) custom-call(bf16[591,768]{1,0:T(8,128)(2,1)} %x_ref.3, f32[8,768]{1,0:T(8,128)} %stack.45.vecs_ref, bf16[768,2304]{1,0:T(8,128)(2,1)} %wqkv_ref.3, bf16[768,768]{1,0:T(8,128)(2,1)} %wout_ref.3), custom_call_target="tpu_custom_call" | custom-call | flops 4800000000 | bytes 1024 | tf_op jit(solution)/shard_map/attend/pallas_call | solution.py:350
  22.9 1.7 collective-permute-start.2
  26.1 4.9 %collective-permute-done.refs_8_.refs_1_ = bf16[608,768]{1,0:T(8,128)(2,1)} collective-permute-done((bf16[608,768]{1,0:T(8,128)(2,1)S(1)}, bf16[608,768]{1,0:T(8,128)(2,1)}, u32[]{:S(2)}, u32[]{:S(2)}) %collective-permute-start) | collective-permute-done | bytes 933920 | tf_op jit(solution)/shard_map/ppermute | solution.py:594
  31.0 24.9 %expert_block.4 = (bf16[591,768]{1,0:T(8,128)(2,1)}, bf16[591,768]{1,0:T(8,128)(2,1)}, bf16[591,3072]{1,0:T(8,128)(2,1)}, bf16[591,3072]{1,0:T(8,128)(2,1)}, bf1...) custom-call(s32[1]{0:T(128)} %bitcast.me_ref, ...), custom_call_target="tpu_custom_call" | custom-call | flops 9600000000 | bytes 1024 | tf_op jit(solution)/shard_map/expert_block/pallas_call | solution.py:397
  57.2 1.7 collective-permute-start.5
  59.0 24.9 %expert_block.5 = (bf16[591,768]{1,0:T(8,128)(2,1)}, bf16[591,768]{1,0:T(8,128)(2,1)}, bf16[591,3072]{1,0:T(8,128)(2,1)}, bf16[591,3072]{1,0:T(8,128)(2,1)}, bf1...) custom-call(s32[1]{0:T(128)} %bitcast.me_ref, ...), custom_call_target="tpu_custom_call" | custom-call | flops 9600000000 | bytes 1024 | tf_op jit(solution)/shard_map/expert_block/pallas_call | solution.py:397
  83.8 5.5 %collective-permute-start.4 = (bf16[591,768]{1,0:T(8,128)(2,1)}, bf16[591,768]{1,0:T(8,128)(2,1)S(1)}, u32[]{:S(2)}, u32[]{:S(2)}) collective-permute-start(bf16[591,768]{1,0:T(8,128)(2,1)} %get-tuple-element.86), channel_id=1, source_target_pairs={{0,1},{3,2},{4,5},{7,6},{8,9},{11,10},{12,13},{15,14},{16,17},{19,... | collective-permute-start | bytes 2723336 | tf_op jit(solution)/shard_map/ppermute | solution.py:555
  89.3 2.3 collective-permute-start.11
  93.8 20.5 %partial_grads.1 = (f32[768,3072]{1,0:T(8,128)}, f32[768,3072]{1,0:T(8,128)}) custom-call(bf16[591,768]{1,0:T(8,128)(2,1)} %get-tuple-element.83.refs_0_, bf16[591,768]{1,0:T(8,128)(2,1)} %collective-permute-done.2.refs_0_.refs_1_, bf16[591,3072]{1,0:T(8,128)(2,1)} %get-tuple-element.89.refs_2_, bf16[591,3072]{1,0:T(8,128)(2,1)} %get-tuple-element.90.refs_3_, ...), custom_call_target="tpu_custom_call" | custom-call | flops 9600000000 | bytes 1024 | tf_op jit(solution)/shard_map/partial_grads/pallas_call | solution.py:453
  119.0 7.0 %collective-permute-done.11.refs_9_.refs_1_ = bf16[591,768]{1,0:T(8,128)(2,1)} collective-permute-done((bf16[591,768]{1,0:T(8,128)(2,1)}, bf16[591,768]{1,0:T(8,128)(2,1)}, u32[]{:S(2)}, u32[]{:S(2)}) %collective-permute-start.11) | collective-permute-done | bytes 907808 | tf_op jit(solution)/shard_map/ppermute | solution.py:555
  126.0 24.9 %expert_block.7 = (bf16[591,768]{1,0:T(8,128)(2,1)}, bf16[591,768]{1,0:T(8,128)(2,1)}, bf16[591,3072]{1,0:T(8,128)(2,1)}, bf16[591,3072]{1,0:T(8,128)(2,1)}, bf1...) custom-call(s32[1]{0:T(128)} %bitcast.me_ref, ...), custom_call_target="tpu_custom_call" | custom-call | flops 9600000000 | bytes 1024 | tf_op jit(solution)/shard_map/expert_block/pallas_call | solution.py:397
  150.9 2.3 broadcast_select_fusion.3.refs_0_.refs_1_
  153.1 4.9 %collective-permute-done.8 = bf16[608,768]{1,0:T(8,128)(2,1)S(1)} collective-permute-done((bf16[608,768]{1,0:T(8,128)(2,1)S(1)}, bf16[608,768]{1,0:T(8,128)(2,1)S(1)}, u32[]{:S(2)}, u32[]{:S(2)}) %collective-permute-start.8) | collective-permute-done | bytes 933920 | tf_op jit(solution)/shard_map/ppermute | solution.py:538
  160.5 5.9 %collective-permute-start.15 = (bf16[591,768]{1,0:T(8,128)(2,1)}, bf16[591,768]{1,0:T(8,128)(2,1)S(1)}, u32[]{:S(2)}, u32[]{:S(2)}) collective-permute-start(bf16[591,768]{1,0:T(8,128)(2,1)} %get-tuple-element.108), channel_id=1, source_target_pairs={{0,1},{3,2},{4,5},{7,6},{8,9},{11,10},{12,13},{15,14},{16,17},{19,... | collective-permute-start | bytes 2723336 | tf_op jit(solution)/shard_map/ppermute | solution.py:560
  170.0 1.5 collective-permute-start.14
  171.5 24.9 %expert_block.6 = (bf16[591,768]{1,0:T(8,128)(2,1)}, bf16[591,768]{1,0:T(8,128)(2,1)}, bf16[591,3072]{1,0:T(8,128)(2,1)}, bf16[591,3072]{1,0:T(8,128)(2,1)}, bf1...) custom-call(s32[1]{0:T(128)} %bitcast.me_ref, ...), custom_call_target="tpu_custom_call" | custom-call | flops 9600000000 | bytes 1024 | tf_op jit(solution)/shard_map/expert_block/pallas_call | solution.py:397
  196.4 4.5 collective-permute-done.12.refs_10_
  201.9 13.9 %final_grads.2.refs_10_ = bf16[8,2,48,3072]{3,2,1,0:T(8,128)(2,1)} custom-call(s32[1]{0:T(128)S(6)} %sub.48.half_ref, bf16[591,768]{1,0:T(8,128)(2,1)} %broadcast_select_fusion.2.refs_0_, bf16[591,768]{1,0:T(8,128)(2,1)} %broadcast_select_fusion.3.refs_0_.refs_1_, bf16[591,3072]{1,0:T(8,128)(2,1)} %get-tuple-element.97.refs_2_, ...), custom_call_target="tpu_custom_call" | custom-call | flops 1600000000 | bytes 1024 | tf_op jit(solution)/shard_map/final_grads/pallas_call | solution.py:471
  216.2 2.8 add_convert_fusion.4
  219.0 1.5 collective-permute-start.19
  221.7 14.2 %final_grads.3 = bf16[8,2,48,3072]{3,2,1,0:T(8,128)(2,1)} custom-call(s32[1]{0:T(128)} %bitcast.5.half_ref.core_ref, bf16[591,768]{1,0:T(8,128)(2,1)} %broadcast_select_fusion.2.refs_0_, bf16[591,768]{1,0:T(8,128)(2,1)} %broadcast_select_fusion.3.refs_0_.refs_1_, bf16[591,3072]{1,0:T(8,128)(2,1)} %get-tuple-element.97.refs_2_, ...), custom_call_target="tpu_custom_call" | custom-call | flops 1600000000 | bytes 1024 | tf_op jit(solution)/shard_map/final_grads/pallas_call | solution.py:471
  237.2 2.3 collective-permute-start.17
  240.8 5.8 %add_convert_fusion.refs_16_ = bf16[8,2,48,3072]{3,2,1,0:T(8,128)(2,1)S(1)} fusion(bf16[8,2,48,3072]{3,2,1,0:T(8,128)(2,1)} %collective-permute-done.20, bf16[8,2,48,3072]{3,2,1,0:T(8,128)(2,1)} %final_grads.3), kind=kLoop, calls=%fused_computation | loop fusion | flops 9437184 | bytes 14155776 | tf_op jit(solution)/shard_map/convert_element_type | solution.py:610
  246.9 1.8 copy-done
  249.8 1.5 collective-permute-start.44
  251.4 1.5 collective-permute-start.48
  253.0 31.0 %attend_back.1 = (bf16[591,768]{1,0:T(8,128)(2,1)}, bf16[8,48,3072]{2,1,0:T(8,128)(2,1)}, bf16[8,48,3072]{2,1,0:T(8,128)(2,1)}, f32[24,768]{1,0:T(8,128)}) custom-call(s32[1]{0:T(128)} %bitcast.5.half_ref.core_ref, bf16[591,768]{1,0:T(8,128)(2,1)} %up_ref.1, bf16[591,768]{1,0:T(8,128)(2,1)} %x_ref.3, f32[591,768]{1,0:T(8,128)} %get-tuple-element.82.hidden_ref, ...), custom_call_target="tpu_custom_call" | custom-call | flops 11200000000 | bytes 1024 | tf_op jit(solution)/shard_map/attend_back/pallas_call | solution.py:371
  284.5 1.7 add_convert_fusion.3
  286.9 1.7 add_convert_fusion.2
  288.6 13.0 %collective-permute-done.45 = bf16[1,2,48,3072]{3,2,1,0:T(8,128)(2,1)S(1)} collective-permute-done((bf16[1,2,48,3072]{3,2,1,0:T(8,128)(2,1)S(1)}, bf16[1,2,48,3072]{3,2,1,0:T(8,128)(2,1)S(1)}, u32[]{:S(2)}, u32[]{:S(2)}) %collective-permute-start.45) | collective-permute-done | bytes 589856 | tf_op jit(solution)/shard_map/ppermute | solution.py:594
  304.1 1.7 collective-permute-start.30
  305.8 10.3 %collective-permute-done.49 = bf16[1,2,48,3072]{3,2,1,0:T(8,128)(2,1)S(1)} collective-permute-done((bf16[1,2,48,3072]{3,2,1,0:T(8,128)(2,1)S(1)}, bf16[1,2,48,3072]{3,2,1,0:T(8,128)(2,1)S(1)}, u32[]{:S(2)}, u32[]{:S(2)}) %collective-permute-start.49) | collective-permute-done | bytes 589856 | tf_op jit(solution)/shard_map/ppermute | solution.py:594
  317.0 1.5 collective-permute-start.28
  318.5 10.9 %collective-permute-done.30 = bf16[2,48,3072]{2,1,0:T(8,128)(2,1)S(1)} collective-permute-done((bf16[2,48,3072]{2,1,0:T(8,128)(2,1)S(1)}, bf16[2,48,3072]{2,1,0:T(8,128)(2,1)S(1)}, u32[]{:S(2)}, u32[]{:S(2)}) %collective-permute-start.30) | collective-permute-done | bytes 589856 | tf_op jit(solution)/shard_map/ppermute | solution.py:594
  329.5 1.5 collective-permute-start.31
  331.0 14.2 %collective-permute-done.28 = bf16[2,48,3072]{2,1,0:T(8,128)(2,1)S(1)} collective-permute-done((bf16[2,48,3072]{2,1,0:T(8,128)(2,1)S(1)}, bf16[2,48,3072]{2,1,0:T(8,128)(2,1)S(1)}, u32[]{:S(2)}, u32[]{:S(2)}) %collective-permute-start.28) | collective-permute-done | bytes 589856 | tf_op jit(solution)/shard_map/ppermute | solution.py:594
  346.0 2.8 collective-permute-done.31
  348.9 3.3 collective-permute-done.29
  352.4 29.9 %collective-permute-start.32 = (bf16[24,3072]{1,0:T(8,128)(2,1)S(1)}, bf16[24,3072]{1,0:T(8,128)(2,1)S(1)}, u32[]{:S(2)}, u32[]{:S(2)}) collective-permute-start(bf16[24,3072]{1,0:T(8,128)(2,1)S(1)} %get-tuple-element.151), channel_id=1, source_target_pairs={{0,1},{1,2},{2,3},{3,0},{4,5},{5,6},{6,7},{7,4},{8,9},{9,10},{10,1... | collective-permute-start | bytes 442376 | tf_op jit(solution)/shard_map/ppermute | solution.py:516
  382.3 2.1 collective-permute-start.33
  384.5 1.6 collective-permute-done.32
  386.1 1.6 collective-permute-start.47
  388.2 6.7 %collective-permute-done.33 = bf16[24,3072]{1,0:T(8,128)(2,1)S(1)} collective-permute-done((bf16[24,3072]{1,0:T(8,128)(2,1)S(1)}, bf16[24,3072]{1,0:T(8,128)(2,1)S(1)}, u32[]{:S(2)}, u32[]{:S(2)}) %collective-permute-start.33) | collective-permute-done | bytes 147488 | tf_op jit(solution)/shard_map/ppermute | solution.py:516
  395.2 1.5 collective-permute-start.51
  396.7 1.9 collective-permute-start.36
  398.7 3.4 collective-permute-done.35
  402.1 3.0 collective-permute-done.36
  405.2 2.1 collective-permute-done.37
  407.3 1.5 collective-permute-start.38
  408.8 6.0 %collective-permute-done.51 = bf16[2,2,48,3072]{3,2,1,0:T(8,128)(2,1)S(1)} collective-permute-done((bf16[2,2,48,3072]{3,2,1,0:T(8,128)(2,1)S(1)}, bf16[2,2,48,3072]{3,2,1,0:T(8,128)(2,1)S(1)}, u32[]{:S(2)}, u32[]{:S(2)}) %collective-permute-start.51) | collective-permute-done | bytes 1179680 | tf_op jit(solution)/shard_map/ppermute | solution.py:594
  415.1 1.5 collective-permute-start.40
  418.8 1.4 collective-permute-start.39
  420.3 1.6 pad_maximum_fusion.refs_0_
  421.9 3.1 collective-permute-done.40
  429.3 9.6 %collective-permute-done.22 = f32[24,768]{1,0:T(8,128)} collective-permute-done((f32[24,768]{1,0:T(8,128)}, f32[24,768]{1,0:T(8,128)}, u32[]{:S(2)}, u32[]{:S(2)}) %collective-permute-start.22) | collective-permute-done | bytes 73760 | tf_op jit(solution)/shard_map/ppermute | solution.py:594
  439.8 1.5 collective-permute-start.23
  442.0 2.3 collective-permute-done.23
  444.3 3.2 collective-permute-start.25
  449.7 1.5 pad_maximum_fusion.3.refs_1_
  451.5 3.2 add_convert_fusion.5
  457.2 3.4 collective-permute-done.24
  461.9 11.3 %assemble.2 = (f32[768,3072]{1,0:T(8,128)}, f32[4,768,768]{2,1,0:T(8,128)}) custom-call(s32[3]{0:T(128)} %pad_add_fusion.ids_ref, bf16[4,2,48,3072]{3,2,1,0:T(8,128)(2,1)} %pad_maximum_fusion.refs_0_, bf16[4,2,48,3072]{3,2,1,0:T(8,128)(2,1)} %copy-done.1, bf16[4,2,48,3072]{3,2,1,0:T(8,128)(2,1)} %collective-permute-done.52.refs_2_, ...), custom_call_target="tpu_custom_call" | custom-call | flops 2000000000 | bytes 1024 | tf_op jit(solution)/shard_map/assemble/pallas_call | solution.py:498
  474.2 6.9 %assemble.3 = (f32[768,2304]{1,0:T(8,128)}, f32[768,768]{1,0:T(8,128)}) custom-call(s32[3]{0:T(128)} %pad_add_fusion.ids_ref, bf16[4,48,3072]{2,1,0:T(8,128)(2,1)} %copy-done.2, bf16[4,48,3072]{2,1,0:T(8,128)(2,1)} %copy-done.3, bf16[4,48,3072]{2,1,0:T(8,128)(2,1)} %collective-permute-done.42.refs_2_, bf16[4,48,3072]{2,1,0:T(8,128)(2,1)} %copy-done.12, ...), custom_call_target="tpu_custom_call" | custom-call | flops 2000000000 | bytes 1024 | tf_op jit(solution)/shard_map/assemble/pallas_call | solution.py:498
  (186 shorter events, 48.9 us)
Async XLA Ops:
  0.7 8.7 %copy-start.28 = (f32[768]{0:T(1024)S(1)}, f32[768]{0:T(1024)}, u32[]{:S(2)}) copy-start(f32[768]{0:T(1024)} %param.27) | copy-start | bytes 9220
  0.7 8.7 %copy-start.29 = (f32[768]{0:T(1024)S(1)}, f32[768]{0:T(1024)}, u32[]{:S(2)}) copy-start(f32[768]{0:T(1024)} %param.28) | copy-start | bytes 9220
  0.7 8.7 %copy-start.30 = (f32[768]{0:T(1024)S(1)}, f32[768]{0:T(1024)}, u32[]{:S(2)}) copy-start(f32[768]{0:T(1024)} %param.29) | copy-start | bytes 9220
  2.7 19.0 %copy-start.15 = (bf16[608,768]{1,0:T(8,128)(2,1)}, bf16[608,768]{1,0:T(8,128)(2,1)S(1)}, u32[]{:S(2)}) copy-start(bf16[608,768]{1,0:T(8,128)(2,1)S(1)} %fusion.1.refs_1_) | copy-start | bytes 2801668
  2.7 23.4 %collective-permute-start.1 = (bf16[608,768]{1,0:T(8,128)(2,1)S(1)}, bf16[608,768]{1,0:T(8,128)(2,1)S(1)}, u32[]{:S(2)}, u32[]{:S(2)}) collective-permute-start(bf16[608,768]{1,0:T(8,128)(2,1)S(1)} %fusion.1.refs_1_), channel_id=1, source_target_pairs={{1,2},{2,1},{5,6},{6,5},{9,10},{10,9},{13,14},{14,13},{17,18},{18,... | collective-permute-start | bytes 2801672 | tf_op jit(solution)/shard_map/ppermute | solution.py:532
  3.4 27.5 %collective-permute-start = (bf16[608,768]{1,0:T(8,128)(2,1)S(1)}, bf16[608,768]{1,0:T(8,128)(2,1)}, u32[]{:S(2)}, u32[]{:S(2)}) collective-permute-start(bf16[608,768]{1,0:T(8,128)(2,1)S(1)} %fusion.1.refs_1_), channel_id=1, source_target_pairs={{0,1},{1,0},{2,3},{3,2},{4,5},{5,4},{6,7},{7,6},{8,9},{9,8},{10,11... | collective-permute-start | bytes 2801672 | tf_op jit(solution)/shard_map/ppermute | solution.py:594
  10.1 14.6 %copy-start.23 = (bf16[768,4]{0,1:T(4,128)(2,1)S(1)}, bf16[768,4]{0,1:T(4,128)(2,1)}, u32[]{:S(2)}) copy-start(bf16[768,4]{0,1:T(4,128)(2,1)} %param.30) | copy-start | bytes 18436
  21.7 34.2 %collective-permute-start.3 = (bf16[591,768]{1,0:T(8,128)(2,1)}, bf16[591,768]{1,0:T(8,128)(2,1)S(1)}, u32[]{:S(2)}, u32[]{:S(2)}) collective-permute-start(bf16[591,768]{1,0:T(8,128)(2,1)} %get-tuple-element.83.refs_0_), channel_id=1, source_target_pairs={{1,2},{2,1},{5,6},{6,5},{9,10},{10,9},{13,14},{14,13},{17,18},{18,... | collective-permute-start | bytes 2723336 | tf_op jit(solution)/shard_map/ppermute | solution.py:532
  22.9 33.0 %collective-permute-start.2 = (bf16[591,768]{1,0:T(8,128)(2,1)}, bf16[591,768]{1,0:T(8,128)(2,1)}, u32[]{:S(2)}, u32[]{:S(2)}) collective-permute-start(bf16[591,768]{1,0:T(8,128)(2,1)} %get-tuple-element.83.refs_0_), channel_id=1, source_target_pairs={{0,1},{1,0},{2,3},{3,2},{4,5},{5,4},{6,7},{7,6},{8,9},{9,8},{10,11... | collective-permute-start | bytes 2723336 | tf_op jit(solution)/shard_map/ppermute | solution.py:594
  55.9 37.0 %collective-permute-start.9 = (bf16[591,768]{1,0:T(8,128)(2,1)S(1)}, bf16[591,768]{1,0:T(8,128)(2,1)S(1)}, u32[]{:S(2)}, u32[]{:S(2)}) collective-permute-start(bf16[591,768]{1,0:T(8,128)(2,1)S(1)} %collective-permute-done.3), channel_id=1, source_target_pairs={{1,0},{2,3},{5,4},{6,7},{9,8},{10,11},{13,12},{14,15},{17,16},{18,... | collective-permute-start | bytes 2723336 | tf_op jit(solution)/shard_map/ppermute | solution.py:537
  57.2 34.4 %copy-start.14 = (bf16[608,768]{1,0:T(8,128)(2,1)S(1)}, bf16[608,768]{1,0:T(8,128)(2,1)}, u32[]{:S(2)}) copy-start(bf16[608,768]{1,0:T(8,128)(2,1)} %copy-done.13) | copy-start | bytes 2801668
  57.2 57.1 %collective-permute-start.5 = (bf16[591,768]{1,0:T(8,128)(2,1)}, bf16[591,768]{1,0:T(8,128)(2,1)}, u32[]{:S(2)}, u32[]{:S(2)}) collective-permute-start(bf16[591,768]{1,0:T(8,128)(2,1)} %collective-permute-done.2.refs_0_.refs_1_), channel_id=1, source_target_pairs={{1,2},{2,1},{5,6},{6,5},{9,10},{10,9},{13,14},{14,13},{17,18},{18,... | collective-permute-start | bytes 2723336 | tf_op jit(solution)/shard_map/ppermute | solution.py:535
  83.8 35.1 %collective-permute-start.4 = (bf16[591,768]{1,0:T(8,128)(2,1)}, bf16[591,768]{1,0:T(8,128)(2,1)S(1)}, u32[]{:S(2)}, u32[]{:S(2)}) collective-permute-start(bf16[591,768]{1,0:T(8,128)(2,1)} %get-tuple-element.86), channel_id=1, source_target_pairs={{0,1},{3,2},{4,5},{7,6},{8,9},{11,10},{12,13},{15,14},{16,17},{19,... | collective-permute-start | bytes 2723336 | tf_op jit(solution)/shard_map/ppermute | solution.py:555
  89.3 36.7 %collective-permute-start.11 = (bf16[591,768]{1,0:T(8,128)(2,1)}, bf16[591,768]{1,0:T(8,128)(2,1)}, u32[]{:S(2)}, u32[]{:S(2)}) collective-permute-start(bf16[591,768]{1,0:T(8,128)(2,1)} %get-tuple-element.96), channel_id=1, source_target_pairs={{0,1},{3,2},{4,5},{7,6},{8,9},{11,10},{12,13},{15,14},{16,17},{19,... | collective-permute-start | bytes 2723336 | tf_op jit(solution)/shard_map/ppermute | solution.py:555
  91.6 26.3 %collective-permute-start.10 = (bf16[608,768]{1,0:T(8,128)(2,1)S(1)}, bf16[608,768]{1,0:T(8,128)(2,1)S(1)}, u32[]{:S(2)}, u32[]{:S(2)}) collective-permute-start(bf16[608,768]{1,0:T(8,128)(2,1)S(1)} %copy-done.14), channel_id=1, source_target_pairs={{1,0},{2,3},{5,4},{6,7},{9,8},{10,11},{13,12},{14,15},{17,16},{18,... | collective-permute-start | bytes 2801672 | tf_op jit(solution)/shard_map/ppermute | solution.py:537
  92.9 23.7 %collective-permute-start.7 = (bf16[608,768]{1,0:T(8,128)(2,1)}, bf16[608,768]{1,0:T(8,128)(2,1)S(1)}, u32[]{:S(2)}, u32[]{:S(2)}) collective-permute-start(bf16[608,768]{1,0:T(8,128)(2,1)} %collective-permute-done.refs_8_.refs_1_), channel_id=1, source_target_pairs={{1,2},{2,1},{5,6},{6,5},{9,10},{10,9},{13,14},{14,13},{17,18},{18,... | collective-permute-start | bytes 2801672 | tf_op jit(solution)/shard_map/ppermute | solution.py:535
  114.3 36.6 %collective-permute-start.6 = (bf16[591,768]{1,0:T(8,128)(2,1)}, bf16[591,768]{1,0:T(8,128)(2,1)}, u32[]{:S(2)}, u32[]{:S(2)}) collective-permute-start(bf16[591,768]{1,0:T(8,128)(2,1)} %collective-permute-done.5), channel_id=1, source_target_pairs={{1,0},{2,3},{5,4},{6,7},{9,8},{10,11},{13,12},{14,15},{17,16},{18,... | collective-permute-start | bytes 2723336 | tf_op jit(solution)/shard_map/ppermute | solution.py:538
  116.6 41.4 %collective-permute-start.8 = (bf16[608,768]{1,0:T(8,128)(2,1)S(1)}, bf16[608,768]{1,0:T(8,128)(2,1)S(1)}, u32[]{:S(2)}, u32[]{:S(2)}) collective-permute-start(bf16[608,768]{1,0:T(8,128)(2,1)S(1)} %collective-permute-done.7), channel_id=1, source_target_pairs={{1,0},{2,3},{5,4},{6,7},{9,8},{10,11},{13,12},{14,15},{17,16},{18,... | collective-permute-start | bytes 2801672 | tf_op jit(solution)/shard_map/ppermute | solution.py:538
  153.1 15.6 %copy-start.21 = (bf16[591,768]{1,0:T(8,128)(2,1)S(1)}, bf16[591,768]{1,0:T(8,128)(2,1)}, u32[]{:S(2)}) copy-start(bf16[591,768]{1,0:T(8,128)(2,1)} %get-tuple-element.96) | copy-start | bytes 2723332
  159.1 8.7 %collective-permute-start.13 = (bf16[591,768]{1,0:T(8,128)(2,1)}, bf16[591,768]{1,0:T(8,128)(2,1)S(1)}, u32[]{:S(2)}, u32[]{:S(2)}) collective-permute-start(bf16[591,768]{1,0:T(8,128)(2,1)} %get-tuple-element.105), channel_id=1, source_target_pairs={{1,2},{2,1},{5,6},{6,5},{9,10},{10,9},{13,14},{14,13},{17,18},{18,... | collective-permute-start | bytes 2723336 | tf_op jit(solution)/shard_map/ppermute | solution.py:561
  159.8 36.6 %collective-permute-start.16 = (bf16[591,768]{1,0:T(8,128)(2,1)}, bf16[591,768]{1,0:T(8,128)(2,1)S(1)}, u32[]{:S(2)}, u32[]{:S(2)}) collective-permute-start(bf16[591,768]{1,0:T(8,128)(2,1)} %get-tuple-element.108), channel_id=1, source_target_pairs={{1,2},{2,1},{5,6},{6,5},{9,10},{10,9},{13,14},{14,13},{17,18},{18,... | collective-permute-start | bytes 2723336 | tf_op jit(solution)/shard_map/ppermute | solution.py:561
  160.5 35.9 %collective-permute-start.15 = (bf16[591,768]{1,0:T(8,128)(2,1)}, bf16[591,768]{1,0:T(8,128)(2,1)S(1)}, u32[]{:S(2)}, u32[]{:S(2)}) collective-permute-start(bf16[591,768]{1,0:T(8,128)(2,1)} %get-tuple-element.108), channel_id=1, source_target_pairs={{0,1},{3,2},{4,5},{7,6},{8,9},{11,10},{12,13},{15,14},{16,17},{19,... | collective-permute-start | bytes 2723336 | tf_op jit(solution)/shard_map/ppermute | solution.py:560
  166.4 34.5 %collective-permute-start.12 = (bf16[591,768]{1,0:T(8,128)(2,1)}, bf16[591,768]{1,0:T(8,128)(2,1)S(1)}, u32[]{:S(2)}, u32[]{:S(2)}) collective-permute-start(bf16[591,768]{1,0:T(8,128)(2,1)} %get-tuple-element.105), channel_id=1, source_target_pairs={{0,1},{3,2},{4,5},{7,6},{8,9},{11,10},{12,13},{15,14},{16,17},{19,... | collective-permute-start | bytes 2723336 | tf_op jit(solution)/shard_map/ppermute | solution.py:560
  170.0 31.0 %collective-permute-start.14 = (bf16[591,768]{1,0:T(8,128)(2,1)}, bf16[591,768]{1,0:T(8,128)(2,1)}, u32[]{:S(2)}, u32[]{:S(2)}) collective-permute-start(bf16[591,768]{1,0:T(8,128)(2,1)} %add_convert_fusion.8), channel_id=1, source_target_pairs={{1,0},{2,3},{5,4},{6,7},{9,8},{10,11},{13,12},{14,15},{17,16},{18,... | collective-permute-start | bytes 2723336 | tf_op jit(solution)/shard_map/ppermute | solution.py:570
  215.8 24.9 %collective-permute-start.20 = (bf16[8,2,48,3072]{3,2,1,0:T(8,128)(2,1)}, bf16[8,2,48,3072]{3,2,1,0:T(8,128)(2,1)}, u32[]{:S(2)}, u32[]{:S(2)}) collective-permute-start(bf16[8,2,48,3072]{3,2,1,0:T(8,128)(2,1)} %final_grads.2.refs_10_), channel_id=1, source_target_pairs={{0,4},{4,0},{8,12},{12,8},{16,20},{20,16},{24,28},{28,24},{1,5},{5... | collective-permute-start | bytes 14155784 | tf_op jit(solution)/shard_map/ppermute | solution.py:594
  219.0 34.0 %collective-permute-start.19 = (bf16[591,768]{1,0:T(8,128)(2,1)}, bf16[591,768]{1,0:T(8,128)(2,1)}, u32[]{:S(2)}, u32[]{:S(2)}) collective-permute-start(bf16[591,768]{1,0:T(8,128)(2,1)} %add_convert_fusion.4), channel_id=1, source_target_pairs={{0,3},{1,2},{2,1},{3,0},{4,7},{5,6},{6,5},{7,4},{8,11},{9,10},{10,... | collective-permute-start | bytes 2723336 | tf_op jit(solution)/shard_map/ppermute | solution.py:594
  221.7 14.2 %copy-start.5 = (bf16[591,768]{1,0:T(8,128)(2,1)S(1)}, bf16[591,768]{1,0:T(8,128)(2,1)}, u32[]{:S(2)}) copy-start(bf16[591,768]{1,0:T(8,128)(2,1)} %copy-done.4) | copy-start | bytes 2723332
  221.7 14.2 %copy-start.20 = (bf16[591,768]{1,0:T(8,128)(2,1)S(1)}, bf16[591,768]{1,0:T(8,128)(2,1)}, u32[]{:S(2)}) copy-start(bf16[591,768]{1,0:T(8,128)(2,1)} %get-tuple-element.109) | copy-start | bytes 2723332
  237.2 66.7 %collective-permute-start.17 = (bf16[591,768]{1,0:T(8,128)(2,1)}, bf16[591,768]{1,0:T(8,128)(2,1)}, u32[]{:S(2)}, u32[]{:S(2)}) collective-permute-start(bf16[591,768]{1,0:T(8,128)(2,1)} %add_convert_fusion.7), channel_id=1, source_target_pairs={{0,3},{1,2},{2,1},{3,0},{4,7},{5,6},{6,5},{7,4},{8,11},{9,10},{10,... | collective-permute-start | bytes 2723336 | tf_op jit(solution)/shard_map/ppermute | solution.py:594
  239.5 64.4 %collective-permute-start.18 = (bf16[591,768]{1,0:T(8,128)(2,1)}, bf16[591,768]{1,0:T(8,128)(2,1)}, u32[]{:S(2)}, u32[]{:S(2)}) collective-permute-start(bf16[591,768]{1,0:T(8,128)(2,1)} %add_convert_fusion.6), channel_id=1, source_target_pairs={{1,0},{2,3},{5,4},{6,7},{9,8},{10,11},{13,12},{14,15},{17,16},{18,... | collective-permute-start | bytes 2723336 | tf_op jit(solution)/shard_map/ppermute | solution.py:570
  249.8 34.2 %collective-permute-start.44 = (bf16[2,2,48,3072]{3,2,1,0:T(8,128)(2,1)}, bf16[2,2,48,3072]{3,2,1,0:T(8,128)(2,1)}, u32[]{:S(2)}, u32[]{:S(2)}) collective-permute-start(bf16[2,2,48,3072]{3,2,1,0:T(8,128)(2,1)} %constant_dynamic-slice_fusion.3), channel_id=1, source_target_pairs={{0,8},{4,12},{8,0},{12,4},{16,24},{20,28},{24,16},{28,20},{1,9},{5... | collective-permute-start | bytes 3538952 | tf_op jit(solution)/shard_map/ppermute | solution.py:594
  251.4 34.8 %collective-permute-start.48 = (bf16[2,2,48,3072]{3,2,1,0:T(8,128)(2,1)S(1)}, bf16[2,2,48,3072]{3,2,1,0:T(8,128)(2,1)}, u32[]{:S(2)}, u32[]{:S(2)}) collective-permute-start(bf16[2,2,48,3072]{3,2,1,0:T(8,128)(2,1)S(1)} %constant_dynamic-slice_fusion.1), channel_id=1, source_target_pairs={{0,16},{4,20},{8,24},{12,28},{16,0},{20,4},{24,8},{28,12},{1,17},{... | collective-permute-start | bytes 3538952 | tf_op jit(solution)/shard_map/ppermute | solution.py:594
  283.9 143.4 %collective-permute-start.21 = (f32[24,768]{1,0:T(8,128)}, f32[24,768]{1,0:T(8,128)S(1)}, u32[]{:S(2)}, u32[]{:S(2)}) collective-permute-start(f32[24,768]{1,0:T(8,128)} %get-tuple-element.128), channel_id=1, source_target_pairs={{0,4},{4,0},{8,12},{12,8},{16,20},{20,16},{24,28},{28,24},{1,5},{5... | collective-permute-start | bytes 221192 | tf_op jit(solution)/shard_map/ppermute | solution.py:594
  284.0 18.4 %collective-permute-start.27 = (bf16[8,48,3072]{2,1,0:T(8,128)(2,1)}, bf16[8,48,3072]{2,1,0:T(8,128)(2,1)S(1)}, u32[]{:S(2)}, u32[]{:S(2)}) collective-permute-start(bf16[8,48,3072]{2,1,0:T(8,128)(2,1)} %get-tuple-element.130), channel_id=1, source_target_pairs={{0,4},{4,0},{8,12},{12,8},{16,20},{20,16},{24,28},{28,24},{1,5},{5... | collective-permute-start | bytes 7077896 | tf_op jit(solution)/shard_map/ppermute | solution.py:594
  286.2 15.4 %collective-permute-start.45 = (bf16[1,2,48,3072]{3,2,1,0:T(8,128)(2,1)S(1)}, bf16[1,2,48,3072]{3,2,1,0:T(8,128)(2,1)S(1)}, u32[]{:S(2)}, u32[]{:S(2)}) collective-permute-start(bf16[1,2,48,3072]{3,2,1,0:T(8,128)(2,1)S(1)} %constant_dynamic-slice_fusion.2), channel_id=1, source_target_pairs={{0,16},{4,20},{8,24},{12,28},{16,0},{20,4},{24,8},{28,12},{1,17},{... | collective-permute-start | bytes 1769480 | tf_op jit(solution)/shard_map/ppermute | solution.py:594
  288.5 14.4 %copy-start.10 = (bf16[8,48,3072]{2,1,0:T(8,128)(2,1)S(1)}, bf16[8,48,3072]{2,1,0:T(8,128)(2,1)}, u32[]{:S(2)}) copy-start(bf16[8,48,3072]{2,1,0:T(8,128)(2,1)} %get-tuple-element.129) | copy-start | bytes 7077892
  301.6 14.5 %collective-permute-start.49 = (bf16[1,2,48,3072]{3,2,1,0:T(8,128)(2,1)S(1)}, bf16[1,2,48,3072]{3,2,1,0:T(8,128)(2,1)S(1)}, u32[]{:S(2)}, u32[]{:S(2)}) collective-permute-start(bf16[1,2,48,3072]{3,2,1,0:T(8,128)(2,1)S(1)} %constant_dynamic-slice_fusion), channel_id=1, source_target_pairs={{0,8},{4,12},{8,0},{12,4},{16,24},{20,28},{24,16},{28,20},{1,9},{5... | collective-permute-start | bytes 1769480 | tf_op jit(solution)/shard_map/ppermute | solution.py:594
  302.4 79.9 %collective-permute-start.46 = (bf16[1,2,48,3072]{3,2,1,0:T(8,128)(2,1)S(1)}, bf16[1,2,48,3072]{3,2,1,0:T(8,128)(2,1)S(1)}, u32[]{:S(2)}, u32[]{:S(2)}) collective-permute-start(bf16[1,2,48,3072]{3,2,1,0:T(8,128)(2,1)S(1)} %add_convert_fusion.10), channel_id=1, source_target_pairs={{0,16},{4,20},{8,24},{12,28},{16,0},{20,4},{24,8},{28,12},{1,17},{... | collective-permute-start | bytes 1769480 | tf_op jit(solution)/shard_map/ppermute | solution.py:594
  304.1 25.2 %collective-permute-start.30 = (bf16[2,48,3072]{2,1,0:T(8,128)(2,1)S(1)}, bf16[2,48,3072]{2,1,0:T(8,128)(2,1)S(1)}, u32[]{:S(2)}, u32[]{:S(2)}) collective-permute-start(bf16[2,48,3072]{2,1,0:T(8,128)(2,1)S(1)} %constant_dynamic-slice_fusion.8), channel_id=1, source_target_pairs={{0,16},{4,20},{8,24},{12,28},{16,0},{20,4},{24,8},{28,12},{1,17},{... | collective-permute-start | bytes 1769480 | tf_op jit(solution)/shard_map/ppermute | solution.py:594
  316.3 78.8 %collective-permute-start.50 = (bf16[1,2,48,3072]{3,2,1,0:T(8,128)(2,1)S(1)}, bf16[1,2,48,3072]{3,2,1,0:T(8,128)(2,1)S(1)}, u32[]{:S(2)}, u32[]{:S(2)}) collective-permute-start(bf16[1,2,48,3072]{3,2,1,0:T(8,128)(2,1)S(1)} %add_convert_fusion.9), channel_id=1, source_target_pairs={{0,8},{4,12},{8,0},{12,4},{16,24},{20,28},{24,16},{28,20},{1,9},{5... | collective-permute-start | bytes 1769480 | tf_op jit(solution)/shard_map/ppermute | solution.py:594
  317.0 28.2 %collective-permute-start.28 = (bf16[2,48,3072]{2,1,0:T(8,128)(2,1)S(1)}, bf16[2,48,3072]{2,1,0:T(8,128)(2,1)S(1)}, u32[]{:S(2)}, u32[]{:S(2)}) collective-permute-start(bf16[2,48,3072]{2,1,0:T(8,128)(2,1)S(1)} %constant_dynamic-slice_fusion.10), channel_id=1, source_target_pairs={{0,8},{4,12},{8,0},{12,4},{16,24},{20,28},{24,16},{28,20},{1,9},{5... | collective-permute-start | bytes 1769480 | tf_op jit(solution)/shard_map/ppermute | solution.py:594
  329.5 19.3 %collective-permute-start.31 = (bf16[1,48,3072]{2,1,0:T(8,128)(2,1)S(1)}, bf16[1,48,3072]{2,1,0:T(8,128)(2,1)S(1)}, u32[]{:S(2)}, u32[]{:S(2)}) collective-permute-start(bf16[1,48,3072]{2,1,0:T(8,128)(2,1)S(1)} %constant_dynamic-slice_fusion.7), channel_id=1, source_target_pairs={{0,8},{4,12},{8,0},{12,4},{16,24},{20,28},{24,16},{28,20},{1,9},{5... | collective-permute-start | bytes 884744 | tf_op jit(solution)/shard_map/ppermute | solution.py:594
  345.4 6.8 %collective-permute-start.29 = (bf16[1,48,3072]{2,1,0:T(8,128)(2,1)S(1)}, bf16[1,48,3072]{2,1,0:T(8,128)(2,1)S(1)}, u32[]{:S(2)}, u32[]{:S(2)}) collective-permute-start(bf16[1,48,3072]{2,1,0:T(8,128)(2,1)S(1)} %constant_dynamic-slice_fusion.9), channel_id=1, source_target_pairs={{0,16},{4,20},{8,24},{12,28},{16,0},{20,4},{24,8},{28,12},{1,17},{... | collective-permute-start | bytes 884744 | tf_op jit(solution)/shard_map/ppermute | solution.py:594
  352.4 33.7 %collective-permute-start.32 = (bf16[24,3072]{1,0:T(8,128)(2,1)S(1)}, bf16[24,3072]{1,0:T(8,128)(2,1)S(1)}, u32[]{:S(2)}, u32[]{:S(2)}) collective-permute-start(bf16[24,3072]{1,0:T(8,128)(2,1)S(1)} %get-tuple-element.151), channel_id=1, source_target_pairs={{0,1},{1,2},{2,3},{3,0},{4,5},{5,6},{6,7},{7,4},{8,9},{9,10},{10,1... | collective-permute-start | bytes 442376 | tf_op jit(solution)/shard_map/ppermute | solution.py:516
  382.3 5.9 %collective-permute-start.34 = (bf16[24,3072]{1,0:T(8,128)(2,1)S(1)}, bf16[24,3072]{1,0:T(8,128)(2,1)S(1)}, u32[]{:S(2)}, u32[]{:S(2)}) collective-permute-start(bf16[24,3072]{1,0:T(8,128)(2,1)S(1)} %get-tuple-element.152), channel_id=1, source_target_pairs={{0,3},{1,0},{2,1},{3,2},{4,7},{5,4},{6,5},{7,6},{8,11},{9,8},{10,9... | collective-permute-start | bytes 442376 | tf_op jit(solution)/shard_map/ppermute | solution.py:516
  382.3 12.5 %collective-permute-start.33 = (bf16[24,3072]{1,0:T(8,128)(2,1)S(1)}, bf16[24,3072]{1,0:T(8,128)(2,1)S(1)}, u32[]{:S(2)}, u32[]{:S(2)}) collective-permute-start(bf16[24,3072]{1,0:T(8,128)(2,1)S(1)} %get-tuple-element.153), channel_id=1, source_target_pairs={{0,2},{1,3},{2,0},{3,1},{4,6},{5,7},{6,4},{7,5},{8,10},{9,11},{10,... | collective-permute-start | bytes 442376 | tf_op jit(solution)/shard_map/ppermute | solution.py:516
  386.1 34.2 %collective-permute-start.47 = (bf16[2,2,48,3072]{3,2,1,0:T(8,128)(2,1)S(1)}, bf16[2,2,48,3072]{3,2,1,0:T(8,128)(2,1)S(1)}, u32[]{:S(2)}, u32[]{:S(2)}) collective-permute-start(bf16[2,2,48,3072]{3,2,1,0:T(8,128)(2,1)S(1)} %pad_maximum_fusion.4), channel_id=1, source_target_pairs={{0,8},{4,12},{8,0},{12,4},{16,24},{20,28},{24,16},{28,20},{1,9},{5... | collective-permute-start | bytes 3538952 | tf_op jit(solution)/shard_map/ppermute | solution.py:594
  395.0 7.1 %collective-permute-start.35 = (bf16[24,3072]{1,0:T(8,128)(2,1)S(1)}, bf16[24,3072]{1,0:T(8,128)(2,1)S(1)}, u32[]{:S(2)}, u32[]{:S(2)}) collective-permute-start(bf16[24,3072]{1,0:T(8,128)(2,1)S(1)} %get-tuple-element.144), channel_id=1, source_target_pairs={{0,1},{1,2},{2,3},{3,0},{4,5},{5,6},{6,7},{7,4},{8,9},{9,10},{10,1... | collective-permute-start | bytes 442376 | tf_op jit(solution)/shard_map/ppermute | solution.py:516
  395.2 19.6 %collective-permute-start.51 = (bf16[2,2,48,3072]{3,2,1,0:T(8,128)(2,1)S(1)}, bf16[2,2,48,3072]{3,2,1,0:T(8,128)(2,1)S(1)}, u32[]{:S(2)}, u32[]{:S(2)}) collective-permute-start(bf16[2,2,48,3072]{3,2,1,0:T(8,128)(2,1)S(1)} %pad_maximum_fusion.5), channel_id=1, source_target_pairs={{0,16},{4,20},{8,24},{12,28},{16,0},{20,4},{24,8},{28,12},{1,17},{... | collective-permute-start | bytes 3538952 | tf_op jit(solution)/shard_map/ppermute | solution.py:594
  396.7 8.5 %collective-permute-start.36 = (bf16[24,3072]{1,0:T(8,128)(2,1)S(1)}, bf16[24,3072]{1,0:T(8,128)(2,1)S(1)}, u32[]{:S(2)}, u32[]{:S(2)}) collective-permute-start(bf16[24,3072]{1,0:T(8,128)(2,1)S(1)} %get-tuple-element.144), channel_id=1, source_target_pairs={{0,2},{1,3},{2,0},{3,1},{4,6},{5,7},{6,4},{7,5},{8,10},{9,11},{10,... | collective-permute-start | bytes 442376 | tf_op jit(solution)/shard_map/ppermute | solution.py:516
  402.1 5.1 %collective-permute-start.37 = (bf16[24,3072]{1,0:T(8,128)(2,1)S(1)}, bf16[24,3072]{1,0:T(8,128)(2,1)S(1)}, u32[]{:S(2)}, u32[]{:S(2)}) collective-permute-start(bf16[24,3072]{1,0:T(8,128)(2,1)S(1)} %get-tuple-element.144), channel_id=1, source_target_pairs={{0,3},{1,0},{2,1},{3,2},{4,7},{5,4},{6,5},{7,6},{8,11},{9,8},{10,9... | collective-permute-start | bytes 442376 | tf_op jit(solution)/shard_map/ppermute | solution.py:516
  407.3 10.7 %collective-permute-start.38 = (bf16[1,48,3072]{2,1,0:T(8,128)(2,1)S(1)}, bf16[1,48,3072]{2,1,0:T(8,128)(2,1)S(1)}, u32[]{:S(2)}, u32[]{:S(2)}) collective-permute-start(bf16[1,48,3072]{2,1,0:T(8,128)(2,1)S(1)} %get-tuple-element.150), channel_id=1, source_target_pairs={{0,16},{4,20},{8,24},{12,28},{16,0},{20,4},{24,8},{28,12},{1,17},{... | collective-permute-start | bytes 884744 | tf_op jit(solution)/shard_map/ppermute | solution.py:594
  415.1 46.8 %collective-permute-start.53 = (bf16[4,2,48,3072]{3,2,1,0:T(8,128)(2,1)S(1)}, bf16[4,2,48,3072]{3,2,1,0:T(8,128)(2,1)}, u32[]{:S(2)}, u32[]{:S(2)}) collective-permute-start(bf16[4,2,48,3072]{3,2,1,0:T(8,128)(2,1)S(1)} %pad_maximum_fusion.1.refs_1_), channel_id=1, source_target_pairs={{0,4},{4,0},{8,12},{12,8},{16,20},{20,16},{24,28},{28,24},{1,5},{5... | collective-permute-start | bytes 7077896 | tf_op jit(solution)/shard_map/ppermute | solution.py:594
  415.1 9.9 %collective-permute-start.40 = (bf16[1,48,3072]{2,1,0:T(8,128)(2,1)S(1)}, bf16[1,48,3072]{2,1,0:T(8,128)(2,1)S(1)}, u32[]{:S(2)}, u32[]{:S(2)}) collective-permute-start(bf16[1,48,3072]{2,1,0:T(8,128)(2,1)S(1)} %get-tuple-element.149), channel_id=1, source_target_pairs={{0,8},{4,12},{8,0},{12,4},{16,24},{20,28},{24,16},{28,20},{1,9},{5... | collective-permute-start | bytes 884744 | tf_op jit(solution)/shard_map/ppermute | solution.py:594
  418.8 28.6 %collective-permute-start.39 = (bf16[2,48,3072]{2,1,0:T(8,128)(2,1)}, bf16[2,48,3072]{2,1,0:T(8,128)(2,1)}, u32[]{:S(2)}, u32[]{:S(2)}) collective-permute-start(bf16[2,48,3072]{2,1,0:T(8,128)(2,1)} %pad_maximum_fusion.7), channel_id=1, source_target_pairs={{0,8},{4,12},{8,0},{12,4},{16,24},{20,28},{24,16},{28,20},{1,9},{5... | collective-permute-start | bytes 1769480 | tf_op jit(solution)/shard_map/ppermute | solution.py:594
  421.9 40.0 %collective-permute-start.52 = (bf16[4,2,48,3072]{3,2,1,0:T(8,128)(2,1)}, bf16[4,2,48,3072]{3,2,1,0:T(8,128)(2,1)}, u32[]{:S(2)}, u32[]{:S(2)}) collective-permute-start(bf16[4,2,48,3072]{3,2,1,0:T(8,128)(2,1)} %pad_maximum_fusion.refs_0_), channel_id=1, source_target_pairs={{0,4},{4,0},{8,12},{12,8},{16,20},{20,16},{24,28},{28,24},{1,5},{5... | collective-permute-start | bytes 7077896 | tf_op jit(solution)/shard_map/ppermute | solution.py:594
  425.9 23.7 %collective-permute-start.41 = (bf16[2,48,3072]{2,1,0:T(8,128)(2,1)}, bf16[2,48,3072]{2,1,0:T(8,128)(2,1)}, u32[]{:S(2)}, u32[]{:S(2)}) collective-permute-start(bf16[2,48,3072]{2,1,0:T(8,128)(2,1)} %pad_maximum_fusion.8), channel_id=1, source_target_pairs={{0,16},{4,20},{8,24},{12,28},{16,0},{20,4},{24,8},{28,12},{1,17},{... | collective-permute-start | bytes 1769480 | tf_op jit(solution)/shard_map/ppermute | solution.py:594
  427.9 10.9 %collective-permute-start.22 = (f32[24,768]{1,0:T(8,128)}, f32[24,768]{1,0:T(8,128)}, u32[]{:S(2)}, u32[]{:S(2)}) collective-permute-start(f32[24,768]{1,0:T(8,128)} %add.223), channel_id=1, source_target_pairs={{0,8},{4,12},{8,0},{12,4},{16,24},{20,28},{24,16},{28,20},{1,9},{5... | collective-permute-start | bytes 221192 | tf_op jit(solution)/shard_map/ppermute | solution.py:594
  439.8 4.4 collective-permute-start.23
  444.3 6.9 %collective-permute-start.25 = (f32[16,768]{1,0:T(8,128)S(1)}, f32[16,768]{1,0:T(8,128)S(1)}, u32[]{:S(2)}, u32[]{:S(2)}) collective-permute-start(f32[16,768]{1,0:T(8,128)S(1)} %slice.101), channel_id=1, source_target_pairs={{0,2},{1,3},{2,0},{3,1},{4,6},{5,7},{6,4},{7,5},{8,10},{9,11},{10,... | collective-permute-start | bytes 147464 | tf_op jit(solution)/shard_map/ppermute | solution.py:516
  447.5 7.2 %collective-permute-start.26 = (f32[16,768]{1,0:T(8,128)S(1)}, f32[16,768]{1,0:T(8,128)S(1)}, u32[]{:S(2)}, u32[]{:S(2)}) collective-permute-start(f32[16,768]{1,0:T(8,128)S(1)} %slice.101), channel_id=1, source_target_pairs={{0,3},{1,0},{2,1},{3,2},{4,7},{5,4},{6,5},{7,6},{8,11},{9,8},{10,9... | collective-permute-start | bytes 147464 | tf_op jit(solution)/shard_map/ppermute | solution.py:516
  449.6 23.6 %collective-permute-start.42 = (bf16[4,48,3072]{2,1,0:T(8,128)(2,1)S(1)}, bf16[4,48,3072]{2,1,0:T(8,128)(2,1)}, u32[]{:S(2)}, u32[]{:S(2)}) collective-permute-start(bf16[4,48,3072]{2,1,0:T(8,128)(2,1)S(1)} %pad_maximum_fusion.2.refs_0_), channel_id=1, source_target_pairs={{0,4},{4,0},{8,12},{12,8},{16,20},{20,16},{24,28},{28,24},{1,5},{5... | collective-permute-start | bytes 3538952 | tf_op jit(solution)/shard_map/ppermute | solution.py:594
  451.2 21.9 %collective-permute-start.43 = (bf16[4,48,3072]{2,1,0:T(8,128)(2,1)S(1)}, bf16[4,48,3072]{2,1,0:T(8,128)(2,1)S(1)}, u32[]{:S(2)}, u32[]{:S(2)}) collective-permute-start(bf16[4,48,3072]{2,1,0:T(8,128)(2,1)S(1)} %pad_maximum_fusion.3.refs_1_), channel_id=1, source_target_pairs={{0,4},{4,0},{8,12},{12,8},{16,20},{20,16},{24,28},{28,24},{1,5},{5... | collective-permute-start | bytes 3538952 | tf_op jit(solution)/shard_map/ppermute | solution.py:594
  454.7 5.9 %collective-permute-start.24 = (f32[16,768]{1,0:T(8,128)S(1)}, f32[16,768]{1,0:T(8,128)S(1)}, u32[]{:S(2)}, u32[]{:S(2)}) collective-permute-start(f32[16,768]{1,0:T(8,128)S(1)} %slice.101), channel_id=1, source_target_pairs={{0,1},{1,2},{2,3},{3,0},{4,5},{5,6},{6,7},{7,4},{8,9},{9,10},{10,1... | collective-permute-start | bytes 147464 | tf_op jit(solution)/shard_map/ppermute | solution.py:516
  (21 other events, 115.4 us)

commit v3 on v2

--- a/solution.py
+++ b/solution.py
@@ -221,8 +221,8 @@
         grad_ref[piece, 1] = grad_out[piece * share : (piece + 1) * share].astype(BF16)
 
 
-def assemble_kernel(write, count, ids_ref, *refs):
-    outs = refs[len(refs) - count :]
+def assemble_kernel(write, ids_ref, *refs):
+    outs = refs[4:]
     at = pl.program_id(0)
     chosen = ((at // 2) ^ ids_ref[0]) * 2 + at % 2
     for which in range(4):
@@ -488,7 +488,7 @@
     )(half, *rows, *gpres, *activs, *geouts, *started, *after)
 
 
-def assemble(ids, groups, write, outs, after):
+def assemble(ids, groups, write, outs):
     blocks = []
     for shape, dim in outs:
         block = tuple(n // 4 if d == dim else n for d, n in enumerate(shape))
@@ -496,19 +496,18 @@
         blocks.append(pl.BlockSpec(block, place))
     rank = groups[0].ndim
     return pl.pallas_call(
-        functools.partial(assemble_kernel, write, len(outs)),
+        functools.partial(assemble_kernel, write),
         out_shape=tuple(jax.ShapeDtypeStruct(shape, F32) for shape, _ in outs),
         grid_spec=pltpu.PrefetchScalarGridSpec(
             num_scalar_prefetch=1,
             grid=(4,),
-            in_specs=[pl.BlockSpec(groups[0].shape, lambda at, ids: (0,) * rank)] * 4
-            + [pl.BlockSpec(memory_space=pl.ANY)] * len(after),
+            in_specs=[pl.BlockSpec(groups[0].shape, lambda at, ids: (0,) * rank)] * 4,
             out_specs=tuple(blocks),
         ),
         compiler_params=params(),
         cost_estimate=cost(5),
         name="assemble",
-    )(ids, *groups, *after)
+    )(ids, *groups)
 
 
 def shift(values, axis, by):
@@ -598,75 +597,111 @@
     return ((lax.axis_index(axis) // bit) % 2).astype(jnp.int32)
 
 
-def halve(values, axis, bit):
+def halves(values, axis, bit):
     mine = axis_bit(axis, bit)
     size = values.shape[0] // 2
     part = lambda which: lax.dynamic_slice_in_dim(values, which * size, size, 0)
-    got = swap(part(1 - mine), axis, bit)
-    return add_rounded(part(mine), got)
+    return part(mine), part(1 - mine)
 
 
 def add_rounded(one, other):
     return (one.astype(F32) + other.astype(F32)).astype(one.dtype)
 
 
-def sum_over(keep, send, axis, write, outs, inner=None, after=(), before_end=()):
-    core = 1
-    values = add_rounded(keep, swap(send, axis, core))
-    if after:
-        values, *_ = lax.optimization_barrier((values, *after))
-    return values, lambda: sum_rest(values, axis, write, outs, inner, before_end)
-
-
-def sum_rest(values, axis, write, outs, inner, before_end):
-    size = lax.axis_size(axis)
-    core, *rest = [1 << b for b in range(size.bit_length() - 1)]
-    pieces = 1 << len(rest)
-    orders = (rest, rest[::-1])
-    parts = []
-    for part, order in zip((values[:pieces], values[pieces:]), orders):
-        for bit in order:
-            part = halve(part, axis, bit)
-        parts.append(part)
-    if inner is not None:
-        joined = jnp.concatenate(parts, axis=0)
-        joined = inner(joined.reshape(-1, joined.shape[-1])).reshape(joined.shape)
-        parts = [joined[:1], joined[1:]]
-    ids = [axis_bit(axis, core)]
-    done = []
-    for part, order in zip(parts, orders):
-        for bit in order[::-1]:
-            part = jnp.concatenate([part, swap(part, axis, bit)], axis=0)
-        done.append(part)
-        ids.append(sum(axis_bit(axis, bit) * (pieces >> at + 1) for at, bit in enumerate(order)))
-    got = [swap(part, axis, core) for part in done]
-    return assemble(jnp.stack(ids), done + got, write, outs, before_end)
-
-
-def sum_direct(values, axis):
-    size = lax.axis_size(axis)
-    me = lax.axis_index(axis)
+def together(*trees):
+    return lax.optimization_barrier(trees)
+
+
+class PieceSum:
+    def __init__(self, core_sum, axis):
+        self.axis = axis
+        bits = [1 << b for b in range(1, lax.axis_size(axis).bit_length() - 1)]
+        self.orders = (bits, bits[::-1])
+        self.steps = len(bits)
+        self.pieces = 1 << self.steps
+        self.parts = (core_sum[: self.pieces], core_sum[self.pieces :])
+
+    def down(self, step):
+        done = []
+        for part, order in zip(self.parts, self.orders):
+            keep, give = halves(part, self.axis, order[step])
+            done.append(add_rounded(keep, swap(give, self.axis, order[step])))
+        self.parts = tuple(done)
+
+    def up(self, step):
+        self.parts = tuple(
+            jnp.concatenate([part, swap(part, self.axis, order[::-1][step])], axis=0)
+            for part, order in zip(self.parts, self.orders)
+        )
+
+    def place(self, write, outs, got):
+        ids = [axis_bit(self.axis, 1)]
+        for order in self.orders:
+            ids.append(sum(axis_bit(self.axis, bit) * (self.pieces >> at + 1) for at, bit in enumerate(order)))
+        return assemble(jnp.stack(ids), (*self.parts, *got), write, outs)
+
+
+def sum_gradients(expert, dense_keep, dense_send, small, shared_rows, expert_out, dense_out, parts):
+    rep, exp = "rep", "exp"
+    last = expert.steps - 1
+    expert.down(0)
+    expert.parts, dense_send, small = together(expert.parts, dense_send, small)
+    for step in range(1, last + 1):
+        expert.down(step)
+    dense_sum = add_rounded(dense_keep, swap(dense_send, rep, 1))
+    small = small + swap(small, rep, 1)
+
+    expert.parts, dense_sum, small = together(expert.parts, dense_sum, small)
+    dense = PieceSum(dense_sum, rep)
+    for step in range(last):
+        expert.up(step)
+        dense.down(step)
+        small = small + swap(small, rep, 2 << step)
+        expert.parts, dense.parts, small = together(expert.parts, dense.parts, small)
+    dense.down(last)
+    small = small + swap(small, rep, 2 << last)
+
+    dense.parts, small, expert.parts, parts = together(dense.parts, small, expert.parts, parts)
+    expert.up(last)
+    shape = (2, -1, *dense.parts[0].shape[1:])
+    joined = jnp.concatenate(dense.parts, axis=0).reshape(-1, shape[-1])
+    share = share_sum(joined, exp)
+    share, small = together(share, small)
+    joined = share_collect(share, exp).reshape(shape)
+    shared = small[:shared_rows]
+    shared = sum([shift(shared, exp, k) for k in range(1, lax.axis_size(exp))], shared)
+    dense.parts = (joined[0], joined[1])
+
+    dense.parts, shared, expert.parts = together(dense.parts, shared, expert.parts)
+    got = [swap(part, rep, 1) for part in expert.parts]
+    for step in range(last):
+        dense.up(step)
+    dense.parts, got, expert.parts = together(dense.parts, got, expert.parts)
+    dense.up(last)
+    placed = expert.place(*expert_out, got)
+    dense.parts, placed = together(dense.parts, placed)
+    got = [swap(part, rep, 1) for part in dense.parts]
+    return placed, dense.place(*dense_out, got), shared, small[shared_rows:], parts
+
+
+def share_sum(values, axis):
+    size, me = lax.axis_size(axis), lax.axis_index(axis)
     share = values.shape[0] // size
     take = lambda owner: lax.dynamic_slice_in_dim(values, (owner % size) * share, share, 0)
     total = take(me).astype(F32)
     for k in range(1, size):
         total = total + shift(take(me + k), axis, k).astype(F32)
-    total = total.astype(values.dtype)
-    result = jnp.zeros_like(values)
-    result = lax.dynamic_update_slice_in_dim(result, total, me * share, 0)
+    return total.astype(values.dtype)
+
+
+def share_collect(share, axis):
+    size, me = lax.axis_size(axis), lax.axis_index(axis)
+    rows = share.shape[0]
+    result = jnp.zeros((size * rows, share.shape[1]), share.dtype)
+    result = lax.dynamic_update_slice_in_dim(result, share, me * rows, 0)
     for k in range(1, size):
-        result = lax.dynamic_update_slice_in_dim(
-            result, shift(total, axis, k), ((me - k) % size) * share, 0
-        )
+        result = lax.dynamic_update_slice_in_dim(result, shift(share, axis, k), ((me - k) % size) * rows, 0)
     return result
-
-
-def sum_small(values, local_rows):
-    for bit in [1 << b for b in range(lax.axis_size("rep").bit_length() - 1)]:
-        values = values + swap(values, "rep", bit)
-    shared = values[: values.shape[0] - local_rows]
-    shared = sum([shift(shared, "exp", k) for k in range(1, lax.axis_size("exp"))], shared)
-    return shared, values[values.shape[0] - local_rows :]
 
 
 def on_device(
@@ -724,24 +759,16 @@
             sums = partial_grads(listed(None), listed(3), listed(2), listed(4))
             early = (sums[0], *backs.sent, *parts.sent)
         elif k == last - 1:
-            backs.send_outward(mixes[last], ups[last])
             early, middle_sent = (), tuple(backs.sent + parts.sent)
+    backs.send_outward(blocks[last][1])
     _, _, activs, gpres, geouts, grouters, gin_bias, gout_bias = zip(*blocks)
     final = lambda half, after: final_grads(
         half, mixes[-2:], gpres[-2:], activs[-2:], geouts[-2:], sums, pieces, after
     )
     send = final(1 - core, middle_sent)
     keep = final(core, (send,))
-    parts.add(last, lax.optimization_barrier((blocks[last][0], keep))[0])
-    parts.send_outward(keep)
-    result = sum((values.astype(F32) for values in parts.sums), hidden).astype(BF16)
-    core_sum, expert_rest = sum_over(
-        keep,
-        send,
-        "rep",
-        write_expert,
-        (((width, hidden_units), 0), ((hidden_units // width, width, width), 1)),
-    )
+    core_sum = add_rounded(keep, swap(send, "rep", 1))
+    expert = PieceSum(core_sum, "rep")
 
     smalls = [part for trio in zip(grouters, gin_bias, gout_bias) for part in trio]
     shared_rows = 8 + -(-experts // 8) * 8
@@ -750,19 +777,19 @@
         core, backs.sums, cotangent, inputs, hidden, qkv, ctx, vecs, w_qkv, w_out,
         smalls, small_rows, pieces, (core_sum,),
     )
-    grad_experts_in, grad_experts_out = expert_rest()
-    _, dense_rest = sum_over(
+    parts.add(last, together(blocks[last][0], grad_inputs)[0])
+    parts.send_outward(grad_inputs)
+    (grad_experts_in, grad_experts_out), (grad_qkv, grad_out), small, own, returned = sum_gradients(
+        expert,
         dense_keep,
         dense_send,
-        "rep",
-        write_dense,
-        (((width, 3 * width), 0), ((width, width), 0)),
-        functools.partial(sum_direct, axis="exp"),
-        tuple(parts.sums[1:]),
-        [grad_experts_out],
+        small,
+        shared_rows,
+        (write_expert, (((width, hidden_units), 0), ((hidden_units // width, width, width), 1))),
+        (write_dense, (((width, 3 * width), 0), ((width, width), 0))),
+        parts.sums,
     )
-    grad_qkv, grad_out = dense_rest()
-    small, own = sum_small(small, small_rows - shared_rows)
+    result = sum((values.astype(F32) for values in returned), hidden).astype(BF16)
     return (
         result,
         grad_inputs,

time: 488 us -> 444 us (0.910)
  starting transfers between devices: 103 us -> 78.7 us
  waiting for transfers between devices: 119 us -> 102 us
  other arithmetic: 37.3 us -> 30.6 us
    ppermute x9, starting transfers between devices: 39.5 us -> 11.9 us  [shift(): lax.ppermute(values, axis, [(i, (i + by) % size) for i in range(size)])]
    ppermute x29, waiting for transfers between devices: 81.7 us -> 55.5 us  [swap(): lax.ppermute(values, axis, [(i, i ^ bit) for i in range(lax.axis_size(axi...]
    ppermute x2, waiting for transfers between devices: 0.01 us -> 13.3 us  [send_outward(): self.sums.append(lax.ppermute(outward, self.axis, OUTWARD))]
    unnamed x65 -> x95, local copies, waits for them, and re-layouts: 6.33 us -> 10.7 us
  transfers between devices with their start and end apart: 54 -> 54, of which waited for: 22 -> 24; matrix products, arithmetic and copies ran while one was open for 8% -> 7% of each run, Pallas kernels for 39% -> 43%
where the time goes in v3:
time: 444 us; the launch traced here: 437 us
  Pallas kernels  209 us (47%)
  waiting for transfers between devices  102 us (23%)
  starting transfers between devices  78.7 us (18%)
  other arithmetic  30.6 us (7%)
  local copies, waits for them, and re-layouts  15.2 us (3%)
    pallas_call x4, Pallas kernels, expert_block(): pl.pallas_call(functools.partial(expert_kernel, len(after)), out_shape=(j...  99.6 us
    ppermute x29, waiting for transfers between devices, swap(): lax.ppermute(values, axis, [(i, i ^ bit) for i in range(lax.axis_size(axi...  55.5 us
    ppermute x29, starting transfers between devices, swap(): lax.ppermute(values, axis, [(i, i ^ bit) for i in range(lax.axis_size(axi...  36.9 us
    pallas_call x1, Pallas kernels, attend_back(): pl.pallas_call(functools.partial(attend_back_kernel, len(smalls), len(gmi...  30.9 us
    pallas_call x2, Pallas kernels, final_grads(): pl.pallas_call(functools.partial(final_grads_kernel, count), out_shape=ja...  28 us
    pallas_call x1, Pallas kernels, partial_grads(): pl.pallas_call(functools.partial(partial_grads_kernel, count), out_shape=...  20.5 us
    pallas_call x2, Pallas kernels, assemble(): pl.pallas_call(functools.partial(assemble_kernel, write), out_shape=tuple...  18.3 us
    ppermute x9, waiting for transfers between devices, shift(): lax.ppermute(values, axis, [(i, (i + by) % size) for i in range(size)])  18.1 us
  transfers between devices with their start and end apart: 54, of which 24 were waited for; matrix products, arithmetic and copies ran while one was open for 7% of the time, Pallas kernels for 43%

profile of v3, /device:TPU:0, one launch (start us, length us, event | category | flops | bytes accessed | tf_op | source)
XLA Modules:
  0.0 437.3 jit_solution(18003626174408414781)
XLA Ops:
  3.4 5.9 %collective-permute-start.2 = (bf16[608,768]{1,0:T(8,128)(2,1)S(1)}, bf16[608,768]{1,0:T(8,128)(2,1)}, u32[]{:S(2)}, u32[]{:S(2)}) collective-permute-start(bf16[608,768]{1,0:T(8,128)(2,1)S(1)} %fusion.1.refs_1_), channel_id=1, source_target_pairs={{0,1},{1,0},{2,3},{3,2},{4,5},{5,4},{6,7},{7,6},{8,9},{9,8},{10,11... | collective-permute-start | bytes 2801672 | tf_op jit(solution)/shard_map/ppermute | solution.py:593
  10.1 11.6 %attend.1 = (bf16[591,2304]{1,0:T(8,128)(2,1)}, bf16[591,768]{1,0:T(8,128)(2,1)}, f32[591,768]{1,0:T(8,128)}, bf16[591,768]{1,0:T(8,128)(2,1)}) custom-call(bf16[591,768]{1,0:T(8,128)(2,1)} %x_ref.3, f32[8,768]{1,0:T(8,128)} %stack.45.vecs_ref, bf16[768,2304]{1,0:T(8,128)(2,1)} %wqkv_ref.3, bf16[768,768]{1,0:T(8,128)(2,1)} %wout_ref.3), custom_call_target="tpu_custom_call" | custom-call | flops 4800000000 | bytes 1024 | tf_op jit(solution)/shard_map/attend/pallas_call | solution.py:350
  22.6 1.7 collective-permute-start
  25.8 5.2 %collective-permute-done.2.refs_8_.refs_1_ = bf16[608,768]{1,0:T(8,128)(2,1)} collective-permute-done((bf16[608,768]{1,0:T(8,128)(2,1)S(1)}, bf16[608,768]{1,0:T(8,128)(2,1)}, u32[]{:S(2)}, u32[]{:S(2)}) %collective-permute-start.2) | collective-permute-done | bytes 933920 | tf_op jit(solution)/shard_map/ppermute | solution.py:593
  31.0 24.9 %expert_block.4 = (bf16[591,768]{1,0:T(8,128)(2,1)}, bf16[591,768]{1,0:T(8,128)(2,1)}, bf16[591,3072]{1,0:T(8,128)(2,1)}, bf16[591,3072]{1,0:T(8,128)(2,1)}, bf1...) custom-call(s32[1]{0:T(128)} %bitcast.1.me_ref, ...), custom_call_target="tpu_custom_call" | custom-call | flops 9600000000 | bytes 1024 | tf_op jit(solution)/shard_map/expert_block/pallas_call | solution.py:397
  57.2 1.7 collective-permute-start.5
  59.0 25.0 %expert_block.5 = (bf16[591,768]{1,0:T(8,128)(2,1)}, bf16[591,768]{1,0:T(8,128)(2,1)}, bf16[591,3072]{1,0:T(8,128)(2,1)}, bf16[591,3072]{1,0:T(8,128)(2,1)}, bf1...) custom-call(s32[1]{0:T(128)} %bitcast.1.me_ref, ...), custom_call_target="tpu_custom_call" | custom-call | flops 9600000000 | bytes 1024 | tf_op jit(solution)/shard_map/expert_block/pallas_call | solution.py:397
  83.9 6.4 %collective-permute-start.9 = (bf16[591,768]{1,0:T(8,128)(2,1)}, bf16[591,768]{1,0:T(8,128)(2,1)}, u32[]{:S(2)}, u32[]{:S(2)}) collective-permute-start(bf16[591,768]{1,0:T(8,128)(2,1)} %get-tuple-element.132), channel_id=1, source_target_pairs={{0,1},{3,2},{4,5},{7,6},{8,9},{11,10},{12,13},{15,14},{16,17},{19,... | collective-permute-start | bytes 2723336 | tf_op jit(solution)/shard_map/ppermute | solution.py:554
  90.3 1.3 collective-permute-start.10
  94.0 20.5 %partial_grads.1 = (f32[768,3072]{1,0:T(8,128)}, f32[768,3072]{1,0:T(8,128)}) custom-call(bf16[591,768]{1,0:T(8,128)(2,1)} %get-tuple-element.121.refs_0_, bf16[591,768]{1,0:T(8,128)(2,1)} %collective-permute-done.refs_0_.refs_1_, bf16[591,3072]{1,0:T(8,128)(2,1)} %get-tuple-element.125.refs_2_, bf16[591,3072]{1,0:T(8,128)(2,1)} %get-tuple-element.126.refs_3_, ...), custom_call_target="tpu_custom_call" | custom-call | flops 9600000000 | bytes 1024 | tf_op jit(solution)/shard_map/partial_grads/pallas_call | solution.py:453
  119.2 6.8 %collective-permute-done.10.refs_10_ = bf16[591,768]{1,0:T(8,128)(2,1)S(1)} collective-permute-done((bf16[591,768]{1,0:T(8,128)(2,1)}, bf16[591,768]{1,0:T(8,128)(2,1)S(1)}, u32[]{:S(2)}, u32[]{:S(2)}) %collective-permute-start.10) | collective-permute-done | bytes 907808 | tf_op jit(solution)/shard_map/ppermute | solution.py:554
  127.0 24.8 %expert_block.6 = (bf16[591,768]{1,0:T(8,128)(2,1)}, bf16[591,768]{1,0:T(8,128)(2,1)}, bf16[591,3072]{1,0:T(8,128)(2,1)}, bf16[591,3072]{1,0:T(8,128)(2,1)}, bf1...) custom-call(s32[1]{0:T(128)} %bitcast.1.me_ref, ...), custom_call_target="tpu_custom_call" | custom-call | flops 9600000000 | bytes 1024 | tf_op jit(solution)/shard_map/expert_block/pallas_call | solution.py:397
  151.8 2.3 broadcast_select_fusion.2.refs_0_.refs_1_
  154.1 4.1 collective-permute-done.11
  160.0 3.2 collective-permute-start.14
  163.9 5.3 %collective-permute-start.12 = (bf16[591,768]{1,0:T(8,128)(2,1)}, bf16[591,768]{1,0:T(8,128)(2,1)}, u32[]{:S(2)}, u32[]{:S(2)}) collective-permute-start(bf16[591,768]{1,0:T(8,128)(2,1)} %get-tuple-element.142), channel_id=1, source_target_pairs={{0,1},{3,2},{4,5},{7,6},{8,9},{11,10},{12,13},{15,14},{16,17},{19,... | collective-permute-start | bytes 2723336 | tf_op jit(solution)/shard_map/ppermute | solution.py:559
  169.3 24.9 %expert_block.7 = (bf16[591,768]{1,0:T(8,128)(2,1)}, bf16[591,768]{1,0:T(8,128)(2,1)}, bf16[591,3072]{1,0:T(8,128)(2,1)}, bf16[591,3072]{1,0:T(8,128)(2,1)}, bf1...) custom-call(s32[1]{0:T(128)} %bitcast.1.me_ref, ...), custom_call_target="tpu_custom_call" | custom-call | flops 9600000000 | bytes 1024 | tf_op jit(solution)/shard_map/expert_block/pallas_call | solution.py:397
  194.3 3.8 collective-permute-done.12.refs_10_
  198.1 13.9 %final_grads.2.refs_10_ = bf16[8,2,48,3072]{3,2,1,0:T(8,128)(2,1)} custom-call(s32[1]{0:T(128)S(6)} %sub.48.half_ref, bf16[591,768]{1,0:T(8,128)(2,1)} %broadcast_select_fusion.3.refs_0_, bf16[591,768]{1,0:T(8,128)(2,1)} %broadcast_select_fusion.2.refs_0_.refs_1_, bf16[591,3072]{1,0:T(8,128)(2,1)} %get-tuple-element.134.refs_2_, ...), custom_call_target="tpu_custom_call" | custom-call | flops 1600000000 | bytes 1024 | tf_op jit(solution)/shard_map/final_grads/pallas_call | solution.py:471
  212.3 1.7 add_convert_fusion.7
  214.0 1.4 add_convert_fusion.8
  215.4 2.5 collective-permute-start.19
  217.9 1.5 collective-permute-start.20
  219.3 14.1 %final_grads.3 = bf16[8,2,48,3072]{3,2,1,0:T(8,128)(2,1)} custom-call(s32[1]{0:T(128)} %bitcast.half_ref.core_ref, bf16[591,768]{1,0:T(8,128)(2,1)} %broadcast_select_fusion.3.refs_0_, bf16[591,768]{1,0:T(8,128)(2,1)} %broadcast_select_fusion.2.refs_0_.refs_1_, bf16[591,3072]{1,0:T(8,128)(2,1)} %get-tuple-element.134.refs_2_, ...), custom_call_target="tpu_custom_call" | custom-call | flops 1600000000 | bytes 1024 | tf_op jit(solution)/shard_map/final_grads/pallas_call | solution.py:471
  234.6 5.8 %add_convert_fusion.refs_16_ = bf16[8,2,48,3072]{3,2,1,0:T(8,128)(2,1)S(1)} fusion(bf16[8,2,48,3072]{3,2,1,0:T(8,128)(2,1)} %collective-permute-done.16, bf16[8,2,48,3072]{3,2,1,0:T(8,128)(2,1)} %final_grads.3), kind=kLoop, calls=%fused_computation | loop fusion | flops 9437184 | bytes 14155776 | tf_op jit(solution)/shard_map/convert_element_type | solution.py:608
  240.9 1.7 copy-done
  242.7 1.4 collective-permute-start.17
  244.8 1.3 collective-permute-start.18
  246.1 13.3 %collective-permute-done.20.refs_3_ = bf16[591,768]{1,0:T(8,128)(2,1)} collective-permute-done((bf16[591,768]{1,0:T(8,128)(2,1)S(1)}, bf16[591,768]{1,0:T(8,128)(2,1)}, u32[]{:S(2)}, u32[]{:S(2)}) %collective-permute-start.20) | collective-permute-done | bytes 907808 | tf_op jit(solution)/shard_map/ppermute | solution.py:569
  259.4 30.9 %attend_back.1 = (bf16[591,768]{1,0:T(8,128)(2,1)}, bf16[8,48,3072]{2,1,0:T(8,128)(2,1)}, bf16[8,48,3072]{2,1,0:T(8,128)(2,1)}, f32[24,768]{1,0:T(8,128)}) custom-call(s32[1]{0:T(128)} %bitcast.half_ref.core_ref, bf16[591,768]{1,0:T(8,128)(2,1)} %up_ref.1, bf16[591,768]{1,0:T(8,128)(2,1)} %x_ref.3, f32[591,768]{1,0:T(8,128)} %get-tuple-element.120.hidden_ref, ...), custom_call_target="tpu_custom_call" | custom-call | flops 11200000000 | bytes 1024 | tf_op jit(solution)/shard_map/attend_back/pallas_call | solution.py:371
  290.3 1.8 add_convert_fusion.3
  293.0 1.7 collective-permute-start.22
  295.0 2.2 collective-permute-start.33
  299.8 1.6 collective-permute-start.21
  301.4 7.4 %collective-permute-done.22 = bf16[1,2,48,3072]{3,2,1,0:T(8,128)(2,1)S(1)} collective-permute-done((bf16[1,2,48,3072]{3,2,1,0:T(8,128)(2,1)S(1)}, bf16[1,2,48,3072]{3,2,1,0:T(8,128)(2,1)S(1)}, u32[]{:S(2)}, u32[]{:S(2)}) %collective-permute-start.22) | collective-permute-done | bytes 589856 | tf_op jit(solution)/shard_map/ppermute | solution.py:593
  309.0 6.2 %collective-permute-done.21 = bf16[1,2,48,3072]{3,2,1,0:T(8,128)(2,1)S(1)} collective-permute-done((bf16[1,2,48,3072]{3,2,1,0:T(8,128)(2,1)S(1)}, bf16[1,2,48,3072]{3,2,1,0:T(8,128)(2,1)S(1)}, u32[]{:S(2)}, u32[]{:S(2)}) %collective-permute-start.21) | collective-permute-done | bytes 589856 | tf_op jit(solution)/shard_map/ppermute | solution.py:593
  317.3 1.5 collective-permute-start.25
  318.9 1.4 collective-permute-start.27
  321.6 1.8 collective-permute-start.28
  323.4 10.2 %collective-permute-done.25 = bf16[1,2,48,3072]{3,2,1,0:T(8,128)(2,1)S(1)} collective-permute-done((bf16[1,2,48,3072]{3,2,1,0:T(8,128)(2,1)S(1)}, bf16[1,2,48,3072]{3,2,1,0:T(8,128)(2,1)S(1)}, u32[]{:S(2)}, u32[]{:S(2)}) %collective-permute-start.25) | collective-permute-done | bytes 589856 | tf_op jit(solution)/shard_map/ppermute | solution.py:593
  333.6 1.3 collective-permute-start.26
  335.2 9.0 %collective-permute-done.28 = bf16[2,48,3072]{2,1,0:T(8,128)(2,1)S(1)} collective-permute-done((bf16[2,48,3072]{2,1,0:T(8,128)(2,1)S(1)}, bf16[2,48,3072]{2,1,0:T(8,128)(2,1)S(1)}, u32[]{:S(2)}, u32[]{:S(2)}) %collective-permute-start.28) | collective-permute-done | bytes 589856 | tf_op jit(solution)/shard_map/ppermute | solution.py:593
  344.4 1.9 collective-permute-done.26
  350.3 2.3 collective-permute-done.32
  352.6 2.3 collective-permute-done.31
  357.6 2.7 collective-permute-start.35
  363.2 1.4 collective-permute-start.45
  365.1 2.3 collective-permute-done.37
  367.5 4.3 collective-permute-done.36
  371.9 1.9 collective-permute-start.43
  374.4 3.0 collective-permute-done.42
  377.4 3.6 collective-permute-start.40
  382.5 5.9 %collective-permute-done.38 = bf16[24,3072]{1,0:T(8,128)(2,1)S(1)} collective-permute-done((bf16[24,3072]{1,0:T(8,128)(2,1)S(1)}, bf16[24,3072]{1,0:T(8,128)(2,1)S(1)}, u32[]{:S(2)}, u32[]{:S(2)}) %collective-permute-start.38) | collective-permute-done | bytes 147488 | tf_op jit(solution)/shard_map/ppermute | solution.py:515
  388.5 1.9 collective-permute-done.39
  390.7 2.3 pad_maximum_fusion.1.refs_1_
  393.9 3.2 collective-permute-start.47
  397.2 5.5 %collective-permute-done.46 = bf16[1,48,3072]{2,1,0:T(8,128)(2,1)S(1)} collective-permute-done((bf16[1,48,3072]{2,1,0:T(8,128)(2,1)S(1)}, bf16[1,48,3072]{2,1,0:T(8,128)(2,1)S(1)}, u32[]{:S(2)}, u32[]{:S(2)}) %collective-permute-start.46) | collective-permute-done | bytes 294944 | tf_op jit(solution)/shard_map/ppermute | solution.py:593
  402.7 1.4 collective-permute-done.47
  404.2 1.5 copy-done.14
  405.7 1.7 collective-permute-start.50
  408.5 11.4 %assemble.2 = (f32[768,3072]{1,0:T(8,128)}, f32[4,768,768]{2,1,0:T(8,128)}) custom-call(s32[3]{0:T(128)} %pad_add_fusion.ids_ref, bf16[4,2,48,3072]{3,2,1,0:T(8,128)(2,1)} %copy-done.1, bf16[4,2,48,3072]{3,2,1,0:T(8,128)(2,1)} %copy-done.4, bf16[4,2,48,3072]{3,2,1,0:T(8,128)(2,1)} %copy-done.13, bf16[4,2,48,3072]{3,2,1,0:T(8,128)(2,1)} %copy-done.14), custom_call_target="tpu_custom_call" | custom-call | flops 2000000000 | bytes 1024 | tf_op jit(solution)/shard_map/assemble/pallas_call | solution.py:498
  420.3 1.4 pad_maximum_fusion.4.refs_0_
  422.4 1.6 add_convert_fusion.4
  430.0 6.9 %assemble.3 = (f32[768,2304]{1,0:T(8,128)}, f32[768,768]{1,0:T(8,128)}) custom-call(s32[3]{0:T(128)} %pad_add_fusion.ids_ref, bf16[4,48,3072]{2,1,0:T(8,128)(2,1)} %copy-done.16, bf16[4,48,3072]{2,1,0:T(8,128)(2,1)} %copy-done.17, bf16[4,48,3072]{2,1,0:T(8,128)(2,1)} %copy-done.44, bf16[4,48,3072]{2,1,0:T(8,128)(2,1)} %copy-done.45), custom_call_target="tpu_custom_call" | custom-call | flops 2000000000 | bytes 1024 | tf_op jit(solution)/shard_map/assemble/pallas_call | solution.py:498
  (217 shorter events, 49.3 us)
Async XLA Ops:
  2.7 19.0 %copy-start.20 = (bf16[608,768]{1,0:T(8,128)(2,1)}, bf16[608,768]{1,0:T(8,128)(2,1)S(1)}, u32[]{:S(2)}) copy-start(bf16[608,768]{1,0:T(8,128)(2,1)S(1)} %fusion.1.refs_1_) | copy-start | bytes 2801668
  2.7 23.1 %collective-permute-start.3 = (bf16[608,768]{1,0:T(8,128)(2,1)S(1)}, bf16[608,768]{1,0:T(8,128)(2,1)S(1)}, u32[]{:S(2)}, u32[]{:S(2)}) collective-permute-start(bf16[608,768]{1,0:T(8,128)(2,1)S(1)} %fusion.1.refs_1_), channel_id=1, source_target_pairs={{1,2},{2,1},{5,6},{6,5},{9,10},{10,9},{13,14},{14,13},{17,18},{18,... | collective-permute-start | bytes 2801672 | tf_op jit(solution)/shard_map/ppermute | solution.py:531
  3.4 27.5 %collective-permute-start.2 = (bf16[608,768]{1,0:T(8,128)(2,1)S(1)}, bf16[608,768]{1,0:T(8,128)(2,1)}, u32[]{:S(2)}, u32[]{:S(2)}) collective-permute-start(bf16[608,768]{1,0:T(8,128)(2,1)S(1)} %fusion.1.refs_1_), channel_id=1, source_target_pairs={{0,1},{1,0},{2,3},{3,2},{4,5},{5,4},{6,7},{7,6},{8,9},{9,8},{10,11... | collective-permute-start | bytes 2801672 | tf_op jit(solution)/shard_map/ppermute | solution.py:593
  10.1 14.3 %copy-start.35 = (bf16[768,4]{0,1:T(4,128)(2,1)S(1)}, bf16[768,4]{0,1:T(4,128)(2,1)}, u32[]{:S(2)}) copy-start(bf16[768,4]{0,1:T(4,128)(2,1)} %param.30) | copy-start | bytes 18436
  21.7 34.2 %collective-permute-start.1 = (bf16[591,768]{1,0:T(8,128)(2,1)}, bf16[591,768]{1,0:T(8,128)(2,1)S(1)}, u32[]{:S(2)}, u32[]{:S(2)}) collective-permute-start(bf16[591,768]{1,0:T(8,128)(2,1)} %get-tuple-element.121.refs_0_), channel_id=1, source_target_pairs={{1,2},{2,1},{5,6},{6,5},{9,10},{10,9},{13,14},{14,13},{17,18},{18,... | collective-permute-start | bytes 2723336 | tf_op jit(solution)/shard_map/ppermute | solution.py:531
  22.6 33.3 %collective-permute-start = (bf16[591,768]{1,0:T(8,128)(2,1)}, bf16[591,768]{1,0:T(8,128)(2,1)}, u32[]{:S(2)}, u32[]{:S(2)}) collective-permute-start(bf16[591,768]{1,0:T(8,128)(2,1)} %get-tuple-element.121.refs_0_), channel_id=1, source_target_pairs={{0,1},{1,0},{2,3},{3,2},{4,5},{5,4},{6,7},{7,6},{8,9},{9,8},{10,11... | collective-permute-start | bytes 2723336 | tf_op jit(solution)/shard_map/ppermute | solution.py:593
  55.9 37.1 %collective-permute-start.4 = (bf16[591,768]{1,0:T(8,128)(2,1)S(1)}, bf16[591,768]{1,0:T(8,128)(2,1)S(1)}, u32[]{:S(2)}, u32[]{:S(2)}) collective-permute-start(bf16[591,768]{1,0:T(8,128)(2,1)S(1)} %collective-permute-done.1), channel_id=1, source_target_pairs={{1,0},{2,3},{5,4},{6,7},{9,8},{10,11},{13,12},{14,15},{17,16},{18,... | collective-permute-start | bytes 2723336 | tf_op jit(solution)/shard_map/ppermute | solution.py:536
  57.2 34.5 %copy-start.19 = (bf16[608,768]{1,0:T(8,128)(2,1)S(1)}, bf16[608,768]{1,0:T(8,128)(2,1)}, u32[]{:S(2)}) copy-start(bf16[608,768]{1,0:T(8,128)(2,1)} %copy-done.18) | copy-start | bytes 2801668
  57.2 57.3 %collective-permute-start.5 = (bf16[591,768]{1,0:T(8,128)(2,1)}, bf16[591,768]{1,0:T(8,128)(2,1)}, u32[]{:S(2)}, u32[]{:S(2)}) collective-permute-start(bf16[591,768]{1,0:T(8,128)(2,1)} %collective-permute-done.refs_0_.refs_1_), channel_id=1, source_target_pairs={{1,2},{2,1},{5,6},{6,5},{9,10},{10,9},{13,14},{14,13},{17,18},{18,... | collective-permute-start | bytes 2723336 | tf_op jit(solution)/shard_map/ppermute | solution.py:534
  83.9 35.3 %collective-permute-start.9 = (bf16[591,768]{1,0:T(8,128)(2,1)}, bf16[591,768]{1,0:T(8,128)(2,1)}, u32[]{:S(2)}, u32[]{:S(2)}) collective-permute-start(bf16[591,768]{1,0:T(8,128)(2,1)} %get-tuple-element.132), channel_id=1, source_target_pairs={{0,1},{3,2},{4,5},{7,6},{8,9},{11,10},{12,13},{15,14},{16,17},{19,... | collective-permute-start | bytes 2723336 | tf_op jit(solution)/shard_map/ppermute | solution.py:554
  90.3 35.7 %collective-permute-start.10 = (bf16[591,768]{1,0:T(8,128)(2,1)}, bf16[591,768]{1,0:T(8,128)(2,1)S(1)}, u32[]{:S(2)}, u32[]{:S(2)}) collective-permute-start(bf16[591,768]{1,0:T(8,128)(2,1)} %get-tuple-element.133), channel_id=1, source_target_pairs={{0,1},{3,2},{4,5},{7,6},{8,9},{11,10},{12,13},{15,14},{16,17},{19,... | collective-permute-start | bytes 2723336 | tf_op jit(solution)/shard_map/ppermute | solution.py:554
  91.7 26.4 %collective-permute-start.7 = (bf16[608,768]{1,0:T(8,128)(2,1)S(1)}, bf16[608,768]{1,0:T(8,128)(2,1)S(1)}, u32[]{:S(2)}, u32[]{:S(2)}) collective-permute-start(bf16[608,768]{1,0:T(8,128)(2,1)S(1)} %copy-done.19), channel_id=1, source_target_pairs={{1,0},{2,3},{5,4},{6,7},{9,8},{10,11},{13,12},{14,15},{17,16},{18,... | collective-permute-start | bytes 2801672 | tf_op jit(solution)/shard_map/ppermute | solution.py:536
  93.0 23.8 %collective-permute-start.8 = (bf16[608,768]{1,0:T(8,128)(2,1)}, bf16[608,768]{1,0:T(8,128)(2,1)S(1)}, u32[]{:S(2)}, u32[]{:S(2)}) collective-permute-start(bf16[608,768]{1,0:T(8,128)(2,1)} %collective-permute-done.2.refs_8_.refs_1_), channel_id=1, source_target_pairs={{1,2},{2,1},{5,6},{6,5},{9,10},{10,9},{13,14},{14,13},{17,18},{18,... | collective-permute-start | bytes 2801672 | tf_op jit(solution)/shard_map/ppermute | solution.py:534
  114.5 37.3 %collective-permute-start.6 = (bf16[591,768]{1,0:T(8,128)(2,1)}, bf16[591,768]{1,0:T(8,128)(2,1)}, u32[]{:S(2)}, u32[]{:S(2)}) collective-permute-start(bf16[591,768]{1,0:T(8,128)(2,1)} %collective-permute-done.5), channel_id=1, source_target_pairs={{1,0},{2,3},{5,4},{6,7},{9,8},{10,11},{13,12},{14,15},{17,16},{18,... | collective-permute-start | bytes 2723336 | tf_op jit(solution)/shard_map/ppermute | solution.py:537
  116.9 41.4 %collective-permute-start.11 = (bf16[608,768]{1,0:T(8,128)(2,1)S(1)}, bf16[608,768]{1,0:T(8,128)(2,1)S(1)}, u32[]{:S(2)}, u32[]{:S(2)}) collective-permute-start(bf16[608,768]{1,0:T(8,128)(2,1)S(1)} %collective-permute-done.8), channel_id=1, source_target_pairs={{1,0},{2,3},{5,4},{6,7},{9,8},{10,11},{13,12},{14,15},{17,16},{18,... | collective-permute-start | bytes 2801672 | tf_op jit(solution)/shard_map/ppermute | solution.py:537
  159.3 34.9 %collective-permute-start.15 = (bf16[591,768]{1,0:T(8,128)(2,1)}, bf16[591,768]{1,0:T(8,128)(2,1)S(1)}, u32[]{:S(2)}, u32[]{:S(2)}) collective-permute-start(bf16[591,768]{1,0:T(8,128)(2,1)} %get-tuple-element.144), channel_id=1, source_target_pairs={{1,2},{2,1},{5,6},{6,5},{9,10},{10,9},{13,14},{14,13},{17,18},{18,... | collective-permute-start | bytes 2723336 | tf_op jit(solution)/shard_map/ppermute | solution.py:560
  160.0 34.2 %collective-permute-start.14 = (bf16[591,768]{1,0:T(8,128)(2,1)}, bf16[591,768]{1,0:T(8,128)(2,1)S(1)}, u32[]{:S(2)}, u32[]{:S(2)}) collective-permute-start(bf16[591,768]{1,0:T(8,128)(2,1)} %get-tuple-element.144), channel_id=1, source_target_pairs={{0,1},{3,2},{4,5},{7,6},{8,9},{11,10},{12,13},{15,14},{16,17},{19,... | collective-permute-start | bytes 2723336 | tf_op jit(solution)/shard_map/ppermute | solution.py:559
  163.2 31.0 %collective-permute-start.13 = (bf16[591,768]{1,0:T(8,128)(2,1)}, bf16[591,768]{1,0:T(8,128)(2,1)S(1)}, u32[]{:S(2)}, u32[]{:S(2)}) collective-permute-start(bf16[591,768]{1,0:T(8,128)(2,1)} %get-tuple-element.142), channel_id=1, source_target_pairs={{1,2},{2,1},{5,6},{6,5},{9,10},{10,9},{13,14},{14,13},{17,18},{18,... | collective-permute-start | bytes 2723336 | tf_op jit(solution)/shard_map/ppermute | solution.py:560
  163.9 34.2 %collective-permute-start.12 = (bf16[591,768]{1,0:T(8,128)(2,1)}, bf16[591,768]{1,0:T(8,128)(2,1)}, u32[]{:S(2)}, u32[]{:S(2)}) collective-permute-start(bf16[591,768]{1,0:T(8,128)(2,1)} %get-tuple-element.142), channel_id=1, source_target_pairs={{0,1},{3,2},{4,5},{7,6},{8,9},{11,10},{12,13},{15,14},{16,17},{19,... | collective-permute-start | bytes 2723336 | tf_op jit(solution)/shard_map/ppermute | solution.py:559
  212.1 22.6 %collective-permute-start.16 = (bf16[8,2,48,3072]{3,2,1,0:T(8,128)(2,1)}, bf16[8,2,48,3072]{3,2,1,0:T(8,128)(2,1)}, u32[]{:S(2)}, u32[]{:S(2)}) collective-permute-start(bf16[8,2,48,3072]{3,2,1,0:T(8,128)(2,1)} %final_grads.2.refs_10_), channel_id=1, source_target_pairs={{0,4},{4,0},{8,12},{12,8},{16,20},{20,16},{24,28},{28,24},{1,5},{5... | collective-permute-start | bytes 14155784 | tf_op jit(solution)/shard_map/ppermute | solution.py:593
  215.4 18.0 %copy-start.10 = (bf16[591,768]{1,0:T(8,128)(2,1)S(1)}, bf16[591,768]{1,0:T(8,128)(2,1)}, u32[]{:S(2)}) copy-start(bf16[591,768]{1,0:T(8,128)(2,1)} %copy-done.9) | copy-start | bytes 2723332
  215.4 18.0 %copy-start.28 = (bf16[591,768]{1,0:T(8,128)(2,1)S(1)}, bf16[591,768]{1,0:T(8,128)(2,1)}, u32[]{:S(2)}) copy-start(bf16[591,768]{1,0:T(8,128)(2,1)} %get-tuple-element.133) | copy-start | bytes 2723332
  215.4 30.7 %collective-permute-start.19 = (bf16[591,768]{1,0:T(8,128)(2,1)S(1)}, bf16[591,768]{1,0:T(8,128)(2,1)}, u32[]{:S(2)}, u32[]{:S(2)}) collective-permute-start(bf16[591,768]{1,0:T(8,128)(2,1)S(1)} %add_convert_fusion.8), channel_id=1, source_target_pairs={{0,3},{1,2},{2,1},{3,0},{4,7},{5,6},{6,5},{7,4},{8,11},{9,10},{10,... | collective-permute-start | bytes 2723336 | tf_op jit(solution)/shard_map/ppermute | solution.py:593
  217.9 41.5 %collective-permute-start.20 = (bf16[591,768]{1,0:T(8,128)(2,1)S(1)}, bf16[591,768]{1,0:T(8,128)(2,1)}, u32[]{:S(2)}, u32[]{:S(2)}) collective-permute-start(bf16[591,768]{1,0:T(8,128)(2,1)S(1)} %add_convert_fusion.7), channel_id=1, source_target_pairs={{1,0},{2,3},{5,4},{6,7},{9,8},{10,11},{13,12},{14,15},{17,16},{18,... | collective-permute-start | bytes 2723336 | tf_op jit(solution)/shard_map/ppermute | solution.py:569
  242.7 47.6 %collective-permute-start.17 = (bf16[2,2,48,3072]{3,2,1,0:T(8,128)(2,1)S(1)}, bf16[2,2,48,3072]{3,2,1,0:T(8,128)(2,1)}, u32[]{:S(2)}, u32[]{:S(2)}) collective-permute-start(bf16[2,2,48,3072]{3,2,1,0:T(8,128)(2,1)S(1)} %constant_dynamic-slice_fusion.10), channel_id=1, source_target_pairs={{0,8},{4,12},{8,0},{12,4},{16,24},{20,28},{24,16},{28,20},{1,9},{5... | collective-permute-start | bytes 3538952 | tf_op jit(solution)/shard_map/ppermute | solution.py:593
  244.8 47.4 %collective-permute-start.18 = (bf16[2,2,48,3072]{3,2,1,0:T(8,128)(2,1)S(1)}, bf16[2,2,48,3072]{3,2,1,0:T(8,128)(2,1)S(1)}, u32[]{:S(2)}, u32[]{:S(2)}) collective-permute-start(bf16[2,2,48,3072]{3,2,1,0:T(8,128)(2,1)S(1)} %constant_dynamic-slice_fusion.9), channel_id=1, source_target_pairs={{0,16},{4,20},{8,24},{12,28},{16,0},{20,4},{24,8},{28,12},{1,17},{... | collective-permute-start | bytes 3538952 | tf_op jit(solution)/shard_map/ppermute | solution.py:593
  259.4 30.9 %copy-start.6 = (bf16[4,2,48,3072]{3,2,1,0:T(8,128)(2,1)S(1)}, bf16[4,2,48,3072]{3,2,1,0:T(8,128)(2,1)}, u32[]{:S(2)}) copy-start(bf16[4,2,48,3072]{3,2,1,0:T(8,128)(2,1)} %copy-done.5) | copy-start | bytes 7077892
  293.0 22.4 %collective-permute-start.23 = (bf16[8,48,3072]{2,1,0:T(8,128)(2,1)S(1)}, bf16[8,48,3072]{2,1,0:T(8,128)(2,1)S(1)}, u32[]{:S(2)}, u32[]{:S(2)}) collective-permute-start(bf16[8,48,3072]{2,1,0:T(8,128)(2,1)S(1)} %copy-done.43), channel_id=1, source_target_pairs={{0,4},{4,0},{8,12},{12,8},{16,20},{20,16},{24,28},{28,24},{1,5},{5... | collective-permute-start | bytes 7077896 | tf_op jit(solution)/shard_map/ppermute | solution.py:593
  293.0 15.8 %collective-permute-start.22 = (bf16[1,2,48,3072]{3,2,1,0:T(8,128)(2,1)S(1)}, bf16[1,2,48,3072]{3,2,1,0:T(8,128)(2,1)S(1)}, u32[]{:S(2)}, u32[]{:S(2)}) collective-permute-start(bf16[1,2,48,3072]{3,2,1,0:T(8,128)(2,1)S(1)} %constant_dynamic-slice_fusion.7), channel_id=1, source_target_pairs={{0,8},{4,12},{8,0},{12,4},{16,24},{20,28},{24,16},{28,20},{1,9},{5... | collective-permute-start | bytes 1769480 | tf_op jit(solution)/shard_map/ppermute | solution.py:593
  295.0 61.3 %collective-permute-start.33 = (bf16[591,768]{1,0:T(8,128)(2,1)S(1)}, bf16[591,768]{1,0:T(8,128)(2,1)S(1)}, u32[]{:S(2)}, u32[]{:S(2)}) collective-permute-start(bf16[591,768]{1,0:T(8,128)(2,1)S(1)} %add_convert_fusion.6), channel_id=1, source_target_pairs={{0,3},{1,2},{2,1},{3,0},{4,7},{5,6},{6,5},{7,4},{8,11},{9,10},{10,... | collective-permute-start | bytes 2723336 | tf_op jit(solution)/shard_map/ppermute | solution.py:593
  297.2 59.1 %collective-permute-start.34 = (bf16[591,768]{1,0:T(8,128)(2,1)S(1)}, bf16[591,768]{1,0:T(8,128)(2,1)S(1)}, u32[]{:S(2)}, u32[]{:S(2)}) collective-permute-start(bf16[591,768]{1,0:T(8,128)(2,1)S(1)} %copy-done.31), channel_id=1, source_target_pairs={{1,0},{2,3},{5,4},{6,7},{9,8},{10,11},{13,12},{14,15},{17,16},{18,... | collective-permute-start | bytes 2723336 | tf_op jit(solution)/shard_map/ppermute | solution.py:569
  298.5 1.3 collective-permute-start.24
  299.8 15.4 %collective-permute-start.21 = (bf16[1,2,48,3072]{3,2,1,0:T(8,128)(2,1)S(1)}, bf16[1,2,48,3072]{3,2,1,0:T(8,128)(2,1)S(1)}, u32[]{:S(2)}, u32[]{:S(2)}) collective-permute-start(bf16[1,2,48,3072]{3,2,1,0:T(8,128)(2,1)S(1)} %constant_dynamic-slice_fusion.8), channel_id=1, source_target_pairs={{0,16},{4,20},{8,24},{12,28},{16,0},{20,4},{24,8},{28,12},{1,17},{... | collective-permute-start | bytes 1769480 | tf_op jit(solution)/shard_map/ppermute | solution.py:593
  301.4 14.0 %copy-start.12 = (bf16[8,48,3072]{2,1,0:T(8,128)(2,1)S(1)}, bf16[8,48,3072]{2,1,0:T(8,128)(2,1)}, u32[]{:S(2)}) copy-start(bf16[8,48,3072]{2,1,0:T(8,128)(2,1)} %get-tuple-element.166) | copy-start | bytes 7077892
  316.5 5.1 %collective-permute-start.29 = (f32[24,768]{1,0:T(8,128)S(1)}, f32[24,768]{1,0:T(8,128)S(1)}, u32[]{:S(2)}, u32[]{:S(2)}) collective-permute-start(f32[24,768]{1,0:T(8,128)S(1)} %add.232), channel_id=1, source_target_pairs={{0,8},{4,12},{8,0},{12,4},{16,24},{20,28},{24,16},{28,20},{1,9},{5... | collective-permute-start | bytes 221192 | tf_op jit(solution)/shard_map/ppermute | solution.py:593
  317.3 16.3 %collective-permute-start.25 = (bf16[1,2,48,3072]{3,2,1,0:T(8,128)(2,1)S(1)}, bf16[1,2,48,3072]{3,2,1,0:T(8,128)(2,1)S(1)}, u32[]{:S(2)}, u32[]{:S(2)}) collective-permute-start(bf16[1,2,48,3072]{3,2,1,0:T(8,128)(2,1)S(1)} %add_convert_fusion.12), channel_id=1, source_target_pairs={{0,16},{4,20},{8,24},{12,28},{16,0},{20,4},{24,8},{28,12},{1,17},{... | collective-permute-start | bytes 1769480 | tf_op jit(solution)/shard_map/ppermute | solution.py:593
  318.9 16.1 %collective-permute-start.27 = (bf16[2,48,3072]{2,1,0:T(8,128)(2,1)S(1)}, bf16[2,48,3072]{2,1,0:T(8,128)(2,1)S(1)}, u32[]{:S(2)}, u32[]{:S(2)}) collective-permute-start(bf16[2,48,3072]{2,1,0:T(8,128)(2,1)S(1)} %constant_dynamic-slice_fusion.6), channel_id=1, source_target_pairs={{0,8},{4,12},{8,0},{12,4},{16,24},{20,28},{24,16},{28,20},{1,9},{5... | collective-permute-start | bytes 1769480 | tf_op jit(solution)/shard_map/ppermute | solution.py:593
  321.6 22.6 %collective-permute-start.28 = (bf16[2,48,3072]{2,1,0:T(8,128)(2,1)S(1)}, bf16[2,48,3072]{2,1,0:T(8,128)(2,1)S(1)}, u32[]{:S(2)}, u32[]{:S(2)}) collective-permute-start(bf16[2,48,3072]{2,1,0:T(8,128)(2,1)S(1)} %constant_dynamic-slice_fusion.5), channel_id=1, source_target_pairs={{0,16},{4,20},{8,24},{12,28},{16,0},{20,4},{24,8},{28,12},{1,17},{... | collective-permute-start | bytes 1769480 | tf_op jit(solution)/shard_map/ppermute | solution.py:593
  333.6 12.7 %collective-permute-start.26 = (bf16[1,2,48,3072]{3,2,1,0:T(8,128)(2,1)S(1)}, bf16[1,2,48,3072]{3,2,1,0:T(8,128)(2,1)S(1)}, u32[]{:S(2)}, u32[]{:S(2)}) collective-permute-start(bf16[1,2,48,3072]{3,2,1,0:T(8,128)(2,1)S(1)} %add_convert_fusion.11), channel_id=1, source_target_pairs={{0,8},{4,12},{8,0},{12,4},{16,24},{20,28},{24,16},{28,20},{1,9},{5... | collective-permute-start | bytes 1769480 | tf_op jit(solution)/shard_map/ppermute | solution.py:593
  347.4 5.2 %collective-permute-start.32 = (f32[24,768]{1,0:T(8,128)S(1)}, f32[24,768]{1,0:T(8,128)S(1)}, u32[]{:S(2)}, u32[]{:S(2)}) collective-permute-start(f32[24,768]{1,0:T(8,128)S(1)} %add.235), channel_id=1, source_target_pairs={{0,16},{4,20},{8,24},{12,28},{16,0},{20,4},{24,8},{28,12},{1,17},{... | collective-permute-start | bytes 221192 | tf_op jit(solution)/shard_map/ppermute | solution.py:593
  348.1 6.8 %collective-permute-start.31 = (bf16[1,48,3072]{2,1,0:T(8,128)(2,1)S(1)}, bf16[1,48,3072]{2,1,0:T(8,128)(2,1)S(1)}, u32[]{:S(2)}, u32[]{:S(2)}) collective-permute-start(bf16[1,48,3072]{2,1,0:T(8,128)(2,1)S(1)} %constant_dynamic-slice_fusion.3), channel_id=1, source_target_pairs={{0,8},{4,12},{8,0},{12,4},{16,24},{20,28},{24,16},{28,20},{1,9},{5... | collective-permute-start | bytes 884744 | tf_op jit(solution)/shard_map/ppermute | solution.py:593
  349.4 6.8 %collective-permute-start.30 = (bf16[1,48,3072]{2,1,0:T(8,128)(2,1)S(1)}, bf16[1,48,3072]{2,1,0:T(8,128)(2,1)S(1)}, u32[]{:S(2)}, u32[]{:S(2)}) collective-permute-start(bf16[1,48,3072]{2,1,0:T(8,128)(2,1)S(1)} %constant_dynamic-slice_fusion.4), channel_id=1, source_target_pairs={{0,16},{4,20},{8,24},{12,28},{16,0},{20,4},{24,8},{28,12},{1,17},{... | collective-permute-start | bytes 884744 | tf_op jit(solution)/shard_map/ppermute | solution.py:593
  352.6 29.3 %copy-start.32 = (f32[24,768]{1,0:T(8,128)}, f32[24,768]{1,0:T(8,128)S(1)}, u32[]{:S(2)}) copy-start(f32[24,768]{1,0:T(8,128)S(1)} %add.238) | copy-start | bytes 221188
  357.6 7.6 %collective-permute-start.35 = (bf16[24,3072]{1,0:T(8,128)(2,1)S(1)}, bf16[24,3072]{1,0:T(8,128)(2,1)S(1)}, u32[]{:S(2)}, u32[]{:S(2)}) collective-permute-start(bf16[24,3072]{1,0:T(8,128)(2,1)S(1)} %get-tuple-element.225), channel_id=1, source_target_pairs={{0,1},{1,2},{2,3},{3,0},{4,5},{5,6},{6,7},{7,4},{8,9},{9,10},{10,1... | collective-permute-start | bytes 442376 | tf_op jit(solution)/shard_map/ppermute | solution.py:515
  360.3 7.1 %collective-permute-start.37 = (bf16[24,3072]{1,0:T(8,128)(2,1)S(1)}, bf16[24,3072]{1,0:T(8,128)(2,1)S(1)}, u32[]{:S(2)}, u32[]{:S(2)}) collective-permute-start(bf16[24,3072]{1,0:T(8,128)(2,1)S(1)} %get-tuple-element.226), channel_id=1, source_target_pairs={{0,3},{1,0},{2,1},{3,2},{4,7},{5,4},{6,5},{7,6},{8,11},{9,8},{10,9... | collective-permute-start | bytes 442376 | tf_op jit(solution)/shard_map/ppermute | solution.py:515
  361.4 10.3 %collective-permute-start.36 = (bf16[24,3072]{1,0:T(8,128)(2,1)S(1)}, bf16[24,3072]{1,0:T(8,128)(2,1)S(1)}, u32[]{:S(2)}, u32[]{:S(2)}) collective-permute-start(bf16[24,3072]{1,0:T(8,128)(2,1)S(1)} %get-tuple-element.227), channel_id=1, source_target_pairs={{0,2},{1,3},{2,0},{3,1},{4,6},{5,7},{6,4},{7,5},{8,10},{9,11},{10,... | collective-permute-start | bytes 442376 | tf_op jit(solution)/shard_map/ppermute | solution.py:515
  362.6 27.9 %collective-permute-start.44 = (bf16[2,2,48,3072]{3,2,1,0:T(8,128)(2,1)S(1)}, bf16[2,2,48,3072]{3,2,1,0:T(8,128)(2,1)S(1)}, u32[]{:S(2)}, u32[]{:S(2)}) collective-permute-start(bf16[2,2,48,3072]{3,2,1,0:T(8,128)(2,1)S(1)} %pad_maximum_fusion.2), channel_id=1, source_target_pairs={{0,8},{4,12},{8,0},{12,4},{16,24},{20,28},{24,16},{28,20},{1,9},{5... | collective-permute-start | bytes 3538952 | tf_op jit(solution)/shard_map/ppermute | solution.py:593
  363.2 27.5 %collective-permute-start.45 = (bf16[2,2,48,3072]{3,2,1,0:T(8,128)(2,1)}, bf16[2,2,48,3072]{3,2,1,0:T(8,128)(2,1)S(1)}, u32[]{:S(2)}, u32[]{:S(2)}) collective-permute-start(bf16[2,2,48,3072]{3,2,1,0:T(8,128)(2,1)} %pad_maximum_fusion.3), channel_id=1, source_target_pairs={{0,16},{4,20},{8,24},{12,28},{16,0},{20,4},{24,8},{28,12},{1,17},{... | collective-permute-start | bytes 3538952 | tf_op jit(solution)/shard_map/ppermute | solution.py:593
  371.9 5.6 %collective-permute-start.42 = (f32[16,768]{1,0:T(8,128)S(1)}, f32[16,768]{1,0:T(8,128)S(1)}, u32[]{:S(2)}, u32[]{:S(2)}) collective-permute-start(f32[16,768]{1,0:T(8,128)S(1)} %slice.84), channel_id=1, source_target_pairs={{0,2},{1,3},{2,0},{3,1},{4,6},{5,7},{6,4},{7,5},{8,10},{9,11},{10,... | collective-permute-start | bytes 147464 | tf_op jit(solution)/shard_map/ppermute | solution.py:515
  371.9 9.1 %collective-permute-start.43 = (f32[16,768]{1,0:T(8,128)S(1)}, f32[16,768]{1,0:T(8,128)S(1)}, u32[]{:S(2)}, u32[]{:S(2)}) collective-permute-start(f32[16,768]{1,0:T(8,128)S(1)} %slice.84), channel_id=1, source_target_pairs={{0,3},{1,0},{2,1},{3,2},{4,7},{5,4},{6,5},{7,6},{8,11},{9,8},{10,9... | collective-permute-start | bytes 147464 | tf_op jit(solution)/shard_map/ppermute | solution.py:515
  373.8 7.2 %collective-permute-start.41 = (f32[16,768]{1,0:T(8,128)S(1)}, f32[16,768]{1,0:T(8,128)S(1)}, u32[]{:S(2)}, u32[]{:S(2)}) collective-permute-start(f32[16,768]{1,0:T(8,128)S(1)} %slice.84), channel_id=1, source_target_pairs={{0,1},{1,2},{2,3},{3,0},{4,5},{5,6},{6,7},{7,4},{8,9},{9,10},{10,1... | collective-permute-start | bytes 147464 | tf_op jit(solution)/shard_map/ppermute | solution.py:515
  377.4 13.0 %collective-permute-start.40 = (bf16[24,3072]{1,0:T(8,128)(2,1)S(1)}, bf16[24,3072]{1,0:T(8,128)(2,1)S(1)}, u32[]{:S(2)}, u32[]{:S(2)}) collective-permute-start(bf16[24,3072]{1,0:T(8,128)(2,1)S(1)} %add_convert_fusion.15), channel_id=1, source_target_pairs={{0,3},{1,0},{2,1},{3,2},{4,7},{5,4},{6,5},{7,6},{8,11},{9,8},{10,9... | collective-permute-start | bytes 442376 | tf_op jit(solution)/shard_map/ppermute | solution.py:515
  381.0 9.4 %collective-permute-start.39 = (bf16[24,3072]{1,0:T(8,128)(2,1)S(1)}, bf16[24,3072]{1,0:T(8,128)(2,1)S(1)}, u32[]{:S(2)}, u32[]{:S(2)}) collective-permute-start(bf16[24,3072]{1,0:T(8,128)(2,1)S(1)} %add_convert_fusion.15), channel_id=1, source_target_pairs={{0,2},{1,3},{2,0},{3,1},{4,6},{5,7},{6,4},{7,5},{8,10},{9,11},{10,... | collective-permute-start | bytes 442376 | tf_op jit(solution)/shard_map/ppermute | solution.py:515
  381.0 7.4 %collective-permute-start.38 = (bf16[24,3072]{1,0:T(8,128)(2,1)S(1)}, bf16[24,3072]{1,0:T(8,128)(2,1)S(1)}, u32[]{:S(2)}, u32[]{:S(2)}) collective-permute-start(bf16[24,3072]{1,0:T(8,128)(2,1)S(1)} %add_convert_fusion.15), channel_id=1, source_target_pairs={{0,1},{1,2},{2,3},{3,0},{4,5},{5,6},{6,7},{7,4},{8,9},{9,10},{10,1... | collective-permute-start | bytes 442376 | tf_op jit(solution)/shard_map/ppermute | solution.py:515
  393.1 11.1 %copy-start.4 = (bf16[4,2,48,3072]{3,2,1,0:T(8,128)(2,1)}, bf16[4,2,48,3072]{3,2,1,0:T(8,128)(2,1)S(1)}, u32[]{:S(2)}) copy-start(bf16[4,2,48,3072]{3,2,1,0:T(8,128)(2,1)S(1)} %pad_maximum_fusion.1.refs_1_) | copy-start | bytes 7077892
  393.1 11.1 %collective-permute-start.48 = (bf16[4,2,48,3072]{3,2,1,0:T(8,128)(2,1)S(1)}, bf16[4,2,48,3072]{3,2,1,0:T(8,128)(2,1)S(1)}, u32[]{:S(2)}, u32[]{:S(2)}) collective-permute-start(bf16[4,2,48,3072]{3,2,1,0:T(8,128)(2,1)S(1)} %pad_maximum_fusion.refs_0_), channel_id=1, source_target_pairs={{0,4},{4,0},{8,12},{12,8},{16,20},{20,16},{24,28},{28,24},{1,5},{5... | collective-permute-start | bytes 7077896 | tf_op jit(solution)/shard_map/ppermute | solution.py:593
  393.2 11.0 %collective-permute-start.49 = (bf16[4,2,48,3072]{3,2,1,0:T(8,128)(2,1)S(1)}, bf16[4,2,48,3072]{3,2,1,0:T(8,128)(2,1)S(1)}, u32[]{:S(2)}, u32[]{:S(2)}) collective-permute-start(bf16[4,2,48,3072]{3,2,1,0:T(8,128)(2,1)S(1)} %pad_maximum_fusion.1.refs_1_), channel_id=1, source_target_pairs={{0,4},{4,0},{8,12},{12,8},{16,20},{20,16},{24,28},{28,24},{1,5},{5... | collective-permute-start | bytes 7077896 | tf_op jit(solution)/shard_map/ppermute | solution.py:593
  393.7 9.0 %collective-permute-start.46 = (bf16[1,48,3072]{2,1,0:T(8,128)(2,1)S(1)}, bf16[1,48,3072]{2,1,0:T(8,128)(2,1)S(1)}, u32[]{:S(2)}, u32[]{:S(2)}) collective-permute-start(bf16[1,48,3072]{2,1,0:T(8,128)(2,1)S(1)} %get-tuple-element.194), channel_id=1, source_target_pairs={{0,16},{4,20},{8,24},{12,28},{16,0},{20,4},{24,8},{28,12},{1,17},{... | collective-permute-start | bytes 884744 | tf_op jit(solution)/shard_map/ppermute | solution.py:593
  393.9 10.2 %collective-permute-start.47 = (bf16[1,48,3072]{2,1,0:T(8,128)(2,1)S(1)}, bf16[1,48,3072]{2,1,0:T(8,128)(2,1)S(1)}, u32[]{:S(2)}, u32[]{:S(2)}) collective-permute-start(bf16[1,48,3072]{2,1,0:T(8,128)(2,1)S(1)} %get-tuple-element.195), channel_id=1, source_target_pairs={{0,8},{4,12},{8,0},{12,4},{16,24},{20,28},{24,16},{28,20},{1,9},{5... | collective-permute-start | bytes 884744 | tf_op jit(solution)/shard_map/ppermute | solution.py:593
  405.7 14.6 %collective-permute-start.50 = (bf16[2,48,3072]{2,1,0:T(8,128)(2,1)S(1)}, bf16[2,48,3072]{2,1,0:T(8,128)(2,1)}, u32[]{:S(2)}, u32[]{:S(2)}) collective-permute-start(bf16[2,48,3072]{2,1,0:T(8,128)(2,1)S(1)} %pad_maximum_fusion.7), channel_id=1, source_target_pairs={{0,8},{4,12},{8,0},{12,4},{16,24},{20,28},{24,16},{28,20},{1,9},{5... | collective-permute-start | bytes 1769480 | tf_op jit(solution)/shard_map/ppermute | solution.py:593
  407.5 14.2 %collective-permute-start.51 = (bf16[2,48,3072]{2,1,0:T(8,128)(2,1)S(1)}, bf16[2,48,3072]{2,1,0:T(8,128)(2,1)S(1)}, u32[]{:S(2)}, u32[]{:S(2)}) collective-permute-start(bf16[2,48,3072]{2,1,0:T(8,128)(2,1)S(1)} %pad_maximum_fusion.8), channel_id=1, source_target_pairs={{0,16},{4,20},{8,24},{12,28},{16,0},{20,4},{24,8},{28,12},{1,17},{... | collective-permute-start | bytes 1769480 | tf_op jit(solution)/shard_map/ppermute | solution.py:593
  408.5 13.9 %copy-start.27 = (bf16[591,768]{1,0:T(8,128)(2,1)S(1)}, bf16[591,768]{1,0:T(8,128)(2,1)}, u32[]{:S(2)}) copy-start(bf16[591,768]{1,0:T(8,128)(2,1)} %copy-done.26) | copy-start | bytes 2723332
  421.8 6.1 %collective-permute-start.52 = (bf16[4,48,3072]{2,1,0:T(8,128)(2,1)S(1)}, bf16[4,48,3072]{2,1,0:T(8,128)(2,1)S(1)}, u32[]{:S(2)}, u32[]{:S(2)}) collective-permute-start(bf16[4,48,3072]{2,1,0:T(8,128)(2,1)S(1)} %pad_maximum_fusion.4.refs_0_), channel_id=1, source_target_pairs={{0,4},{4,0},{8,12},{12,8},{16,20},{20,16},{24,28},{28,24},{1,5},{5... | collective-permute-start | bytes 3538952 | tf_op jit(solution)/shard_map/ppermute | solution.py:593
  421.9 6.0 %collective-permute-start.53 = (bf16[4,48,3072]{2,1,0:T(8,128)(2,1)S(1)}, bf16[4,48,3072]{2,1,0:T(8,128)(2,1)S(1)}, u32[]{:S(2)}, u32[]{:S(2)}) collective-permute-start(bf16[4,48,3072]{2,1,0:T(8,128)(2,1)S(1)} %pad_maximum_fusion.5.refs_1_), channel_id=1, source_target_pairs={{0,4},{4,0},{8,12},{12,8},{16,20},{20,16},{24,28},{28,24},{1,5},{5... | collective-permute-start | bytes 3538952 | tf_op jit(solution)/shard_map/ppermute | solution.py:593
  (36 other events, 137.5 us)

commit v4 on v3

--- a/solution.py
+++ b/solution.py
@@ -16,10 +16,14 @@
 LANES = 128
 PAIR = LANES // HEAD_DIM
 SEQ_PAD = 208
-FF_TILE = 512
+FF_TILE = 768
 ROUTE_ROWS = 16
 VMEM_BYTES = 58 * 2**20
 COST_FLOPS = 4e8
+OWN_COST = 24
+NEAR_COST = 24
+OTHER_COST = 1
+PARTIAL_COST = 1
 FINAL_COST = 4
 BACK_COST = 28
 TAIL_SCALE = 0.305
@@ -389,7 +393,7 @@
     )(core, up, inputs, hidden, qkv, ctx, vecs, w_qkv, w_out, *gmixes, *smalls, *after)
 
 
-def expert_block(me, rows, up, router, router_t, w_in, b_in, w_out, b_out, after=()):
+def expert_block(me, rows, up, router, router_t, w_in, b_in, w_out, b_out, after=(), micros=1):
     toks, width = rows.shape
     experts = router.shape[1]
     hidden = w_in.shape[1]
@@ -438,7 +442,7 @@
             ],
         ),
         compiler_params=params(),
-        cost_estimate=cost(24),
+        cost_estimate=cost(micros),
         name="expert_block",
     )(me, rows, up, router, router_t, w_in, b_in, w_out, b_out, *after)
 
@@ -457,7 +461,7 @@
         in_specs=[fixed] * count + [tile] * (2 * count) + [fixed] * count,
         out_specs=(total,) * 2,
         compiler_params=params(),
-        cost_estimate=cost(12 * count),
+        cost_estimate=cost(PARTIAL_COST),
         name="partial_grads",
     )(*rows, *gpres, *activs, *geouts)
 
@@ -524,18 +528,22 @@
     return (place == 0) | (place == lax.axis_size(axis) - 1)
 
 
-def gather_blocks(values, axis, hold=None):
-    if lax.axis_size(axis) != 4:
-        return ring_gather(values, axis), ()
-    near = swap(values, axis, 1)
-    inner = lax.ppermute(values, axis, INNER_SWAP)
-    if hold is not None:
-        near, inner = hold(near, inner)
-    far = lax.ppermute(near, axis, INNER_SWAP)
-    end = at_end(axis)
-    second = jnp.where(end, lax.ppermute(inner, axis, OUTWARD), far)
-    third = jnp.where(end, lax.ppermute(far, axis, OUTWARD), inner)
-    return [values, near, second, third], (near, inner)
+class LineGather:
+    def __init__(self, values, axis):
+        self.axis, self.own = axis, values
+        self.near = swap(values, axis, 1)
+        self.inner = lax.ppermute(values, axis, INNER_SWAP)
+
+    def pass_on(self, *before):
+        self.near, self.inner, *_ = together(self.near, self.inner, *before)
+        self.far = lax.ppermute(self.near, self.axis, INNER_SWAP)
+        self.outer = lax.ppermute(self.inner, self.axis, OUTWARD)
+
+    def finish(self, *before):
+        self.far, *_ = together(self.far, *before)
+        last = lax.ppermute(self.far, self.axis, OUTWARD)
+        end = at_end(self.axis)
+        return jnp.where(end, self.outer, self.far), jnp.where(end, last, self.inner)
 
 
 INWARD = [(0, 1), (3, 2)]
@@ -736,20 +744,33 @@
     named = named.at[tail - toks : tail - toks + routes.shape[1], :toks].set(routes.T.astype(BF16))
 
     pieces = lax.axis_size("rep")
-    ups, first_ups = gather_blocks(jnp.concatenate([cotangent, named], axis=0), "exp")
+    up_rows = jnp.concatenate([cotangent, named], axis=0)
+    line = lax.axis_size("exp") == 4
+    up_line = LineGather(up_rows, "exp") if line else None
     qkv, ctx, hidden, mixed = attend(inputs, vecs, w_qkv, w_out)
+    mixed_line = LineGather(mixed, "exp") if line else None
+
     router_t = router.T.astype(F32)
     w_in, w_mid = experts_in[0], experts_out[0]
-    run_block = lambda rows, up, after: expert_block(
-        me, rows, up, router, router_t, w_in, experts_in_bias, w_mid, experts_out_bias, after
+    run_block = lambda rows, up, after, micros: expert_block(
+        me, rows, up, router, router_t, w_in, experts_in_bias, w_mid, experts_out_bias, after, micros
     )
-    blocks, sums = [run_block(mixed, ups[0], first_ups)], None
-    mixes, _ = gather_blocks(mixed, "exp", lambda *got: lax.optimization_barrier((*got, blocks[0][0]))[:2])
-    last = len(mixes) - 1
+    if line:
+        up_line.pass_on()
+        blocks = [run_block(mixed, up_rows, (up_line.near, up_line.inner), OWN_COST)]
+        mixed_line.pass_on(blocks[0][0])
+        mixes, ups = [mixed, mixed_line.near], [up_rows, up_line.near]
+    else:
+        mixes, ups = ring_gather(mixed, "exp"), ring_gather(up_rows, "exp")
+        blocks = [run_block(mixed, up_rows, (), OWN_COST)]
+    last = lax.axis_size("exp") - 1
     backs, parts = Returns(blocks[0][1], "exp"), Returns(blocks[0][0], "exp")
     sums, early = None, ()
     for k in range(1, last + 1):
-        blocks.append(run_block(mixes[k], ups[k], early))
+        blocks.append(run_block(mixes[k], ups[k], early, NEAR_COST if k == 1 else OTHER_COST))
+        if k == 1 and last == 3:
+            ups += up_line.finish(blocks[1][0])
+            mixes += mixed_line.finish(blocks[1][0])
         hold = (mixes[last], ups[last]) if k == last - 1 else ()
         backs.add(k, blocks[k][1], *hold)
         if k < last:
@@ -757,9 +778,10 @@
         if k == last - 2:
             listed = lambda which: [mixes[j] if which is None else blocks[j][which] for j in range(k + 1)]
             sums = partial_grads(listed(None), listed(3), listed(2), listed(4))
-            early = (sums[0], *backs.sent, *parts.sent)
+            early = (sums[0],)
+            near_sent = (*backs.sent, *parts.sent)
         elif k == last - 1:
-            early, middle_sent = (), tuple(backs.sent + parts.sent)
+            early, middle_sent = near_sent, tuple(backs.sent + parts.sent)
     backs.send_outward(blocks[last][1])
     _, _, activs, gpres, geouts, grouters, gin_bias, gout_bias = zip(*blocks)
     final = lambda half, after: final_grads(

time: 444 us -> 441 us (level)
  Pallas kernels: 209 us -> 203 us
  waiting for transfers between devices: 102 us -> 96.2 us
  other arithmetic: 30.6 us -> 35.1 us
  starting transfers between devices: 78.7 us -> 83.2 us
    ppermute x2, starting transfers between devices: 7.74 us -> 16.6 us  [add(): self.sent = [lax.ppermute(values, self.axis, INWARD)]]
    ppermute x2, waiting for transfers between devices: 6.83 us -> 0.01 us  [add(): self.sent = [lax.ppermute(values, self.axis, INWARD)]]
    pallas_call x4, Pallas kernels: 99.6 us -> 93.3 us  [expert_block(): pl.pallas_call(functools.partial(expert_kernel, len(after)), out_shape=(j...]
    ppermute x29, starting transfers between devices: 36.9 us -> 32 us  [swap(): lax.ppermute(values, axis, [(i, i ^ bit) for i in range(lax.axis_size(axi...]
    unnamed x95 -> x93, local copies, waits for them, and re-layouts: 10.7 us -> 9.83 us
  transfers between devices with their start and end apart: 54 -> 54, of which waited for: 24 -> 22; matrix products, arithmetic and copies ran while one was open for 7% -> 8% of each run, Pallas kernels for 43% -> 42%
where the time goes in v4:
time: 441 us; the launch traced here: 435 us
  Pallas kernels  203 us (46%)
  waiting for transfers between devices  96.2 us (22%)
  starting transfers between devices  83.2 us (19%)
  other arithmetic  35.1 us (8%)
  local copies, waits for them, and re-layouts  14.9 us (3%)
    pallas_call x4, Pallas kernels, expert_block(): pl.pallas_call(functools.partial(expert_kernel, len(after)), out_shape=(j...  93.3 us
    ppermute x29, waiting for transfers between devices, swap(): lax.ppermute(values, axis, [(i, i ^ bit) for i in range(lax.axis_size(axi...  56.7 us
    ppermute x29, starting transfers between devices, swap(): lax.ppermute(values, axis, [(i, i ^ bit) for i in range(lax.axis_size(axi...  32 us
    pallas_call x1, Pallas kernels, attend_back(): pl.pallas_call(functools.partial(attend_back_kernel, len(smalls), len(gmi...  30.9 us
    pallas_call x2, Pallas kernels, final_grads(): pl.pallas_call(functools.partial(final_grads_kernel, count), out_shape=ja...  28.2 us
    pallas_call x1, Pallas kernels, partial_grads(): pl.pallas_call(functools.partial(partial_grads_kernel, count), out_shape=...  20.6 us
    ppermute x9, waiting for transfers between devices, shift(): lax.ppermute(values, axis, [(i, (i + by) % size) for i in range(size)])  18.8 us
    pallas_call x2, Pallas kernels, assemble(): pl.pallas_call(functools.partial(assemble_kernel, write), out_shape=tuple...  18.1 us
  transfers between devices with their start and end apart: 54, of which 22 were waited for; matrix products, arithmetic and copies ran while one was open for 8% of the time, Pallas kernels for 42%

profile of v4, /device:TPU:0, one launch (start us, length us, event | category | flops | bytes accessed | tf_op | source)
XLA Modules:
  0.0 434.6 jit_solution(2511105444364186064)
XLA Ops:
  3.4 5.9 %collective-permute-start.2 = (bf16[608,768]{1,0:T(8,128)(2,1)S(1)}, bf16[608,768]{1,0:T(8,128)(2,1)}, u32[]{:S(2)}, u32[]{:S(2)}) collective-permute-start(bf16[608,768]{1,0:T(8,128)(2,1)S(1)} %fusion.1.refs_1_), channel_id=1, source_target_pairs={{0,1},{1,0},{2,3},{3,2},{4,5},{5,4},{6,7},{7,6},{8,9},{9,8},{10,11... | collective-permute-start | bytes 2801672 | tf_op jit(solution)/shard_map/ppermute | solution.py:601
  10.1 11.6 %attend.1 = (bf16[591,2304]{1,0:T(8,128)(2,1)}, bf16[591,768]{1,0:T(8,128)(2,1)}, f32[591,768]{1,0:T(8,128)}, bf16[591,768]{1,0:T(8,128)(2,1)}) custom-call(bf16[591,768]{1,0:T(8,128)(2,1)} %x_ref.3, f32[8,768]{1,0:T(8,128)} %stack.45.vecs_ref, bf16[768,2304]{1,0:T(8,128)(2,1)} %wqkv_ref.3, bf16[768,768]{1,0:T(8,128)(2,1)} %wout_ref.3), custom_call_target="tpu_custom_call" | custom-call | flops 4800000000 | bytes 1024 | tf_op jit(solution)/shard_map/attend/pallas_call | solution.py:354
  21.7 1.7 collective-permute-start.1
  25.7 5.2 %collective-permute-done.2.refs_8_.refs_1_ = bf16[608,768]{1,0:T(8,128)(2,1)} collective-permute-done((bf16[608,768]{1,0:T(8,128)(2,1)S(1)}, bf16[608,768]{1,0:T(8,128)(2,1)}, u32[]{:S(2)}, u32[]{:S(2)}) %collective-permute-start.2) | collective-permute-done | bytes 933920 | tf_op jit(solution)/shard_map/ppermute | solution.py:601
  31.0 23.3 %expert_block.4 = (bf16[591,768]{1,0:T(8,128)(2,1)}, bf16[591,768]{1,0:T(8,128)(2,1)}, bf16[591,3072]{1,0:T(8,128)(2,1)}, bf16[591,3072]{1,0:T(8,128)(2,1)}, bf1...) custom-call(s32[1]{0:T(128)} %bitcast.1.me_ref, ...), custom_call_target="tpu_custom_call" | custom-call | flops 9600000000 | bytes 1024 | tf_op jit(solution)/shard_map/expert_block/pallas_call | solution.py:401
  54.3 1.6 collective-permute-start.5
  57.9 1.5 collective-permute-start.4
  59.4 23.3 %expert_block.5 = (bf16[591,768]{1,0:T(8,128)(2,1)}, bf16[591,768]{1,0:T(8,128)(2,1)}, bf16[591,3072]{1,0:T(8,128)(2,1)}, bf16[591,3072]{1,0:T(8,128)(2,1)}, bf1...) custom-call(s32[1]{0:T(128)} %bitcast.1.me_ref, bf16[591,768]{1,0:T(8,128)(2,1)} %copy-done.22, ...), custom_call_target="tpu_custom_call" | custom-call | flops 9600000000 | bytes 1024 | tf_op jit(solution)/shard_map/expert_block/pallas_call | solution.py:401
  84.1 9.4 %collective-permute-start.11 = (bf16[591,768]{1,0:T(8,128)(2,1)}, bf16[591,768]{1,0:T(8,128)(2,1)S(1)}, u32[]{:S(2)}, u32[]{:S(2)}) collective-permute-start(bf16[591,768]{1,0:T(8,128)(2,1)} %get-tuple-element.131), channel_id=1, source_target_pairs={{0,1},{3,2},{4,5},{7,6},{8,9},{11,10},{12,13},{15,14},{16,17},{19,... | collective-permute-start | bytes 2723336 | tf_op jit(solution)/shard_map/ppermute | solution.py:562
  94.8 20.6 %partial_grads.1 = (f32[768,3072]{1,0:T(8,128)}, f32[768,3072]{1,0:T(8,128)}) custom-call(bf16[591,768]{1,0:T(8,128)(2,1)} %get-tuple-element.125.refs_0_, bf16[591,768]{1,0:T(8,128)(2,1)} %copy-done.22, bf16[591,3072]{1,0:T(8,128)(2,1)} %get-tuple-element.134.refs_2_, bf16[591,3072]{1,0:T(8,128)(2,1)} %get-tuple-element.135.refs_3_, ...), custom_call_target="tpu_custom_call" | custom-call | flops 400000000 | bytes 1024 | tf_op jit(solution)/shard_map/partial_grads/pallas_call | solution.py:457
  115.4 7.2 %collective-permute-start.10 = (bf16[591,768]{1,0:T(8,128)(2,1)S(1)}, bf16[591,768]{1,0:T(8,128)(2,1)}, u32[]{:S(2)}, u32[]{:S(2)}) collective-permute-start(bf16[591,768]{1,0:T(8,128)(2,1)S(1)} %copy-done.27), channel_id=1, source_target_pairs={{0,1},{3,2},{4,5},{7,6},{8,9},{11,10},{12,13},{15,14},{16,17},{19,... | collective-permute-start | bytes 2723336 | tf_op jit(solution)/shard_map/ppermute | solution.py:562
  122.6 2.2 broadcast_select_fusion.3.refs_0_
  125.8 23.3 %expert_block.6 = (bf16[591,768]{1,0:T(8,128)(2,1)}, bf16[591,768]{1,0:T(8,128)(2,1)}, bf16[591,3072]{1,0:T(8,128)(2,1)}, bf16[591,3072]{1,0:T(8,128)(2,1)}, bf1...) custom-call(s32[1]{0:T(128)} %bitcast.1.me_ref, ...), custom_call_target="tpu_custom_call" | custom-call | flops 400000000 | bytes 1024 | tf_op jit(solution)/shard_map/expert_block/pallas_call | solution.py:401
  149.1 2.3 broadcast_select_fusion.2.refs_0_.refs_1_
  153.1 3.0 collective-permute-start.14
  156.2 1.6 collective-permute-start.13
  157.8 3.5 collective-permute-start.12
  162.3 23.4 %expert_block.7 = (bf16[591,768]{1,0:T(8,128)(2,1)}, bf16[591,768]{1,0:T(8,128)(2,1)}, bf16[591,3072]{1,0:T(8,128)(2,1)}, bf16[591,3072]{1,0:T(8,128)(2,1)}, bf1...) custom-call(s32[1]{0:T(128)} %bitcast.1.me_ref, ...), custom_call_target="tpu_custom_call" | custom-call | flops 400000000 | bytes 1024 | tf_op jit(solution)/shard_map/expert_block/pallas_call | solution.py:401
  185.8 6.4 %collective-permute-done.12.refs_10_ = bf16[591,768]{1,0:T(8,128)(2,1)} collective-permute-done((bf16[591,768]{1,0:T(8,128)(2,1)}, bf16[591,768]{1,0:T(8,128)(2,1)}, u32[]{:S(2)}, u32[]{:S(2)}) %collective-permute-start.12) | collective-permute-done | bytes 907808 | tf_op jit(solution)/shard_map/ppermute | solution.py:567
  192.2 14.0 %final_grads.2.refs_10_ = bf16[8,2,48,3072]{3,2,1,0:T(8,128)(2,1)} custom-call(s32[1]{0:T(128)S(6)} %sub.48.half_ref, bf16[591,768]{1,0:T(8,128)(2,1)} %broadcast_select_fusion.3.refs_0_, bf16[591,768]{1,0:T(8,128)(2,1)} %broadcast_select_fusion.2.refs_0_.refs_1_, bf16[591,3072]{1,0:T(8,128)(2,1)} %get-tuple-element.141.refs_2_, ...), custom_call_target="tpu_custom_call" | custom-call | flops 1600000000 | bytes 1024 | tf_op jit(solution)/shard_map/final_grads/pallas_call | solution.py:475
  206.4 2.4 add_convert_fusion.7
  208.8 2.4 add_convert_fusion.8
  212.4 1.5 collective-permute-start.20
  213.9 14.2 %final_grads.3 = bf16[8,2,48,3072]{3,2,1,0:T(8,128)(2,1)} custom-call(s32[1]{0:T(128)} %bitcast.half_ref.core_ref, bf16[591,768]{1,0:T(8,128)(2,1)} %broadcast_select_fusion.3.refs_0_, bf16[591,768]{1,0:T(8,128)(2,1)} %broadcast_select_fusion.2.refs_0_.refs_1_, bf16[591,3072]{1,0:T(8,128)(2,1)} %get-tuple-element.141.refs_2_, ...), custom_call_target="tpu_custom_call" | custom-call | flops 1600000000 | bytes 1024 | tf_op jit(solution)/shard_map/final_grads/pallas_call | solution.py:475
  229.3 5.8 %add_convert_fusion.refs_16_ = bf16[8,2,48,3072]{3,2,1,0:T(8,128)(2,1)S(1)} fusion(bf16[8,2,48,3072]{3,2,1,0:T(8,128)(2,1)} %collective-permute-done.16, bf16[8,2,48,3072]{3,2,1,0:T(8,128)(2,1)} %final_grads.3), kind=kLoop, calls=%fused_computation | loop fusion | flops 9437184 | bytes 14155776 | tf_op jit(solution)/shard_map/convert_element_type | solution.py:616
  235.4 1.8 copy-done
  237.4 1.6 collective-permute-start.17
  239.5 1.5 collective-permute-start.18
  241.0 14.2 %collective-permute-done.20.refs_3_ = bf16[591,768]{1,0:T(8,128)(2,1)} collective-permute-done((bf16[591,768]{1,0:T(8,128)(2,1)}, bf16[591,768]{1,0:T(8,128)(2,1)}, u32[]{:S(2)}, u32[]{:S(2)}) %collective-permute-start.20) | collective-permute-done | bytes 907808 | tf_op jit(solution)/shard_map/ppermute | solution.py:577
  255.3 30.9 %attend_back.1 = (bf16[591,768]{1,0:T(8,128)(2,1)}, bf16[8,48,3072]{2,1,0:T(8,128)(2,1)}, bf16[8,48,3072]{2,1,0:T(8,128)(2,1)}, f32[24,768]{1,0:T(8,128)}) custom-call(s32[1]{0:T(128)} %bitcast.half_ref.core_ref, bf16[591,768]{1,0:T(8,128)(2,1)} %up_ref.1, bf16[591,768]{1,0:T(8,128)(2,1)} %x_ref.3, f32[591,768]{1,0:T(8,128)} %get-tuple-element.124.hidden_ref, ...), custom_call_target="tpu_custom_call" | custom-call | flops 11200000000 | bytes 1024 | tf_op jit(solution)/shard_map/attend_back/pallas_call | solution.py:375
  286.2 1.8 add_convert_fusion.3
  289.0 1.6 collective-permute-start.22
  294.7 1.5 collective-permute-start.21
  296.2 8.5 %collective-permute-done.22 = bf16[1,2,48,3072]{3,2,1,0:T(8,128)(2,1)S(1)} collective-permute-done((bf16[1,2,48,3072]{3,2,1,0:T(8,128)(2,1)S(1)}, bf16[1,2,48,3072]{3,2,1,0:T(8,128)(2,1)S(1)}, u32[]{:S(2)}, u32[]{:S(2)}) %collective-permute-start.22) | collective-permute-done | bytes 589856 | tf_op jit(solution)/shard_map/ppermute | solution.py:601
  304.9 5.2 %collective-permute-done.21 = bf16[1,2,48,3072]{3,2,1,0:T(8,128)(2,1)S(1)} collective-permute-done((bf16[1,2,48,3072]{3,2,1,0:T(8,128)(2,1)S(1)}, bf16[1,2,48,3072]{3,2,1,0:T(8,128)(2,1)S(1)}, u32[]{:S(2)}, u32[]{:S(2)}) %collective-permute-start.21) | collective-permute-done | bytes 589856 | tf_op jit(solution)/shard_map/ppermute | solution.py:601
  312.1 1.5 collective-permute-start.25
  313.7 1.4 collective-permute-start.27
  315.1 1.4 collective-permute-done.29
  316.5 1.7 collective-permute-start.28
  318.2 10.2 %collective-permute-done.25 = bf16[1,2,48,3072]{3,2,1,0:T(8,128)(2,1)S(1)} collective-permute-done((bf16[1,2,48,3072]{3,2,1,0:T(8,128)(2,1)S(1)}, bf16[1,2,48,3072]{3,2,1,0:T(8,128)(2,1)S(1)}, u32[]{:S(2)}, u32[]{:S(2)}) %collective-permute-start.25) | collective-permute-done | bytes 589856 | tf_op jit(solution)/shard_map/ppermute | solution.py:601
  328.4 1.4 collective-permute-start.26
  330.0 9.0 %collective-permute-done.28 = bf16[2,48,3072]{2,1,0:T(8,128)(2,1)S(1)} collective-permute-done((bf16[2,48,3072]{2,1,0:T(8,128)(2,1)S(1)}, bf16[2,48,3072]{2,1,0:T(8,128)(2,1)S(1)}, u32[]{:S(2)}, u32[]{:S(2)}) %collective-permute-start.28) | collective-permute-done | bytes 589856 | tf_op jit(solution)/shard_map/ppermute | solution.py:601
  339.2 1.9 collective-permute-done.26
  345.1 2.3 collective-permute-done.32
  347.4 2.2 collective-permute-done.31
  352.1 3.5 collective-permute-start.35
  355.9 2.9 collective-permute-start.36
  359.5 1.4 collective-permute-start.45
  360.9 1.5 collective-permute-done.37
  362.4 4.3 collective-permute-done.36
  367.2 2.6 collective-permute-start.43
  370.4 2.0 collective-permute-done.42
  372.4 2.3 collective-permute-start.40
  374.8 1.6 collective-permute-done.41
  377.4 6.3 %collective-permute-done.38 = bf16[24,3072]{1,0:T(8,128)(2,1)S(1)} collective-permute-done((bf16[24,3072]{1,0:T(8,128)(2,1)S(1)}, bf16[24,3072]{1,0:T(8,128)(2,1)S(1)}, u32[]{:S(2)}, u32[]{:S(2)}) %collective-permute-start.38) | collective-permute-done | bytes 147488 | tf_op jit(solution)/shard_map/ppermute | solution.py:519
  383.6 3.1 collective-permute-done.39
  387.1 2.3 pad_maximum_fusion.1.refs_1_
  391.4 7.7 %collective-permute-done.46 = bf16[1,48,3072]{2,1,0:T(8,128)(2,1)S(1)} collective-permute-done((bf16[1,48,3072]{2,1,0:T(8,128)(2,1)S(1)}, bf16[1,48,3072]{2,1,0:T(8,128)(2,1)S(1)}, u32[]{:S(2)}, u32[]{:S(2)}) %collective-permute-start.46) | collective-permute-done | bytes 294944 | tf_op jit(solution)/shard_map/ppermute | solution.py:601
  399.2 1.4 copy-done.14
  400.6 1.4 copy-done.15
  404.9 11.3 %assemble.2 = (f32[768,3072]{1,0:T(8,128)}, f32[4,768,768]{2,1,0:T(8,128)}) custom-call(s32[3]{0:T(128)} %pad_add_fusion.ids_ref, bf16[4,2,48,3072]{3,2,1,0:T(8,128)(2,1)} %copy-done.1, bf16[4,2,48,3072]{3,2,1,0:T(8,128)(2,1)} %copy-done.4, bf16[4,2,48,3072]{3,2,1,0:T(8,128)(2,1)} %copy-done.14, bf16[4,2,48,3072]{3,2,1,0:T(8,128)(2,1)} %copy-done.15), custom_call_target="tpu_custom_call" | custom-call | flops 2000000000 | bytes 1024 | tf_op jit(solution)/shard_map/assemble/pallas_call | solution.py:502
  416.9 2.0 pad_maximum_fusion.5.refs_1_
  419.5 2.7 add_convert_fusion.4
  427.2 6.9 %assemble.3 = (f32[768,2304]{1,0:T(8,128)}, f32[768,768]{1,0:T(8,128)}) custom-call(s32[3]{0:T(128)} %pad_add_fusion.ids_ref, bf16[4,48,3072]{2,1,0:T(8,128)(2,1)} %copy-done.17, bf16[4,48,3072]{2,1,0:T(8,128)(2,1)} %copy-done.18, bf16[4,48,3072]{2,1,0:T(8,128)(2,1)} %copy-done.44, bf16[4,48,3072]{2,1,0:T(8,128)(2,1)} %collective-permute-done.53.refs_3_), custom_call_target="tpu_custom_call" | custom-call | flops 2000000000 | bytes 1024 | tf_op jit(solution)/shard_map/assemble/pallas_call | solution.py:502
  (215 shorter events, 46.1 us)
Async XLA Ops:
  2.7 19.0 %copy-start.21 = (bf16[608,768]{1,0:T(8,128)(2,1)}, bf16[608,768]{1,0:T(8,128)(2,1)S(1)}, u32[]{:S(2)}) copy-start(bf16[608,768]{1,0:T(8,128)(2,1)S(1)} %fusion.1.refs_1_) | copy-start | bytes 2801668
  2.7 23.0 %collective-permute-start.3 = (bf16[608,768]{1,0:T(8,128)(2,1)S(1)}, bf16[608,768]{1,0:T(8,128)(2,1)S(1)}, u32[]{:S(2)}, u32[]{:S(2)}) collective-permute-start(bf16[608,768]{1,0:T(8,128)(2,1)S(1)} %fusion.1.refs_1_), channel_id=1, source_target_pairs={{1,2},{2,1},{5,6},{6,5},{9,10},{10,9},{13,14},{14,13},{17,18},{18,... | collective-permute-start | bytes 2801672 | tf_op jit(solution)/shard_map/ppermute | solution.py:535
  3.4 27.5 %collective-permute-start.2 = (bf16[608,768]{1,0:T(8,128)(2,1)S(1)}, bf16[608,768]{1,0:T(8,128)(2,1)}, u32[]{:S(2)}, u32[]{:S(2)}) collective-permute-start(bf16[608,768]{1,0:T(8,128)(2,1)S(1)} %fusion.1.refs_1_), channel_id=1, source_target_pairs={{0,1},{1,0},{2,3},{3,2},{4,5},{5,4},{6,7},{7,6},{8,9},{9,8},{10,11... | collective-permute-start | bytes 2801672 | tf_op jit(solution)/shard_map/ppermute | solution.py:601
  10.1 14.2 %copy-start.35 = (bf16[768,4]{0,1:T(4,128)(2,1)S(1)}, bf16[768,4]{0,1:T(4,128)(2,1)}, u32[]{:S(2)}) copy-start(bf16[768,4]{0,1:T(4,128)(2,1)} %param.30) | copy-start | bytes 18436
  21.7 32.6 %collective-permute-start.1 = (bf16[591,768]{1,0:T(8,128)(2,1)}, bf16[591,768]{1,0:T(8,128)(2,1)}, u32[]{:S(2)}, u32[]{:S(2)}) collective-permute-start(bf16[591,768]{1,0:T(8,128)(2,1)} %get-tuple-element.125.refs_0_), channel_id=1, source_target_pairs={{1,2},{2,1},{5,6},{6,5},{9,10},{10,9},{13,14},{14,13},{17,18},{18,... | collective-permute-start | bytes 2723336 | tf_op jit(solution)/shard_map/ppermute | solution.py:535
  23.4 30.9 %collective-permute-start = (bf16[591,768]{1,0:T(8,128)(2,1)}, bf16[591,768]{1,0:T(8,128)(2,1)S(1)}, u32[]{:S(2)}, u32[]{:S(2)}) collective-permute-start(bf16[591,768]{1,0:T(8,128)(2,1)} %get-tuple-element.125.refs_0_), channel_id=1, source_target_pairs={{0,1},{1,0},{2,3},{3,2},{4,5},{5,4},{6,7},{7,6},{8,9},{9,8},{10,11... | collective-permute-start | bytes 2723336 | tf_op jit(solution)/shard_map/ppermute | solution.py:601
  54.3 28.4 %collective-permute-start.5 = (bf16[591,768]{1,0:T(8,128)(2,1)S(1)}, bf16[591,768]{1,0:T(8,128)(2,1)}, u32[]{:S(2)}, u32[]{:S(2)}) collective-permute-start(bf16[591,768]{1,0:T(8,128)(2,1)S(1)} %collective-permute-done.refs_0_.refs_1_), channel_id=1, source_target_pairs={{1,2},{2,1},{5,6},{6,5},{9,10},{10,9},{13,14},{14,13},{17,18},{18,... | collective-permute-start | bytes 2723336 | tf_op jit(solution)/shard_map/ppermute | solution.py:539
  55.9 37.6 %collective-permute-start.8 = (bf16[608,768]{1,0:T(8,128)(2,1)}, bf16[608,768]{1,0:T(8,128)(2,1)S(1)}, u32[]{:S(2)}, u32[]{:S(2)}) collective-permute-start(bf16[608,768]{1,0:T(8,128)(2,1)} %collective-permute-done.2.refs_8_.refs_1_), channel_id=1, source_target_pairs={{1,2},{2,1},{5,6},{6,5},{9,10},{10,9},{13,14},{14,13},{17,18},{18,... | collective-permute-start | bytes 2801672 | tf_op jit(solution)/shard_map/ppermute | solution.py:539
  56.6 68.1 %collective-permute-start.7 = (bf16[608,768]{1,0:T(8,128)(2,1)}, bf16[608,768]{1,0:T(8,128)(2,1)S(1)}, u32[]{:S(2)}, u32[]{:S(2)}) collective-permute-start(bf16[608,768]{1,0:T(8,128)(2,1)} %copy-done.19), channel_id=1, source_target_pairs={{1,0},{2,3},{5,4},{6,7},{9,8},{10,11},{13,12},{14,15},{17,16},{18,... | collective-permute-start | bytes 2801672 | tf_op jit(solution)/shard_map/ppermute | solution.py:540
  57.9 57.4 %collective-permute-start.4 = (bf16[591,768]{1,0:T(8,128)(2,1)}, bf16[591,768]{1,0:T(8,128)(2,1)}, u32[]{:S(2)}, u32[]{:S(2)}) collective-permute-start(bf16[591,768]{1,0:T(8,128)(2,1)} %collective-permute-done.1), channel_id=1, source_target_pairs={{1,0},{2,3},{5,4},{6,7},{9,8},{10,11},{13,12},{14,15},{17,16},{18,... | collective-permute-start | bytes 2723336 | tf_op jit(solution)/shard_map/ppermute | solution.py:540
  82.8 66.3 %collective-permute-start.6 = (bf16[591,768]{1,0:T(8,128)(2,1)}, bf16[591,768]{1,0:T(8,128)(2,1)}, u32[]{:S(2)}, u32[]{:S(2)}) collective-permute-start(bf16[591,768]{1,0:T(8,128)(2,1)} %collective-permute-done.5), channel_id=1, source_target_pairs={{1,0},{2,3},{5,4},{6,7},{9,8},{10,11},{13,12},{14,15},{17,16},{18,... | collective-permute-start | bytes 2723336 | tf_op jit(solution)/shard_map/ppermute | solution.py:544
  84.1 77.3 %collective-permute-start.11 = (bf16[591,768]{1,0:T(8,128)(2,1)}, bf16[591,768]{1,0:T(8,128)(2,1)S(1)}, u32[]{:S(2)}, u32[]{:S(2)}) collective-permute-start(bf16[591,768]{1,0:T(8,128)(2,1)} %get-tuple-element.131), channel_id=1, source_target_pairs={{0,1},{3,2},{4,5},{7,6},{8,9},{11,10},{12,13},{15,14},{16,17},{19,... | collective-permute-start | bytes 2723336 | tf_op jit(solution)/shard_map/ppermute | solution.py:562
  93.5 57.9 %collective-permute-start.9 = (bf16[608,768]{1,0:T(8,128)(2,1)S(1)}, bf16[608,768]{1,0:T(8,128)(2,1)S(1)}, u32[]{:S(2)}, u32[]{:S(2)}) collective-permute-start(bf16[608,768]{1,0:T(8,128)(2,1)S(1)} %collective-permute-done.8), channel_id=1, source_target_pairs={{1,0},{2,3},{5,4},{6,7},{9,8},{10,11},{13,12},{14,15},{17,16},{18,... | collective-permute-start | bytes 2801672 | tf_op jit(solution)/shard_map/ppermute | solution.py:544
  94.8 20.6 %copy-start.27 = (bf16[591,768]{1,0:T(8,128)(2,1)S(1)}, bf16[591,768]{1,0:T(8,128)(2,1)}, u32[]{:S(2)}) copy-start(bf16[591,768]{1,0:T(8,128)(2,1)} %get-tuple-element.142) | copy-start | bytes 2723332
  115.4 42.4 %collective-permute-start.10 = (bf16[591,768]{1,0:T(8,128)(2,1)S(1)}, bf16[591,768]{1,0:T(8,128)(2,1)}, u32[]{:S(2)}, u32[]{:S(2)}) collective-permute-start(bf16[591,768]{1,0:T(8,128)(2,1)S(1)} %copy-done.27), channel_id=1, source_target_pairs={{0,1},{3,2},{4,5},{7,6},{8,9},{11,10},{12,13},{15,14},{16,17},{19,... | collective-permute-start | bytes 2723336 | tf_op jit(solution)/shard_map/ppermute | solution.py:562
  152.4 33.3 %collective-permute-start.15 = (bf16[591,768]{1,0:T(8,128)(2,1)}, bf16[591,768]{1,0:T(8,128)(2,1)S(1)}, u32[]{:S(2)}, u32[]{:S(2)}) collective-permute-start(bf16[591,768]{1,0:T(8,128)(2,1)} %get-tuple-element.152), channel_id=1, source_target_pairs={{1,2},{2,1},{5,6},{6,5},{9,10},{10,9},{13,14},{14,13},{17,18},{18,... | collective-permute-start | bytes 2723336 | tf_op jit(solution)/shard_map/ppermute | solution.py:568
  153.1 32.6 %collective-permute-start.14 = (bf16[591,768]{1,0:T(8,128)(2,1)}, bf16[591,768]{1,0:T(8,128)(2,1)S(1)}, u32[]{:S(2)}, u32[]{:S(2)}) collective-permute-start(bf16[591,768]{1,0:T(8,128)(2,1)} %get-tuple-element.152), channel_id=1, source_target_pairs={{0,1},{3,2},{4,5},{7,6},{8,9},{11,10},{12,13},{15,14},{16,17},{19,... | collective-permute-start | bytes 2723336 | tf_op jit(solution)/shard_map/ppermute | solution.py:567
  156.2 29.6 %collective-permute-start.13 = (bf16[591,768]{1,0:T(8,128)(2,1)}, bf16[591,768]{1,0:T(8,128)(2,1)}, u32[]{:S(2)}, u32[]{:S(2)}) collective-permute-start(bf16[591,768]{1,0:T(8,128)(2,1)} %get-tuple-element.150), channel_id=1, source_target_pairs={{1,2},{2,1},{5,6},{6,5},{9,10},{10,9},{13,14},{14,13},{17,18},{18,... | collective-permute-start | bytes 2723336 | tf_op jit(solution)/shard_map/ppermute | solution.py:568
  157.8 34.4 %collective-permute-start.12 = (bf16[591,768]{1,0:T(8,128)(2,1)}, bf16[591,768]{1,0:T(8,128)(2,1)}, u32[]{:S(2)}, u32[]{:S(2)}) collective-permute-start(bf16[591,768]{1,0:T(8,128)(2,1)} %get-tuple-element.150), channel_id=1, source_target_pairs={{0,1},{3,2},{4,5},{7,6},{8,9},{11,10},{12,13},{15,14},{16,17},{19,... | collective-permute-start | bytes 2723336 | tf_op jit(solution)/shard_map/ppermute | solution.py:567
  192.2 14.2 %copy-start.28 = (bf16[591,768]{1,0:T(8,128)(2,1)S(1)}, bf16[591,768]{1,0:T(8,128)(2,1)}, u32[]{:S(2)}) copy-start(bf16[591,768]{1,0:T(8,128)(2,1)} %get-tuple-element.142) | copy-start | bytes 2723332
  206.2 23.1 %collective-permute-start.16 = (bf16[8,2,48,3072]{3,2,1,0:T(8,128)(2,1)}, bf16[8,2,48,3072]{3,2,1,0:T(8,128)(2,1)}, u32[]{:S(2)}, u32[]{:S(2)}) collective-permute-start(bf16[8,2,48,3072]{3,2,1,0:T(8,128)(2,1)} %final_grads.2.refs_10_), channel_id=1, source_target_pairs={{0,4},{4,0},{8,12},{12,8},{16,20},{20,16},{24,28},{28,24},{1,5},{5... | collective-permute-start | bytes 14155784 | tf_op jit(solution)/shard_map/ppermute | solution.py:601
  211.2 16.9 %copy-start.12 = (bf16[591,768]{1,0:T(8,128)(2,1)S(1)}, bf16[591,768]{1,0:T(8,128)(2,1)}, u32[]{:S(2)}) copy-start(bf16[591,768]{1,0:T(8,128)(2,1)} %copy-done.11) | copy-start | bytes 2723332
  211.2 16.9 %copy-start.26 = (bf16[591,768]{1,0:T(8,128)(2,1)S(1)}, bf16[591,768]{1,0:T(8,128)(2,1)}, u32[]{:S(2)}) copy-start(bf16[591,768]{1,0:T(8,128)(2,1)} %get-tuple-element.131) | copy-start | bytes 2723332
  211.2 29.8 %collective-permute-start.19 = (bf16[591,768]{1,0:T(8,128)(2,1)}, bf16[591,768]{1,0:T(8,128)(2,1)}, u32[]{:S(2)}, u32[]{:S(2)}) collective-permute-start(bf16[591,768]{1,0:T(8,128)(2,1)} %add_convert_fusion.8), channel_id=1, source_target_pairs={{0,3},{1,2},{2,1},{3,0},{4,7},{5,6},{6,5},{7,4},{8,11},{9,10},{10,... | collective-permute-start | bytes 2723336 | tf_op jit(solution)/shard_map/ppermute | solution.py:601
  212.4 42.9 %collective-permute-start.20 = (bf16[591,768]{1,0:T(8,128)(2,1)}, bf16[591,768]{1,0:T(8,128)(2,1)}, u32[]{:S(2)}, u32[]{:S(2)}) collective-permute-start(bf16[591,768]{1,0:T(8,128)(2,1)} %add_convert_fusion.7), channel_id=1, source_target_pairs={{1,0},{2,3},{5,4},{6,7},{9,8},{10,11},{13,12},{14,15},{17,16},{18,... | collective-permute-start | bytes 2723336 | tf_op jit(solution)/shard_map/ppermute | solution.py:577
  237.4 48.8 %collective-permute-start.17 = (bf16[2,2,48,3072]{3,2,1,0:T(8,128)(2,1)S(1)}, bf16[2,2,48,3072]{3,2,1,0:T(8,128)(2,1)}, u32[]{:S(2)}, u32[]{:S(2)}) collective-permute-start(bf16[2,2,48,3072]{3,2,1,0:T(8,128)(2,1)S(1)} %constant_dynamic-slice_fusion.10), channel_id=1, source_target_pairs={{0,8},{4,12},{8,0},{12,4},{16,24},{20,28},{24,16},{28,20},{1,9},{5... | collective-permute-start | bytes 3538952 | tf_op jit(solution)/shard_map/ppermute | solution.py:601
  239.5 48.6 %collective-permute-start.18 = (bf16[2,2,48,3072]{3,2,1,0:T(8,128)(2,1)S(1)}, bf16[2,2,48,3072]{3,2,1,0:T(8,128)(2,1)S(1)}, u32[]{:S(2)}, u32[]{:S(2)}) collective-permute-start(bf16[2,2,48,3072]{3,2,1,0:T(8,128)(2,1)S(1)} %constant_dynamic-slice_fusion.9), channel_id=1, source_target_pairs={{0,16},{4,20},{8,24},{12,28},{16,0},{20,4},{24,8},{28,12},{1,17},{... | collective-permute-start | bytes 3538952 | tf_op jit(solution)/shard_map/ppermute | solution.py:601
  255.3 30.9 %copy-start.6 = (bf16[4,2,48,3072]{3,2,1,0:T(8,128)(2,1)S(1)}, bf16[4,2,48,3072]{3,2,1,0:T(8,128)(2,1)}, u32[]{:S(2)}) copy-start(bf16[4,2,48,3072]{3,2,1,0:T(8,128)(2,1)} %copy-done.5) | copy-start | bytes 7077892
  288.9 21.4 %collective-permute-start.23 = (bf16[8,48,3072]{2,1,0:T(8,128)(2,1)S(1)}, bf16[8,48,3072]{2,1,0:T(8,128)(2,1)S(1)}, u32[]{:S(2)}, u32[]{:S(2)}) collective-permute-start(bf16[8,48,3072]{2,1,0:T(8,128)(2,1)S(1)} %copy-done.43), channel_id=1, source_target_pairs={{0,4},{4,0},{8,12},{12,8},{16,20},{20,16},{24,28},{28,24},{1,5},{5... | collective-permute-start | bytes 7077896 | tf_op jit(solution)/shard_map/ppermute | solution.py:601
  289.0 15.8 %collective-permute-start.22 = (bf16[1,2,48,3072]{3,2,1,0:T(8,128)(2,1)S(1)}, bf16[1,2,48,3072]{3,2,1,0:T(8,128)(2,1)S(1)}, u32[]{:S(2)}, u32[]{:S(2)}) collective-permute-start(bf16[1,2,48,3072]{3,2,1,0:T(8,128)(2,1)S(1)} %constant_dynamic-slice_fusion.7), channel_id=1, source_target_pairs={{0,8},{4,12},{8,0},{12,4},{16,24},{20,28},{24,16},{28,20},{1,9},{5... | collective-permute-start | bytes 1769480 | tf_op jit(solution)/shard_map/ppermute | solution.py:601
  290.8 60.3 %collective-permute-start.33 = (bf16[591,768]{1,0:T(8,128)(2,1)S(1)}, bf16[591,768]{1,0:T(8,128)(2,1)S(1)}, u32[]{:S(2)}, u32[]{:S(2)}) collective-permute-start(bf16[591,768]{1,0:T(8,128)(2,1)S(1)} %add_convert_fusion.6), channel_id=1, source_target_pairs={{0,3},{1,2},{2,1},{3,0},{4,7},{5,6},{6,5},{7,4},{8,11},{9,10},{10,... | collective-permute-start | bytes 2723336 | tf_op jit(solution)/shard_map/ppermute | solution.py:601
  292.1 59.1 %collective-permute-start.34 = (bf16[591,768]{1,0:T(8,128)(2,1)S(1)}, bf16[591,768]{1,0:T(8,128)(2,1)}, u32[]{:S(2)}, u32[]{:S(2)}) collective-permute-start(bf16[591,768]{1,0:T(8,128)(2,1)S(1)} %copy-done.31), channel_id=1, source_target_pairs={{1,0},{2,3},{5,4},{6,7},{9,8},{10,11},{13,12},{14,15},{17,16},{18,... | collective-permute-start | bytes 2723336 | tf_op jit(solution)/shard_map/ppermute | solution.py:577
  293.4 1.3 collective-permute-start.24
  294.7 15.4 %collective-permute-start.21 = (bf16[1,2,48,3072]{3,2,1,0:T(8,128)(2,1)S(1)}, bf16[1,2,48,3072]{3,2,1,0:T(8,128)(2,1)S(1)}, u32[]{:S(2)}, u32[]{:S(2)}) collective-permute-start(bf16[1,2,48,3072]{3,2,1,0:T(8,128)(2,1)S(1)} %constant_dynamic-slice_fusion.8), channel_id=1, source_target_pairs={{0,16},{4,20},{8,24},{12,28},{16,0},{20,4},{24,8},{28,12},{1,17},{... | collective-permute-start | bytes 1769480 | tf_op jit(solution)/shard_map/ppermute | solution.py:601
  296.2 14.0 %copy-start.13 = (bf16[8,48,3072]{2,1,0:T(8,128)(2,1)S(1)}, bf16[8,48,3072]{2,1,0:T(8,128)(2,1)}, u32[]{:S(2)}) copy-start(bf16[8,48,3072]{2,1,0:T(8,128)(2,1)} %get-tuple-element.174) | copy-start | bytes 7077892
  311.4 5.1 %collective-permute-start.29 = (f32[24,768]{1,0:T(8,128)S(1)}, f32[24,768]{1,0:T(8,128)S(1)}, u32[]{:S(2)}, u32[]{:S(2)}) collective-permute-start(f32[24,768]{1,0:T(8,128)S(1)} %add.232), channel_id=1, source_target_pairs={{0,8},{4,12},{8,0},{12,4},{16,24},{20,28},{24,16},{28,20},{1,9},{5... | collective-permute-start | bytes 221192 | tf_op jit(solution)/shard_map/ppermute | solution.py:601
  312.1 16.3 %collective-permute-start.25 = (bf16[1,2,48,3072]{3,2,1,0:T(8,128)(2,1)S(1)}, bf16[1,2,48,3072]{3,2,1,0:T(8,128)(2,1)S(1)}, u32[]{:S(2)}, u32[]{:S(2)}) collective-permute-start(bf16[1,2,48,3072]{3,2,1,0:T(8,128)(2,1)S(1)} %add_convert_fusion.12), channel_id=1, source_target_pairs={{0,16},{4,20},{8,24},{12,28},{16,0},{20,4},{24,8},{28,12},{1,17},{... | collective-permute-start | bytes 1769480 | tf_op jit(solution)/shard_map/ppermute | solution.py:601
  313.7 16.2 %collective-permute-start.27 = (bf16[2,48,3072]{2,1,0:T(8,128)(2,1)S(1)}, bf16[2,48,3072]{2,1,0:T(8,128)(2,1)S(1)}, u32[]{:S(2)}, u32[]{:S(2)}) collective-permute-start(bf16[2,48,3072]{2,1,0:T(8,128)(2,1)S(1)} %constant_dynamic-slice_fusion.6), channel_id=1, source_target_pairs={{0,8},{4,12},{8,0},{12,4},{16,24},{20,28},{24,16},{28,20},{1,9},{5... | collective-permute-start | bytes 1769480 | tf_op jit(solution)/shard_map/ppermute | solution.py:601
  316.5 22.5 %collective-permute-start.28 = (bf16[2,48,3072]{2,1,0:T(8,128)(2,1)S(1)}, bf16[2,48,3072]{2,1,0:T(8,128)(2,1)S(1)}, u32[]{:S(2)}, u32[]{:S(2)}) collective-permute-start(bf16[2,48,3072]{2,1,0:T(8,128)(2,1)S(1)} %constant_dynamic-slice_fusion.5), channel_id=1, source_target_pairs={{0,16},{4,20},{8,24},{12,28},{16,0},{20,4},{24,8},{28,12},{1,17},{... | collective-permute-start | bytes 1769480 | tf_op jit(solution)/shard_map/ppermute | solution.py:601
  328.4 12.7 %collective-permute-start.26 = (bf16[1,2,48,3072]{3,2,1,0:T(8,128)(2,1)S(1)}, bf16[1,2,48,3072]{3,2,1,0:T(8,128)(2,1)S(1)}, u32[]{:S(2)}, u32[]{:S(2)}) collective-permute-start(bf16[1,2,48,3072]{3,2,1,0:T(8,128)(2,1)S(1)} %add_convert_fusion.11), channel_id=1, source_target_pairs={{0,8},{4,12},{8,0},{12,4},{16,24},{20,28},{24,16},{28,20},{1,9},{5... | collective-permute-start | bytes 1769480 | tf_op jit(solution)/shard_map/ppermute | solution.py:601
  342.2 5.2 %collective-permute-start.32 = (f32[24,768]{1,0:T(8,128)S(1)}, f32[24,768]{1,0:T(8,128)S(1)}, u32[]{:S(2)}, u32[]{:S(2)}) collective-permute-start(f32[24,768]{1,0:T(8,128)S(1)} %add.235), channel_id=1, source_target_pairs={{0,16},{4,20},{8,24},{12,28},{16,0},{20,4},{24,8},{28,12},{1,17},{... | collective-permute-start | bytes 221192 | tf_op jit(solution)/shard_map/ppermute | solution.py:601
  342.9 6.8 %collective-permute-start.31 = (bf16[1,48,3072]{2,1,0:T(8,128)(2,1)S(1)}, bf16[1,48,3072]{2,1,0:T(8,128)(2,1)S(1)}, u32[]{:S(2)}, u32[]{:S(2)}) collective-permute-start(bf16[1,48,3072]{2,1,0:T(8,128)(2,1)S(1)} %constant_dynamic-slice_fusion.3), channel_id=1, source_target_pairs={{0,8},{4,12},{8,0},{12,4},{16,24},{20,28},{24,16},{28,20},{1,9},{5... | collective-permute-start | bytes 884744 | tf_op jit(solution)/shard_map/ppermute | solution.py:601
  344.3 6.8 %collective-permute-start.30 = (bf16[1,48,3072]{2,1,0:T(8,128)(2,1)S(1)}, bf16[1,48,3072]{2,1,0:T(8,128)(2,1)S(1)}, u32[]{:S(2)}, u32[]{:S(2)}) collective-permute-start(bf16[1,48,3072]{2,1,0:T(8,128)(2,1)S(1)} %constant_dynamic-slice_fusion.4), channel_id=1, source_target_pairs={{0,16},{4,20},{8,24},{12,28},{16,0},{20,4},{24,8},{28,12},{1,17},{... | collective-permute-start | bytes 884744 | tf_op jit(solution)/shard_map/ppermute | solution.py:601
  347.4 29.3 %copy-start.32 = (f32[24,768]{1,0:T(8,128)}, f32[24,768]{1,0:T(8,128)S(1)}, u32[]{:S(2)}) copy-start(f32[24,768]{1,0:T(8,128)S(1)} %add.238) | copy-start | bytes 221188
  351.1 19.3 %copy-start.24 = (bf16[591,768]{1,0:T(8,128)(2,1)}, bf16[591,768]{1,0:T(8,128)(2,1)S(1)}, u32[]{:S(2)}) copy-start(bf16[591,768]{1,0:T(8,128)(2,1)S(1)} %collective-permute-done.33) | copy-start | bytes 2723332
  352.1 8.8 %collective-permute-start.35 = (bf16[24,3072]{1,0:T(8,128)(2,1)}, bf16[24,3072]{1,0:T(8,128)(2,1)S(1)}, u32[]{:S(2)}, u32[]{:S(2)}) collective-permute-start(bf16[24,3072]{1,0:T(8,128)(2,1)} %get-tuple-element.233), channel_id=1, source_target_pairs={{0,1},{1,2},{2,3},{3,0},{4,5},{5,6},{6,7},{7,4},{8,9},{9,10},{10,1... | collective-permute-start | bytes 442376 | tf_op jit(solution)/shard_map/ppermute | solution.py:519
  355.6 6.8 %collective-permute-start.37 = (bf16[24,3072]{1,0:T(8,128)(2,1)S(1)}, bf16[24,3072]{1,0:T(8,128)(2,1)S(1)}, u32[]{:S(2)}, u32[]{:S(2)}) collective-permute-start(bf16[24,3072]{1,0:T(8,128)(2,1)S(1)} %get-tuple-element.234), channel_id=1, source_target_pairs={{0,3},{1,0},{2,1},{3,2},{4,7},{5,4},{6,5},{7,6},{8,11},{9,8},{10,9... | collective-permute-start | bytes 442376 | tf_op jit(solution)/shard_map/ppermute | solution.py:519
  355.9 10.8 %collective-permute-start.36 = (bf16[24,3072]{1,0:T(8,128)(2,1)S(1)}, bf16[24,3072]{1,0:T(8,128)(2,1)S(1)}, u32[]{:S(2)}, u32[]{:S(2)}) collective-permute-start(bf16[24,3072]{1,0:T(8,128)(2,1)S(1)} %get-tuple-element.235), channel_id=1, source_target_pairs={{0,2},{1,3},{2,0},{3,1},{4,6},{5,7},{6,4},{7,5},{8,10},{9,11},{10,... | collective-permute-start | bytes 442376 | tf_op jit(solution)/shard_map/ppermute | solution.py:519
  358.8 28.1 %collective-permute-start.44 = (bf16[2,2,48,3072]{3,2,1,0:T(8,128)(2,1)S(1)}, bf16[2,2,48,3072]{3,2,1,0:T(8,128)(2,1)S(1)}, u32[]{:S(2)}, u32[]{:S(2)}) collective-permute-start(bf16[2,2,48,3072]{3,2,1,0:T(8,128)(2,1)S(1)} %pad_maximum_fusion.2), channel_id=1, source_target_pairs={{0,8},{4,12},{8,0},{12,4},{16,24},{20,28},{24,16},{28,20},{1,9},{5... | collective-permute-start | bytes 3538952 | tf_op jit(solution)/shard_map/ppermute | solution.py:601
  359.5 27.6 %collective-permute-start.45 = (bf16[2,2,48,3072]{3,2,1,0:T(8,128)(2,1)}, bf16[2,2,48,3072]{3,2,1,0:T(8,128)(2,1)S(1)}, u32[]{:S(2)}, u32[]{:S(2)}) collective-permute-start(bf16[2,2,48,3072]{3,2,1,0:T(8,128)(2,1)} %pad_maximum_fusion.3), channel_id=1, source_target_pairs={{0,16},{4,20},{8,24},{12,28},{16,0},{20,4},{24,8},{28,12},{1,17},{... | collective-permute-start | bytes 3538952 | tf_op jit(solution)/shard_map/ppermute | solution.py:601
  366.7 5.7 %collective-permute-start.42 = (f32[16,768]{1,0:T(8,128)S(1)}, f32[16,768]{1,0:T(8,128)S(1)}, u32[]{:S(2)}, u32[]{:S(2)}) collective-permute-start(f32[16,768]{1,0:T(8,128)S(1)} %slice.84), channel_id=1, source_target_pairs={{0,2},{1,3},{2,0},{3,1},{4,6},{5,7},{6,4},{7,5},{8,10},{9,11},{10,... | collective-permute-start | bytes 147464 | tf_op jit(solution)/shard_map/ppermute | solution.py:519
  367.2 7.5 %collective-permute-start.43 = (f32[16,768]{1,0:T(8,128)S(1)}, f32[16,768]{1,0:T(8,128)S(1)}, u32[]{:S(2)}, u32[]{:S(2)}) collective-permute-start(f32[16,768]{1,0:T(8,128)S(1)} %slice.84), channel_id=1, source_target_pairs={{0,3},{1,0},{2,1},{3,2},{4,7},{5,4},{6,5},{7,6},{8,11},{9,8},{10,9... | collective-permute-start | bytes 147464 | tf_op jit(solution)/shard_map/ppermute | solution.py:519
  369.8 6.6 %collective-permute-start.41 = (f32[16,768]{1,0:T(8,128)S(1)}, f32[16,768]{1,0:T(8,128)S(1)}, u32[]{:S(2)}, u32[]{:S(2)}) collective-permute-start(f32[16,768]{1,0:T(8,128)S(1)} %slice.84), channel_id=1, source_target_pairs={{0,1},{1,2},{2,3},{3,0},{4,5},{5,6},{6,7},{7,4},{8,9},{9,10},{10,1... | collective-permute-start | bytes 147464 | tf_op jit(solution)/shard_map/ppermute | solution.py:519
  372.4 14.3 %collective-permute-start.40 = (bf16[24,3072]{1,0:T(8,128)(2,1)S(1)}, bf16[24,3072]{1,0:T(8,128)(2,1)S(1)}, u32[]{:S(2)}, u32[]{:S(2)}) collective-permute-start(bf16[24,3072]{1,0:T(8,128)(2,1)S(1)} %add_convert_fusion.15), channel_id=1, source_target_pairs={{0,3},{1,0},{2,1},{3,2},{4,7},{5,4},{6,5},{7,6},{8,11},{9,8},{10,9... | collective-permute-start | bytes 442376 | tf_op jit(solution)/shard_map/ppermute | solution.py:519
  374.8 12.0 %collective-permute-start.39 = (bf16[24,3072]{1,0:T(8,128)(2,1)S(1)}, bf16[24,3072]{1,0:T(8,128)(2,1)S(1)}, u32[]{:S(2)}, u32[]{:S(2)}) collective-permute-start(bf16[24,3072]{1,0:T(8,128)(2,1)S(1)} %add_convert_fusion.15), channel_id=1, source_target_pairs={{0,2},{1,3},{2,0},{3,1},{4,6},{5,7},{6,4},{7,5},{8,10},{9,11},{10,... | collective-permute-start | bytes 442376 | tf_op jit(solution)/shard_map/ppermute | solution.py:519
  376.4 7.2 %collective-permute-start.38 = (bf16[24,3072]{1,0:T(8,128)(2,1)S(1)}, bf16[24,3072]{1,0:T(8,128)(2,1)S(1)}, u32[]{:S(2)}, u32[]{:S(2)}) collective-permute-start(bf16[24,3072]{1,0:T(8,128)(2,1)S(1)} %add_convert_fusion.15), channel_id=1, source_target_pairs={{0,1},{1,2},{2,3},{3,0},{4,5},{5,6},{6,7},{7,4},{8,9},{9,10},{10,1... | collective-permute-start | bytes 442376 | tf_op jit(solution)/shard_map/ppermute | solution.py:519
  389.5 9.7 %collective-permute-start.48 = (bf16[4,2,48,3072]{3,2,1,0:T(8,128)(2,1)S(1)}, bf16[4,2,48,3072]{3,2,1,0:T(8,128)(2,1)S(1)}, u32[]{:S(2)}, u32[]{:S(2)}) collective-permute-start(bf16[4,2,48,3072]{3,2,1,0:T(8,128)(2,1)S(1)} %pad_maximum_fusion.refs_0_), channel_id=1, source_target_pairs={{0,4},{4,0},{8,12},{12,8},{16,20},{20,16},{24,28},{28,24},{1,5},{5... | collective-permute-start | bytes 7077896 | tf_op jit(solution)/shard_map/ppermute | solution.py:601
  389.5 9.7 %collective-permute-start.49 = (bf16[4,2,48,3072]{3,2,1,0:T(8,128)(2,1)S(1)}, bf16[4,2,48,3072]{3,2,1,0:T(8,128)(2,1)S(1)}, u32[]{:S(2)}, u32[]{:S(2)}) collective-permute-start(bf16[4,2,48,3072]{3,2,1,0:T(8,128)(2,1)S(1)} %pad_maximum_fusion.1.refs_1_), channel_id=1, source_target_pairs={{0,4},{4,0},{8,12},{12,8},{16,20},{20,16},{24,28},{28,24},{1,5},{5... | collective-permute-start | bytes 7077896 | tf_op jit(solution)/shard_map/ppermute | solution.py:601
  390.0 9.0 %collective-permute-start.46 = (bf16[1,48,3072]{2,1,0:T(8,128)(2,1)S(1)}, bf16[1,48,3072]{2,1,0:T(8,128)(2,1)S(1)}, u32[]{:S(2)}, u32[]{:S(2)}) collective-permute-start(bf16[1,48,3072]{2,1,0:T(8,128)(2,1)S(1)} %get-tuple-element.202), channel_id=1, source_target_pairs={{0,16},{4,20},{8,24},{12,28},{16,0},{20,4},{24,8},{28,12},{1,17},{... | collective-permute-start | bytes 884744 | tf_op jit(solution)/shard_map/ppermute | solution.py:601
  390.3 8.8 %collective-permute-start.47 = (bf16[1,48,3072]{2,1,0:T(8,128)(2,1)S(1)}, bf16[1,48,3072]{2,1,0:T(8,128)(2,1)S(1)}, u32[]{:S(2)}, u32[]{:S(2)}) collective-permute-start(bf16[1,48,3072]{2,1,0:T(8,128)(2,1)S(1)} %get-tuple-element.203), channel_id=1, source_target_pairs={{0,8},{4,12},{8,0},{12,4},{16,24},{20,28},{24,16},{28,20},{1,9},{5... | collective-permute-start | bytes 884744 | tf_op jit(solution)/shard_map/ppermute | solution.py:601
  402.0 14.5 %collective-permute-start.50 = (bf16[2,48,3072]{2,1,0:T(8,128)(2,1)S(1)}, bf16[2,48,3072]{2,1,0:T(8,128)(2,1)S(1)}, u32[]{:S(2)}, u32[]{:S(2)}) collective-permute-start(bf16[2,48,3072]{2,1,0:T(8,128)(2,1)S(1)} %pad_maximum_fusion.7), channel_id=1, source_target_pairs={{0,8},{4,12},{8,0},{12,4},{16,24},{20,28},{24,16},{28,20},{1,9},{5... | collective-permute-start | bytes 1769480 | tf_op jit(solution)/shard_map/ppermute | solution.py:601
  403.0 14.0 %collective-permute-start.51 = (bf16[2,48,3072]{2,1,0:T(8,128)(2,1)S(1)}, bf16[2,48,3072]{2,1,0:T(8,128)(2,1)}, u32[]{:S(2)}, u32[]{:S(2)}) collective-permute-start(bf16[2,48,3072]{2,1,0:T(8,128)(2,1)S(1)} %pad_maximum_fusion.8), channel_id=1, source_target_pairs={{0,16},{4,20},{8,24},{12,28},{16,0},{20,4},{24,8},{28,12},{1,17},{... | collective-permute-start | bytes 1769480 | tf_op jit(solution)/shard_map/ppermute | solution.py:601
  418.9 7.3 %collective-permute-start.52 = (bf16[4,48,3072]{2,1,0:T(8,128)(2,1)S(1)}, bf16[4,48,3072]{2,1,0:T(8,128)(2,1)S(1)}, u32[]{:S(2)}, u32[]{:S(2)}) collective-permute-start(bf16[4,48,3072]{2,1,0:T(8,128)(2,1)S(1)} %pad_maximum_fusion.4.refs_0_), channel_id=1, source_target_pairs={{0,4},{4,0},{8,12},{12,8},{16,20},{20,16},{24,28},{28,24},{1,5},{5... | collective-permute-start | bytes 3538952 | tf_op jit(solution)/shard_map/ppermute | solution.py:601
  419.0 7.2 %collective-permute-start.53 = (bf16[4,48,3072]{2,1,0:T(8,128)(2,1)S(1)}, bf16[4,48,3072]{2,1,0:T(8,128)(2,1)}, u32[]{:S(2)}, u32[]{:S(2)}) collective-permute-start(bf16[4,48,3072]{2,1,0:T(8,128)(2,1)S(1)} %pad_maximum_fusion.5.refs_1_), channel_id=1, source_target_pairs={{0,4},{4,0},{8,12},{12,8},{16,20},{20,16},{24,28},{28,24},{1,5},{5... | collective-permute-start | bytes 3538952 | tf_op jit(solution)/shard_map/ppermute | solution.py:601
  (35 other events, 157.5 us)

commit v5 on v4

--- a/solution.py
+++ b/solution.py
@@ -26,6 +26,7 @@
 PARTIAL_COST = 1
 FINAL_COST = 4
 BACK_COST = 28
+MARK_COST = 400
 TAIL_SCALE = 0.305
 TAIL_COEFS = (
     0.1216396663821839,
@@ -102,17 +103,33 @@
     return weights * (1.0 / jnp.sum(weights, axis=-1, keepdims=True))
 
 
+class Fetch:
+    def __init__(self, pairs, sems, first=0):
+        self.copies = [
+            pltpu.make_async_copy(source, target, sems.at[first + at]) for at, (source, target) in enumerate(pairs)
+        ]
+        for copy in self.copies:
+            copy.start()
+
+    def wait(self, *which):
+        for at in which:
+            self.copies[at].wait()
+
+
 def attend_kernel(
-    x_ref, vecs_ref, wqkv_ref, wout_ref,
-    qkv_ref, ctx_ref, hidden_ref, mixed_ref,
-    qkv_s, ctx_s,
+    x_hbm, vecs_ref, wqkv_hbm, wout_hbm,
+    qkv_hbm, ctx_ref, hidden_ref, mixed_ref,
+    qkv_s, ctx_s, x_ref, wqkv_ref, wout_ref, qkv_ref, sems,
 ):
+    fetch = Fetch(((x_hbm, x_ref), (wqkv_hbm, wqkv_ref), (wout_hbm, wout_ref)), sems)
+    fetch.wait(0)
     toks, width = x_ref.shape
     spare = qkv_s.shape[0] - toks
     x = x_ref[...].astype(F32)
     vec = lambda name: vecs_ref[VECS.index(name) : VECS.index(name) + 1, :]
     unit, _ = unit_norm(x)
     normed = (unit * vec("g1") + vec("b1")).astype(BF16)
+    fetch.wait(1)
     for part, bias in ((0, "qb"), (1, None), (2, "vb")):
         cols = pl.ds(part * width, width)
         joined = dot(normed, wqkv_ref[:, cols])
@@ -121,6 +138,7 @@
         joined = joined.astype(BF16)
         qkv_ref[:, cols] = joined
         qkv_s[0:toks, cols] = joined.astype(F32)
+    store = Fetch(((qkv_ref, qkv_hbm),), sems, 3)
     qkv_s[toks:, :] = jnp.zeros((spare, 3 * width), F32)
     masks = pair_masks(SEQ_PAD)
     for img in range(toks // SEQ):
@@ -133,10 +151,12 @@
             ctx_s[rows, at : at + LANES] = unstack_heads(dot(probs, value), masks)
     ctx = ctx_s[0:toks, :].astype(BF16)
     ctx_ref[...] = ctx
+    fetch.wait(2)
     hidden = x + dot(ctx, wout_ref[...]) + vec("ob")
     hidden_ref[...] = hidden
     unit2, _ = unit_norm(hidden)
     mixed_ref[...] = (unit2 * vec("g2") + vec("b2")).astype(BF16)
+    store.wait(0)
 
 
 def expert_kernel(
@@ -253,10 +273,17 @@
 
 
 def attend_back_kernel(
-    count, sums, core_ref, up_ref, x_ref, hidden_ref, qkv_ref, ctx_ref, vecs_ref, wqkv_ref, wout_ref, *refs,
+    count, sums, core_ref, vecs_ref, *refs,
 ):
-    *refs, ginput_ref, keep_ref, send_ref, small_ref, qkv_s, gctx_s, gjoin_s = refs
-    gmix_refs, refs = refs[:sums], refs[sums:]
+    loaded = sums + 7
+    *refs, sems = refs
+    refs, held = refs[:-loaded], refs[-loaded:]
+    *refs, ginput_ref, keep_hbm, send_hbm, small_ref, qkv_s, gctx_s, gjoin_s, keep_ref, send_ref = refs
+    fetch = Fetch(zip(refs[:loaded], held), sems)
+    refs = refs[loaded:]
+    gmix_refs = held[:sums]
+    hidden_ref, up_ref, wout_ref, ctx_ref, qkv_ref, x_ref, wqkv_ref = held[sums:]
+    fetch.wait(*range(sums + 2))
     toks, width = x_ref.shape
     spare = qkv_s.shape[0] - toks
     vec = lambda name: vecs_ref[VECS.index(name) : VECS.index(name) + 1, :]
@@ -281,10 +308,12 @@
     m2 = gmix * vec("g2")
     ghidden = up_ref[...].astype(F32) + scale2 * (m2 - row_mean(m2) - unit2 * row_mean(m2 * unit2))
     gatt = ghidden.astype(BF16)
+    fetch.wait(sums + 2, sums + 3)
     grad_ob = column_sum(gatt.astype(F32))
     put(dot_lt(ctx_ref[...], gatt), 3 * width)
     gctx_s[0:toks, :] = dot_rt(gatt, wout_ref[...]).astype(BF16).astype(F32)
     gctx_s[toks:, :] = jnp.zeros((spare, width), F32)
+    fetch.wait(sums + 4)
     qkv_s[0:toks, :] = qkv_ref[...].astype(F32)
     qkv_s[toks:, :] = jnp.zeros((spare, 3 * width), F32)
     masks = pair_masks(SEQ_PAD)
@@ -309,10 +338,12 @@
     gjoin = gjoin_s[0:toks, :].astype(BF16)
     grad_qb = column_sum(gjoin[:, :width].astype(F32))
     grad_vb = column_sum(gjoin[:, 2 * width :].astype(F32))
+    fetch.wait(sums + 5, sums + 6)
     x = x_ref[...].astype(F32)
     unit1, scale1 = unit_norm(x)
     normed = (unit1 * vec("g1") + vec("b1")).astype(BF16)
     put(dot_lt(normed, gjoin), 0)
+    store = Fetch(((keep_ref, keep_hbm), (send_ref, send_hbm)), sems, loaded)
     gnormed = dot_rt(gjoin, wqkv_ref[...])
     grad_g1 = column_sum(gnormed * unit1)
     grad_b1 = column_sum(gnormed)
@@ -330,6 +361,7 @@
         small_ref[at + tile : at + tile + 1, :] = in_sum[:, tile * width : (tile + 1) * width]
     at += in_sum.shape[1] // width
     small_ref[at : at + 1, :] = out_sum
+    store.wait(0, 1)
 
 
 def params(**more):
@@ -342,6 +374,10 @@
 
 def whole():
     return pl.BlockSpec(memory_space=pltpu.VMEM)
+
+
+def outside():
+    return pl.BlockSpec(memory_space=pl.ANY)
 
 
 def scalars():
@@ -359,9 +395,17 @@
             jax.ShapeDtypeStruct((toks, width), F32),
             jax.ShapeDtypeStruct((toks, width), BF16),
         ),
-        in_specs=[whole()] * 4,
-        out_specs=(whole(),) * 4,
-        scratch_shapes=[pltpu.VMEM((padded, 3 * width), F32), pltpu.VMEM((padded, width), F32)],
+        in_specs=[outside(), whole(), outside(), outside()],
+        out_specs=(outside(), whole(), whole(), whole()),
+        scratch_shapes=[
+            pltpu.VMEM((padded, 3 * width), F32),
+            pltpu.VMEM((padded, width), F32),
+            pltpu.VMEM((toks, width), BF16),
+            pltpu.VMEM((width, 3 * width), BF16),
+            pltpu.VMEM((width, width), BF16),
+            pltpu.VMEM((toks, 3 * width), BF16),
+            pltpu.SemaphoreType.DMA((4,)),
+        ],
         compiler_params=params(),
         cost_estimate=cost(12),
         name="attend",
@@ -371,6 +415,7 @@
 def attend_back(core, gmixes, up, inputs, hidden, qkv, ctx, vecs, w_qkv, w_out, smalls, small_rows, pieces, after):
     toks, width = inputs.shape
     padded = -(-(toks - SEQ + SEQ_PAD) // 16) * 16
+    loaded = (*gmixes, hidden, up, w_out, ctx, qkv, inputs, w_qkv)
     half = jax.ShapeDtypeStruct((pieces, width // (2 * pieces), 4 * width), BF16)
     return pl.pallas_call(
         functools.partial(attend_back_kernel, len(smalls), len(gmixes)),
@@ -380,17 +425,40 @@
             half,
             jax.ShapeDtypeStruct((small_rows, width), F32),
         ),
-        in_specs=[scalars()] + [whole()] * (8 + len(gmixes) + len(smalls)) + [pl.BlockSpec(memory_space=pl.ANY)] * len(after),
-        out_specs=(whole(),) * 4,
+        in_specs=[scalars(), whole()]
+        + [outside()] * len(loaded)
+        + [whole()] * len(smalls)
+        + [outside()] * len(after),
+        out_specs=(whole(), outside(), outside(), whole()),
         scratch_shapes=[
             pltpu.VMEM((padded, 3 * width), F32),
             pltpu.VMEM((padded, width), F32),
             pltpu.VMEM((padded, 3 * width), F32),
+            pltpu.VMEM(half.shape, BF16),
+            pltpu.VMEM(half.shape, BF16),
+            *(pltpu.VMEM(array.shape, array.dtype) for array in loaded),
+            pltpu.SemaphoreType.DMA((len(loaded) + 2,)),
         ],
         compiler_params=params(),
         cost_estimate=cost(BACK_COST),
         name="attend_back",
-    )(core, up, inputs, hidden, qkv, ctx, vecs, w_qkv, w_out, *gmixes, *smalls, *after)
+    )(core, vecs, *loaded, *smalls, *after)
+
+
+def marker_kernel(*refs):
+    refs[-1][...] = jnp.zeros_like(refs[-1])
+
+
+def marker(micros, *arrays):
+    return pl.pallas_call(
+        marker_kernel,
+        out_shape=jax.ShapeDtypeStruct((8, LANES), F32),
+        in_specs=[outside()] * len(arrays),
+        out_specs=whole(),
+        compiler_params=params(),
+        cost_estimate=cost(micros),
+        name="marker",
+    )(*arrays)
 
 
 def expert_block(me, rows, up, router, router_t, w_in, b_in, w_out, b_out, after=(), micros=1):
@@ -781,7 +849,7 @@
             early = (sums[0],)
             near_sent = (*backs.sent, *parts.sent)
         elif k == last - 1:
-            early, middle_sent = near_sent, tuple(backs.sent + parts.sent)
+            early, middle_sent = near_sent, tuple(backs.sent)
     backs.send_outward(blocks[last][1])
     _, _, activs, gpres, geouts, grouters, gin_bias, gout_bias = zip(*blocks)
     final = lambda half, after: final_grads(
@@ -797,7 +865,7 @@
     small_rows = shared_rows + -(-(hidden_units // width + 1) // 8) * 8
     grad_inputs, dense_keep, dense_send, small = attend_back(
         core, backs.sums, cotangent, inputs, hidden, qkv, ctx, vecs, w_qkv, w_out,
-        smalls, small_rows, pieces, (core_sum,),
+        smalls, small_rows, pieces, (core_sum, marker(MARK_COST, *backs.sums[1:])),
     )
     parts.add(last, together(blocks[last][0], grad_inputs)[0])
     parts.send_outward(grad_inputs)

time: 441 us -> 424 us (0.961)
  waiting for transfers between devices: 96.2 us -> 66.8 us
  starting transfers between devices: 83.2 us -> 96.9 us
    ppermute x2, waiting for transfers between devices: 14.3 us -> 0.08 us  [send_outward(): self.sums.append(lax.ppermute(outward, self.axis, OUTWARD))]
    ppermute x9, starting transfers between devices: 12.9 us -> 21.4 us  [shift(): lax.ppermute(values, axis, [(i, (i + by) % size) for i in range(size)])]
    ppermute x9, waiting for transfers between devices: 18.8 us -> 11.1 us  [shift(): lax.ppermute(values, axis, [(i, (i + by) % size) for i in range(size)])]
    ppermute x2, waiting for transfers between devices: 6.41 us -> 0.01 us  [add(): self.through = lax.ppermute(values, self.axis, INWARD)]
    unnamed x93 -> x73, local copies, waits for them, and re-layouts: 9.83 us -> 12.1 us
  transfers between devices with their start and end apart: 54 -> 54, of which waited for: 22 -> 20; matrix products, arithmetic and copies ran while one was open for 8% -> 8% of each run, Pallas kernels for 42% -> 47%
where the time goes in v5:
time: 424 us; the launch traced here: 417 us
  Pallas kernels  203 us (48%)
  starting transfers between devices  96.9 us (23%)
  waiting for transfers between devices  66.8 us (16%)
  other arithmetic  30.9 us (7%)
  local copies, waits for them, and re-layouts  17.4 us (4%)
    pallas_call x4, Pallas kernels, expert_block(): pl.pallas_call(functools.partial(expert_kernel, len(after)), out_shape=(j...  93.4 us
    ppermute x29, waiting for transfers between devices, swap(): lax.ppermute(values, axis, [(i, i ^ bit) for i in range(lax.axis_size(axi...  55.6 us
    ppermute x29, starting transfers between devices, swap(): lax.ppermute(values, axis, [(i, i ^ bit) for i in range(lax.axis_size(axi...  31.9 us
    pallas_call x1, Pallas kernels, attend_back(): pl.pallas_call(functools.partial(attend_back_kernel, len(smalls), len(gmi...  29.6 us
    pallas_call x2, Pallas kernels, final_grads(): pl.pallas_call(functools.partial(final_grads_kernel, count), out_shape=ja...  28.1 us
    ppermute x9, starting transfers between devices, shift(): lax.ppermute(values, axis, [(i, (i + by) % size) for i in range(size)])  21.4 us
    pallas_call x1, Pallas kernels, partial_grads(): pl.pallas_call(functools.partial(partial_grads_kernel, count), out_shape=...  20.5 us
    ppermute x2, starting transfers between devices, add(): self.sent = [lax.ppermute(values, self.axis, INWARD)]  19.6 us
  transfers between devices with their start and end apart: 54, of which 20 were waited for; matrix products, arithmetic and copies ran while one was open for 8% of the time, Pallas kernels for 47%

profile of v5, /device:TPU:0, one launch (start us, length us, event | category | flops | bytes accessed | tf_op | source)
XLA Modules:
  0.0 417.1 jit_solution(6969948886900052341)
XLA Ops:
  2.7 3.1 collective-permute-start.2
  7.3 12.9 %attend.1 = (bf16[591,2304]{1,0:T(8,128)(2,1)}, bf16[591,768]{1,0:T(8,128)(2,1)}, f32[591,768]{1,0:T(8,128)}, bf16[591,768]{1,0:T(8,128)(2,1)}) custom-call(bf16[591,768]{1,0:T(8,128)(2,1)} %refs_9_.1, f32[8,768]{1,0:T(8,128)} %stack.45.vecs_ref, bf16[768,2304]{1,0:T(8,128)(2,1)} %refs_10_.1, bf16[768,768]{1,0:T(8,128)(2,1)} %refs_6_.1), custom_call_target="tpu_custom_call" | custom-call | flops 4800000000 | bytes 1024 | tf_op jit(solution)/shard_map/attend/pallas_call | solution.py:390
  20.2 4.4 %collective-permute-start = (bf16[591,768]{1,0:T(8,128)(2,1)}, bf16[591,768]{1,0:T(8,128)(2,1)S(1)}, u32[]{:S(2)}, u32[]{:S(2)}) collective-permute-start(bf16[591,768]{1,0:T(8,128)(2,1)} %get-tuple-element.125.refs_0_), channel_id=1, source_target_pairs={{0,1},{1,0},{2,3},{3,2},{4,5},{5,4},{6,7},{7,6},{8,9},{9,8},{10,11... | collective-permute-start | bytes 2723336 | tf_op jit(solution)/shard_map/ppermute | solution.py:669
  24.6 1.8 collective-permute-start.1
  28.8 23.3 %expert_block.4 = (bf16[591,768]{1,0:T(8,128)(2,1)}, bf16[591,768]{1,0:T(8,128)(2,1)}, bf16[591,3072]{1,0:T(8,128)(2,1)}, bf16[591,3072]{1,0:T(8,128)(2,1)}, bf1...) custom-call(s32[1]{0:T(128)} %bitcast.1.me_ref, ...), custom_call_target="tpu_custom_call" | custom-call | flops 9600000000 | bytes 1024 | tf_op jit(solution)/shard_map/expert_block/pallas_call | solution.py:469
  52.1 1.6 collective-permute-start.5
  55.7 1.5 collective-permute-start.4
  57.3 23.5 %expert_block.5 = (bf16[591,768]{1,0:T(8,128)(2,1)}, bf16[591,768]{1,0:T(8,128)(2,1)}, bf16[591,3072]{1,0:T(8,128)(2,1)}, bf16[591,3072]{1,0:T(8,128)(2,1)}, bf1...) custom-call(s32[1]{0:T(128)} %bitcast.1.me_ref, bf16[591,768]{1,0:T(8,128)(2,1)} %copy-done.16, ...), custom_call_target="tpu_custom_call" | custom-call | flops 9600000000 | bytes 1024 | tf_op jit(solution)/shard_map/expert_block/pallas_call | solution.py:469
  80.8 1.3 collective-permute-start.6
  82.1 11.1 %collective-permute-start.11 = (bf16[591,768]{1,0:T(8,128)(2,1)}, bf16[591,768]{1,0:T(8,128)(2,1)S(1)}, u32[]{:S(2)}, u32[]{:S(2)}) collective-permute-start(bf16[591,768]{1,0:T(8,128)(2,1)} %get-tuple-element.131), channel_id=1, source_target_pairs={{0,1},{3,2},{4,5},{7,6},{8,9},{11,10},{12,13},{15,14},{16,17},{19,... | collective-permute-start | bytes 2723336 | tf_op jit(solution)/shard_map/ppermute | solution.py:630
  94.5 20.5 %partial_grads.1 = (f32[768,3072]{1,0:T(8,128)}, f32[768,3072]{1,0:T(8,128)}) custom-call(bf16[591,768]{1,0:T(8,128)(2,1)} %get-tuple-element.125.refs_0_, bf16[591,768]{1,0:T(8,128)(2,1)} %copy-done.16, bf16[591,3072]{1,0:T(8,128)(2,1)} %get-tuple-element.134.refs_2_, bf16[591,3072]{1,0:T(8,128)(2,1)} %get-tuple-element.135.refs_3_, ...), custom_call_target="tpu_custom_call" | custom-call | flops 400000000 | bytes 1024 | tf_op jit(solution)/shard_map/partial_grads/pallas_call | solution.py:525
  115.0 8.5 %collective-permute-start.10 = (bf16[591,768]{1,0:T(8,128)(2,1)}, bf16[591,768]{1,0:T(8,128)(2,1)}, u32[]{:S(2)}, u32[]{:S(2)}) collective-permute-start(bf16[591,768]{1,0:T(8,128)(2,1)} %get-tuple-element.142), channel_id=1, source_target_pairs={{0,1},{3,2},{4,5},{7,6},{8,9},{11,10},{12,13},{15,14},{16,17},{19,... | collective-permute-start | bytes 2723336 | tf_op jit(solution)/shard_map/ppermute | solution.py:630
  123.6 2.2 broadcast_select_fusion.3.refs_0_
  126.8 23.4 %expert_block.6 = (bf16[591,768]{1,0:T(8,128)(2,1)}, bf16[591,768]{1,0:T(8,128)(2,1)}, bf16[591,3072]{1,0:T(8,128)(2,1)}, bf16[591,3072]{1,0:T(8,128)(2,1)}, bf1...) custom-call(s32[1]{0:T(128)} %bitcast.1.me_ref, ...), custom_call_target="tpu_custom_call" | custom-call | flops 400000000 | bytes 1024 | tf_op jit(solution)/shard_map/expert_block/pallas_call | solution.py:469
  153.5 3.9 collective-permute-start.12
  159.2 23.3 %expert_block.7 = (bf16[591,768]{1,0:T(8,128)(2,1)}, bf16[591,768]{1,0:T(8,128)(2,1)}, bf16[591,3072]{1,0:T(8,128)(2,1)}, bf16[591,3072]{1,0:T(8,128)(2,1)}, bf1...) custom-call(s32[1]{0:T(128)} %bitcast.1.me_ref, ...), custom_call_target="tpu_custom_call" | custom-call | flops 400000000 | bytes 1024 | tf_op jit(solution)/shard_map/expert_block/pallas_call | solution.py:469
  182.5 1.8 add_convert_fusion.7
  186.9 1.5 collective-permute-start.17
  188.4 5.7 %collective-permute-start.31 = (bf16[591,768]{1,0:T(8,128)(2,1)}, bf16[591,768]{1,0:T(8,128)(2,1)}, u32[]{:S(2)}, u32[]{:S(2)}) collective-permute-start(bf16[591,768]{1,0:T(8,128)(2,1)} %get-tuple-element.188), channel_id=1, source_target_pairs={{0,1},{3,2},{4,5},{7,6},{8,9},{11,10},{12,13},{15,14},{16,17},{19,... | collective-permute-start | bytes 2723336 | tf_op jit(solution)/shard_map/ppermute | solution.py:635
  194.1 14.0 %final_grads.2.refs_10_ = bf16[8,2,48,3072]{3,2,1,0:T(8,128)(2,1)} custom-call(s32[1]{0:T(128)S(6)} %sub.48.half_ref, bf16[591,768]{1,0:T(8,128)(2,1)} %broadcast_select_fusion.3.refs_0_, bf16[591,768]{1,0:T(8,128)(2,1)} %broadcast_select_fusion.2.refs_0_.refs_1_, bf16[591,3072]{1,0:T(8,128)(2,1)} %get-tuple-element.141.refs_2_, ...), custom_call_target="tpu_custom_call" | custom-call | flops 1600000000 | bytes 1024 | tf_op jit(solution)/shard_map/final_grads/pallas_call | solution.py:543
  208.1 14.2 %final_grads.3 = bf16[8,2,48,3072]{3,2,1,0:T(8,128)(2,1)} custom-call(s32[1]{0:T(128)} %bitcast.half_ref.core_ref, bf16[591,768]{1,0:T(8,128)(2,1)} %broadcast_select_fusion.3.refs_0_, bf16[591,768]{1,0:T(8,128)(2,1)} %broadcast_select_fusion.2.refs_0_.refs_1_, bf16[591,3072]{1,0:T(8,128)(2,1)} %get-tuple-element.141.refs_2_, ...), custom_call_target="tpu_custom_call" | custom-call | flops 1600000000 | bytes 1024 | tf_op jit(solution)/shard_map/final_grads/pallas_call | solution.py:543
  224.2 5.8 %add_convert_fusion.refs_23_ = bf16[8,2,48,3072]{3,2,1,0:T(8,128)(2,1)S(1)} fusion(bf16[8,2,48,3072]{3,2,1,0:T(8,128)(2,1)} %collective-permute-done.14, bf16[8,2,48,3072]{3,2,1,0:T(8,128)(2,1)} %final_grads.3), kind=kLoop, calls=%fused_computation | loop fusion | flops 9437184 | bytes 14155776 | tf_op jit(solution)/shard_map/convert_element_type | solution.py:684
  230.3 1.8 copy-done
  233.2 1.5 collective-permute-start.16
  234.8 1.6 collective-permute-start.15
  236.4 29.6 %attend_back.1 = (bf16[591,768]{1,0:T(8,128)(2,1)}, bf16[8,48,3072]{2,1,0:T(8,128)(2,1)}, bf16[8,48,3072]{2,1,0:T(8,128)(2,1)}, f32[24,768]{1,0:T(8,128)}) custom-call(s32[1]{0:T(128)} %bitcast.half_ref.core_ref, f32[8,768]{1,0:T(8,128)} %stack.45.vecs_ref, bf16[591,768]{1,0:T(8,128)(2,1)} %get-tuple-element.151.refs_0_, ...), custom_call_target="tpu_custom_call" | custom-call | flops 11200000000 | bytes 1024 | tf_op jit(solution)/shard_map/attend_back/pallas_call | solution.py:420
  267.3 1.7 add_convert_fusion.2
  269.0 1.8 add_convert_fusion.3
  271.6 1.4 add_convert_fusion.6
  273.1 2.3 collective-permute-start.32
  277.2 9.6 %collective-permute-done.20 = bf16[1,2,48,3072]{3,2,1,0:T(8,128)(2,1)S(1)} collective-permute-done((bf16[1,2,48,3072]{3,2,1,0:T(8,128)(2,1)S(1)}, bf16[1,2,48,3072]{3,2,1,0:T(8,128)(2,1)S(1)}, u32[]{:S(2)}, u32[]{:S(2)}) %collective-permute-start.20) | collective-permute-done | bytes 589856 | tf_op jit(solution)/shard_map/ppermute | solution.py:669
  287.0 5.1 %collective-permute-done.19 = bf16[1,2,48,3072]{3,2,1,0:T(8,128)(2,1)S(1)} collective-permute-done((bf16[1,2,48,3072]{3,2,1,0:T(8,128)(2,1)S(1)}, bf16[1,2,48,3072]{3,2,1,0:T(8,128)(2,1)S(1)}, u32[]{:S(2)}, u32[]{:S(2)}) %collective-permute-start.19) | collective-permute-done | bytes 589856 | tf_op jit(solution)/shard_map/ppermute | solution.py:669
  293.2 1.6 collective-permute-start.27
  296.2 2.1 collective-permute-done.27
  298.4 1.6 collective-permute-start.25
  300.0 11.4 %collective-permute-done.24 = bf16[1,2,48,3072]{3,2,1,0:T(8,128)(2,1)S(1)} collective-permute-done((bf16[1,2,48,3072]{3,2,1,0:T(8,128)(2,1)S(1)}, bf16[1,2,48,3072]{3,2,1,0:T(8,128)(2,1)S(1)}, u32[]{:S(2)}, u32[]{:S(2)}) %collective-permute-start.24) | collective-permute-done | bytes 589856 | tf_op jit(solution)/shard_map/ppermute | solution.py:669
  312.1 10.7 %collective-permute-done.25 = bf16[2,48,3072]{2,1,0:T(8,128)(2,1)S(1)} collective-permute-done((bf16[2,48,3072]{2,1,0:T(8,128)(2,1)S(1)}, bf16[2,48,3072]{2,1,0:T(8,128)(2,1)S(1)}, u32[]{:S(2)}, u32[]{:S(2)}) %collective-permute-start.25) | collective-permute-done | bytes 589856 | tf_op jit(solution)/shard_map/ppermute | solution.py:669
  322.9 1.4 collective-permute-done.23
  326.3 1.6 collective-permute-start.28
  327.8 2.5 collective-permute-done.30
  330.3 2.4 collective-permute-done.29
  335.2 6.7 %collective-permute-start.35 = (bf16[24,3072]{1,0:T(8,128)(2,1)}, bf16[24,3072]{1,0:T(8,128)(2,1)S(1)}, u32[]{:S(2)}, u32[]{:S(2)}) collective-permute-start(bf16[24,3072]{1,0:T(8,128)(2,1)} %get-tuple-element.233), channel_id=1, source_target_pairs={{0,1},{1,2},{2,3},{3,0},{4,5},{5,6},{6,7},{7,4},{8,9},{9,10},{10,1... | collective-permute-start | bytes 442376 | tf_op jit(solution)/shard_map/ppermute | solution.py:587
  342.5 2.9 collective-permute-start.37
  346.6 1.7 collective-permute-start.44
  348.3 1.9 collective-permute-done.36
  350.3 3.1 collective-permute-start.41
  353.4 3.4 collective-permute-start.42
  356.9 1.4 collective-permute-done.41
  359.0 1.6 collective-permute-done.42
  360.6 1.8 collective-permute-start.39
  362.4 2.1 collective-permute-start.40
  364.6 1.5 collective-permute-done.38
  366.1 4.6 %collective-permute-done.39 = bf16[24,3072]{1,0:T(8,128)(2,1)S(1)} collective-permute-done((bf16[24,3072]{1,0:T(8,128)(2,1)S(1)}, bf16[24,3072]{1,0:T(8,128)(2,1)S(1)}, u32[]{:S(2)}, u32[]{:S(2)}) %collective-permute-start.39) | collective-permute-done | bytes 147488 | tf_op jit(solution)/shard_map/ppermute | solution.py:587
  371.1 2.3 pad_maximum_fusion.refs_0_
  374.0 1.6 collective-permute-start.47
  375.7 1.5 collective-permute-start.46
  377.2 5.8 %collective-permute-done.47 = bf16[1,48,3072]{2,1,0:T(8,128)(2,1)S(1)} collective-permute-done((bf16[1,48,3072]{2,1,0:T(8,128)(2,1)S(1)}, bf16[1,48,3072]{2,1,0:T(8,128)(2,1)S(1)}, u32[]{:S(2)}, u32[]{:S(2)}) %collective-permute-start.47) | collective-permute-done | bytes 294944 | tf_op jit(solution)/shard_map/ppermute | solution.py:669
  383.1 1.3 collective-permute-done.46
  384.5 1.4 copy-done.8
  385.9 1.4 copy-done.9
  387.3 1.5 collective-permute-start.51
  389.8 11.3 %assemble.2 = (f32[768,3072]{1,0:T(8,128)}, f32[4,768,768]{2,1,0:T(8,128)}) custom-call(s32[3]{0:T(128)} %pad_add_fusion.ids_ref, bf16[4,2,48,3072]{3,2,1,0:T(8,128)(2,1)} %copy-done.2, bf16[4,2,48,3072]{3,2,1,0:T(8,128)(2,1)} %copy-done.1, bf16[4,2,48,3072]{3,2,1,0:T(8,128)(2,1)} %copy-done.8, bf16[4,2,48,3072]{3,2,1,0:T(8,128)(2,1)} %copy-done.9), custom_call_target="tpu_custom_call" | custom-call | flops 2000000000 | bytes 1024 | tf_op jit(solution)/shard_map/assemble/pallas_call | solution.py:570
  403.9 1.5 add_convert_fusion.4
  410.0 6.9 %assemble.3 = (f32[768,2304]{1,0:T(8,128)}, f32[768,768]{1,0:T(8,128)}) custom-call(s32[3]{0:T(128)} %pad_add_fusion.ids_ref, bf16[4,48,3072]{2,1,0:T(8,128)(2,1)} %copy-done.12, bf16[4,48,3072]{2,1,0:T(8,128)(2,1)} %copy-done.11, bf16[4,48,3072]{2,1,0:T(8,128)(2,1)} %copy-done.33, bf16[4,48,3072]{2,1,0:T(8,128)(2,1)} %copy-done.34), custom_call_target="tpu_custom_call" | custom-call | flops 2000000000 | bytes 1024 | tf_op jit(solution)/shard_map/assemble/pallas_call | solution.py:570
  (196 shorter events, 45.1 us)
Async XLA Ops:
  0.7 5.9 %copy-start.28 = (f32[768]{0:T(1024)S(1)}, f32[768]{0:T(1024)}, u32[]{:S(2)}) copy-start(f32[768]{0:T(1024)} %param.25) | copy-start | bytes 9220
  0.7 5.9 %copy-start.29 = (f32[768]{0:T(1024)S(1)}, f32[768]{0:T(1024)}, u32[]{:S(2)}) copy-start(f32[768]{0:T(1024)} %param.27) | copy-start | bytes 9220
  0.7 5.9 %copy-start.30 = (f32[768]{0:T(1024)S(1)}, f32[768]{0:T(1024)}, u32[]{:S(2)}) copy-start(f32[768]{0:T(1024)} %param.28) | copy-start | bytes 9220
  0.7 5.9 %copy-start.31 = (f32[768]{0:T(1024)S(1)}, f32[768]{0:T(1024)}, u32[]{:S(2)}) copy-start(f32[768]{0:T(1024)} %param.29) | copy-start | bytes 9220
  2.7 17.5 %copy-start.15 = (bf16[608,768]{1,0:T(8,128)(2,1)}, bf16[608,768]{1,0:T(8,128)(2,1)S(1)}, u32[]{:S(2)}) copy-start(bf16[608,768]{1,0:T(8,128)(2,1)S(1)} %fusion.1.refs_1_) | copy-start | bytes 2801668
  2.7 25.2 %collective-permute-start.2 = (bf16[608,768]{1,0:T(8,128)(2,1)S(1)}, bf16[608,768]{1,0:T(8,128)(2,1)}, u32[]{:S(2)}, u32[]{:S(2)}) collective-permute-start(bf16[608,768]{1,0:T(8,128)(2,1)S(1)} %fusion.1.refs_1_), channel_id=1, source_target_pairs={{0,1},{1,0},{2,3},{3,2},{4,5},{5,4},{6,7},{7,6},{8,9},{9,8},{10,11... | collective-permute-start | bytes 2801672 | tf_op jit(solution)/shard_map/ppermute | solution.py:669
  5.8 22.1 %collective-permute-start.3 = (bf16[608,768]{1,0:T(8,128)(2,1)S(1)}, bf16[608,768]{1,0:T(8,128)(2,1)S(1)}, u32[]{:S(2)}, u32[]{:S(2)}) collective-permute-start(bf16[608,768]{1,0:T(8,128)(2,1)S(1)} %fusion.1.refs_1_), channel_id=1, source_target_pairs={{1,2},{2,1},{5,6},{6,5},{9,10},{10,9},{13,14},{14,13},{17,18},{18,... | collective-permute-start | bytes 2801672 | tf_op jit(solution)/shard_map/ppermute | solution.py:603
  7.3 19.1 %copy-start.24 = (bf16[768,4]{0,1:T(4,128)(2,1)S(1)}, bf16[768,4]{0,1:T(4,128)(2,1)}, u32[]{:S(2)}) copy-start(bf16[768,4]{0,1:T(4,128)(2,1)} %param.30) | copy-start | bytes 18436
  20.2 31.9 %collective-permute-start = (bf16[591,768]{1,0:T(8,128)(2,1)}, bf16[591,768]{1,0:T(8,128)(2,1)S(1)}, u32[]{:S(2)}, u32[]{:S(2)}) collective-permute-start(bf16[591,768]{1,0:T(8,128)(2,1)} %get-tuple-element.125.refs_0_), channel_id=1, source_target_pairs={{0,1},{1,0},{2,3},{3,2},{4,5},{5,4},{6,7},{7,6},{8,9},{9,8},{10,11... | collective-permute-start | bytes 2723336 | tf_op jit(solution)/shard_map/ppermute | solution.py:669
  24.6 27.5 %collective-permute-start.1 = (bf16[591,768]{1,0:T(8,128)(2,1)}, bf16[591,768]{1,0:T(8,128)(2,1)}, u32[]{:S(2)}, u32[]{:S(2)}) collective-permute-start(bf16[591,768]{1,0:T(8,128)(2,1)} %get-tuple-element.125.refs_0_), channel_id=1, source_target_pairs={{1,2},{2,1},{5,6},{6,5},{9,10},{10,9},{13,14},{14,13},{17,18},{18,... | collective-permute-start | bytes 2723336 | tf_op jit(solution)/shard_map/ppermute | solution.py:603
  52.1 28.7 %collective-permute-start.5 = (bf16[591,768]{1,0:T(8,128)(2,1)S(1)}, bf16[591,768]{1,0:T(8,128)(2,1)}, u32[]{:S(2)}, u32[]{:S(2)}) collective-permute-start(bf16[591,768]{1,0:T(8,128)(2,1)S(1)} %collective-permute-done.refs_0_.refs_1_), channel_id=1, source_target_pairs={{1,2},{2,1},{5,6},{6,5},{9,10},{10,9},{13,14},{14,13},{17,18},{18,... | collective-permute-start | bytes 2723336 | tf_op jit(solution)/shard_map/ppermute | solution.py:607
  53.7 39.5 %collective-permute-start.8 = (bf16[608,768]{1,0:T(8,128)(2,1)}, bf16[608,768]{1,0:T(8,128)(2,1)S(1)}, u32[]{:S(2)}, u32[]{:S(2)}) collective-permute-start(bf16[608,768]{1,0:T(8,128)(2,1)} %collective-permute-done.2.refs_8_.refs_1_), channel_id=1, source_target_pairs={{1,2},{2,1},{5,6},{6,5},{9,10},{10,9},{13,14},{14,13},{17,18},{18,... | collective-permute-start | bytes 2801672 | tf_op jit(solution)/shard_map/ppermute | solution.py:607
  54.4 71.3 %collective-permute-start.7 = (bf16[608,768]{1,0:T(8,128)(2,1)}, bf16[608,768]{1,0:T(8,128)(2,1)S(1)}, u32[]{:S(2)}, u32[]{:S(2)}) collective-permute-start(bf16[608,768]{1,0:T(8,128)(2,1)} %copy-done.13), channel_id=1, source_target_pairs={{1,0},{2,3},{5,4},{6,7},{9,8},{10,11},{13,12},{14,15},{17,16},{18,... | collective-permute-start | bytes 2801672 | tf_op jit(solution)/shard_map/ppermute | solution.py:608
  55.7 59.3 %collective-permute-start.4 = (bf16[591,768]{1,0:T(8,128)(2,1)}, bf16[591,768]{1,0:T(8,128)(2,1)}, u32[]{:S(2)}, u32[]{:S(2)}) collective-permute-start(bf16[591,768]{1,0:T(8,128)(2,1)} %collective-permute-done.1), channel_id=1, source_target_pairs={{1,0},{2,3},{5,4},{6,7},{9,8},{10,11},{13,12},{14,15},{17,16},{18,... | collective-permute-start | bytes 2723336 | tf_op jit(solution)/shard_map/ppermute | solution.py:608
  80.8 69.4 %collective-permute-start.6 = (bf16[591,768]{1,0:T(8,128)(2,1)}, bf16[591,768]{1,0:T(8,128)(2,1)S(1)}, u32[]{:S(2)}, u32[]{:S(2)}) collective-permute-start(bf16[591,768]{1,0:T(8,128)(2,1)} %collective-permute-done.5), channel_id=1, source_target_pairs={{1,0},{2,3},{5,4},{6,7},{9,8},{10,11},{13,12},{14,15},{17,16},{18,... | collective-permute-start | bytes 2723336 | tf_op jit(solution)/shard_map/ppermute | solution.py:612
  82.1 76.2 %collective-permute-start.11 = (bf16[591,768]{1,0:T(8,128)(2,1)}, bf16[591,768]{1,0:T(8,128)(2,1)S(1)}, u32[]{:S(2)}, u32[]{:S(2)}) collective-permute-start(bf16[591,768]{1,0:T(8,128)(2,1)} %get-tuple-element.131), channel_id=1, source_target_pairs={{0,1},{3,2},{4,5},{7,6},{8,9},{11,10},{12,13},{15,14},{16,17},{19,... | collective-permute-start | bytes 2723336 | tf_op jit(solution)/shard_map/ppermute | solution.py:630
  93.2 58.1 %collective-permute-start.9 = (bf16[608,768]{1,0:T(8,128)(2,1)S(1)}, bf16[608,768]{1,0:T(8,128)(2,1)S(1)}, u32[]{:S(2)}, u32[]{:S(2)}) collective-permute-start(bf16[608,768]{1,0:T(8,128)(2,1)S(1)} %collective-permute-done.8), channel_id=1, source_target_pairs={{1,0},{2,3},{5,4},{6,7},{9,8},{10,11},{13,12},{14,15},{17,16},{18,... | collective-permute-start | bytes 2801672 | tf_op jit(solution)/shard_map/ppermute | solution.py:612
  115.0 43.2 %collective-permute-start.10 = (bf16[591,768]{1,0:T(8,128)(2,1)}, bf16[591,768]{1,0:T(8,128)(2,1)}, u32[]{:S(2)}, u32[]{:S(2)}) collective-permute-start(bf16[591,768]{1,0:T(8,128)(2,1)} %get-tuple-element.142), channel_id=1, source_target_pairs={{0,1},{3,2},{4,5},{7,6},{8,9},{11,10},{12,13},{15,14},{16,17},{19,... | collective-permute-start | bytes 2723336 | tf_op jit(solution)/shard_map/ppermute | solution.py:630
  152.8 29.7 %collective-permute-start.13 = (bf16[591,768]{1,0:T(8,128)(2,1)}, bf16[591,768]{1,0:T(8,128)(2,1)S(1)}, u32[]{:S(2)}, u32[]{:S(2)}) collective-permute-start(bf16[591,768]{1,0:T(8,128)(2,1)} %get-tuple-element.150), channel_id=1, source_target_pairs={{1,2},{2,1},{5,6},{6,5},{9,10},{10,9},{13,14},{14,13},{17,18},{18,... | collective-permute-start | bytes 2723336 | tf_op jit(solution)/shard_map/ppermute | solution.py:636
  153.5 32.1 %collective-permute-start.12 = (bf16[591,768]{1,0:T(8,128)(2,1)}, bf16[591,768]{1,0:T(8,128)(2,1)S(1)}, u32[]{:S(2)}, u32[]{:S(2)}) collective-permute-start(bf16[591,768]{1,0:T(8,128)(2,1)} %get-tuple-element.150), channel_id=1, source_target_pairs={{0,1},{3,2},{4,5},{7,6},{8,9},{11,10},{12,13},{15,14},{16,17},{19,... | collective-permute-start | bytes 2723336 | tf_op jit(solution)/shard_map/ppermute | solution.py:635
  157.4 64.9 %collective-permute-start.33 = (bf16[591,768]{1,0:T(8,128)(2,1)}, bf16[591,768]{1,0:T(8,128)(2,1)S(1)}, u32[]{:S(2)}, u32[]{:S(2)}) collective-permute-start(bf16[591,768]{1,0:T(8,128)(2,1)} %get-tuple-element.188), channel_id=1, source_target_pairs={{1,2},{2,1},{5,6},{6,5},{9,10},{10,9},{13,14},{14,13},{17,18},{18,... | collective-permute-start | bytes 2723336 | tf_op jit(solution)/shard_map/ppermute | solution.py:636
  184.3 39.3 %collective-permute-start.18 = (bf16[591,768]{1,0:T(8,128)(2,1)S(1)}, bf16[591,768]{1,0:T(8,128)(2,1)}, u32[]{:S(2)}, u32[]{:S(2)}) collective-permute-start(bf16[591,768]{1,0:T(8,128)(2,1)S(1)} %add_convert_fusion.7), channel_id=1, source_target_pairs={{1,0},{2,3},{5,4},{6,7},{9,8},{10,11},{13,12},{14,15},{17,16},{18,... | collective-permute-start | bytes 2723336 | tf_op jit(solution)/shard_map/ppermute | solution.py:645
  185.6 8.4 %copy-start.6 = (bf16[591,768]{1,0:T(8,128)(2,1)}, bf16[591,768]{1,0:T(8,128)(2,1)S(1)}, u32[]{:S(2)}) copy-start(bf16[591,768]{1,0:T(8,128)(2,1)S(1)} %collective-permute-done.12.refs_10_) | copy-start | bytes 2723332
  186.9 36.7 %collective-permute-start.17 = (bf16[591,768]{1,0:T(8,128)(2,1)}, bf16[591,768]{1,0:T(8,128)(2,1)}, u32[]{:S(2)}, u32[]{:S(2)}) collective-permute-start(bf16[591,768]{1,0:T(8,128)(2,1)} %add_convert_fusion.8), channel_id=1, source_target_pairs={{0,3},{1,2},{2,1},{3,0},{4,7},{5,6},{6,5},{7,4},{8,11},{9,10},{10,... | collective-permute-start | bytes 2723336 | tf_op jit(solution)/shard_map/ppermute | solution.py:669
  188.4 83.3 %collective-permute-start.31 = (bf16[591,768]{1,0:T(8,128)(2,1)}, bf16[591,768]{1,0:T(8,128)(2,1)}, u32[]{:S(2)}, u32[]{:S(2)}) collective-permute-start(bf16[591,768]{1,0:T(8,128)(2,1)} %get-tuple-element.188), channel_id=1, source_target_pairs={{0,1},{3,2},{4,5},{7,6},{8,9},{11,10},{12,13},{15,14},{16,17},{19,... | collective-permute-start | bytes 2723336 | tf_op jit(solution)/shard_map/ppermute | solution.py:635
  208.0 14.3 %copy-start.20 = (bf16[591,768]{1,0:T(8,128)(2,1)S(1)}, bf16[591,768]{1,0:T(8,128)(2,1)}, u32[]{:S(2)}) copy-start(bf16[591,768]{1,0:T(8,128)(2,1)} %get-tuple-element.131) | copy-start | bytes 2723332
  208.0 16.1 %collective-permute-start.14 = (bf16[8,2,48,3072]{3,2,1,0:T(8,128)(2,1)}, bf16[8,2,48,3072]{3,2,1,0:T(8,128)(2,1)}, u32[]{:S(2)}, u32[]{:S(2)}) collective-permute-start(bf16[8,2,48,3072]{3,2,1,0:T(8,128)(2,1)} %final_grads.2.refs_10_), channel_id=1, source_target_pairs={{0,4},{4,0},{8,12},{12,8},{16,20},{20,16},{24,28},{28,24},{1,5},{5... | collective-permute-start | bytes 14155784 | tf_op jit(solution)/shard_map/ppermute | solution.py:669
  233.2 34.0 %collective-permute-start.16 = (bf16[2,2,48,3072]{3,2,1,0:T(8,128)(2,1)}, bf16[2,2,48,3072]{3,2,1,0:T(8,128)(2,1)}, u32[]{:S(2)}, u32[]{:S(2)}) collective-permute-start(bf16[2,2,48,3072]{3,2,1,0:T(8,128)(2,1)} %constant_dynamic-slice_fusion.9), channel_id=1, source_target_pairs={{0,16},{4,20},{8,24},{12,28},{16,0},{20,4},{24,8},{28,12},{1,17},{... | collective-permute-start | bytes 3538952 | tf_op jit(solution)/shard_map/ppermute | solution.py:669
  234.8 34.1 %collective-permute-start.15 = (bf16[2,2,48,3072]{3,2,1,0:T(8,128)(2,1)S(1)}, bf16[2,2,48,3072]{3,2,1,0:T(8,128)(2,1)}, u32[]{:S(2)}, u32[]{:S(2)}) collective-permute-start(bf16[2,2,48,3072]{3,2,1,0:T(8,128)(2,1)S(1)} %constant_dynamic-slice_fusion.10), channel_id=1, source_target_pairs={{0,8},{4,12},{8,0},{12,4},{16,24},{20,28},{24,16},{28,20},{1,9},{5... | collective-permute-start | bytes 3538952 | tf_op jit(solution)/shard_map/ppermute | solution.py:669
  265.9 67.6 %collective-permute-start.34 = (bf16[591,768]{1,0:T(8,128)(2,1)}, bf16[591,768]{1,0:T(8,128)(2,1)S(1)}, u32[]{:S(2)}, u32[]{:S(2)}) collective-permute-start(bf16[591,768]{1,0:T(8,128)(2,1)} %add_convert_fusion.5), channel_id=1, source_target_pairs={{1,0},{2,3},{5,4},{6,7},{9,8},{10,11},{13,12},{14,15},{17,16},{18,... | collective-permute-start | bytes 2723336 | tf_op jit(solution)/shard_map/ppermute | solution.py:645
  271.0 21.2 %collective-permute-start.21 = (bf16[8,48,3072]{2,1,0:T(8,128)(2,1)S(1)}, bf16[8,48,3072]{2,1,0:T(8,128)(2,1)S(1)}, u32[]{:S(2)}, u32[]{:S(2)}) collective-permute-start(bf16[8,48,3072]{2,1,0:T(8,128)(2,1)S(1)} %copy-done.32), channel_id=1, source_target_pairs={{0,4},{4,0},{8,12},{12,8},{16,20},{20,16},{24,28},{28,24},{1,5},{5... | collective-permute-start | bytes 7077896 | tf_op jit(solution)/shard_map/ppermute | solution.py:669
  271.0 15.8 %collective-permute-start.20 = (bf16[1,2,48,3072]{3,2,1,0:T(8,128)(2,1)S(1)}, bf16[1,2,48,3072]{3,2,1,0:T(8,128)(2,1)S(1)}, u32[]{:S(2)}, u32[]{:S(2)}) collective-permute-start(bf16[1,2,48,3072]{3,2,1,0:T(8,128)(2,1)S(1)} %constant_dynamic-slice_fusion.7), channel_id=1, source_target_pairs={{0,8},{4,12},{8,0},{12,4},{16,24},{20,28},{24,16},{28,20},{1,9},{5... | collective-permute-start | bytes 1769480 | tf_op jit(solution)/shard_map/ppermute | solution.py:669
  273.1 60.5 %collective-permute-start.32 = (bf16[591,768]{1,0:T(8,128)(2,1)S(1)}, bf16[591,768]{1,0:T(8,128)(2,1)S(1)}, u32[]{:S(2)}, u32[]{:S(2)}) collective-permute-start(bf16[591,768]{1,0:T(8,128)(2,1)S(1)} %add_convert_fusion.6), channel_id=1, source_target_pairs={{0,3},{1,2},{2,1},{3,0},{4,7},{5,6},{6,5},{7,4},{8,11},{9,10},{10,... | collective-permute-start | bytes 2723336 | tf_op jit(solution)/shard_map/ppermute | solution.py:669
  275.4 1.3 collective-permute-start.22
  276.7 15.4 %collective-permute-start.19 = (bf16[1,2,48,3072]{3,2,1,0:T(8,128)(2,1)S(1)}, bf16[1,2,48,3072]{3,2,1,0:T(8,128)(2,1)S(1)}, u32[]{:S(2)}, u32[]{:S(2)}) collective-permute-start(bf16[1,2,48,3072]{3,2,1,0:T(8,128)(2,1)S(1)} %constant_dynamic-slice_fusion.8), channel_id=1, source_target_pairs={{0,16},{4,20},{8,24},{12,28},{16,0},{20,4},{24,8},{28,12},{1,17},{... | collective-permute-start | bytes 1769480 | tf_op jit(solution)/shard_map/ppermute | solution.py:669
  277.2 15.0 %copy-start.7 = (bf16[8,48,3072]{2,1,0:T(8,128)(2,1)S(1)}, bf16[8,48,3072]{2,1,0:T(8,128)(2,1)}, u32[]{:S(2)}) copy-start(bf16[8,48,3072]{2,1,0:T(8,128)(2,1)} %get-tuple-element.172) | copy-start | bytes 7077892
  293.2 5.2 %collective-permute-start.27 = (f32[24,768]{1,0:T(8,128)S(1)}, f32[24,768]{1,0:T(8,128)S(1)}, u32[]{:S(2)}, u32[]{:S(2)}) collective-permute-start(f32[24,768]{1,0:T(8,128)S(1)} %add.232), channel_id=1, source_target_pairs={{0,8},{4,12},{8,0},{12,4},{16,24},{20,28},{24,16},{28,20},{1,9},{5... | collective-permute-start | bytes 221192 | tf_op jit(solution)/shard_map/ppermute | solution.py:669
  295.0 16.3 %collective-permute-start.24 = (bf16[1,2,48,3072]{3,2,1,0:T(8,128)(2,1)S(1)}, bf16[1,2,48,3072]{3,2,1,0:T(8,128)(2,1)S(1)}, u32[]{:S(2)}, u32[]{:S(2)}) collective-permute-start(bf16[1,2,48,3072]{3,2,1,0:T(8,128)(2,1)S(1)} %add_convert_fusion.11), channel_id=1, source_target_pairs={{0,8},{4,12},{8,0},{12,4},{16,24},{20,28},{24,16},{28,20},{1,9},{5... | collective-permute-start | bytes 1769480 | tf_op jit(solution)/shard_map/ppermute | solution.py:669
  295.6 16.3 %collective-permute-start.26 = (bf16[2,48,3072]{2,1,0:T(8,128)(2,1)S(1)}, bf16[2,48,3072]{2,1,0:T(8,128)(2,1)S(1)}, u32[]{:S(2)}, u32[]{:S(2)}) collective-permute-start(bf16[2,48,3072]{2,1,0:T(8,128)(2,1)S(1)} %constant_dynamic-slice_fusion.5), channel_id=1, source_target_pairs={{0,16},{4,20},{8,24},{12,28},{16,0},{20,4},{24,8},{28,12},{1,17},{... | collective-permute-start | bytes 1769480 | tf_op jit(solution)/shard_map/ppermute | solution.py:669
  298.4 24.4 %collective-permute-start.25 = (bf16[2,48,3072]{2,1,0:T(8,128)(2,1)S(1)}, bf16[2,48,3072]{2,1,0:T(8,128)(2,1)S(1)}, u32[]{:S(2)}, u32[]{:S(2)}) collective-permute-start(bf16[2,48,3072]{2,1,0:T(8,128)(2,1)S(1)} %constant_dynamic-slice_fusion.6), channel_id=1, source_target_pairs={{0,8},{4,12},{8,0},{12,4},{16,24},{20,28},{24,16},{28,20},{1,9},{5... | collective-permute-start | bytes 1769480 | tf_op jit(solution)/shard_map/ppermute | solution.py:669
  311.3 13.0 %collective-permute-start.23 = (bf16[1,2,48,3072]{3,2,1,0:T(8,128)(2,1)S(1)}, bf16[1,2,48,3072]{3,2,1,0:T(8,128)(2,1)S(1)}, u32[]{:S(2)}, u32[]{:S(2)}) collective-permute-start(bf16[1,2,48,3072]{3,2,1,0:T(8,128)(2,1)S(1)} %add_convert_fusion.12), channel_id=1, source_target_pairs={{0,16},{4,20},{8,24},{12,28},{16,0},{20,4},{24,8},{28,12},{1,17},{... | collective-permute-start | bytes 1769480 | tf_op jit(solution)/shard_map/ppermute | solution.py:669
  325.4 4.9 %collective-permute-start.30 = (f32[24,768]{1,0:T(8,128)S(1)}, f32[24,768]{1,0:T(8,128)S(1)}, u32[]{:S(2)}, u32[]{:S(2)}) collective-permute-start(f32[24,768]{1,0:T(8,128)S(1)} %add.235), channel_id=1, source_target_pairs={{0,16},{4,20},{8,24},{12,28},{16,0},{20,4},{24,8},{28,12},{1,17},{... | collective-permute-start | bytes 221192 | tf_op jit(solution)/shard_map/ppermute | solution.py:669
  325.9 6.8 %collective-permute-start.29 = (bf16[1,48,3072]{2,1,0:T(8,128)(2,1)S(1)}, bf16[1,48,3072]{2,1,0:T(8,128)(2,1)S(1)}, u32[]{:S(2)}, u32[]{:S(2)}) collective-permute-start(bf16[1,48,3072]{2,1,0:T(8,128)(2,1)S(1)} %constant_dynamic-slice_fusion.3), channel_id=1, source_target_pairs={{0,8},{4,12},{8,0},{12,4},{16,24},{20,28},{24,16},{28,20},{1,9},{5... | collective-permute-start | bytes 884744 | tf_op jit(solution)/shard_map/ppermute | solution.py:669
  326.3 7.2 %collective-permute-start.28 = (bf16[1,48,3072]{2,1,0:T(8,128)(2,1)S(1)}, bf16[1,48,3072]{2,1,0:T(8,128)(2,1)S(1)}, u32[]{:S(2)}, u32[]{:S(2)}) collective-permute-start(bf16[1,48,3072]{2,1,0:T(8,128)(2,1)S(1)} %constant_dynamic-slice_fusion.4), channel_id=1, source_target_pairs={{0,16},{4,20},{8,24},{12,28},{16,0},{20,4},{24,8},{28,12},{1,17},{... | collective-permute-start | bytes 884744 | tf_op jit(solution)/shard_map/ppermute | solution.py:669
  335.2 13.2 %collective-permute-start.35 = (bf16[24,3072]{1,0:T(8,128)(2,1)}, bf16[24,3072]{1,0:T(8,128)(2,1)S(1)}, u32[]{:S(2)}, u32[]{:S(2)}) collective-permute-start(bf16[24,3072]{1,0:T(8,128)(2,1)} %get-tuple-element.233), channel_id=1, source_target_pairs={{0,1},{1,2},{2,3},{3,0},{4,5},{5,6},{6,7},{7,4},{8,9},{9,10},{10,1... | collective-permute-start | bytes 442376 | tf_op jit(solution)/shard_map/ppermute | solution.py:587
  341.8 8.4 %collective-permute-start.36 = (bf16[24,3072]{1,0:T(8,128)(2,1)S(1)}, bf16[24,3072]{1,0:T(8,128)(2,1)S(1)}, u32[]{:S(2)}, u32[]{:S(2)}) collective-permute-start(bf16[24,3072]{1,0:T(8,128)(2,1)S(1)} %get-tuple-element.235), channel_id=1, source_target_pairs={{0,2},{1,3},{2,0},{3,1},{4,6},{5,7},{6,4},{7,5},{8,10},{9,11},{10,... | collective-permute-start | bytes 442376 | tf_op jit(solution)/shard_map/ppermute | solution.py:587
  342.5 7.7 %collective-permute-start.37 = (bf16[24,3072]{1,0:T(8,128)(2,1)S(1)}, bf16[24,3072]{1,0:T(8,128)(2,1)S(1)}, u32[]{:S(2)}, u32[]{:S(2)}) collective-permute-start(bf16[24,3072]{1,0:T(8,128)(2,1)S(1)} %get-tuple-element.234), channel_id=1, source_target_pairs={{0,3},{1,0},{2,1},{3,2},{4,7},{5,4},{6,5},{7,6},{8,11},{9,8},{10,9... | collective-permute-start | bytes 442376 | tf_op jit(solution)/shard_map/ppermute | solution.py:587
  345.4 25.4 %collective-permute-start.45 = (bf16[2,2,48,3072]{3,2,1,0:T(8,128)(2,1)S(1)}, bf16[2,2,48,3072]{3,2,1,0:T(8,128)(2,1)S(1)}, u32[]{:S(2)}, u32[]{:S(2)}) collective-permute-start(bf16[2,2,48,3072]{3,2,1,0:T(8,128)(2,1)S(1)} %pad_maximum_fusion.3), channel_id=1, source_target_pairs={{0,16},{4,20},{8,24},{12,28},{16,0},{20,4},{24,8},{28,12},{1,17},{... | collective-permute-start | bytes 3538952 | tf_op jit(solution)/shard_map/ppermute | solution.py:669
  346.6 24.5 %collective-permute-start.44 = (bf16[2,2,48,3072]{3,2,1,0:T(8,128)(2,1)}, bf16[2,2,48,3072]{3,2,1,0:T(8,128)(2,1)S(1)}, u32[]{:S(2)}, u32[]{:S(2)}) collective-permute-start(bf16[2,2,48,3072]{3,2,1,0:T(8,128)(2,1)} %pad_maximum_fusion.2), channel_id=1, source_target_pairs={{0,8},{4,12},{8,0},{12,4},{16,24},{20,28},{24,16},{28,20},{1,9},{5... | collective-permute-start | bytes 3538952 | tf_op jit(solution)/shard_map/ppermute | solution.py:669
  350.3 8.0 %collective-permute-start.41 = (f32[16,768]{1,0:T(8,128)S(1)}, f32[16,768]{1,0:T(8,128)S(1)}, u32[]{:S(2)}, u32[]{:S(2)}) collective-permute-start(f32[16,768]{1,0:T(8,128)S(1)} %slice.84), channel_id=1, source_target_pairs={{0,1},{1,2},{2,3},{3,0},{4,5},{5,6},{6,7},{7,4},{8,9},{9,10},{10,1... | collective-permute-start | bytes 147464 | tf_op jit(solution)/shard_map/ppermute | solution.py:587
  353.4 7.2 %collective-permute-start.42 = (f32[16,768]{1,0:T(8,128)S(1)}, f32[16,768]{1,0:T(8,128)S(1)}, u32[]{:S(2)}, u32[]{:S(2)}) collective-permute-start(f32[16,768]{1,0:T(8,128)S(1)} %slice.84), channel_id=1, source_target_pairs={{0,2},{1,3},{2,0},{3,1},{4,6},{5,7},{6,4},{7,5},{8,10},{9,11},{10,... | collective-permute-start | bytes 147464 | tf_op jit(solution)/shard_map/ppermute | solution.py:587
  356.8 5.6 %collective-permute-start.43 = (f32[16,768]{1,0:T(8,128)S(1)}, f32[16,768]{1,0:T(8,128)S(1)}, u32[]{:S(2)}, u32[]{:S(2)}) collective-permute-start(f32[16,768]{1,0:T(8,128)S(1)} %slice.84), channel_id=1, source_target_pairs={{0,3},{1,0},{2,1},{3,2},{4,7},{5,4},{6,5},{7,6},{8,11},{9,8},{10,9... | collective-permute-start | bytes 147464 | tf_op jit(solution)/shard_map/ppermute | solution.py:587
  358.3 7.8 %collective-permute-start.38 = (bf16[24,3072]{1,0:T(8,128)(2,1)S(1)}, bf16[24,3072]{1,0:T(8,128)(2,1)S(1)}, u32[]{:S(2)}, u32[]{:S(2)}) collective-permute-start(bf16[24,3072]{1,0:T(8,128)(2,1)S(1)} %add_convert_fusion.15), channel_id=1, source_target_pairs={{0,1},{1,2},{2,3},{3,0},{4,5},{5,6},{6,7},{7,4},{8,9},{9,10},{10,1... | collective-permute-start | bytes 442376 | tf_op jit(solution)/shard_map/ppermute | solution.py:587
  360.6 10.2 %collective-permute-start.39 = (bf16[24,3072]{1,0:T(8,128)(2,1)S(1)}, bf16[24,3072]{1,0:T(8,128)(2,1)S(1)}, u32[]{:S(2)}, u32[]{:S(2)}) collective-permute-start(bf16[24,3072]{1,0:T(8,128)(2,1)S(1)} %add_convert_fusion.15), channel_id=1, source_target_pairs={{0,2},{1,3},{2,0},{3,1},{4,6},{5,7},{6,4},{7,5},{8,10},{9,11},{10,... | collective-permute-start | bytes 442376 | tf_op jit(solution)/shard_map/ppermute | solution.py:587
  362.4 8.4 %collective-permute-start.40 = (bf16[24,3072]{1,0:T(8,128)(2,1)S(1)}, bf16[24,3072]{1,0:T(8,128)(2,1)S(1)}, u32[]{:S(2)}, u32[]{:S(2)}) collective-permute-start(bf16[24,3072]{1,0:T(8,128)(2,1)S(1)} %add_convert_fusion.15), channel_id=1, source_target_pairs={{0,3},{1,0},{2,1},{3,2},{4,7},{5,4},{6,5},{7,6},{8,11},{9,8},{10,9... | collective-permute-start | bytes 442376 | tf_op jit(solution)/shard_map/ppermute | solution.py:587
  373.4 11.1 %copy-start.2 = (bf16[4,2,48,3072]{3,2,1,0:T(8,128)(2,1)}, bf16[4,2,48,3072]{3,2,1,0:T(8,128)(2,1)S(1)}, u32[]{:S(2)}) copy-start(bf16[4,2,48,3072]{3,2,1,0:T(8,128)(2,1)S(1)} %pad_maximum_fusion.refs_0_) | copy-start | bytes 7077892
  373.4 11.0 %collective-permute-start.48 = (bf16[4,2,48,3072]{3,2,1,0:T(8,128)(2,1)S(1)}, bf16[4,2,48,3072]{3,2,1,0:T(8,128)(2,1)S(1)}, u32[]{:S(2)}, u32[]{:S(2)}) collective-permute-start(bf16[4,2,48,3072]{3,2,1,0:T(8,128)(2,1)S(1)} %pad_maximum_fusion.refs_0_), channel_id=1, source_target_pairs={{0,4},{4,0},{8,12},{12,8},{16,20},{20,16},{24,28},{28,24},{1,5},{5... | collective-permute-start | bytes 7077896 | tf_op jit(solution)/shard_map/ppermute | solution.py:669
  373.5 10.9 %collective-permute-start.49 = (bf16[4,2,48,3072]{3,2,1,0:T(8,128)(2,1)S(1)}, bf16[4,2,48,3072]{3,2,1,0:T(8,128)(2,1)S(1)}, u32[]{:S(2)}, u32[]{:S(2)}) collective-permute-start(bf16[4,2,48,3072]{3,2,1,0:T(8,128)(2,1)S(1)} %pad_maximum_fusion.1.refs_1_), channel_id=1, source_target_pairs={{0,4},{4,0},{8,12},{12,8},{16,20},{20,16},{24,28},{28,24},{1,5},{5... | collective-permute-start | bytes 7077896 | tf_op jit(solution)/shard_map/ppermute | solution.py:669
  374.0 9.0 %collective-permute-start.47 = (bf16[1,48,3072]{2,1,0:T(8,128)(2,1)S(1)}, bf16[1,48,3072]{2,1,0:T(8,128)(2,1)S(1)}, u32[]{:S(2)}, u32[]{:S(2)}) collective-permute-start(bf16[1,48,3072]{2,1,0:T(8,128)(2,1)S(1)} %get-tuple-element.203), channel_id=1, source_target_pairs={{0,8},{4,12},{8,0},{12,4},{16,24},{20,28},{24,16},{28,20},{1,9},{5... | collective-permute-start | bytes 884744 | tf_op jit(solution)/shard_map/ppermute | solution.py:669
  375.7 8.7 %collective-permute-start.46 = (bf16[1,48,3072]{2,1,0:T(8,128)(2,1)S(1)}, bf16[1,48,3072]{2,1,0:T(8,128)(2,1)S(1)}, u32[]{:S(2)}, u32[]{:S(2)}) collective-permute-start(bf16[1,48,3072]{2,1,0:T(8,128)(2,1)S(1)} %get-tuple-element.202), channel_id=1, source_target_pairs={{0,16},{4,20},{8,24},{12,28},{16,0},{20,4},{24,8},{28,12},{1,17},{... | collective-permute-start | bytes 884744 | tf_op jit(solution)/shard_map/ppermute | solution.py:669
  387.3 14.2 %collective-permute-start.51 = (bf16[2,48,3072]{2,1,0:T(8,128)(2,1)S(1)}, bf16[2,48,3072]{2,1,0:T(8,128)(2,1)S(1)}, u32[]{:S(2)}, u32[]{:S(2)}) collective-permute-start(bf16[2,48,3072]{2,1,0:T(8,128)(2,1)S(1)} %pad_maximum_fusion.8), channel_id=1, source_target_pairs={{0,16},{4,20},{8,24},{12,28},{16,0},{20,4},{24,8},{28,12},{1,17},{... | collective-permute-start | bytes 1769480 | tf_op jit(solution)/shard_map/ppermute | solution.py:669
  388.8 13.9 %collective-permute-start.50 = (bf16[2,48,3072]{2,1,0:T(8,128)(2,1)S(1)}, bf16[2,48,3072]{2,1,0:T(8,128)(2,1)S(1)}, u32[]{:S(2)}, u32[]{:S(2)}) collective-permute-start(bf16[2,48,3072]{2,1,0:T(8,128)(2,1)S(1)} %pad_maximum_fusion.7), channel_id=1, source_target_pairs={{0,8},{4,12},{8,0},{12,4},{16,24},{20,28},{24,16},{28,20},{1,9},{5... | collective-permute-start | bytes 1769480 | tf_op jit(solution)/shard_map/ppermute | solution.py:669
  402.8 5.1 %collective-permute-start.52 = (bf16[4,48,3072]{2,1,0:T(8,128)(2,1)S(1)}, bf16[4,48,3072]{2,1,0:T(8,128)(2,1)S(1)}, u32[]{:S(2)}, u32[]{:S(2)}) collective-permute-start(bf16[4,48,3072]{2,1,0:T(8,128)(2,1)S(1)} %pad_maximum_fusion.4.refs_0_), channel_id=1, source_target_pairs={{0,4},{4,0},{8,12},{12,8},{16,20},{20,16},{24,28},{28,24},{1,5},{5... | collective-permute-start | bytes 3538952 | tf_op jit(solution)/shard_map/ppermute | solution.py:669
  402.9 5.0 %collective-permute-start.53 = (bf16[4,48,3072]{2,1,0:T(8,128)(2,1)S(1)}, bf16[4,48,3072]{2,1,0:T(8,128)(2,1)S(1)}, u32[]{:S(2)}, u32[]{:S(2)}) collective-permute-start(bf16[4,48,3072]{2,1,0:T(8,128)(2,1)S(1)} %pad_maximum_fusion.5.refs_1_), channel_id=1, source_target_pairs={{0,4},{4,0},{8,12},{12,8},{16,20},{20,16},{24,28},{28,24},{1,5},{5... | collective-permute-start | bytes 3538952 | tf_op jit(solution)/shard_map/ppermute | solution.py:669
  (25 other events, 69.7 us)

commit v6 on v5

--- a/solution.py
+++ b/solution.py
@@ -117,19 +117,16 @@
 
 
 def attend_kernel(
-    x_hbm, vecs_ref, wqkv_hbm, wout_hbm,
-    qkv_hbm, ctx_ref, hidden_ref, mixed_ref,
-    qkv_s, ctx_s, x_ref, wqkv_ref, wout_ref, qkv_ref, sems,
+    x_ref, vecs_ref, wqkv_ref, wout_ref,
+    qkv_ref, ctx_ref, hidden_ref, mixed_ref,
+    qkv_s, ctx_s,
 ):
-    fetch = Fetch(((x_hbm, x_ref), (wqkv_hbm, wqkv_ref), (wout_hbm, wout_ref)), sems)
-    fetch.wait(0)
     toks, width = x_ref.shape
     spare = qkv_s.shape[0] - toks
     x = x_ref[...].astype(F32)
     vec = lambda name: vecs_ref[VECS.index(name) : VECS.index(name) + 1, :]
     unit, _ = unit_norm(x)
     normed = (unit * vec("g1") + vec("b1")).astype(BF16)
-    fetch.wait(1)
     for part, bias in ((0, "qb"), (1, None), (2, "vb")):
         cols = pl.ds(part * width, width)
         joined = dot(normed, wqkv_ref[:, cols])
@@ -138,7 +135,6 @@
         joined = joined.astype(BF16)
         qkv_ref[:, cols] = joined
         qkv_s[0:toks, cols] = joined.astype(F32)
-    store = Fetch(((qkv_ref, qkv_hbm),), sems, 3)
     qkv_s[toks:, :] = jnp.zeros((spare, 3 * width), F32)
     masks = pair_masks(SEQ_PAD)
     for img in range(toks // SEQ):
@@ -151,12 +147,10 @@
             ctx_s[rows, at : at + LANES] = unstack_heads(dot(probs, value), masks)
     ctx = ctx_s[0:toks, :].astype(BF16)
     ctx_ref[...] = ctx
-    fetch.wait(2)
     hidden = x + dot(ctx, wout_ref[...]) + vec("ob")
     hidden_ref[...] = hidden
     unit2, _ = unit_norm(hidden)
     mixed_ref[...] = (unit2 * vec("g2") + vec("b2")).astype(BF16)
-    store.wait(0)
 
 
 def expert_kernel(
@@ -395,17 +389,9 @@
             jax.ShapeDtypeStruct((toks, width), F32),
             jax.ShapeDtypeStruct((toks, width), BF16),
         ),
-        in_specs=[outside(), whole(), outside(), outside()],
-        out_specs=(outside(), whole(), whole(), whole()),
-        scratch_shapes=[
-            pltpu.VMEM((padded, 3 * width), F32),
-            pltpu.VMEM((padded, width), F32),
-            pltpu.VMEM((toks, width), BF16),
-            pltpu.VMEM((width, 3 * width), BF16),
-            pltpu.VMEM((width, width), BF16),
-            pltpu.VMEM((toks, 3 * width), BF16),
-            pltpu.SemaphoreType.DMA((4,)),
-        ],
+        in_specs=[whole()] * 4,
+        out_specs=(whole(),) * 4,
+        scratch_shapes=[pltpu.VMEM((padded, 3 * width), F32), pltpu.VMEM((padded, width), F32)],
         compiler_params=params(),
         cost_estimate=cost(12),
         name="attend",
@@ -837,15 +823,16 @@
     for k in range(1, last + 1):
         blocks.append(run_block(mixes[k], ups[k], early, NEAR_COST if k == 1 else OTHER_COST))
         if k == 1 and last == 3:
-            ups += up_line.finish(blocks[1][0])
-            mixes += mixed_line.finish(blocks[1][0])
+            sums = partial_grads(*([x[j] for j in range(2)] for x in (mixes, *zip(*[(b[3], b[2], b[4]) for b in blocks]))))
+            ups += up_line.finish(sums[0])
+            mixes += mixed_line.finish(sums[0])
         hold = (mixes[last], ups[last]) if k == last - 1 else ()
         backs.add(k, blocks[k][1], *hold)
         if k < last:
             parts.add(k, blocks[k][0], *hold)
         if k == last - 2:
             listed = lambda which: [mixes[j] if which is None else blocks[j][which] for j in range(k + 1)]
-            sums = partial_grads(listed(None), listed(3), listed(2), listed(4))
+            sums = sums or partial_grads(listed(None), listed(3), listed(2), listed(4))
             early = (sums[0],)
             near_sent = (*backs.sent, *parts.sent)
         elif k == last - 1:

time: 424 us -> 422 us (level)
  starting transfers between devices: 96.9 us -> 92 us
    unnamed x73 -> x71, local copies, waits for them, and re-layouts: 12.1 us -> 10.9 us
  transfers between devices with their start and end apart: 54 -> 54, of which waited for: 20 -> 21; matrix products, arithmetic and copies ran while one was open for 8% -> 8% of each run, Pallas kernels for 47% -> 47%
where the time goes in v6:
time: 422 us; the launch traced here: 414 us
  Pallas kernels  202 us (48%)
  starting transfers between devices  92 us (22%)
  waiting for transfers between devices  69.3 us (16%)
  other arithmetic  33.4 us (8%)
  local copies, waits for them, and re-layouts  16.2 us (4%)
    pallas_call x4, Pallas kernels, expert_block(): pl.pallas_call(functools.partial(expert_kernel, len(after)), out_shape=(j...  93.1 us
    ppermute x29, waiting for transfers between devices, swap(): lax.ppermute(values, axis, [(i, i ^ bit) for i in range(lax.axis_size(axi...  56.7 us
    ppermute x29, starting transfers between devices, swap(): lax.ppermute(values, axis, [(i, i ^ bit) for i in range(lax.axis_size(axi...  31.9 us
    pallas_call x1, Pallas kernels, attend_back(): pl.pallas_call(functools.partial(attend_back_kernel, len(smalls), len(gmi...  29.5 us
    pallas_call x2, Pallas kernels, final_grads(): pl.pallas_call(functools.partial(final_grads_kernel, count), out_shape=ja...  28 us
    ppermute x9, starting transfers between devices, shift(): lax.ppermute(values, axis, [(i, (i + by) % size) for i in range(size)])  21.2 us
    pallas_call x1, Pallas kernels, partial_grads(): pl.pallas_call(functools.partial(partial_grads_kernel, count), out_shape=...  20.5 us
    pallas_call x2, Pallas kernels, assemble(): pl.pallas_call(functools.partial(assemble_kernel, write), out_shape=tuple...  18.1 us
  transfers between devices with their start and end apart: 54, of which 21 were waited for; matrix products, arithmetic and copies ran while one was open for 8% of the time, Pallas kernels for 47%

profile of v6, /device:TPU:0, one launch (start us, length us, event | category | flops | bytes accessed | tf_op | source)
XLA Modules:
  0.0 414.2 jit_solution(6525445744881117703)
XLA Ops:
  2.7 3.1 collective-permute-start.2
  7.3 11.6 %attend.1 = (bf16[591,2304]{1,0:T(8,128)(2,1)}, bf16[591,768]{1,0:T(8,128)(2,1)}, f32[591,768]{1,0:T(8,128)}, bf16[591,768]{1,0:T(8,128)(2,1)}) custom-call(bf16[591,768]{1,0:T(8,128)(2,1)} %refs_9_.1, f32[8,768]{1,0:T(8,128)} %stack.45.vecs_ref, bf16[768,2304]{1,0:T(8,128)(2,1)} %refs_10_.1, bf16[768,768]{1,0:T(8,128)(2,1)} %refs_6_.1), custom_call_target="tpu_custom_call" | custom-call | flops 4800000000 | bytes 1024 | tf_op jit(solution)/shard_map/attend/pallas_call | solution.py:384
  18.9 4.3 %collective-permute-start = (bf16[591,768]{1,0:T(8,128)(2,1)}, bf16[591,768]{1,0:T(8,128)(2,1)}, u32[]{:S(2)}, u32[]{:S(2)}) collective-permute-start(bf16[591,768]{1,0:T(8,128)(2,1)} %get-tuple-element.125.refs_0_), channel_id=1, source_target_pairs={{0,1},{1,0},{2,3},{3,2},{4,5},{5,4},{6,7},{7,6},{8,9},{9,8},{10,11... | collective-permute-start | bytes 2723336 | tf_op jit(solution)/shard_map/ppermute | solution.py:655
  23.3 1.6 collective-permute-start.1
  28.2 1.5 collective-permute-start.7
  29.7 23.3 %expert_block.4 = (bf16[591,768]{1,0:T(8,128)(2,1)}, bf16[591,768]{1,0:T(8,128)(2,1)}, bf16[591,3072]{1,0:T(8,128)(2,1)}, bf16[591,3072]{1,0:T(8,128)(2,1)}, bf1...) custom-call(s32[1]{0:T(128)} %bitcast.1.me_ref, ...), custom_call_target="tpu_custom_call" | custom-call | flops 9600000000 | bytes 1024 | tf_op jit(solution)/shard_map/expert_block/pallas_call | solution.py:455
  53.0 1.6 collective-permute-start.5
  54.6 1.5 collective-permute-start.4
  56.1 23.3 %expert_block.5 = (bf16[591,768]{1,0:T(8,128)(2,1)}, bf16[591,768]{1,0:T(8,128)(2,1)}, bf16[591,3072]{1,0:T(8,128)(2,1)}, bf16[591,3072]{1,0:T(8,128)(2,1)}, bf1...) custom-call(s32[1]{0:T(128)} %bitcast.1.me_ref, ...), custom_call_target="tpu_custom_call" | custom-call | flops 9600000000 | bytes 1024 | tf_op jit(solution)/shard_map/expert_block/pallas_call | solution.py:455
  79.4 20.5 %partial_grads.1 = (f32[768,3072]{1,0:T(8,128)}, f32[768,3072]{1,0:T(8,128)}) custom-call(bf16[591,768]{1,0:T(8,128)(2,1)} %get-tuple-element.125.refs_0_, bf16[591,768]{1,0:T(8,128)(2,1)} %collective-permute-done.refs_0_.refs_1_, bf16[591,3072]{1,0:T(8,128)(2,1)} %get-tuple-element.131.refs_2_, bf16[591,3072]{1,0:T(8,128)(2,1)} %get-tuple-element.132.refs_3_, ...), custom_call_target="tpu_custom_call" | custom-call | flops 400000000 | bytes 1024 | tf_op jit(solution)/shard_map/partial_grads/pallas_call | solution.py:511
  102.6 14.3 %collective-permute-start.10 = (bf16[591,768]{1,0:T(8,128)(2,1)}, bf16[591,768]{1,0:T(8,128)(2,1)}, u32[]{:S(2)}, u32[]{:S(2)}) collective-permute-start(bf16[591,768]{1,0:T(8,128)(2,1)} %get-tuple-element.141), channel_id=1, source_target_pairs={{0,1},{3,2},{4,5},{7,6},{8,9},{11,10},{12,13},{15,14},{16,17},{19,... | collective-permute-start | bytes 2723336 | tf_op jit(solution)/shard_map/ppermute | solution.py:616
  116.8 1.8 collective-permute-start.11
  118.6 2.2 broadcast_select_fusion.3.refs_0_
  121.9 23.3 %expert_block.6 = (bf16[591,768]{1,0:T(8,128)(2,1)}, bf16[591,768]{1,0:T(8,128)(2,1)}, bf16[591,3072]{1,0:T(8,128)(2,1)}, bf16[591,3072]{1,0:T(8,128)(2,1)}, bf1...) custom-call(s32[1]{0:T(128)} %bitcast.1.me_ref, ...), custom_call_target="tpu_custom_call" | custom-call | flops 400000000 | bytes 1024 | tf_op jit(solution)/shard_map/expert_block/pallas_call | solution.py:455
  145.2 2.3 broadcast_select_fusion.2.refs_0_.refs_1_
  148.8 2.2 broadcast_select_fusion.refs_1_
  151.7 2.8 collective-permute-start.12
  156.4 23.3 %expert_block.7 = (bf16[591,768]{1,0:T(8,128)(2,1)}, bf16[591,768]{1,0:T(8,128)(2,1)}, bf16[591,3072]{1,0:T(8,128)(2,1)}, bf16[591,3072]{1,0:T(8,128)(2,1)}, bf1...) custom-call(s32[1]{0:T(128)} %bitcast.1.me_ref, ...), custom_call_target="tpu_custom_call" | custom-call | flops 400000000 | bytes 1024 | tf_op jit(solution)/shard_map/expert_block/pallas_call | solution.py:455
  179.7 1.8 add_convert_fusion.7
  184.1 1.5 collective-permute-start.17
  185.6 5.7 %collective-permute-start.31 = (bf16[591,768]{1,0:T(8,128)(2,1)}, bf16[591,768]{1,0:T(8,128)(2,1)}, u32[]{:S(2)}, u32[]{:S(2)}) collective-permute-start(bf16[591,768]{1,0:T(8,128)(2,1)} %get-tuple-element.188), channel_id=1, source_target_pairs={{0,1},{3,2},{4,5},{7,6},{8,9},{11,10},{12,13},{15,14},{16,17},{19,... | collective-permute-start | bytes 2723336 | tf_op jit(solution)/shard_map/ppermute | solution.py:621
  191.3 14.0 %final_grads.2.refs_10_ = bf16[8,2,48,3072]{3,2,1,0:T(8,128)(2,1)} custom-call(s32[1]{0:T(128)S(6)} %sub.48.half_ref, bf16[591,768]{1,0:T(8,128)(2,1)} %broadcast_select_fusion.3.refs_0_, bf16[591,768]{1,0:T(8,128)(2,1)} %broadcast_select_fusion.2.refs_0_.refs_1_, bf16[591,3072]{1,0:T(8,128)(2,1)} %get-tuple-element.140.refs_2_, ...), custom_call_target="tpu_custom_call" | custom-call | flops 1600000000 | bytes 1024 | tf_op jit(solution)/shard_map/final_grads/pallas_call | solution.py:529
  205.3 14.1 %final_grads.3 = bf16[8,2,48,3072]{3,2,1,0:T(8,128)(2,1)} custom-call(s32[1]{0:T(128)} %bitcast.half_ref.core_ref, bf16[591,768]{1,0:T(8,128)(2,1)} %broadcast_select_fusion.3.refs_0_, bf16[591,768]{1,0:T(8,128)(2,1)} %broadcast_select_fusion.2.refs_0_.refs_1_, bf16[591,3072]{1,0:T(8,128)(2,1)} %get-tuple-element.140.refs_2_, ...), custom_call_target="tpu_custom_call" | custom-call | flops 1600000000 | bytes 1024 | tf_op jit(solution)/shard_map/final_grads/pallas_call | solution.py:529
  221.2 5.8 %add_convert_fusion.refs_23_ = bf16[8,2,48,3072]{3,2,1,0:T(8,128)(2,1)S(1)} fusion(bf16[8,2,48,3072]{3,2,1,0:T(8,128)(2,1)} %collective-permute-done.14, bf16[8,2,48,3072]{3,2,1,0:T(8,128)(2,1)} %final_grads.3), kind=kLoop, calls=%fused_computation | loop fusion | flops 9437184 | bytes 14155776 | tf_op jit(solution)/shard_map/convert_element_type | solution.py:670
  227.3 1.8 copy-done
  230.3 1.5 collective-permute-start.16
  231.9 1.6 collective-permute-start.15
  233.4 29.5 %attend_back.1 = (bf16[591,768]{1,0:T(8,128)(2,1)}, bf16[8,48,3072]{2,1,0:T(8,128)(2,1)}, bf16[8,48,3072]{2,1,0:T(8,128)(2,1)}, f32[24,768]{1,0:T(8,128)}) custom-call(s32[1]{0:T(128)} %bitcast.half_ref.core_ref, f32[8,768]{1,0:T(8,128)} %stack.45.vecs_ref, bf16[591,768]{1,0:T(8,128)(2,1)} %get-tuple-element.151.refs_0_, ...), custom_call_target="tpu_custom_call" | custom-call | flops 11200000000 | bytes 1024 | tf_op jit(solution)/shard_map/attend_back/pallas_call | solution.py:406
  264.3 1.7 add_convert_fusion.2
  266.0 1.8 add_convert_fusion.3
  268.6 1.4 add_convert_fusion.6
  270.1 2.4 collective-permute-start.32
  274.3 9.6 %collective-permute-done.20 = bf16[1,2,48,3072]{3,2,1,0:T(8,128)(2,1)S(1)} collective-permute-done((bf16[1,2,48,3072]{3,2,1,0:T(8,128)(2,1)S(1)}, bf16[1,2,48,3072]{3,2,1,0:T(8,128)(2,1)S(1)}, u32[]{:S(2)}, u32[]{:S(2)}) %collective-permute-start.20) | collective-permute-done | bytes 589856 | tf_op jit(solution)/shard_map/ppermute | solution.py:655
  284.0 5.2 %collective-permute-done.19 = bf16[1,2,48,3072]{3,2,1,0:T(8,128)(2,1)S(1)} collective-permute-done((bf16[1,2,48,3072]{3,2,1,0:T(8,128)(2,1)S(1)}, bf16[1,2,48,3072]{3,2,1,0:T(8,128)(2,1)S(1)}, u32[]{:S(2)}, u32[]{:S(2)}) %collective-permute-start.19) | collective-permute-done | bytes 589856 | tf_op jit(solution)/shard_map/ppermute | solution.py:655
  290.3 1.6 collective-permute-start.27
  293.3 2.2 collective-permute-done.27
  295.5 1.6 collective-permute-start.25
  297.1 11.4 %collective-permute-done.24 = bf16[1,2,48,3072]{3,2,1,0:T(8,128)(2,1)S(1)} collective-permute-done((bf16[1,2,48,3072]{3,2,1,0:T(8,128)(2,1)S(1)}, bf16[1,2,48,3072]{3,2,1,0:T(8,128)(2,1)S(1)}, u32[]{:S(2)}, u32[]{:S(2)}) %collective-permute-start.24) | collective-permute-done | bytes 589856 | tf_op jit(solution)/shard_map/ppermute | solution.py:655
  309.2 10.7 %collective-permute-done.25 = bf16[2,48,3072]{2,1,0:T(8,128)(2,1)S(1)} collective-permute-done((bf16[2,48,3072]{2,1,0:T(8,128)(2,1)S(1)}, bf16[2,48,3072]{2,1,0:T(8,128)(2,1)S(1)}, u32[]{:S(2)}, u32[]{:S(2)}) %collective-permute-start.25) | collective-permute-done | bytes 589856 | tf_op jit(solution)/shard_map/ppermute | solution.py:655
  320.0 1.4 collective-permute-done.23
  323.3 1.6 collective-permute-start.28
  324.9 2.5 collective-permute-done.30
  327.4 2.4 collective-permute-done.29
  332.2 6.6 %collective-permute-start.35 = (bf16[24,3072]{1,0:T(8,128)(2,1)}, bf16[24,3072]{1,0:T(8,128)(2,1)S(1)}, u32[]{:S(2)}, u32[]{:S(2)}) collective-permute-start(bf16[24,3072]{1,0:T(8,128)(2,1)} %get-tuple-element.233), channel_id=1, source_target_pairs={{0,1},{1,2},{2,3},{3,0},{4,5},{5,6},{6,7},{7,4},{8,9},{9,10},{10,1... | collective-permute-start | bytes 442376 | tf_op jit(solution)/shard_map/ppermute | solution.py:573
  339.5 2.9 collective-permute-start.37
  343.6 1.7 collective-permute-start.44
  345.3 2.0 collective-permute-done.36
  347.4 3.0 collective-permute-start.41
  350.4 3.4 collective-permute-start.42
  353.8 1.4 collective-permute-done.41
  355.9 1.6 collective-permute-done.42
  357.5 1.8 collective-permute-start.39
  359.4 2.1 collective-permute-start.40
  361.5 1.5 collective-permute-done.38
  363.1 4.6 %collective-permute-done.39 = bf16[24,3072]{1,0:T(8,128)(2,1)S(1)} collective-permute-done((bf16[24,3072]{1,0:T(8,128)(2,1)S(1)}, bf16[24,3072]{1,0:T(8,128)(2,1)S(1)}, u32[]{:S(2)}, u32[]{:S(2)}) %collective-permute-start.39) | collective-permute-done | bytes 147488 | tf_op jit(solution)/shard_map/ppermute | solution.py:573
  368.1 2.3 pad_maximum_fusion.refs_0_
  371.0 1.7 collective-permute-start.47
  372.7 1.5 collective-permute-start.46
  374.2 5.8 %collective-permute-done.47 = bf16[1,48,3072]{2,1,0:T(8,128)(2,1)S(1)} collective-permute-done((bf16[1,48,3072]{2,1,0:T(8,128)(2,1)S(1)}, bf16[1,48,3072]{2,1,0:T(8,128)(2,1)S(1)}, u32[]{:S(2)}, u32[]{:S(2)}) %collective-permute-start.47) | collective-permute-done | bytes 294944 | tf_op jit(solution)/shard_map/ppermute | solution.py:655
  382.8 1.4 copy-done.9
  384.3 1.5 collective-permute-start.51
  386.8 11.3 %assemble.2 = (f32[768,3072]{1,0:T(8,128)}, f32[4,768,768]{2,1,0:T(8,128)}) custom-call(s32[3]{0:T(128)} %pad_add_fusion.ids_ref, bf16[4,2,48,3072]{3,2,1,0:T(8,128)(2,1)} %copy-done.2, bf16[4,2,48,3072]{3,2,1,0:T(8,128)(2,1)} %copy-done.1, bf16[4,2,48,3072]{3,2,1,0:T(8,128)(2,1)} %copy-done.8, bf16[4,2,48,3072]{3,2,1,0:T(8,128)(2,1)} %copy-done.9), custom_call_target="tpu_custom_call" | custom-call | flops 2000000000 | bytes 1024 | tf_op jit(solution)/shard_map/assemble/pallas_call | solution.py:556
  401.0 1.5 add_convert_fusion.4
  407.1 6.9 %assemble.3 = (f32[768,2304]{1,0:T(8,128)}, f32[768,768]{1,0:T(8,128)}) custom-call(s32[3]{0:T(128)} %pad_add_fusion.ids_ref, bf16[4,48,3072]{2,1,0:T(8,128)(2,1)} %copy-done.12, bf16[4,48,3072]{2,1,0:T(8,128)(2,1)} %copy-done.11, bf16[4,48,3072]{2,1,0:T(8,128)(2,1)} %copy-done.32, bf16[4,48,3072]{2,1,0:T(8,128)(2,1)} %copy-done.33), custom_call_target="tpu_custom_call" | custom-call | flops 2000000000 | bytes 1024 | tf_op jit(solution)/shard_map/assemble/pallas_call | solution.py:556
  (194 shorter events, 46.8 us)
Async XLA Ops:
  0.7 5.9 %copy-start.27 = (f32[768]{0:T(1024)S(1)}, f32[768]{0:T(1024)}, u32[]{:S(2)}) copy-start(f32[768]{0:T(1024)} %param.25) | copy-start | bytes 9220
  0.7 5.9 %copy-start.28 = (f32[768]{0:T(1024)S(1)}, f32[768]{0:T(1024)}, u32[]{:S(2)}) copy-start(f32[768]{0:T(1024)} %param.27) | copy-start | bytes 9220
  0.7 5.9 %copy-start.29 = (f32[768]{0:T(1024)S(1)}, f32[768]{0:T(1024)}, u32[]{:S(2)}) copy-start(f32[768]{0:T(1024)} %param.28) | copy-start | bytes 9220
  0.7 5.9 %copy-start.30 = (f32[768]{0:T(1024)S(1)}, f32[768]{0:T(1024)}, u32[]{:S(2)}) copy-start(f32[768]{0:T(1024)} %param.29) | copy-start | bytes 9220
  2.7 16.2 %copy-start.15 = (bf16[608,768]{1,0:T(8,128)(2,1)}, bf16[608,768]{1,0:T(8,128)(2,1)S(1)}, u32[]{:S(2)}) copy-start(bf16[608,768]{1,0:T(8,128)(2,1)S(1)} %fusion.1.refs_1_) | copy-start | bytes 2801668
  2.7 24.7 %collective-permute-start.2 = (bf16[608,768]{1,0:T(8,128)(2,1)S(1)}, bf16[608,768]{1,0:T(8,128)(2,1)}, u32[]{:S(2)}, u32[]{:S(2)}) collective-permute-start(bf16[608,768]{1,0:T(8,128)(2,1)S(1)} %fusion.1.refs_1_), channel_id=1, source_target_pairs={{0,1},{1,0},{2,3},{3,2},{4,5},{5,4},{6,7},{7,6},{8,9},{9,8},{10,11... | collective-permute-start | bytes 2801672 | tf_op jit(solution)/shard_map/ppermute | solution.py:655
  5.8 21.6 %collective-permute-start.3 = (bf16[608,768]{1,0:T(8,128)(2,1)S(1)}, bf16[608,768]{1,0:T(8,128)(2,1)S(1)}, u32[]{:S(2)}, u32[]{:S(2)}) collective-permute-start(bf16[608,768]{1,0:T(8,128)(2,1)S(1)} %fusion.1.refs_1_), channel_id=1, source_target_pairs={{1,2},{2,1},{5,6},{6,5},{9,10},{10,9},{13,14},{14,13},{17,18},{18,... | collective-permute-start | bytes 2801672 | tf_op jit(solution)/shard_map/ppermute | solution.py:589
  7.3 17.5 %copy-start.23 = (bf16[768,4]{0,1:T(4,128)(2,1)S(1)}, bf16[768,4]{0,1:T(4,128)(2,1)}, u32[]{:S(2)}) copy-start(bf16[768,4]{0,1:T(4,128)(2,1)} %param.30) | copy-start | bytes 18436
  18.9 34.1 %collective-permute-start = (bf16[591,768]{1,0:T(8,128)(2,1)}, bf16[591,768]{1,0:T(8,128)(2,1)}, u32[]{:S(2)}, u32[]{:S(2)}) collective-permute-start(bf16[591,768]{1,0:T(8,128)(2,1)} %get-tuple-element.125.refs_0_), channel_id=1, source_target_pairs={{0,1},{1,0},{2,3},{3,2},{4,5},{5,4},{6,7},{7,6},{8,9},{9,8},{10,11... | collective-permute-start | bytes 2723336 | tf_op jit(solution)/shard_map/ppermute | solution.py:655
  23.3 29.7 %collective-permute-start.1 = (bf16[591,768]{1,0:T(8,128)(2,1)}, bf16[591,768]{1,0:T(8,128)(2,1)}, u32[]{:S(2)}, u32[]{:S(2)}) collective-permute-start(bf16[591,768]{1,0:T(8,128)(2,1)} %get-tuple-element.125.refs_0_), channel_id=1, source_target_pairs={{1,2},{2,1},{5,6},{6,5},{9,10},{10,9},{13,14},{14,13},{17,18},{18,... | collective-permute-start | bytes 2723336 | tf_op jit(solution)/shard_map/ppermute | solution.py:589
  27.4 73.8 %collective-permute-start.8 = (bf16[608,768]{1,0:T(8,128)(2,1)}, bf16[608,768]{1,0:T(8,128)(2,1)S(1)}, u32[]{:S(2)}, u32[]{:S(2)}) collective-permute-start(bf16[608,768]{1,0:T(8,128)(2,1)} %collective-permute-done.2.refs_8_.refs_1_), channel_id=1, source_target_pairs={{1,2},{2,1},{5,6},{6,5},{9,10},{10,9},{13,14},{14,13},{17,18},{18,... | collective-permute-start | bytes 2801672 | tf_op jit(solution)/shard_map/ppermute | solution.py:593
  28.2 92.7 %collective-permute-start.7 = (bf16[608,768]{1,0:T(8,128)(2,1)S(1)}, bf16[608,768]{1,0:T(8,128)(2,1)S(1)}, u32[]{:S(2)}, u32[]{:S(2)}) collective-permute-start(bf16[608,768]{1,0:T(8,128)(2,1)S(1)} %collective-permute-done.3.refs_9_), channel_id=1, source_target_pairs={{1,0},{2,3},{5,4},{6,7},{9,8},{10,11},{13,12},{14,15},{17,16},{18,... | collective-permute-start | bytes 2801672 | tf_op jit(solution)/shard_map/ppermute | solution.py:594
  53.0 46.9 %collective-permute-start.5 = (bf16[591,768]{1,0:T(8,128)(2,1)}, bf16[591,768]{1,0:T(8,128)(2,1)}, u32[]{:S(2)}, u32[]{:S(2)}) collective-permute-start(bf16[591,768]{1,0:T(8,128)(2,1)} %collective-permute-done.refs_0_.refs_1_), channel_id=1, source_target_pairs={{1,2},{2,1},{5,6},{6,5},{9,10},{10,9},{13,14},{14,13},{17,18},{18,... | collective-permute-start | bytes 2723336 | tf_op jit(solution)/shard_map/ppermute | solution.py:593
  54.6 62.2 %collective-permute-start.4 = (bf16[591,768]{1,0:T(8,128)(2,1)}, bf16[591,768]{1,0:T(8,128)(2,1)}, u32[]{:S(2)}, u32[]{:S(2)}) collective-permute-start(bf16[591,768]{1,0:T(8,128)(2,1)} %collective-permute-done.1), channel_id=1, source_target_pairs={{1,0},{2,3},{5,4},{6,7},{9,8},{10,11},{13,12},{14,15},{17,16},{18,... | collective-permute-start | bytes 2723336 | tf_op jit(solution)/shard_map/ppermute | solution.py:594
  99.9 45.2 %collective-permute-start.6 = (bf16[591,768]{1,0:T(8,128)(2,1)}, bf16[591,768]{1,0:T(8,128)(2,1)}, u32[]{:S(2)}, u32[]{:S(2)}) collective-permute-start(bf16[591,768]{1,0:T(8,128)(2,1)} %collective-permute-done.5), channel_id=1, source_target_pairs={{1,0},{2,3},{5,4},{6,7},{9,8},{10,11},{13,12},{14,15},{17,16},{18,... | collective-permute-start | bytes 2723336 | tf_op jit(solution)/shard_map/ppermute | solution.py:598
  101.2 47.5 %collective-permute-start.9 = (bf16[608,768]{1,0:T(8,128)(2,1)S(1)}, bf16[608,768]{1,0:T(8,128)(2,1)}, u32[]{:S(2)}, u32[]{:S(2)}) collective-permute-start(bf16[608,768]{1,0:T(8,128)(2,1)S(1)} %collective-permute-done.8), channel_id=1, source_target_pairs={{1,0},{2,3},{5,4},{6,7},{9,8},{10,11},{13,12},{14,15},{17,16},{18,... | collective-permute-start | bytes 2801672 | tf_op jit(solution)/shard_map/ppermute | solution.py:598
  102.6 52.9 %collective-permute-start.10 = (bf16[591,768]{1,0:T(8,128)(2,1)}, bf16[591,768]{1,0:T(8,128)(2,1)}, u32[]{:S(2)}, u32[]{:S(2)}) collective-permute-start(bf16[591,768]{1,0:T(8,128)(2,1)} %get-tuple-element.141), channel_id=1, source_target_pairs={{0,1},{3,2},{4,5},{7,6},{8,9},{11,10},{12,13},{15,14},{16,17},{19,... | collective-permute-start | bytes 2723336 | tf_op jit(solution)/shard_map/ppermute | solution.py:616
  116.8 38.6 %collective-permute-start.11 = (bf16[591,768]{1,0:T(8,128)(2,1)}, bf16[591,768]{1,0:T(8,128)(2,1)S(1)}, u32[]{:S(2)}, u32[]{:S(2)}) collective-permute-start(bf16[591,768]{1,0:T(8,128)(2,1)} %get-tuple-element.142), channel_id=1, source_target_pairs={{0,1},{3,2},{4,5},{7,6},{8,9},{11,10},{12,13},{15,14},{16,17},{19,... | collective-permute-start | bytes 2723336 | tf_op jit(solution)/shard_map/ppermute | solution.py:616
  151.0 28.7 %collective-permute-start.13 = (bf16[591,768]{1,0:T(8,128)(2,1)}, bf16[591,768]{1,0:T(8,128)(2,1)S(1)}, u32[]{:S(2)}, u32[]{:S(2)}) collective-permute-start(bf16[591,768]{1,0:T(8,128)(2,1)} %get-tuple-element.150), channel_id=1, source_target_pairs={{1,2},{2,1},{5,6},{6,5},{9,10},{10,9},{13,14},{14,13},{17,18},{18,... | collective-permute-start | bytes 2723336 | tf_op jit(solution)/shard_map/ppermute | solution.py:622
  151.7 31.1 %collective-permute-start.12 = (bf16[591,768]{1,0:T(8,128)(2,1)}, bf16[591,768]{1,0:T(8,128)(2,1)S(1)}, u32[]{:S(2)}, u32[]{:S(2)}) collective-permute-start(bf16[591,768]{1,0:T(8,128)(2,1)} %get-tuple-element.150), channel_id=1, source_target_pairs={{0,1},{3,2},{4,5},{7,6},{8,9},{11,10},{12,13},{15,14},{16,17},{19,... | collective-permute-start | bytes 2723336 | tf_op jit(solution)/shard_map/ppermute | solution.py:621
  154.5 64.9 %collective-permute-start.33 = (bf16[591,768]{1,0:T(8,128)(2,1)}, bf16[591,768]{1,0:T(8,128)(2,1)S(1)}, u32[]{:S(2)}, u32[]{:S(2)}) collective-permute-start(bf16[591,768]{1,0:T(8,128)(2,1)} %get-tuple-element.188), channel_id=1, source_target_pairs={{1,2},{2,1},{5,6},{6,5},{9,10},{10,9},{13,14},{14,13},{17,18},{18,... | collective-permute-start | bytes 2723336 | tf_op jit(solution)/shard_map/ppermute | solution.py:622
  181.5 39.1 %collective-permute-start.18 = (bf16[591,768]{1,0:T(8,128)(2,1)S(1)}, bf16[591,768]{1,0:T(8,128)(2,1)}, u32[]{:S(2)}, u32[]{:S(2)}) collective-permute-start(bf16[591,768]{1,0:T(8,128)(2,1)S(1)} %add_convert_fusion.7), channel_id=1, source_target_pairs={{1,0},{2,3},{5,4},{6,7},{9,8},{10,11},{13,12},{14,15},{17,16},{18,... | collective-permute-start | bytes 2723336 | tf_op jit(solution)/shard_map/ppermute | solution.py:631
  182.8 8.4 %copy-start.6 = (bf16[591,768]{1,0:T(8,128)(2,1)}, bf16[591,768]{1,0:T(8,128)(2,1)S(1)}, u32[]{:S(2)}) copy-start(bf16[591,768]{1,0:T(8,128)(2,1)S(1)} %collective-permute-done.12.refs_10_) | copy-start | bytes 2723332
  184.1 36.6 %collective-permute-start.17 = (bf16[591,768]{1,0:T(8,128)(2,1)}, bf16[591,768]{1,0:T(8,128)(2,1)}, u32[]{:S(2)}, u32[]{:S(2)}) collective-permute-start(bf16[591,768]{1,0:T(8,128)(2,1)} %add_convert_fusion.8), channel_id=1, source_target_pairs={{0,3},{1,2},{2,1},{3,0},{4,7},{5,6},{6,5},{7,4},{8,11},{9,10},{10,... | collective-permute-start | bytes 2723336 | tf_op jit(solution)/shard_map/ppermute | solution.py:655
  185.6 83.1 %collective-permute-start.31 = (bf16[591,768]{1,0:T(8,128)(2,1)}, bf16[591,768]{1,0:T(8,128)(2,1)}, u32[]{:S(2)}, u32[]{:S(2)}) collective-permute-start(bf16[591,768]{1,0:T(8,128)(2,1)} %get-tuple-element.188), channel_id=1, source_target_pairs={{0,1},{3,2},{4,5},{7,6},{8,9},{11,10},{12,13},{15,14},{16,17},{19,... | collective-permute-start | bytes 2723336 | tf_op jit(solution)/shard_map/ppermute | solution.py:621
  205.2 14.2 %copy-start.19 = (bf16[591,768]{1,0:T(8,128)(2,1)S(1)}, bf16[591,768]{1,0:T(8,128)(2,1)}, u32[]{:S(2)}) copy-start(bf16[591,768]{1,0:T(8,128)(2,1)} %get-tuple-element.142) | copy-start | bytes 2723332
  205.3 16.0 %collective-permute-start.14 = (bf16[8,2,48,3072]{3,2,1,0:T(8,128)(2,1)}, bf16[8,2,48,3072]{3,2,1,0:T(8,128)(2,1)}, u32[]{:S(2)}, u32[]{:S(2)}) collective-permute-start(bf16[8,2,48,3072]{3,2,1,0:T(8,128)(2,1)} %final_grads.2.refs_10_), channel_id=1, source_target_pairs={{0,4},{4,0},{8,12},{12,8},{16,20},{20,16},{24,28},{28,24},{1,5},{5... | collective-permute-start | bytes 14155784 | tf_op jit(solution)/shard_map/ppermute | solution.py:655
  230.3 34.0 %collective-permute-start.16 = (bf16[2,2,48,3072]{3,2,1,0:T(8,128)(2,1)}, bf16[2,2,48,3072]{3,2,1,0:T(8,128)(2,1)}, u32[]{:S(2)}, u32[]{:S(2)}) collective-permute-start(bf16[2,2,48,3072]{3,2,1,0:T(8,128)(2,1)} %constant_dynamic-slice_fusion.9), channel_id=1, source_target_pairs={{0,16},{4,20},{8,24},{12,28},{16,0},{20,4},{24,8},{28,12},{1,17},{... | collective-permute-start | bytes 3538952 | tf_op jit(solution)/shard_map/ppermute | solution.py:655
  231.9 34.1 %collective-permute-start.15 = (bf16[2,2,48,3072]{3,2,1,0:T(8,128)(2,1)S(1)}, bf16[2,2,48,3072]{3,2,1,0:T(8,128)(2,1)}, u32[]{:S(2)}, u32[]{:S(2)}) collective-permute-start(bf16[2,2,48,3072]{3,2,1,0:T(8,128)(2,1)S(1)} %constant_dynamic-slice_fusion.10), channel_id=1, source_target_pairs={{0,8},{4,12},{8,0},{12,4},{16,24},{20,28},{24,16},{28,20},{1,9},{5... | collective-permute-start | bytes 3538952 | tf_op jit(solution)/shard_map/ppermute | solution.py:655
  263.0 67.7 %collective-permute-start.34 = (bf16[591,768]{1,0:T(8,128)(2,1)}, bf16[591,768]{1,0:T(8,128)(2,1)S(1)}, u32[]{:S(2)}, u32[]{:S(2)}) collective-permute-start(bf16[591,768]{1,0:T(8,128)(2,1)} %add_convert_fusion.5), channel_id=1, source_target_pairs={{1,0},{2,3},{5,4},{6,7},{9,8},{10,11},{13,12},{14,15},{17,16},{18,... | collective-permute-start | bytes 2723336 | tf_op jit(solution)/shard_map/ppermute | solution.py:631
  268.0 21.3 %collective-permute-start.21 = (bf16[8,48,3072]{2,1,0:T(8,128)(2,1)S(1)}, bf16[8,48,3072]{2,1,0:T(8,128)(2,1)S(1)}, u32[]{:S(2)}, u32[]{:S(2)}) collective-permute-start(bf16[8,48,3072]{2,1,0:T(8,128)(2,1)S(1)} %copy-done.31), channel_id=1, source_target_pairs={{0,4},{4,0},{8,12},{12,8},{16,20},{20,16},{24,28},{28,24},{1,5},{5... | collective-permute-start | bytes 7077896 | tf_op jit(solution)/shard_map/ppermute | solution.py:655
  268.0 15.8 %collective-permute-start.20 = (bf16[1,2,48,3072]{3,2,1,0:T(8,128)(2,1)S(1)}, bf16[1,2,48,3072]{3,2,1,0:T(8,128)(2,1)S(1)}, u32[]{:S(2)}, u32[]{:S(2)}) collective-permute-start(bf16[1,2,48,3072]{3,2,1,0:T(8,128)(2,1)S(1)} %constant_dynamic-slice_fusion.7), channel_id=1, source_target_pairs={{0,8},{4,12},{8,0},{12,4},{16,24},{20,28},{24,16},{28,20},{1,9},{5... | collective-permute-start | bytes 1769480 | tf_op jit(solution)/shard_map/ppermute | solution.py:655
  270.1 60.6 %collective-permute-start.32 = (bf16[591,768]{1,0:T(8,128)(2,1)S(1)}, bf16[591,768]{1,0:T(8,128)(2,1)S(1)}, u32[]{:S(2)}, u32[]{:S(2)}) collective-permute-start(bf16[591,768]{1,0:T(8,128)(2,1)S(1)} %add_convert_fusion.6), channel_id=1, source_target_pairs={{0,3},{1,2},{2,1},{3,0},{4,7},{5,6},{6,5},{7,4},{8,11},{9,10},{10,... | collective-permute-start | bytes 2723336 | tf_op jit(solution)/shard_map/ppermute | solution.py:655
  272.5 1.3 collective-permute-start.22
  273.8 15.4 %collective-permute-start.19 = (bf16[1,2,48,3072]{3,2,1,0:T(8,128)(2,1)S(1)}, bf16[1,2,48,3072]{3,2,1,0:T(8,128)(2,1)S(1)}, u32[]{:S(2)}, u32[]{:S(2)}) collective-permute-start(bf16[1,2,48,3072]{3,2,1,0:T(8,128)(2,1)S(1)} %constant_dynamic-slice_fusion.8), channel_id=1, source_target_pairs={{0,16},{4,20},{8,24},{12,28},{16,0},{20,4},{24,8},{28,12},{1,17},{... | collective-permute-start | bytes 1769480 | tf_op jit(solution)/shard_map/ppermute | solution.py:655
  274.3 15.0 %copy-start.7 = (bf16[8,48,3072]{2,1,0:T(8,128)(2,1)S(1)}, bf16[8,48,3072]{2,1,0:T(8,128)(2,1)}, u32[]{:S(2)}) copy-start(bf16[8,48,3072]{2,1,0:T(8,128)(2,1)} %get-tuple-element.172) | copy-start | bytes 7077892
  290.3 5.2 %collective-permute-start.27 = (f32[24,768]{1,0:T(8,128)S(1)}, f32[24,768]{1,0:T(8,128)S(1)}, u32[]{:S(2)}, u32[]{:S(2)}) collective-permute-start(f32[24,768]{1,0:T(8,128)S(1)} %add.232), channel_id=1, source_target_pairs={{0,8},{4,12},{8,0},{12,4},{16,24},{20,28},{24,16},{28,20},{1,9},{5... | collective-permute-start | bytes 221192 | tf_op jit(solution)/shard_map/ppermute | solution.py:655
  292.1 16.3 %collective-permute-start.24 = (bf16[1,2,48,3072]{3,2,1,0:T(8,128)(2,1)S(1)}, bf16[1,2,48,3072]{3,2,1,0:T(8,128)(2,1)S(1)}, u32[]{:S(2)}, u32[]{:S(2)}) collective-permute-start(bf16[1,2,48,3072]{3,2,1,0:T(8,128)(2,1)S(1)} %add_convert_fusion.11), channel_id=1, source_target_pairs={{0,8},{4,12},{8,0},{12,4},{16,24},{20,28},{24,16},{28,20},{1,9},{5... | collective-permute-start | bytes 1769480 | tf_op jit(solution)/shard_map/ppermute | solution.py:655
  292.7 16.3 %collective-permute-start.26 = (bf16[2,48,3072]{2,1,0:T(8,128)(2,1)S(1)}, bf16[2,48,3072]{2,1,0:T(8,128)(2,1)S(1)}, u32[]{:S(2)}, u32[]{:S(2)}) collective-permute-start(bf16[2,48,3072]{2,1,0:T(8,128)(2,1)S(1)} %constant_dynamic-slice_fusion.5), channel_id=1, source_target_pairs={{0,16},{4,20},{8,24},{12,28},{16,0},{20,4},{24,8},{28,12},{1,17},{... | collective-permute-start | bytes 1769480 | tf_op jit(solution)/shard_map/ppermute | solution.py:655
  295.5 24.4 %collective-permute-start.25 = (bf16[2,48,3072]{2,1,0:T(8,128)(2,1)S(1)}, bf16[2,48,3072]{2,1,0:T(8,128)(2,1)S(1)}, u32[]{:S(2)}, u32[]{:S(2)}) collective-permute-start(bf16[2,48,3072]{2,1,0:T(8,128)(2,1)S(1)} %constant_dynamic-slice_fusion.6), channel_id=1, source_target_pairs={{0,8},{4,12},{8,0},{12,4},{16,24},{20,28},{24,16},{28,20},{1,9},{5... | collective-permute-start | bytes 1769480 | tf_op jit(solution)/shard_map/ppermute | solution.py:655
  308.4 13.0 %collective-permute-start.23 = (bf16[1,2,48,3072]{3,2,1,0:T(8,128)(2,1)S(1)}, bf16[1,2,48,3072]{3,2,1,0:T(8,128)(2,1)S(1)}, u32[]{:S(2)}, u32[]{:S(2)}) collective-permute-start(bf16[1,2,48,3072]{3,2,1,0:T(8,128)(2,1)S(1)} %add_convert_fusion.12), channel_id=1, source_target_pairs={{0,16},{4,20},{8,24},{12,28},{16,0},{20,4},{24,8},{28,12},{1,17},{... | collective-permute-start | bytes 1769480 | tf_op jit(solution)/shard_map/ppermute | solution.py:655
  322.5 4.9 %collective-permute-start.30 = (f32[24,768]{1,0:T(8,128)S(1)}, f32[24,768]{1,0:T(8,128)S(1)}, u32[]{:S(2)}, u32[]{:S(2)}) collective-permute-start(f32[24,768]{1,0:T(8,128)S(1)} %add.235), channel_id=1, source_target_pairs={{0,16},{4,20},{8,24},{12,28},{16,0},{20,4},{24,8},{28,12},{1,17},{... | collective-permute-start | bytes 221192 | tf_op jit(solution)/shard_map/ppermute | solution.py:655
  323.0 6.8 %collective-permute-start.29 = (bf16[1,48,3072]{2,1,0:T(8,128)(2,1)S(1)}, bf16[1,48,3072]{2,1,0:T(8,128)(2,1)S(1)}, u32[]{:S(2)}, u32[]{:S(2)}) collective-permute-start(bf16[1,48,3072]{2,1,0:T(8,128)(2,1)S(1)} %constant_dynamic-slice_fusion.3), channel_id=1, source_target_pairs={{0,8},{4,12},{8,0},{12,4},{16,24},{20,28},{24,16},{28,20},{1,9},{5... | collective-permute-start | bytes 884744 | tf_op jit(solution)/shard_map/ppermute | solution.py:655
  323.3 7.2 %collective-permute-start.28 = (bf16[1,48,3072]{2,1,0:T(8,128)(2,1)S(1)}, bf16[1,48,3072]{2,1,0:T(8,128)(2,1)S(1)}, u32[]{:S(2)}, u32[]{:S(2)}) collective-permute-start(bf16[1,48,3072]{2,1,0:T(8,128)(2,1)S(1)} %constant_dynamic-slice_fusion.4), channel_id=1, source_target_pairs={{0,16},{4,20},{8,24},{12,28},{16,0},{20,4},{24,8},{28,12},{1,17},{... | collective-permute-start | bytes 884744 | tf_op jit(solution)/shard_map/ppermute | solution.py:655
  332.2 13.1 %collective-permute-start.35 = (bf16[24,3072]{1,0:T(8,128)(2,1)}, bf16[24,3072]{1,0:T(8,128)(2,1)S(1)}, u32[]{:S(2)}, u32[]{:S(2)}) collective-permute-start(bf16[24,3072]{1,0:T(8,128)(2,1)} %get-tuple-element.233), channel_id=1, source_target_pairs={{0,1},{1,2},{2,3},{3,0},{4,5},{5,6},{6,7},{7,4},{8,9},{9,10},{10,1... | collective-permute-start | bytes 442376 | tf_op jit(solution)/shard_map/ppermute | solution.py:573
  338.8 8.5 %collective-permute-start.36 = (bf16[24,3072]{1,0:T(8,128)(2,1)S(1)}, bf16[24,3072]{1,0:T(8,128)(2,1)S(1)}, u32[]{:S(2)}, u32[]{:S(2)}) collective-permute-start(bf16[24,3072]{1,0:T(8,128)(2,1)S(1)} %get-tuple-element.235), channel_id=1, source_target_pairs={{0,2},{1,3},{2,0},{3,1},{4,6},{5,7},{6,4},{7,5},{8,10},{9,11},{10,... | collective-permute-start | bytes 442376 | tf_op jit(solution)/shard_map/ppermute | solution.py:573
  339.5 7.8 %collective-permute-start.37 = (bf16[24,3072]{1,0:T(8,128)(2,1)S(1)}, bf16[24,3072]{1,0:T(8,128)(2,1)S(1)}, u32[]{:S(2)}, u32[]{:S(2)}) collective-permute-start(bf16[24,3072]{1,0:T(8,128)(2,1)S(1)} %get-tuple-element.234), channel_id=1, source_target_pairs={{0,3},{1,0},{2,1},{3,2},{4,7},{5,4},{6,5},{7,6},{8,11},{9,8},{10,9... | collective-permute-start | bytes 442376 | tf_op jit(solution)/shard_map/ppermute | solution.py:573
  342.4 25.4 %collective-permute-start.45 = (bf16[2,2,48,3072]{3,2,1,0:T(8,128)(2,1)S(1)}, bf16[2,2,48,3072]{3,2,1,0:T(8,128)(2,1)S(1)}, u32[]{:S(2)}, u32[]{:S(2)}) collective-permute-start(bf16[2,2,48,3072]{3,2,1,0:T(8,128)(2,1)S(1)} %pad_maximum_fusion.3), channel_id=1, source_target_pairs={{0,16},{4,20},{8,24},{12,28},{16,0},{20,4},{24,8},{28,12},{1,17},{... | collective-permute-start | bytes 3538952 | tf_op jit(solution)/shard_map/ppermute | solution.py:655
  343.6 24.5 %collective-permute-start.44 = (bf16[2,2,48,3072]{3,2,1,0:T(8,128)(2,1)}, bf16[2,2,48,3072]{3,2,1,0:T(8,128)(2,1)S(1)}, u32[]{:S(2)}, u32[]{:S(2)}) collective-permute-start(bf16[2,2,48,3072]{3,2,1,0:T(8,128)(2,1)} %pad_maximum_fusion.2), channel_id=1, source_target_pairs={{0,8},{4,12},{8,0},{12,4},{16,24},{20,28},{24,16},{28,20},{1,9},{5... | collective-permute-start | bytes 3538952 | tf_op jit(solution)/shard_map/ppermute | solution.py:655
  347.4 7.9 %collective-permute-start.41 = (f32[16,768]{1,0:T(8,128)S(1)}, f32[16,768]{1,0:T(8,128)S(1)}, u32[]{:S(2)}, u32[]{:S(2)}) collective-permute-start(f32[16,768]{1,0:T(8,128)S(1)} %slice.84), channel_id=1, source_target_pairs={{0,1},{1,2},{2,3},{3,0},{4,5},{5,6},{6,7},{7,4},{8,9},{9,10},{10,1... | collective-permute-start | bytes 147464 | tf_op jit(solution)/shard_map/ppermute | solution.py:573
  350.4 7.2 %collective-permute-start.42 = (f32[16,768]{1,0:T(8,128)S(1)}, f32[16,768]{1,0:T(8,128)S(1)}, u32[]{:S(2)}, u32[]{:S(2)}) collective-permute-start(f32[16,768]{1,0:T(8,128)S(1)} %slice.84), channel_id=1, source_target_pairs={{0,2},{1,3},{2,0},{3,1},{4,6},{5,7},{6,4},{7,5},{8,10},{9,11},{10,... | collective-permute-start | bytes 147464 | tf_op jit(solution)/shard_map/ppermute | solution.py:573
  353.8 5.6 %collective-permute-start.43 = (f32[16,768]{1,0:T(8,128)S(1)}, f32[16,768]{1,0:T(8,128)S(1)}, u32[]{:S(2)}, u32[]{:S(2)}) collective-permute-start(f32[16,768]{1,0:T(8,128)S(1)} %slice.84), channel_id=1, source_target_pairs={{0,3},{1,0},{2,1},{3,2},{4,7},{5,4},{6,5},{7,6},{8,11},{9,8},{10,9... | collective-permute-start | bytes 147464 | tf_op jit(solution)/shard_map/ppermute | solution.py:573
  355.3 7.8 %collective-permute-start.38 = (bf16[24,3072]{1,0:T(8,128)(2,1)S(1)}, bf16[24,3072]{1,0:T(8,128)(2,1)S(1)}, u32[]{:S(2)}, u32[]{:S(2)}) collective-permute-start(bf16[24,3072]{1,0:T(8,128)(2,1)S(1)} %add_convert_fusion.15), channel_id=1, source_target_pairs={{0,1},{1,2},{2,3},{3,0},{4,5},{5,6},{6,7},{7,4},{8,9},{9,10},{10,1... | collective-permute-start | bytes 442376 | tf_op jit(solution)/shard_map/ppermute | solution.py:573
  357.5 10.2 %collective-permute-start.39 = (bf16[24,3072]{1,0:T(8,128)(2,1)S(1)}, bf16[24,3072]{1,0:T(8,128)(2,1)S(1)}, u32[]{:S(2)}, u32[]{:S(2)}) collective-permute-start(bf16[24,3072]{1,0:T(8,128)(2,1)S(1)} %add_convert_fusion.15), channel_id=1, source_target_pairs={{0,2},{1,3},{2,0},{3,1},{4,6},{5,7},{6,4},{7,5},{8,10},{9,11},{10,... | collective-permute-start | bytes 442376 | tf_op jit(solution)/shard_map/ppermute | solution.py:573
  359.4 8.4 %collective-permute-start.40 = (bf16[24,3072]{1,0:T(8,128)(2,1)S(1)}, bf16[24,3072]{1,0:T(8,128)(2,1)S(1)}, u32[]{:S(2)}, u32[]{:S(2)}) collective-permute-start(bf16[24,3072]{1,0:T(8,128)(2,1)S(1)} %add_convert_fusion.15), channel_id=1, source_target_pairs={{0,3},{1,0},{2,1},{3,2},{4,7},{5,4},{6,5},{7,6},{8,11},{9,8},{10,9... | collective-permute-start | bytes 442376 | tf_op jit(solution)/shard_map/ppermute | solution.py:573
  370.4 11.1 %copy-start.2 = (bf16[4,2,48,3072]{3,2,1,0:T(8,128)(2,1)}, bf16[4,2,48,3072]{3,2,1,0:T(8,128)(2,1)S(1)}, u32[]{:S(2)}) copy-start(bf16[4,2,48,3072]{3,2,1,0:T(8,128)(2,1)S(1)} %pad_maximum_fusion.refs_0_) | copy-start | bytes 7077892
  370.4 11.0 %collective-permute-start.48 = (bf16[4,2,48,3072]{3,2,1,0:T(8,128)(2,1)S(1)}, bf16[4,2,48,3072]{3,2,1,0:T(8,128)(2,1)S(1)}, u32[]{:S(2)}, u32[]{:S(2)}) collective-permute-start(bf16[4,2,48,3072]{3,2,1,0:T(8,128)(2,1)S(1)} %pad_maximum_fusion.refs_0_), channel_id=1, source_target_pairs={{0,4},{4,0},{8,12},{12,8},{16,20},{20,16},{24,28},{28,24},{1,5},{5... | collective-permute-start | bytes 7077896 | tf_op jit(solution)/shard_map/ppermute | solution.py:655
  370.5 11.0 %collective-permute-start.49 = (bf16[4,2,48,3072]{3,2,1,0:T(8,128)(2,1)S(1)}, bf16[4,2,48,3072]{3,2,1,0:T(8,128)(2,1)S(1)}, u32[]{:S(2)}, u32[]{:S(2)}) collective-permute-start(bf16[4,2,48,3072]{3,2,1,0:T(8,128)(2,1)S(1)} %pad_maximum_fusion.1.refs_1_), channel_id=1, source_target_pairs={{0,4},{4,0},{8,12},{12,8},{16,20},{20,16},{24,28},{28,24},{1,5},{5... | collective-permute-start | bytes 7077896 | tf_op jit(solution)/shard_map/ppermute | solution.py:655
  371.0 9.0 %collective-permute-start.47 = (bf16[1,48,3072]{2,1,0:T(8,128)(2,1)S(1)}, bf16[1,48,3072]{2,1,0:T(8,128)(2,1)S(1)}, u32[]{:S(2)}, u32[]{:S(2)}) collective-permute-start(bf16[1,48,3072]{2,1,0:T(8,128)(2,1)S(1)} %get-tuple-element.203), channel_id=1, source_target_pairs={{0,8},{4,12},{8,0},{12,4},{16,24},{20,28},{24,16},{28,20},{1,9},{5... | collective-permute-start | bytes 884744 | tf_op jit(solution)/shard_map/ppermute | solution.py:655
  372.7 8.7 %collective-permute-start.46 = (bf16[1,48,3072]{2,1,0:T(8,128)(2,1)S(1)}, bf16[1,48,3072]{2,1,0:T(8,128)(2,1)S(1)}, u32[]{:S(2)}, u32[]{:S(2)}) collective-permute-start(bf16[1,48,3072]{2,1,0:T(8,128)(2,1)S(1)} %get-tuple-element.202), channel_id=1, source_target_pairs={{0,16},{4,20},{8,24},{12,28},{16,0},{20,4},{24,8},{28,12},{1,17},{... | collective-permute-start | bytes 884744 | tf_op jit(solution)/shard_map/ppermute | solution.py:655
  384.3 14.2 %collective-permute-start.51 = (bf16[2,48,3072]{2,1,0:T(8,128)(2,1)S(1)}, bf16[2,48,3072]{2,1,0:T(8,128)(2,1)S(1)}, u32[]{:S(2)}, u32[]{:S(2)}) collective-permute-start(bf16[2,48,3072]{2,1,0:T(8,128)(2,1)S(1)} %pad_maximum_fusion.8), channel_id=1, source_target_pairs={{0,16},{4,20},{8,24},{12,28},{16,0},{20,4},{24,8},{28,12},{1,17},{... | collective-permute-start | bytes 1769480 | tf_op jit(solution)/shard_map/ppermute | solution.py:655
  385.8 13.9 %collective-permute-start.50 = (bf16[2,48,3072]{2,1,0:T(8,128)(2,1)S(1)}, bf16[2,48,3072]{2,1,0:T(8,128)(2,1)S(1)}, u32[]{:S(2)}, u32[]{:S(2)}) collective-permute-start(bf16[2,48,3072]{2,1,0:T(8,128)(2,1)S(1)} %pad_maximum_fusion.7), channel_id=1, source_target_pairs={{0,8},{4,12},{8,0},{12,4},{16,24},{20,28},{24,16},{28,20},{1,9},{5... | collective-permute-start | bytes 1769480 | tf_op jit(solution)/shard_map/ppermute | solution.py:655
  399.8 5.2 %collective-permute-start.52 = (bf16[4,48,3072]{2,1,0:T(8,128)(2,1)S(1)}, bf16[4,48,3072]{2,1,0:T(8,128)(2,1)S(1)}, u32[]{:S(2)}, u32[]{:S(2)}) collective-permute-start(bf16[4,48,3072]{2,1,0:T(8,128)(2,1)S(1)} %pad_maximum_fusion.4.refs_0_), channel_id=1, source_target_pairs={{0,4},{4,0},{8,12},{12,8},{16,20},{20,16},{24,28},{28,24},{1,5},{5... | collective-permute-start | bytes 3538952 | tf_op jit(solution)/shard_map/ppermute | solution.py:655
  399.9 5.1 %collective-permute-start.53 = (bf16[4,48,3072]{2,1,0:T(8,128)(2,1)S(1)}, bf16[4,48,3072]{2,1,0:T(8,128)(2,1)S(1)}, u32[]{:S(2)}, u32[]{:S(2)}) collective-permute-start(bf16[4,48,3072]{2,1,0:T(8,128)(2,1)S(1)} %pad_maximum_fusion.5.refs_1_), channel_id=1, source_target_pairs={{0,4},{4,0},{8,12},{12,8},{16,20},{20,16},{24,28},{28,24},{1,5},{5... | collective-permute-start | bytes 3538952 | tf_op jit(solution)/shard_map/ppermute | solution.py:655
  (24 other events, 68.2 us)
